TPU v7x, 32 devices: a whole 2x2x4 slice. The times are simulated.
32 devices in a mesh: row: 8 (over y, x, core), col: 4 (over z).
Axes of the slice: x: 2, y: 2, z: 4, core: 2. Of those that a mesh axis runs over, the one named last changes fastest.
Arguments:
- inputs: bfloat16 [2048, 2048], P('row', 'col'), may hold values from -6 to 6
- cotangent: bfloat16 [2048, 2048], P('row', 'col'), may hold values from -6 to 6
- lengths: int32 [8], P('row'), may hold values from 128 to 256, as said below
- adapter_pick: int32 [8], P('row'), may hold values from 0 to 7
- attn_route: int32 [2048, 2], P('row'), may hold values from 0 to 7, all different within a row; in each aligned block of 256 rows (0 to 255, 256 to 511, ...) at most 80 rows name the same one
- ffn_route: int32 [2048, 2], P('row'), may hold values from 0 to 3, all different within a row; in each aligned block of 256 rows (0 to 255, 256 to 511, ...) at most 160 rows name the same one
- norm_one: float32 [2048], replicated, may hold values from 0.5 to 1.5
- norm_two: float32 [2048], replicated, may hold values from 0.5 to 1.5
- router_attn: bfloat16 [2048, 8], replicated, may hold values from -0.09375 to 0.09375
- router_ffn: bfloat16 [2048, 4], replicated, may hold values from -0.09375 to 0.09375
- kv_weight: bfloat16 [2, 2048, 2048], P(None, 'row', 'col'), may hold values from -0.125 to 0.125
- query_weight: bfloat16 [8, 2048, 2048], P(None, 'row', 'col'), may hold values from -0.125 to 0.125
- out_weight: bfloat16 [8, 2048, 2048], P(None, 'row', 'col'), may hold values from -0.5 to 0.5
- inner_weight: bfloat16 [4, 2048, 2, 5632], P(None, 'row', None, 'col'), may hold values from -0.125 to 0.125
- down_weight: bfloat16 [4, 2048, 5632], P(None, 'row', 'col'), may hold values from -0.078125 to 0.078125
- query_left: bfloat16 [8, 2048, 16], P(None, 'row'), may hold values from -0.125 to 0.125
- query_right: bfloat16 [8, 16, 2048], P(None, None, 'col'), may hold values from -1.5 to 1.5
- kv_left: bfloat16 [8, 2048, 16], P(None, 'row'), may hold values from -0.125 to 0.125
- kv_right: bfloat16 [8, 16, 2, 2048], P(None, None, None, 'col'), may hold values from -1.5 to 1.5
- out_left: bfloat16 [8, 2048, 16], P(None, 'row'), may hold values from -1.5 to 1.5
- out_right: bfloat16 [8, 16, 2048], P(None, None, 'col'), may hold values from -0.5 to 0.5
- inner_left: bfloat16 [8, 2048, 16], P(None, 'row'), may hold values from -0.125 to 0.125
- inner_right: bfloat16 [8, 16, 2, 5632], P(None, None, None, 'col'), may hold values from -1.5 to 1.5
- down_left: bfloat16 [8, 2048, 16], P(None, 'row'), may hold values from -1.5 to 1.5
- down_right: bfloat16 [8, 16, 5632], P(None, None, 'col'), may hold values from -0.078125 to 0.078125
Outputs:
- output: bfloat16 [2048, 2048], P('row', 'col')
- grad_inputs: float32 [2048, 2048], P('row', 'col')
- grad_query_left: float32 [8, 2048, 16], P(None, 'row')
- grad_query_right: float32 [8, 16, 2048], P(None, None, 'col')
- grad_kv_left: float32 [8, 2048, 16], P(None, 'row')
- grad_kv_right: float32 [8, 16, 2, 2048], P(None, None, None, 'col')
- grad_out_left: float32 [8, 2048, 16], P(None, 'row')
- grad_out_right: float32 [8, 16, 2048], P(None, None, 'col')
- grad_inner_left: float32 [8, 2048, 16], P(None, 'row')
- grad_inner_right: float32 [8, 16, 2, 5632], P(None, None, None, 'col')
- grad_down_left: float32 [8, 2048, 16], P(None, 'row')
- grad_down_right: float32 [8, 16, 5632], P(None, None, 'col')
Inputs may be any that keep to these rules, and one draw needn't show every extreme that they name: `lengths`: every sequence has 128 to 256 tokens; some sequence has exactly 256. `attn_route`: within each aligned block of 256 rows (one row group) no attention expert is named more than 80 times; the two experts of a row differ. `ffn_route`: within each aligned block of 256 rows no feed-forward expert is named more than 160 times; the two experts of a row differ.
All inputs are finite; a program needn't handle non-finite values.
Results may differ from a plain program's by a relative error of at most 0.017.
Values may be sent and summed in bfloat16 or wider, within the bound.
A program may use at most 384 MiB of HBM per device.

v0:
```python
import jax
import jax.numpy as jnp
from jax import lax
from jax.sharding import PartitionSpec as P

HEAD_DIM = 128
EXP_ATT = 8
EXP_FF = 4
TOPK = 2
ADAPT = 8
CAP_ATT = 80
CAP_FF = 160


EPSILON = 1e-06
ROPE_BASE = 10000.0
HIGHEST = lax.Precision.HIGHEST


def shortened(value):
    return jax.tree.map(lambda a: a.astype(jnp.bfloat16) if a.dtype == jnp.float32 else a, value)


def tables(count, head_width):
    position = jnp.arange(count).astype(jnp.float32)
    frequency = ROPE_BASE ** (-jnp.arange(head_width // 2).astype(jnp.float32) * 2.0 / head_width)
    angle = position[:, None] * frequency[None, :]
    return (jnp.cos(angle), jnp.sin(angle))


def rotate(values, cosine, sine):
    half_width = values.shape[-1] // 2
    shape = (values.shape[0],) + (1,) * (values.ndim - 2) + (half_width,)
    cos_part = cosine.reshape(shape)
    sin_part = sine.reshape(shape)
    first = values[..., :half_width]
    second = values[..., half_width:]
    return jnp.concatenate(
        [first * cos_part - second * sin_part, second * cos_part + first * sin_part], axis=-1
    )


def dispatch(route, experts, capacity):
    slots = route.shape[0] * route.shape[1]
    flat_route = route.reshape(slots)
    onehot = (flat_route[:, None] == jnp.arange(experts, dtype=jnp.int32)[None, :]).astype(
        jnp.int32
    )
    earlier = jnp.cumsum(onehot, axis=0) - onehot
    position = jnp.sum(earlier * onehot, axis=1)
    target = flat_route * capacity + position
    source = (
        jnp.full((experts * capacity,), slots, jnp.int32)
        .at[target]
        .set(jnp.arange(slots, dtype=jnp.int32))
    )
    return (target, source)


def router_back(gates, grad_gates, route, experts):
    centred = gates * (grad_gates - jnp.sum(gates * grad_gates, axis=1, keepdims=True))
    onehot = (route[:, :, None] == jnp.arange(experts, dtype=jnp.int32)[None, None, :]).astype(
        jnp.float32
    )
    return jnp.sum(centred[:, :, None] * onehot, axis=1)


def spread_pick(adapter, grad):
    chosen = (jnp.arange(ADAPT, dtype=jnp.int32) == adapter).astype(jnp.float32)
    return chosen.reshape((ADAPT,) + (1,) * grad.ndim) * grad[None]


def pad_rows(table):
    return jnp.concatenate([table, jnp.zeros((1,) + table.shape[1:], table.dtype)], axis=0)


def on_device(
    inputs,
    cotangent,
    lengths,
    adapter_pick,
    attn_route,
    ffn_route,
    norm_one,
    norm_two,
    router_attn,
    router_ffn,
    kv_weight,
    query_weight,
    out_weight,
    inner_weight,
    down_weight,
    query_left,
    query_right,
    kv_left,
    kv_right,
    out_left,
    out_right,
    inner_left,
    inner_right,
    down_left,
    down_right,
):
    count = inputs.shape[0]
    slice_width = inputs.shape[1]
    width = router_attn.shape[0]
    col_index = lax.axis_index("col")
    length = lengths[0]
    adapter = adapter_pick[0]
    position = jnp.arange(count)
    valid = (position < length).astype(jnp.float32)
    cosine, sine = tables(count, HEAD_DIM)
    block_rows = min(512, count)
    blocks = count // block_rows
    starts = jnp.arange(blocks, dtype=jnp.int32) * block_rows
    scaling = HEAD_DIM ** (-0.5)

    def features(part):
        return lax.all_gather(part, "col", axis=1, tiled=True)

    def partials(part):
        return lax.psum_scatter(part, "col", scatter_dimension=1, tiled=True)

    def token_total(parts):
        return lax.psum(parts, "col")

    def own_columns(table):
        return lax.dynamic_slice_in_dim(table, col_index * slice_width, slice_width, 0)

    gathered = (
        lax.all_gather(kv_weight, "row", axis=1, tiled=True),
        lax.all_gather(query_weight, "row", axis=1, tiled=True),
        lax.all_gather(out_weight, "row", axis=1, tiled=True),
        lax.all_gather(query_left, "row", axis=1, tiled=True),
        lax.all_gather(kv_left, "row", axis=1, tiled=True),
        lax.all_gather(out_left, "row", axis=1, tiled=True),
        lax.all_gather(inner_left, "row", axis=1, tiled=True),
        lax.all_gather(down_left, "row", axis=1, tiled=True),
    )
    kv_full = gathered[0]
    query_full = gathered[1]
    out_full = gathered[2]
    left_query = gathered[3][adapter]
    left_kv = gathered[4][adapter]
    left_out_wide = gathered[5][adapter].astype(jnp.float32)
    left_inner = gathered[6][adapter]
    left_down_low = gathered[7][adapter]
    left_down_wide = left_down_low.astype(jnp.float32)
    right_query = query_right[adapter].astype(jnp.float32)
    right_kv_low = kv_right[adapter]
    right_kv = right_kv_low.astype(jnp.float32)
    right_out_low = out_right[adapter]
    right_out = right_out_low.astype(jnp.float32)
    right_inner = inner_right[adapter].astype(jnp.float32)
    right_down_low = down_right[adapter]
    right_down = right_down_low.astype(jnp.float32)
    x_full = features(inputs)
    x_wide = x_full.astype(jnp.float32)
    scale_one = lax.rsqrt(jnp.mean(x_wide * x_wide, axis=1, keepdims=True) + EPSILON)
    hidden_one = (x_wide * scale_one * norm_one).astype(jnp.bfloat16)
    chosen_attn = jnp.take_along_axis(
        jnp.dot(hidden_one, router_attn, preferred_element_type=jnp.float32), attn_route, axis=1
    )
    gates_attn = jax.nn.softmax(chosen_attn, axis=1)
    target_attn, source_attn = dispatch(attn_route, EXP_ATT, CAP_ATT)
    rows_attn = source_attn // TOPK
    rank_query = jnp.dot(hidden_one, left_query, preferred_element_type=jnp.float32)
    rank_kv = jnp.dot(hidden_one, left_kv, preferred_element_type=jnp.float32)
    kv_raw = jnp.einsum(
        "td,sdw->stw", hidden_one, kv_full, preferred_element_type=jnp.float32
    ) + jnp.einsum("tr,rsw->stw", rank_kv, right_kv, precision=HIGHEST)
    heads_local = kv_raw.shape[2] // HEAD_DIM
    keys = rotate(kv_raw[0].reshape(count, heads_local, HEAD_DIM), cosine, sine).astype(
        jnp.bfloat16
    )
    values = kv_raw[1].reshape(count, heads_local, HEAD_DIM).astype(jnp.bfloat16)
    hidden_pad = pad_rows(hidden_one)
    query_buf = jnp.einsum(
        "ecd,edw->ecw",
        hidden_pad[rows_attn].reshape(EXP_ATT, CAP_ATT, width),
        query_full,
        preferred_element_type=jnp.float32,
    )
    query_width = query_buf.shape[2]
    query_raw = query_buf.reshape(EXP_ATT * CAP_ATT, query_width)[target_attn] + jnp.repeat(
        jnp.dot(rank_query, right_query, precision=HIGHEST), TOPK, axis=0
    )
    queries = rotate(query_raw.reshape(count, TOPK, heads_local, HEAD_DIM), cosine, sine).astype(
        jnp.bfloat16
    )

    def allowed_keys(start):
        query_rows = start + jnp.arange(block_rows)
        return (position[None, :] <= query_rows[:, None]) & (position[None, :] < length)

    def attend(block_items):
        query_block, start = block_items
        scores = (
            jnp.einsum("bkhd,jhd->hkbj", query_block, keys, preferred_element_type=jnp.float32)
            * scaling
        )
        scores = jnp.where(allowed_keys(start)[None, None], scores, -1e30)
        row_max = jnp.max(scores, axis=-1, keepdims=True)
        exponent = jnp.exp(scores - row_max)
        row_total = jnp.sum(exponent, axis=-1, keepdims=True)
        probability = (exponent / row_total).astype(jnp.bfloat16)
        result = jnp.einsum(
            "hkbj,jhd->bkhd", probability, values, preferred_element_type=jnp.float32
        ).astype(jnp.bfloat16)
        return (result, (row_max + jnp.log(row_total))[..., 0])

    query_blocks = queries.reshape(blocks, block_rows, TOPK, heads_local, HEAD_DIM)
    attended_blocks, log_totals = lax.map(attend, (query_blocks, starts))
    attended = attended_blocks.reshape(count * TOPK, query_width)
    attended_pad = pad_rows(attended)
    out_buf = jnp.einsum(
        "ecw,edw->ecd",
        attended_pad[source_attn].reshape(EXP_ATT, CAP_ATT, query_width),
        out_full,
        preferred_element_type=jnp.float32,
    )
    out_slots = out_buf.reshape(EXP_ATT * CAP_ATT, width)[target_attn].reshape(count, TOPK, width)
    attended_slots = attended.reshape(count, TOPK, query_width)
    attended_wide = attended_slots.astype(jnp.float32)
    low_slots_attn = jnp.einsum(
        "tkw,rw->tkr", attended_slots, right_out_low, preferred_element_type=jnp.float32
    )
    low_out_part = jnp.sum(low_slots_attn * gates_attn[:, :, None], axis=1)
    branch_attn = jnp.sum(out_slots * gates_attn[:, :, None], axis=1) + jnp.dot(
        low_out_part, left_out_wide.T, precision=HIGHEST
    )
    x_local = inputs.astype(jnp.float32)
    middle = x_local + partials(branch_attn)
    square_sum, low_out_full = token_total((jnp.sum(middle * middle, axis=1), low_out_part))
    scale_two = lax.rsqrt(square_sum[:, None] / width + EPSILON)
    hidden_two = features((middle * scale_two * own_columns(norm_two)).astype(jnp.bfloat16))
    chosen_ffn = jnp.take_along_axis(
        jnp.dot(hidden_two, router_ffn, preferred_element_type=jnp.float32), ffn_route, axis=1
    )
    gates_ffn = jax.nn.softmax(chosen_ffn, axis=1)
    target_ffn, source_ffn = dispatch(ffn_route, EXP_FF, CAP_FF)
    rank_inner = jnp.dot(hidden_two, left_inner, preferred_element_type=jnp.float32)
    inner_adapt = jnp.einsum("tr,rsf->tsf", rank_inner, right_inner, precision=HIGHEST)
    inner_pad = pad_rows(inner_adapt)
    two_pad = pad_rows(hidden_two)
    kept_experts = []
    gate_ups = []
    mixed_bufs = []
    down_bufs = []
    for expert in range(EXP_FF):
        inner_full, down_full = (
            lax.all_gather(inner_weight[expert], "row", axis=0, tiled=True),
            lax.all_gather(down_weight[expert], "row", axis=0, tiled=True),
        )
        kept_experts.append((inner_full, down_full))
        expert_rows = source_ffn[expert * CAP_FF : (expert + 1) * CAP_FF] // TOPK
        gate_up = (
            jnp.einsum(
                "cd,dsf->csf", two_pad[expert_rows], inner_full, preferred_element_type=jnp.float32
            )
            + inner_pad[expert_rows]
        )
        mixed = (jax.nn.silu(gate_up[:, 0]) * gate_up[:, 1]).astype(jnp.bfloat16)
        down_bufs.append(
            jnp.einsum("cf,df->cd", mixed, down_full, preferred_element_type=jnp.float32)
        )
        gate_ups.append(gate_up)
        mixed_bufs.append(mixed)
    down_buf = jnp.stack(down_bufs)
    mixed_buf = jnp.stack(mixed_bufs)
    hidden_ffn = mixed_buf.shape[2]
    down_slots = down_buf.reshape(EXP_FF * CAP_FF, width)[target_ffn].reshape(count, TOPK, width)
    mixed_slots = mixed_buf.reshape(EXP_FF * CAP_FF, hidden_ffn)[target_ffn].reshape(
        count, TOPK, hidden_ffn
    )
    low_slots_ffn = jnp.einsum(
        "tkf,rf->tkr", mixed_slots, right_down_low, preferred_element_type=jnp.float32
    )
    low_down_part = jnp.sum(low_slots_ffn * gates_ffn[:, :, None], axis=1)
    branch_ffn = jnp.sum(down_slots * gates_ffn[:, :, None], axis=1) + jnp.dot(
        low_down_part, left_down_wide.T, precision=HIGHEST
    )
    output = ((middle + partials(branch_ffn)) * valid[:, None]).astype(jnp.bfloat16)
    masked_cot = cotangent * valid.astype(jnp.bfloat16)[:, None]
    cot_local = masked_cot.astype(jnp.float32)
    grad_ffn_low = features(masked_cot)
    grad_ffn = grad_ffn_low.astype(jnp.float32)
    grad_low_down = jnp.dot(grad_ffn_low, left_down_low, preferred_element_type=jnp.float32)
    grad_gates_part = jnp.sum(down_slots * grad_ffn[:, None, :], axis=-1) + jnp.sum(
        low_slots_ffn * grad_low_down[:, None, :], axis=-1
    )
    grad_gates_ffn, low_down_full = token_total((grad_gates_part, low_down_part))
    gates_ffn_pad = pad_rows(gates_ffn.reshape(count * TOPK))
    grad_ffn_pad = pad_rows(grad_ffn)
    low_down_pad = pad_rows(grad_low_down)
    grad_two_part = jnp.zeros((count + 1, width), jnp.float32)
    grad_inner_total = jnp.zeros((count + 1, 2, hidden_ffn), jnp.float32)
    grad_right_down = jnp.zeros(right_down.shape, jnp.float32)
    for expert in range(EXP_FF):
        inner_full, down_full = (
            lax.all_gather(inner_weight[expert], "row", axis=0, tiled=True),
            lax.all_gather(down_weight[expert], "row", axis=0, tiled=True),
        )
        expert_slots = source_ffn[expert * CAP_FF : (expert + 1) * CAP_FF]
        expert_rows = expert_slots // TOPK
        slot_gates = gates_ffn_pad[expert_slots]
        grad_down = (slot_gates[:, None] * grad_ffn_pad[expert_rows]).astype(jnp.bfloat16)
        low_rows = slot_gates[:, None] * low_down_pad[expert_rows]
        grad_mixed = jnp.einsum(
            "cd,df->cf", grad_down, down_full, preferred_element_type=jnp.float32
        ) + jnp.dot(low_rows, right_down, precision=HIGHEST)
        grad_right_down = grad_right_down + jnp.einsum(
            "cr,cf->rf", low_rows, mixed_bufs[expert].astype(jnp.float32), precision=HIGHEST
        )
        gate_part = gate_ups[expert][:, 0]
        up_part = gate_ups[expert][:, 1]
        gate_sigmoid = jax.nn.sigmoid(gate_part)
        grad_gate = grad_mixed * up_part * gate_sigmoid * (1.0 + gate_part * (1.0 - gate_sigmoid))
        grad_up = grad_mixed * gate_part * gate_sigmoid
        grad_gate_up = jnp.stack([grad_gate, grad_up], axis=1).astype(jnp.bfloat16)
        grad_two_part = grad_two_part.at[expert_rows].add(
            jnp.einsum("csf,dsf->cd", grad_gate_up, inner_full, preferred_element_type=jnp.float32)
        )
        grad_inner_total = grad_inner_total.at[expert_rows].add(grad_gate_up.astype(jnp.float32))
    grad_inner = grad_inner_total[:count]
    grad_right_inner = jnp.einsum("tr,tsf->rsf", rank_inner, grad_inner, precision=HIGHEST)
    grad_rank_inner = jnp.einsum("tsf,rsf->tr", grad_inner, right_inner, precision=HIGHEST)
    grad_two_part = grad_two_part[:count] + jnp.dot(
        grad_rank_inner, left_inner.astype(jnp.float32).T, precision=HIGHEST
    )
    logits_ffn_grad = router_back(gates_ffn, grad_gates_ffn, ffn_route, EXP_FF)
    grad_two = partials(grad_two_part) + jnp.dot(
        logits_ffn_grad, own_columns(router_ffn).astype(jnp.float32).T, precision=HIGHEST
    )
    scaled_two = grad_two * own_columns(norm_two)
    inner_sum, rank_inner_full = token_total(
        (jnp.sum(scaled_two * middle, axis=1), grad_rank_inner)
    )
    grad_middle = (
        cot_local + scale_two * scaled_two - middle * scale_two**3 * inner_sum[:, None] / width
    )
    grad_full = lax.all_gather(grad_middle, "col", axis=1, tiled=True)
    grad_low_out = jnp.dot(grad_full, left_out_wide, precision=HIGHEST)
    grad_gates_attn_part = jnp.sum(out_slots * grad_full[:, None, :], axis=-1) + jnp.sum(
        low_slots_attn * grad_low_out[:, None, :], axis=-1
    )
    (grad_gates_attn,) = token_total((grad_gates_attn_part,))
    kv_back, query_back, out_back = (
        lax.all_gather(kv_weight, "row", axis=1, tiled=True),
        lax.all_gather(query_weight, "row", axis=1, tiled=True),
        lax.all_gather(out_weight, "row", axis=1, tiled=True),
    )
    gates_attn_flat = gates_attn.reshape(count * TOPK)
    slot_gates_attn = pad_rows(gates_attn_flat)[source_attn]
    grad_out_buf = (
        (slot_gates_attn[:, None] * pad_rows(grad_full)[rows_attn])
        .astype(jnp.bfloat16)
        .reshape(EXP_ATT, CAP_ATT, width)
    )
    grad_att_buf = jnp.einsum(
        "ecd,edw->ecw", grad_out_buf, out_back, preferred_element_type=jnp.float32
    )
    low_attn_rows = gates_attn_flat[:, None] * jnp.repeat(grad_low_out, TOPK, axis=0)
    grad_attended = (
        grad_att_buf.reshape(EXP_ATT * CAP_ATT, query_width)[target_attn]
        + jnp.dot(low_attn_rows, right_out, precision=HIGHEST)
    ).astype(jnp.bfloat16)
    grad_right_out = jnp.einsum(
        "tkr,tkw->rw",
        gates_attn[:, :, None] * grad_low_out[:, None, :],
        attended_wide,
        precision=HIGHEST,
    )

    def attend_back(carry, block_items):
        grad_keys, grad_values = carry
        query_block, grad_block, log_block, start = block_items
        scores = (
            jnp.einsum("bkhd,jhd->hkbj", query_block, keys, preferred_element_type=jnp.float32)
            * scaling
        )
        scores = jnp.where(allowed_keys(start)[None, None], scores, -1e30)
        probability = jnp.exp(scores - log_block[..., None])
        grad_prob = jnp.einsum(
            "bkhd,jhd->hkbj", grad_block, values, preferred_element_type=jnp.float32
        )
        centre = jnp.sum(probability * grad_prob, axis=-1, keepdims=True)
        grad_scores = (probability * (grad_prob - centre)).astype(jnp.bfloat16)
        grad_query = (
            jnp.einsum("hkbj,jhd->bkhd", grad_scores, keys, preferred_element_type=jnp.float32)
            * scaling
        )
        grad_keys = (
            grad_keys
            + jnp.einsum(
                "hkbj,bkhd->jhd", grad_scores, query_block, preferred_element_type=jnp.float32
            )
            * scaling
        )
        grad_values = grad_values + jnp.einsum(
            "hkbj,bkhd->jhd",
            probability.astype(jnp.bfloat16),
            grad_block,
            preferred_element_type=jnp.float32,
        )
        return ((grad_keys, grad_values), grad_query)

    empty_heads = jnp.zeros((count, heads_local, HEAD_DIM), jnp.float32)
    grad_blocks = grad_attended.reshape(blocks, block_rows, TOPK, heads_local, HEAD_DIM)
    (grad_keys, grad_values), grad_query_blocks = lax.scan(
        attend_back, (empty_heads, empty_heads), (query_blocks, grad_blocks, log_totals, starts)
    )
    grad_query_raw = (
        rotate(grad_query_blocks.reshape(count, TOPK, heads_local, HEAD_DIM), cosine, -sine)
        .reshape(count * TOPK, query_width)
        .astype(jnp.bfloat16)
    )
    grad_key_raw = rotate(grad_keys, cosine, -sine).reshape(count, heads_local * HEAD_DIM)
    grad_kv = jnp.stack([grad_key_raw, grad_values.reshape(count, heads_local * HEAD_DIM)]).astype(
        jnp.bfloat16
    )
    grad_query_buf = pad_rows(grad_query_raw)[source_attn].reshape(EXP_ATT, CAP_ATT, query_width)
    grad_one_part = (
        jnp.zeros((count + 1, width), jnp.float32)
        .at[rows_attn]
        .add(
            jnp.einsum(
                "ecw,edw->ecd", grad_query_buf, query_back, preferred_element_type=jnp.float32
            ).reshape(EXP_ATT * CAP_ATT, width)
        )
    )
    grad_one_part = grad_one_part[:count] + jnp.einsum(
        "stw,sdw->td", grad_kv, kv_back, preferred_element_type=jnp.float32
    )
    grad_query_sum = jnp.sum(
        grad_query_raw.astype(jnp.float32).reshape(count, TOPK, query_width), axis=1
    )
    grad_right_query = jnp.dot(rank_query.T, grad_query_sum, precision=HIGHEST)
    grad_rank_query = jnp.dot(grad_query_sum, right_query.T, precision=HIGHEST)
    grad_kv_wide = grad_kv.astype(jnp.float32)
    grad_right_kv = jnp.einsum("tr,stw->rsw", rank_kv, grad_kv_wide, precision=HIGHEST)
    grad_rank_kv = jnp.einsum(
        "stw,rsw->tr", grad_kv, right_kv_low, preferred_element_type=jnp.float32
    )
    grad_one_part = (
        grad_one_part
        + jnp.dot(grad_rank_query, left_query.astype(jnp.float32).T, precision=HIGHEST)
        + jnp.dot(grad_rank_kv, left_kv.astype(jnp.float32).T, precision=HIGHEST)
    )
    logits_attn_grad = router_back(gates_attn, grad_gates_attn, attn_route, EXP_ATT)
    grad_one = partials(grad_one_part) + jnp.dot(
        logits_attn_grad, own_columns(router_attn).astype(jnp.float32).T, precision=HIGHEST
    )
    scaled_one = grad_one * own_columns(norm_one)
    outer_sum, rank_query_full, rank_kv_full = token_total(
        (jnp.sum(scaled_one * x_local, axis=1), grad_rank_query, grad_rank_kv)
    )
    grad_inputs = (
        grad_middle + scale_one * scaled_one - x_local * scale_one**3 * outer_sum[:, None] / width
    )
    hidden_one_wide = hidden_one.astype(jnp.float32)
    hidden_two_wide = hidden_two.astype(jnp.float32)
    dense_left = (
        jnp.dot(hidden_one_wide.T, rank_query_full, precision=HIGHEST),
        jnp.dot(hidden_one_wide.T, rank_kv_full, precision=HIGHEST),
        jnp.dot(grad_full.T, low_out_full, precision=HIGHEST),
        jnp.dot(hidden_two_wide.T, rank_inner_full, precision=HIGHEST),
        jnp.dot(grad_ffn.T, low_down_full, precision=HIGHEST),
    )
    dense_right = (
        grad_right_query,
        grad_right_kv,
        grad_right_out,
        grad_right_inner,
        grad_right_down,
    )
    left_grads = jax.tree.map(
        lambda part: part.astype(jnp.float32),
        lax.psum_scatter(
            shortened(tuple((spread_pick(adapter, part) for part in dense_left))),
            "row",
            scatter_dimension=1,
            tiled=True,
        ),
    )
    right_grads = jax.tree.map(
        lambda part: part.astype(jnp.float32),
        lax.psum(shortened(tuple((spread_pick(adapter, part) for part in dense_right))), "row"),
    )
    return (
        output,
        grad_inputs,
        left_grads[0],
        right_grads[0],
        left_grads[1],
        right_grads[1],
        left_grads[2],
        right_grads[2],
        left_grads[3],
        right_grads[3],
        left_grads[4],
        right_grads[4],
    )


def solution(mesh):
    placed = (
        P("row", "col"),
        P("row", "col"),
        P("row"),
        P("row"),
        P("row", None),
        P("row", None),
        P(),
        P(),
        P(),
        P(),
        P(None, "row", "col"),
        P(None, "row", "col"),
        P(None, "row", "col"),
        P(None, "row", None, "col"),
        P(None, "row", "col"),
        P(None, "row", None),
        P(None, None, "col"),
        P(None, "row", None),
        P(None, None, None, "col"),
        P(None, "row", None),
        P(None, None, "col"),
        P(None, "row", None),
        P(None, None, None, "col"),
        P(None, "row", None),
        P(None, None, "col"),
    )
    return jax.shard_map(
        on_device,
        mesh=mesh,
        in_specs=placed,
        out_specs=(
            P("row", "col"),
            P("row", "col"),
            P(None, "row", None),
            P(None, None, "col"),
            P(None, "row", None),
            P(None, None, None, "col"),
            P(None, "row", None),
            P(None, None, "col"),
            P(None, "row", None),
            P(None, None, None, "col"),
            P(None, "row", None),
            P(None, None, "col"),
        ),
        check_vma=False,
    )
```

profile of v0, /device:TPU:9, one launch (start us, length us, event | category | flops | bytes accessed | tf_op | source)
XLA Modules:
  0.0 1599.0 jit_solution(2296157511682466486)
XLA Ops:
  20.4 12.5 all_gather.75
  32.9 12.1 all_gather.73
  45.1 15.5 all_gather.77
  86.2 85.5 %all-gather.28.cloned.1.call-done = bf16[8,2048,512]{2,1,0:T(8,128)(2,1)} async-done(((bf16[8,256,512]{2,1,0:T(8,128)(2,1)}), bf16[8,2048,512]{2,1,0:T(8,128)(2,1)}) %all-gather.28.cloned.1.call-update) | async-done | bytes 16777232 | tf_op jit(solution)/shard_map/all_gather | solution.py:132
  171.7 9.6 fusion.333
  191.4 71.9 %all-gather.30.cloned.1.call-done = bf16[8,2048,512]{2,1,0:T(8,128)(2,1)} async-done(((bf16[8,256,512]{2,1,0:T(8,128)(2,1)}), bf16[8,2048,512]{2,1,0:T(8,128)(2,1)}) %all-gather.30.cloned.1.call-update) | async-done | bytes 16777232 | tf_op jit(solution)/shard_map/all_gather | solution.py:133
  263.3 13.2 fusion.334
  276.5 7.9 gather_fusion.3
  284.5 5.9 reshape.796
  291.8 8.9 multiply_reduce_fusion.3
  306.7 38.6 %reduce-scatter.10.cloned.1.call-done = f32[256,512]{1,0:T(8,128)} async-done(((f32[256,2048]{1,0:T(8,128)}), f32[256,512]{1,0:T(8,128)}) %reduce-scatter.10.cloned.1.call-update) | async-done | bytes 524304 | tf_op jit(solution)/shard_map/reduce_scatter | solution.py:122
  346.5 9.0 psum.105
  362.1 6.9 fusion.313
  384.8 14.6 all_gather.80
  399.4 11.3 all_gather.88
  447.4 6.2 gather_fusion.11
  453.6 6.0 gather_fusion.9
  459.6 5.9 gather_fusion.7
  465.5 5.8 gather_fusion.5
  471.8 5.2 gather_fusion.31
  483.0 5.3 fusion.28
  488.3 34.2 %all-gather.38.cloned.1.call-done = bf16[1,2048,2,1408]{3,1,2,0:T(8,128)(2,1)} async-done(((bf16[1,256,2,1408]{3,1,2,0:T(8,128)(2,1)}), bf16[1,2048,2,1408]{3,1,2,0:T(8,128)(2,1)}) %all-gather.38.cloned.1.call-update) | async-done | bytes 11534352 | tf_op jit(solution)/shard_map/all_gather | solution.py:252
  522.5 6.7 fusion.32
  533.6 5.0 fusion.51
  546.5 21.2 %all-gather.48.cloned.1.call-done = bf16[1,2048,1408]{2,1,0:T(8,128)(2,1)} async-done(((bf16[1,256,1408]{2,1,0:T(8,128)(2,1)}), bf16[1,2048,1408]{2,1,0:T(8,128)(2,1)}) %all-gather.48.cloned.1.call-update) | async-done | bytes 5767184 | tf_op jit(solution)/shard_map/all_gather | solution.py:253
  567.7 5.2 fusion.20
  572.9 64.6 %all-gather.46.cloned.1.call-done = bf16[1,2048,2,1408]{3,1,2,0:T(8,128)(2,1)} async-done(((bf16[1,256,2,1408]{3,1,2,0:T(8,128)(2,1)}), bf16[1,2048,2,1408]{3,1,2,0:T(8,128)(2,1)}) %all-gather.46.cloned.1.call-update) | async-done | bytes 11534352 | tf_op jit(solution)/shard_map/all_gather | solution.py:252
  637.5 7.1 fusion.38
  650.9 31.8 %all-gather.44.cloned.1.call-done = bf16[1,2048,1408]{2,1,0:T(8,128)(2,1)} async-done(((bf16[1,256,1408]{2,1,0:T(8,128)(2,1)}), bf16[1,2048,1408]{2,1,0:T(8,128)(2,1)}) %all-gather.44.cloned.1.call-update) | async-done | bytes 5767184 | tf_op jit(solution)/shard_map/all_gather | solution.py:253
  682.8 5.2 fusion.24
  688.0 65.2 %all-gather.42.cloned.1.call-done = bf16[1,2048,2,1408]{3,1,2,0:T(8,128)(2,1)} async-done(((bf16[1,256,2,1408]{3,1,2,0:T(8,128)(2,1)}), bf16[1,2048,2,1408]{3,1,2,0:T(8,128)(2,1)}) %all-gather.42.cloned.1.call-update) | async-done | bytes 11534352 | tf_op jit(solution)/shard_map/all_gather | solution.py:252
  753.1 6.9 fusion.35
  765.9 32.5 %all-gather.52.cloned.1.call-done = bf16[1,2048,1408]{2,1,0:T(8,128)(2,1)} async-done(((bf16[1,256,1408]{2,1,0:T(8,128)(2,1)}), bf16[1,2048,1408]{2,1,0:T(8,128)(2,1)}) %all-gather.52.cloned.1.call-update) | async-done | bytes 5767184 | tf_op jit(solution)/shard_map/all_gather | solution.py:253
  798.4 5.2 fusion.16
  803.6 64.4 %all-gather.50.cloned.1.call-done = bf16[1,2048,2,1408]{3,1,2,0:T(8,128)(2,1)} async-done(((bf16[1,256,2,1408]{3,1,2,0:T(8,128)(2,1)}), bf16[1,2048,2,1408]{3,1,2,0:T(8,128)(2,1)}) %all-gather.50.cloned.1.call-update) | async-done | bytes 11534352 | tf_op jit(solution)/shard_map/all_gather | solution.py:252
  868.0 6.9 fusion.41
  882.7 24.8 %scatter_fusion.3 = f32[257,2,1408]{2,1,0:T(2,128)} fusion(f32[257,2,1408]{2,1,0:T(2,128)} %broadcast_in_dim.94, s32[160]{0:T(256)S(1)} %copy-done.164, f32[160,2,1408]{2,1,0:T(2,128)} %copy.477), kind=kCustom, calls=%fused_computation.38 | custom fusion | flops 450560 | bytes 5407360 | tf_op jit(solution)/shard_map/scatter-add | solution.py:324
  907.5 24.7 %scatter_fusion.4 = f32[257,2,1408]{2,1,0:T(2,128)} fusion(f32[257,2,1408]{2,1,0:T(2,128)} %scatter_fusion.3, s32[160]{0:T(256)S(1)} %get-tuple-element.126, f32[160,2,1408]{2,1,0:T(2,128)} %copy.478), kind=kCustom, calls=%fused_computation.39 | custom fusion | flops 450560 | bytes 5407360 | tf_op jit(solution)/shard_map/scatter-add | solution.py:324
  932.3 24.5 %scatter_fusion.5 = f32[257,2,1408]{2,1,0:T(2,128)} fusion(f32[257,2,1408]{2,1,0:T(2,128)} %scatter_fusion.4, s32[160]{0:T(256)S(1)} %get-tuple-element.127, f32[160,2,1408]{2,1,0:T(2,128)} %copy.479), kind=kCustom, calls=%fused_computation.40 | custom fusion | flops 450560 | bytes 5407360 | tf_op jit(solution)/shard_map/scatter-add | solution.py:324
  956.8 24.7 %scatter_fusion.6 = f32[257,2,1408]{2,1,0:T(2,128)} fusion(f32[257,2,1408]{2,1,0:T(2,128)} %scatter_fusion.5, s32[160]{0:T(256)S(1)} %get-tuple-element.128, f32[160,2,1408]{2,1,0:T(2,128)} %copy.480), kind=kCustom, calls=%fused_computation.41 | custom fusion | flops 450560 | bytes 5407360 | tf_op jit(solution)/shard_map/scatter-add | solution.py:324
  987.5 9.2 fusion.54
  1000.9 9.4 fusion.57
  1014.6 9.4 fusion.60
  1032.4 4.8 fusion.63
  1037.2 5.0 fusion.69
  1051.7 8.1 gather_fusion.12
  1059.9 5.9 reshape.800
  1078.6 9.4 multiply_reduce_fusion.1
  1091.4 7.4 psum.106
  1100.6 10.3 psum.107
  1111.0 22.1 %reduce-scatter.12.cloned.1.call-done = f32[256,512]{1,0:T(8,128)} async-done(((f32[256,2048]{1,0:T(8,128)}), f32[256,512]{1,0:T(8,128)}) %reduce-scatter.12.cloned.1.call-update) | async-done | bytes 524304 | tf_op jit(solution)/shard_map/reduce_scatter | solution.py:122
  1138.9 42.3 %all-gather.36.cloned.1.call-done = f32[256,2048]{1,0:T(8,128)} async-done(((f32[256,512]{1,0:T(8,128)}), f32[256,2048]{1,0:T(8,128)}) %all-gather.36.cloned.1.call-update) | async-done | bytes 2097168 | tf_op jit(solution)/shard_map/all_gather | solution.py:342
  1191.0 10.4 fusion.48
  1219.9 13.2 fusion.337
  1233.1 15.4 scatter_custom_fusion.10
  1268.7 9.4 psum.108
  1280.3 19.8 %reduce-scatter.16.cloned.1.call-done = f32[256,512]{1,0:T(8,128)} async-done(((f32[256,2048]{1,0:T(8,128)}), f32[256,512]{1,0:T(8,128)}) %reduce-scatter.16.cloned.1.call-update) | async-done | bytes 524304 | tf_op jit(solution)/shard_map/reduce_scatter | solution.py:122
  1304.9 33.3 %all-reduce.13.cloned.1.call-done = (f32[256]{0:T(256)}, f32[256,16]{0,1:T(8,128)}, f32[256,16]{0,1:T(8,128)}, f32[256,16]{0,1:T(8,128)}, f32[256,16]{0,1:T(8,128)}, /*index=5*/f32[256,16]{0,1:T(8,128)}) async-done(((f32[256]{0:T(256)}, f32[256,16]{0,1:T(8,128)}, f32[256,16]{0,1:T(8,128)}, f32[256,16]{0,1:T(8,128)}, f32[256,16]{0,1:T(8,128)}, /*index=5*/f32[256,16]{0,1:T(8,128)}), (f32[256]{0:T(256)}, ...) | async-done | bytes 82960 | tf_op jit(solution)/shard_map/psum | solution.py:125
  1348.6 56.1 %all-reduce.15.cloned.1.call-done = (bf16[8,16,512]{2,1,0:T(8,128)(2,1)}, bf16[8,16,2,512]{3,2,1,0:T(2,128)(2,1)}, bf16[8,16,512]{2,1,0:T(8,128)(2,1)}, bf16[8,1...) async-done(((bf16[8,16,512]{2,1,0:T(8,128)(2,1)}, bf16[8,16,2,512]{3,2,1,0:T(2,128)(2,1)}, bf16[8,16,512]{2,1,0:T(8,128)(2,1)}, bf16[8,16,2,1408]{3,2,1,0:T(2,128)(2,1)}, ...) | async-done | bytes 1605648 | tf_op jit(solution)/shard_map/psum | solution.py:488
  1414.6 27.0 %reduce-scatter.18.cloned.1.call-done = bf16[8,256,16]{1,2,0:T(8,128)(2,1)} async-done(((bf16[8,2048,16]{1,2,0:T(8,128)(2,1)}), bf16[8,256,16]{1,2,0:T(8,128)(2,1)}) %reduce-scatter.18.cloned.1.call-update) | async-done | bytes 65552 | tf_op jit(solution)/shard_map/reduce_scatter | solution.py:479
  1443.1 36.0 %reduce-scatter.24.cloned.1.call-done = bf16[8,256,16]{1,2,0:T(8,128)(2,1)} async-done(((bf16[8,2048,16]{1,2,0:T(8,128)(2,1)}), bf16[8,256,16]{1,2,0:T(8,128)(2,1)}) %reduce-scatter.24.cloned.1.call-update) | async-done | bytes 65552 | tf_op jit(solution)/shard_map/reduce_scatter | solution.py:479
  1480.6 35.5 %reduce-scatter.22.cloned.1.call-done = bf16[8,256,16]{1,2,0:T(8,128)(2,1)} async-done(((bf16[8,2048,16]{1,2,0:T(8,128)(2,1)}), bf16[8,256,16]{1,2,0:T(8,128)(2,1)}) %reduce-scatter.22.cloned.1.call-update) | async-done | bytes 65552 | tf_op jit(solution)/shard_map/reduce_scatter | solution.py:479
  1517.7 36.0 %reduce-scatter.20.cloned.1.call-done = bf16[8,256,16]{1,2,0:T(8,128)(2,1)} async-done(((bf16[8,2048,16]{1,2,0:T(8,128)(2,1)}), bf16[8,256,16]{1,2,0:T(8,128)(2,1)}) %reduce-scatter.20.cloned.1.call-update) | async-done | bytes 65552 | tf_op jit(solution)/shard_map/reduce_scatter | solution.py:479
  1555.2 35.5 %reduce-scatter.26.cloned.1.call-done = bf16[8,256,16]{1,2,0:T(8,128)(2,1)} async-done(((bf16[8,2048,16]{1,2,0:T(8,128)(2,1)}), bf16[8,256,16]{1,2,0:T(8,128)(2,1)}) %reduce-scatter.26.cloned.1.call-update) | async-done | bytes 65552 | tf_op jit(solution)/shard_map/reduce_scatter | solution.py:479
  (678 shorter events, 290.9 us)
Async XLA Ops:
  7.2 403.5 %copy-start = (bf16[8,16,2,1408]{3,2,1,0:T(2,128)(2,1)S(1)}, bf16[8,16,2,1408]{3,2,1,0:T(2,128)(2,1)}, u32[]{:S(2)}) copy-start(bf16[8,16,2,1408]{3,2,1,0:T(2,128)(2,1)} %param.47) | copy-start | bytes 2162692
  7.2 54.6 %all-gather.24.cloned.1.call-start = ((), (), s32[]{:S(2)}) async-start(), calls=%async_computation.9 | async-start | bytes 1310720 | tf_op jit(solution)/shard_map/all_gather | solution.py:119
  7.9 71.9 %all-gather.26.cloned.1.call-start = ((), (), s32[]{:S(2)}) async-start(), calls=%async_computation.10 | async-start | bytes 4718592 | tf_op jit(solution)/shard_map/all_gather | solution.py:131
  8.7 163.0 %all-gather.28.cloned.1.call-start = ((), (), s32[]{:S(2)}) async-start(), calls=%async_computation.11 | async-start | bytes 18874368 | tf_op jit(solution)/shard_map/all_gather | solution.py:132
  9.5 253.9 %all-gather.30.cloned.1.call-start = ((), (), s32[]{:S(2)}) async-start(), calls=%async_computation.12 | async-start | bytes 18874368 | tf_op jit(solution)/shard_map/all_gather | solution.py:133
  10.0 335.2 %reduce-scatter.10.cloned.1.call-start = ((), (), s32[]{:S(2)}) async-start(), calls=%async_computation.13 | async-start | bytes 2621440 | tf_op jit(solution)/shard_map/reduce_scatter | solution.py:122
  12.6 51.4 %copy-start.156 = (f32[2048]{0:T(1024)S(1)}, f32[2048]{0:T(1024)}, u32[]{:S(2)}) copy-start(f32[2048]{0:T(1024)} %param.31) | copy-start | bytes 24580
  19.5 257.0 %copy-start.131 = (s32[1024]{0:T(1024)}, s32[1024]{0:T(1024)S(1)}, u32[]{:S(2)}) copy-start(s32[1024]{0:T(1024)S(1)} %pad_clamp_fusion.10) | copy-start | bytes 12292
  19.6 45.9 %copy-start.146 = (s32[640]{0:T(1024)}, s32[640]{0:T(1024)S(1)}, u32[]{:S(2)}) copy-start(s32[640]{0:T(1024)S(1)} %get-tuple-element.133) | copy-start | bytes 7684
  19.6 168.7 %copy-start.114 = (s32[1024]{0:T(1024)}, s32[1024]{0:T(1024)S(1)}, u32[]{:S(2)}) copy-start(s32[1024]{0:T(1024)S(1)} %pad_clamp_fusion.9) | copy-start | bytes 12292
  19.6 51.2 %copy-start.126 = (s32[1024]{0:T(1024)}, s32[1024]{0:T(1024)S(1)}, u32[]{:S(2)}) copy-start(s32[1024]{0:T(1024)S(1)} %pad_clamp_fusion.11) | copy-start | bytes 12292
  20.4 62.9 %copy-start.98 = (bf16[1,16,2,512]{3,2,1,0:T(2,128)(2,1)}, bf16[1,16,2,512]{3,2,1,0:T(2,128)(2,1)S(1)}, u32[]{:S(2)}) copy-start(bf16[1,16,2,512]{3,2,1,0:T(2,128)(2,1)S(1)} %constant_dynamic-slice_fusion.1) | copy-start | bytes 98308
  61.8 122.7 %copy-start.35 = (f32[256,64]{1,0:T(8,128)}, f32[256,64]{1,0:T(8,128)S(1)}, u32[]{:S(2)}) copy-start(f32[256,64]{1,0:T(8,128)S(1)} %get-tuple-element.136) | copy-start | bytes 196612
  69.9 220.4 %copy-start.116 = (f32[256,2]{0,1:T(2,128)}, f32[256,2]{0,1:T(2,128)S(1)}, u32[]{:S(2)}) copy-start(f32[256,2]{0,1:T(2,128)S(1)} %fusion.296) | copy-start | bytes 6148
  86.2 98.9 %copy-start.37 = (bf16[256,4,64]{2,0,1:T(8,128)(2,1)}, bf16[256,4,64]{2,0,1:T(8,128)(2,1)S(1)}, u32[]{:S(2)}) copy-start(bf16[256,4,64]{2,0,1:T(8,128)(2,1)S(1)} %get-tuple-element.112) | copy-start | bytes 393220
  187.8 102.6 %copy-start.32 = (bf16[256,2,4,128]{0,3,2,1:T(8,128)(2,1)}, bf16[256,2,4,128]{0,3,2,1:T(8,128)(2,1)S(1)}, u32[]{:S(2)}) copy-start(bf16[256,2,4,128]{0,3,2,1:T(8,128)(2,1)S(1)} %copy.450) | copy-start | bytes 1572868
  304.1 41.2 %copy-start.22 = (bf16[256,512]{1,0:T(8,128)(2,1)S(1)}, bf16[256,512]{1,0:T(8,128)(2,1)}, u32[]{:S(2)}) copy-start(bf16[256,512]{1,0:T(8,128)(2,1)} %param.25) | copy-start | bytes 786436
  304.1 107.4 %all-gather.34.cloned.1.call-start = ((), (), s32[]{:S(2)}) async-start(), calls=%async_computation.16 | async-start | bytes 1310720 | tf_op jit(solution)/shard_map/all_gather | solution.py:119
  305.0 57.0 %copy-start.177 = (bf16[256]{0:T(256)(128)(2,1)}, bf16[256]{0:T(256)(128)(2,1)S(1)}, u32[]{:S(2)}) copy-start(bf16[256]{0:T(256)(128)(2,1)S(1)} %convert_convert_fusion) | copy-start | bytes 1540
  305.8 125.9 %all-gather.32.cloned.1.call-start = ((), (), s32[]{:S(2)}) async-start(), calls=%async_computation.14 | async-start | bytes 1310720 | tf_op jit(solution)/shard_map/all_gather | solution.py:119
  306.7 55.3 %copy-start.135 = (f32[512]{0:T(512)}, f32[512]{0:T(512)S(1)}, u32[]{:S(2)}) copy-start(f32[512]{0:T(512)S(1)} %dynamic_slice.64) | copy-start | bytes 6148
  358.6 124.4 %all-gather.40.cloned.1.call-start = ((), (), s32[]{:S(2)}) async-start(), calls=%async_computation.26 | async-start | bytes 6488064 | tf_op jit(solution)/shard_map/all_gather | solution.py:253
  362.0 160.4 %all-gather.38.cloned.1.call-start = ((), (), s32[]{:S(2)}) async-start(), calls=%async_computation.25 | async-start | bytes 12976128 | tf_op jit(solution)/shard_map/all_gather | solution.py:252
  370.3 197.5 %all-gather.48.cloned.1.call-start = ((), (), s32[]{:S(2)}) async-start(), calls=%async_computation.30 | async-start | bytes 6488064 | tf_op jit(solution)/shard_map/all_gather | solution.py:253
  370.9 266.7 %all-gather.46.cloned.1.call-start = ((), (), s32[]{:S(2)}) async-start(), calls=%async_computation.29 | async-start | bytes 12976128 | tf_op jit(solution)/shard_map/all_gather | solution.py:252
  373.6 309.2 %all-gather.44.cloned.1.call-start = ((), (), s32[]{:S(2)}) async-start(), calls=%async_computation.28 | async-start | bytes 6488064 | tf_op jit(solution)/shard_map/all_gather | solution.py:253
  374.2 379.0 %all-gather.42.cloned.1.call-start = ((), (), s32[]{:S(2)}) async-start(), calls=%async_computation.27 | async-start | bytes 12976128 | tf_op jit(solution)/shard_map/all_gather | solution.py:252
  376.8 421.6 %all-gather.52.cloned.1.call-start = ((), (), s32[]{:S(2)}) async-start(), calls=%async_computation.32 | async-start | bytes 6488064 | tf_op jit(solution)/shard_map/all_gather | solution.py:253
  377.4 490.6 %all-gather.50.cloned.1.call-start = ((), (), s32[]{:S(2)}) async-start(), calls=%async_computation.31 | async-start | bytes 12976128 | tf_op jit(solution)/shard_map/all_gather | solution.py:252
  378.8 720.2 %reduce-scatter.14.cloned.1.call-start = ((), (), s32[]{:S(2)}) async-start(), calls=%async_computation.17 | async-start | bytes 2621440 | tf_op jit(solution)/shard_map/reduce_scatter | solution.py:122
  382.3 525.2 %copy-start.144 = (s32[160]{0:T(256)}, s32[160]{0:T(256)S(1)}, u32[]{:S(2)}) copy-start(s32[160]{0:T(256)S(1)} %get-tuple-element.126) | copy-start | bytes 1924
  382.3 550.0 %copy-start.142 = (s32[160]{0:T(256)}, s32[160]{0:T(256)S(1)}, u32[]{:S(2)}) copy-start(s32[160]{0:T(256)S(1)} %get-tuple-element.127) | copy-start | bytes 1924
  382.3 574.5 %copy-start.140 = (s32[160]{0:T(256)}, s32[160]{0:T(256)S(1)}, u32[]{:S(2)}) copy-start(s32[160]{0:T(256)S(1)} %get-tuple-element.128) | copy-start | bytes 1924
  382.9 43.9 %copy-start.149 = (s32[1024]{0:T(1024)}, s32[1024]{0:T(1024)S(1)}, u32[]{:S(2)}) copy-start(s32[1024]{0:T(1024)S(1)} %pad_clamp_fusion.8) | copy-start | bytes 12292
  382.9 40.5 %copy-start.151 = (s32[1024]{0:T(1024)}, s32[1024]{0:T(1024)S(1)}, u32[]{:S(2)}) copy-start(s32[1024]{0:T(1024)S(1)} %pad_clamp_fusion.7) | copy-start | bytes 12292
  383.0 51.2 %copy-start.153 = (s32[1024]{0:T(1024)}, s32[1024]{0:T(1024)S(1)}, u32[]{:S(2)}) copy-start(s32[1024]{0:T(1024)S(1)} %pad_clamp_fusion.6) | copy-start | bytes 12292
  383.0 50.1 %copy-start.154 = (s32[1024]{0:T(1024)}, s32[1024]{0:T(1024)S(1)}, u32[]{:S(2)}) copy-start(s32[1024]{0:T(1024)S(1)} %pad_clamp_fusion.5) | copy-start | bytes 12292
  478.9 396.0 %copy-start.165 = (f32[160]{0:T(256)}, f32[160]{0:T(256)S(1)}, u32[]{:S(2)}) copy-start(f32[160]{0:T(256)S(1)} %gather_fusion.23) | copy-start | bytes 1924
  480.2 164.4 %copy-start.167 = (f32[160]{0:T(256)}, f32[160]{0:T(256)S(1)}, u32[]{:S(2)}) copy-start(f32[160]{0:T(256)S(1)} %gather_fusion.20) | copy-start | bytes 1924
  481.6 278.5 %copy-start.169 = (f32[160]{0:T(256)}, f32[160]{0:T(256)S(1)}, u32[]{:S(2)}) copy-start(f32[160]{0:T(256)S(1)} %gather_fusion.17) | copy-start | bytes 1924
  482.9 46.2 %copy-start.171 = (f32[160]{0:T(256)}, f32[160]{0:T(256)S(1)}, u32[]{:S(2)}) copy-start(f32[160]{0:T(256)S(1)} %gather_fusion.14) | copy-start | bytes 1924
  482.9 39.5 %copy-start.21 = (f32[160,2,1408]{2,1,0:T(2,128)S(1)}, f32[160,2,1408]{2,1,0:T(2,128)}, u32[]{:S(2)}) copy-start(f32[160,2,1408]{2,1,0:T(2,128)} %gather_fusion.5) | copy-start | bytes 5406724
  488.3 40.9 %copy-start.83 = (f32[160,16]{1,0:T(8,128)S(1)}, f32[160,16]{1,0:T(8,128)}, u32[]{:S(2)}) copy-start(f32[160,16]{1,0:T(8,128)} %gather_fusion.16) | copy-start | bytes 30724
  762.0 280.3 %copy-start.46 = (bf16[160,1408]{1,0:T(8,128)(2,1)}, bf16[160,1408]{1,0:T(8,128)(2,1)S(1)}, u32[]{:S(2)}) copy-start(bf16[160,1408]{1,0:T(8,128)(2,1)S(1)} %get-tuple-element.108) | copy-start | bytes 1351684
  803.6 71.4 %copy-start.85 = (f32[160,16]{1,0:T(8,128)S(1)}, f32[160,16]{1,0:T(8,128)}, u32[]{:S(2)}) copy-start(f32[160,16]{1,0:T(8,128)} %gather_fusion.25) | copy-start | bytes 30724
  987.5 40.6 %copy-start.93 = (f32[256,16]{0,1:T(8,128)}, f32[256,16]{0,1:T(8,128)S(1)}, u32[]{:S(2)}) copy-start(f32[256,16]{0,1:T(8,128)S(1)} %fusion.94) | copy-start | bytes 49156
  1031.4 101.7 %reduce-scatter.12.cloned.1.call-start = ((), (), s32[]{:S(2)}) async-start(), calls=%async_computation.15 | async-start | bytes 2621440 | tf_op jit(solution)/shard_map/reduce_scatter | solution.py:122
  1091.2 41.9 %copy-start.58 = (bf16[256,512]{1,0:T(8,128)(2,1)S(1)}, bf16[256,512]{1,0:T(8,128)(2,1)}, u32[]{:S(2)}) copy-start(bf16[256,512]{1,0:T(8,128)(2,1)} %param.26) | copy-start | bytes 786436
  1091.2 41.9 %copy-start.162 = (f32[256]{0:T(256)S(1)}, f32[256]{0:T(256)}, u32[]{:S(2)}) copy-start(f32[256]{0:T(256)} %copy-done.161) | copy-start | bytes 3076
  1091.2 41.9 %copy-start.176 = (f32[256]{0:T(256)S(1)}, f32[256]{0:T(256)}, u32[]{:S(2)}) copy-start(f32[256]{0:T(256)} %get-tuple-element.139) | copy-start | bytes 3076
  1091.3 41.9 %copy-start.178 = (bf16[256]{0:T(256)(128)(2,1)S(1)}, bf16[256]{0:T(256)(128)(2,1)}, u32[]{:S(2)}) copy-start(bf16[256]{0:T(256)(128)(2,1)} %copy-done.177) | copy-start | bytes 1540
  1091.3 89.9 %all-gather.36.cloned.1.call-start = ((), (), s32[]{:S(2)}) async-start(), calls=%async_computation.18 | async-start | bytes 2621440 | tf_op jit(solution)/shard_map/all_gather | solution.py:342
  1135.3 164.7 %reduce-scatter.16.cloned.1.call-start = ((), (), s32[]{:S(2)}) async-start(), calls=%async_computation.19 | async-start | bytes 2621440 | tf_op jit(solution)/shard_map/reduce_scatter | solution.py:122
  1138.8 45.1 %copy-start.100 = (f32[256,2,16]{0,2,1:T(8,128)S(1)}, f32[256,2,16]{0,2,1:T(8,128)}, u32[]{:S(2)}) copy-start(f32[256,2,16]{0,2,1:T(8,128)} %get-tuple-element.151) | copy-start | bytes 98308
  1138.8 45.1 %copy-start.117 = (f32[256,2]{0,1:T(2,128)S(1)}, f32[256,2]{0,1:T(2,128)}, u32[]{:S(2)}) copy-start(f32[256,2]{0,1:T(2,128)} %copy-done.116) | copy-start | bytes 6148
  1257.6 80.6 %all-reduce.13.cloned.1.call-start = ((), (), s32[]{:S(2)}) async-start(), calls=%async_computation.33 | async-start | bytes 165888 | tf_op jit(solution)/shard_map/psum | solution.py:125
  1278.8 59.4 %copy-start.5 = (bf16[256,2048]{1,0:T(8,128)(2,1)S(1)}, bf16[256,2048]{1,0:T(8,128)(2,1)}, u32[]{:S(2)}) copy-start(bf16[256,2048]{1,0:T(8,128)(2,1)} %copy-done.4) | copy-start | bytes 3145732
  1302.9 101.8 %all-reduce.15.cloned.1.call-start = ((), (), s32[]{:S(2)}) async-start(), calls=%async_computation.34 | async-start | bytes 3211264 | tf_op jit(solution)/shard_map/psum | solution.py:488
  1304.6 137.0 %reduce-scatter.18.cloned.1.call-start = ((), (), s32[]{:S(2)}) async-start(), calls=%async_computation.20 | async-start | bytes 589824 | tf_op jit(solution)/shard_map/reduce_scatter | solution.py:479
  1346.0 133.1 %reduce-scatter.24.cloned.1.call-start = ((), (), s32[]{:S(2)}) async-start(), calls=%async_computation.23 | async-start | bytes 589824 | tf_op jit(solution)/shard_map/reduce_scatter | solution.py:479
  1346.7 169.4 %reduce-scatter.22.cloned.1.call-start = ((), (), s32[]{:S(2)}) async-start(), calls=%async_computation.22 | async-start | bytes 589824 | tf_op jit(solution)/shard_map/reduce_scatter | solution.py:479
  1347.3 206.4 %reduce-scatter.20.cloned.1.call-start = ((), (), s32[]{:S(2)}) async-start(), calls=%async_computation.21 | async-start | bytes 589824 | tf_op jit(solution)/shard_map/reduce_scatter | solution.py:479
  1348.1 242.6 %reduce-scatter.26.cloned.1.call-start = ((), (), s32[]{:S(2)}) async-start(), calls=%async_computation.24 | async-start | bytes 589824 | tf_op jit(solution)/shard_map/reduce_scatter | solution.py:479
  1412.0 180.2 %copy-start.1 = (bf16[8,16,2,1408]{3,2,1,0:T(2,128)(2,1)S(1)}, bf16[8,16,2,1408]{3,2,1,0:T(2,128)(2,1)}, u32[]{:S(2)}) copy-start(bf16[8,16,2,1408]{3,2,1,0:T(2,128)(2,1)} %param.47) | copy-start | bytes 2162692
  (144 other events, 978.3 us)
Sparse Core Ops, SparseCore 0:
  9.6 28.8 all-gather.23
  40.4 39.4 all-gather.25
  81.8 89.8 all-gather.27
  173.4 89.8 all-gather.29
  304.2 41.0 reduce-scatter.9
  347.4 29.3 all-gather.33
  379.0 27.4 all-gather.31
  409.1 43.5 all-gather.39
  454.7 67.6 all-gather.37
  524.3 43.3 all-gather.47
  569.8 67.6 all-gather.45
  639.4 43.3 all-gather.43
  685.4 67.6 all-gather.41
  755.0 43.3 all-gather.51
  800.3 67.6 all-gather.49
  1031.5 41.2 reduce-scatter.13
  1091.4 41.6 reduce-scatter.11
  1135.5 45.6 all-gather.35
  1257.7 42.3 reduce-scatter.15
  1303.2 34.8 all-reduce.12
  1343.7 60.9 all-reduce.14
  1407.8 33.7 reduce-scatter.17
  1445.0 34.1 reduce-scatter.23
  1482.1 34.0 reduce-scatter.21
  1519.5 34.1 reduce-scatter.19
  1556.6 34.0 reduce-scatter.25
where the time goes:
time: 1610 us; the launch traced here: 1600 us
  waiting for transfers between devices  861 us (53%)
  matrix products  219 us (14%)
  other arithmetic  206 us (13%)
  local copies, waits for them, and re-layouts  190 us (12%)
  blocking collectives  102 us (6%)
  between operations  18.3 us (1%)
    all_gather x4, waiting for transfers between devices, on_device(): lax.all_gather(inner_weight[expert], 'row', axis=0, tiled=True)  228 us
    reduce_scatter x5, waiting for transfers between devices, on_device(): lax.psum_scatter(shortened(tuple((spread_pick(adapter, part) for part in...  170 us
    scatter-add x4, other arithmetic, on_device(): grad_inner_total.at[expert_rows].add(grad_gate_up.astype(jnp.float32))  98.8 us
    all_gather x4, waiting for transfers between devices, on_device(): lax.all_gather(down_weight[expert], 'row', axis=0, tiled=True)  85.5 us
    all_gather x1, waiting for transfers between devices, on_device(): lax.all_gather(query_weight, 'row', axis=1, tiled=True)  85.5 us
    reduce_scatter x4, waiting for transfers between devices, partials(): return lax.psum_scatter(part, 'col', scatter_dimension=1, tiled=True)  80.6 us
    all_gather x1, waiting for transfers between devices, on_device(): lax.all_gather(out_weight, 'row', axis=1, tiled=True)  71.9 us
    psum x1, waiting for transfers between devices, on_device(): lax.psum(shortened(tuple((spread_pick(adapter, part) for part in dense_ri...  56.1 us
  transfers between devices with their start and end apart: 26, of which 21 were waited for; matrix products, arithmetic and copies ran while one was open for 20% of the time, Pallas kernels for 0%

commit v1 on v0

v1 whole, which is shorter than its diff:
```python
import jax
import jax.numpy as jnp
from jax import lax
from jax.sharding import PartitionSpec as P

HEAD_DIM = 128
EXP_ATT = 8
EXP_FF = 4
TOPK = 2
ADAPT = 8
RANK = 16
CAP_ATT = 80
CAP_FF = 160
EPSILON = 1e-06
ROPE_BASE = 10000.0
HIGHEST = lax.Precision.HIGHEST
F32 = jnp.float32
BF16 = jnp.bfloat16


def mm(spec, a, b):
    return jnp.einsum(spec, a, b, preferred_element_type=F32)


def exact(spec, a, b):
    return jnp.einsum(spec, a, b, precision=HIGHEST, preferred_element_type=F32)


def tables(count, head_width):
    position = jnp.arange(count).astype(F32)
    frequency = ROPE_BASE ** (-jnp.arange(head_width // 2).astype(F32) * 2.0 / head_width)
    angle = position[:, None] * frequency[None, :]
    return (jnp.cos(angle), jnp.sin(angle))


def rotate(values, cosine, sine):
    half = values.shape[-1] // 2
    first = values[..., :half]
    second = values[..., half:]
    return jnp.concatenate(
        [first * cosine - second * sine, second * cosine + first * sine], axis=-1
    )


def slot_rows(route, experts, capacity):
    count = route.shape[0]
    chosen = (route[:, :, None] == jnp.arange(experts, dtype=jnp.int32)).astype(BF16)
    per_token = jnp.sum(chosen, axis=1)
    place = jnp.arange(count)
    before = (place[None, :] < place[:, None]).astype(BF16)
    earlier = mm("tu,ue->te", before, per_token)
    inside = jnp.stack([jnp.zeros_like(chosen[:, 0]), chosen[:, 0]], axis=1).astype(F32)
    position = jnp.sum((earlier[:, None, :] + inside) * chosen.astype(F32), axis=2)
    return route * capacity + position.astype(jnp.int32)


def xor_chunks(array, axis, parts, index):
    shape = array.shape
    size = shape[axis] // parts
    step = 1
    while step < parts:
        view = array.reshape(
            shape[:axis] + (parts // (2 * step), 2, step * size) + shape[axis + 1 :]
        )
        first = lax.index_in_dim(view, 0, axis + 1, keepdims=True)
        second = lax.index_in_dim(view, 1, axis + 1, keepdims=True)
        flipped = jnp.concatenate([second, first], axis=axis + 1)
        array = jnp.where((index // step) % 2 == 1, flipped, view).reshape(shape)
        step *= 2
    return array


def chosen_of(logits, route, experts):
    onehot = (route[:, :, None] == jnp.arange(experts, dtype=jnp.int32)).astype(F32)
    return jnp.sum(onehot * logits[:, None, :], axis=2)


def router_back(gates, grad_gates, route, experts):
    centred = gates * (grad_gates - jnp.sum(gates * grad_gates, axis=1, keepdims=True))
    onehot = (route[:, :, None] == jnp.arange(experts, dtype=jnp.int32)).astype(F32)
    return jnp.sum(centred[:, :, None] * onehot, axis=1)


def on_device(
    inputs,
    cotangent,
    lengths,
    adapter_pick,
    attn_route,
    ffn_route,
    norm_one,
    norm_two,
    router_attn,
    router_ffn,
    kv_weight,
    query_weight,
    out_weight,
    inner_weight,
    down_weight,
    query_left,
    query_right,
    kv_left,
    kv_right,
    out_left,
    out_right,
    inner_left,
    inner_right,
    down_left,
    down_right,
):
    count, slice_width = inputs.shape
    width = router_attn.shape[0]
    rows_axis = lax.axis_size("row")
    replicas = rows_axis // EXP_FF
    row = lax.axis_index("row")
    col = lax.axis_index("col")
    expert = row // replicas
    depth = inner_weight.shape[1]
    units = inner_weight.shape[3]
    length = lengths[0]
    adapter = adapter_pick[0]
    position = jnp.arange(count)
    valid = (position < length).astype(F32)
    cosine, sine = tables(count, HEAD_DIM)
    scaling = HEAD_DIM ** (-0.5)

    def swap(value, offset):
        return lax.ppermute(value, "row", [(i, i ^ offset) for i in range(rows_axis)])

    def features(part):
        return lax.all_gather(part, "col", axis=1, tiled=True)

    def partials(part):
        return lax.psum_scatter(
            part.astype(BF16), "col", scatter_dimension=1, tiled=True
        ).astype(F32)

    def own_columns(table):
        return lax.dynamic_slice_in_dim(table, col * slice_width, slice_width, 0)

    kv_full = lax.all_gather(kv_weight, "row", axis=1, tiled=True)
    query_full = lax.all_gather(query_weight, "row", axis=1, tiled=True)
    out_full = lax.all_gather(out_weight, "row", axis=1, tiled=True)

    near = []
    for j in range(EXP_FF):
        which = expert ^ j
        inner_own = lax.dynamic_index_in_dim(inner_weight, which, 0, keepdims=False)
        down_own = lax.dynamic_index_in_dim(down_weight, which, 0, keepdims=False)
        piece = jnp.concatenate([inner_own[:, 0], inner_own[:, 1], down_own], axis=1)
        near.append(swap(piece, j * replicas) if j else piece)
    chunks = []
    for j in range(EXP_FF):
        for i in range(replicas):
            chunks.append(swap(near[j], i) if i else near[j])
    expert_block = jnp.concatenate(chunks, axis=0)
    gate_up_block = expert_block[:, : 2 * units]
    down_block = expert_block[:, 2 * units :]

    picks = lax.all_gather(adapter_pick, "row", axis=0, tiled=True)
    pick_onehot = (picks[:, None] == jnp.arange(ADAPT, dtype=jnp.int32)[None, :]).astype(BF16)
    lefts_own = jnp.stack(
        [query_left, kv_left, out_left, inner_left, down_left], axis=1
    ).swapaxes(2, 3)
    lefts_sent = mm(
        "ga,ax->gx", pick_onehot, lefts_own.reshape(ADAPT, 5 * RANK * depth)
    ).astype(BF16)
    lefts = lax.all_to_all(
        lefts_sent.reshape(rows_axis, 5 * RANK, depth), "row", 0, 0, tiled=False
    )
    lefts = lefts.swapaxes(0, 1).reshape(5, RANK, width)
    left_query, left_kv, left_out, left_inner, left_down = (lefts[i] for i in range(5))
    right_query = query_right[adapter].astype(F32)
    right_kv = kv_right[adapter].astype(F32)
    right_out = out_right[adapter].astype(F32)
    right_inner_all = inner_right.reshape(ADAPT * RANK, 2 * units)
    right_down_all = down_right.reshape(ADAPT * RANK, units)
    own_adapter = (jnp.arange(ADAPT, dtype=jnp.int32) == adapter).astype(F32)

    def spread(low):
        return (own_adapter[None, :, None] * low[:, None, :]).reshape(count, ADAPT * RANK)

    def unspread(high):
        return jnp.sum(
            own_adapter[None, :, None] * high.reshape(count, ADAPT, RANK), axis=1
        )

    slots_attn = slot_rows(attn_route, EXP_ATT, CAP_ATT)
    slots_ffn = slot_rows(ffn_route, EXP_FF, CAP_FF)
    rows_attn = jnp.arange(EXP_ATT * CAP_ATT, dtype=jnp.int32)
    pick_attn = [
        (rows_attn[:, None] == slots_attn[None, :, k]).astype(BF16) for k in range(TOPK)
    ]
    pick_attn_any = pick_attn[0] + pick_attn[1]
    pick_attn_both = jnp.concatenate(pick_attn, axis=1)
    order = (expert ^ jnp.arange(EXP_FF, dtype=jnp.int32))[:, None] * CAP_FF
    rows_ffn = (order + jnp.arange(CAP_FF, dtype=jnp.int32)[None, :]).reshape(EXP_FF * CAP_FF)
    pick_ffn = [(rows_ffn[:, None] == slots_ffn[None, :, k]).astype(BF16) for k in range(TOPK)]
    pick_ffn_any = pick_ffn[0] + pick_ffn[1]

    def trade(rows):
        blocks = rows.reshape(EXP_FF, CAP_FF, rows.shape[1])
        return jnp.concatenate(
            [blocks[j] if j == 0 else swap(blocks[j], j * replicas) for j in range(EXP_FF)]
        )

    masked_cot = cotangent * valid.astype(BF16)[:, None]
    cot_full = features(masked_cot)
    grad_low_down = mm("td,rd->tr", cot_full, left_down)
    cot_rows = trade(
        mm(
            "ct,td->cd",
            pick_ffn_any,
            jnp.concatenate([cot_full, spread(grad_low_down).astype(BF16)], axis=1),
        ).astype(BF16)
    )

    x_full = features(inputs)
    x_wide = x_full.astype(F32)
    scale_one = lax.rsqrt(jnp.mean(x_wide * x_wide, axis=1, keepdims=True) + EPSILON)
    hidden_one = (x_wide * scale_one * norm_one).astype(BF16)
    gates_attn = jax.nn.softmax(
        chosen_of(mm("td,de->te", hidden_one, router_attn), attn_route, EXP_ATT), axis=1
    )
    rank_query = mm("td,rd->tr", hidden_one, left_query)
    rank_kv = mm("td,rd->tr", hidden_one, left_kv)
    kv_raw = mm("td,sdw->stw", hidden_one, kv_full) + mm(
        "tr,rsw->stw", rank_kv.astype(BF16), right_kv.astype(BF16)
    )
    query_width = kv_raw.shape[2]
    heads = query_width // HEAD_DIM
    keys = rotate(
        kv_raw[0].reshape(count, heads, HEAD_DIM), cosine[:, None], sine[:, None]
    ).astype(BF16)
    values = kv_raw[1].reshape(count, heads, HEAD_DIM).astype(BF16)
    small = jnp.concatenate([rank_query, gates_attn, cosine, sine], axis=1)
    small_rows = exact("ct,tx->cx", pick_attn_any.astype(F32), small)
    rank_query_rows = small_rows[:, :RANK]
    gate_rows = exact("ct,tx->cx", pick_attn[0].astype(F32), gates_attn[:, :1]) + exact(
        "ct,tx->cx", pick_attn[1].astype(F32), gates_attn[:, 1:]
    )
    half = HEAD_DIM // 2
    cosine_rows = small_rows[:, RANK + TOPK : RANK + TOPK + half]
    sine_rows = small_rows[:, RANK + TOPK + half :]
    hidden_rows = mm("ct,td->cd", pick_attn_any, hidden_one).astype(BF16)
    query_rows = mm(
        "ecd,edw->ecw", hidden_rows.reshape(EXP_ATT, CAP_ATT, width), query_full
    ).reshape(EXP_ATT * CAP_ATT, query_width) + mm(
        "cr,rw->cw", rank_query_rows.astype(BF16), right_query.astype(BF16)
    )
    query_rows = (
        rotate(
            query_rows.reshape(EXP_ATT * CAP_ATT, heads, HEAD_DIM),
            cosine_rows[:, None],
            sine_rows[:, None],
        )
        .astype(BF16)
        .reshape(EXP_ATT * CAP_ATT, query_width)
    )
    queries = (
        mm("cx,cw->xw", pick_attn_both, query_rows)
        .astype(BF16)
        .reshape(TOPK, count, heads, HEAD_DIM)
    )
    allowed = (position[None, :] <= position[:, None]) & (position[None, :] < length)
    scores = mm("kbhd,jhd->hkbj", queries, keys) * scaling
    scores = jnp.where(allowed[None, None], scores, -1e30)
    exponent = jnp.exp(scores - jnp.max(scores, axis=-1, keepdims=True))
    probability = exponent / jnp.sum(exponent, axis=-1, keepdims=True)
    probs = probability.astype(BF16)
    attended = mm("hkbj,jhd->kbhd", probs, values).astype(BF16).reshape(TOPK * count, query_width)
    attended_rows = mm("cx,xw->cw", pick_attn_both, attended).astype(BF16)
    out_rows = mm(
        "ecw,edw->ecd", attended_rows.reshape(EXP_ATT, CAP_ATT, query_width), out_full
    ).reshape(EXP_ATT * CAP_ATT, width)
    low_rows = mm("cw,rw->cr", attended_rows, right_out.astype(BF16))
    out_ext = (jnp.concatenate([out_rows, low_rows], axis=1) * gate_rows).astype(BF16)
    combined = mm("ct,cd->td", pick_attn_any, out_ext)
    low_out_part = combined[:, width:]
    branch_attn = combined[:, :width] + mm("tr,rd->td", low_out_part.astype(BF16), left_out)
    x_local = inputs.astype(F32)
    middle = x_local + partials(branch_attn)
    square_sum, low_out_full = lax.psum((jnp.sum(middle * middle, axis=1), low_out_part), "col")
    scale_two = lax.rsqrt(square_sum[:, None] / width + EPSILON)
    hidden_two = features((middle * scale_two * own_columns(norm_two)).astype(BF16))

    gates_ffn = jax.nn.softmax(
        chosen_of(mm("td,de->te", hidden_two, router_ffn), ffn_route, EXP_FF), axis=1
    )
    rank_inner = mm("td,rd->tr", hidden_two, left_inner)
    hidden_ext = jnp.concatenate([hidden_two, spread(rank_inner).astype(BF16)], axis=1)
    hidden_out = mm("ct,td->cd", pick_ffn_any, hidden_ext).astype(BF16)
    gate_high = gates_ffn.astype(BF16)
    gate_low = (gates_ffn - gate_high.astype(F32)).astype(BF16)
    gate_out = sum(
        mm("ct,tx->cx", pick_ffn[k], jnp.stack([gate_high[:, k], gate_low[:, k]], axis=1))
        for k in range(TOPK)
    )
    gate_out = jnp.pad(gate_out, ((0, 0), (0, 126))).astype(BF16)
    hidden_in = trade(jnp.concatenate([hidden_out, gate_out], axis=1))
    gate_in = (
        hidden_in[:, width + 128].astype(F32) + hidden_in[:, width + 129].astype(F32)
    )[:, None]
    hidden_in_ext = hidden_in[:, width : width + 128]
    hidden_in = xor_chunks(hidden_in[:, :width], 1, rows_axis, row)
    cot_in_ext = cot_rows[:, width:]
    cot_in = xor_chunks(cot_rows[:, :width], 1, rows_axis, row)
    grad_mixed = mm("cd,df->cf", cot_in, down_block) + mm("cr,rf->cf", cot_in_ext, right_down_all)
    gate_up = mm("cd,df->cf", hidden_in, gate_up_block) + mm(
        "cr,rf->cf", hidden_in_ext, right_inner_all
    )
    gate_part = gate_up[:, :units]
    up_part = gate_up[:, units:]
    sig = jax.nn.sigmoid(gate_part)
    mixed = (gate_part * sig * up_part).astype(BF16)
    gate_grad_rows = jnp.sum(mixed.astype(F32) * grad_mixed, axis=1, keepdims=True)
    grad_mixed = grad_mixed * gate_in
    grad_gate_up = jnp.concatenate(
        [
            grad_mixed * up_part * sig * (1.0 + gate_part * (1.0 - sig)),
            grad_mixed * gate_part * sig,
        ],
        axis=1,
    ).astype(BF16)
    grad_rows = xor_chunks(
        mm("cf,df->cd", grad_gate_up, gate_up_block).astype(BF16), 1, rows_axis, row
    )
    grad_rank_rows = mm("cf,rf->cr", grad_gate_up, right_inner_all).astype(BF16)
    gg_high = gate_grad_rows.astype(BF16)
    gg_low = (gate_grad_rows - gg_high.astype(F32)).astype(BF16)
    grad_msg = jnp.concatenate(
        [grad_rows, grad_rank_rows, jnp.pad(jnp.concatenate([gg_high, gg_low], 1), ((0, 0), (0, 126)))],
        axis=1,
    )
    grad_back = trade(grad_msg)
    down_rows = xor_chunks(
        (mm("cf,df->cd", mixed, down_block) * gate_in).astype(BF16), 1, rows_axis, row
    )
    down_low_rows = (mm("cf,rf->cr", mixed, right_down_all) * gate_in).astype(BF16)
    down_back = trade(jnp.concatenate([down_rows, down_low_rows], axis=1))
    grad_right_inner = mm("cr,cf->rf", hidden_in_ext, grad_gate_up)
    grad_right_down = mm("cr,cf->rf", (cot_in_ext.astype(F32) * gate_in).astype(BF16), mixed)
    ffn_rights = lax.psum(
        jnp.concatenate([grad_right_inner, grad_right_down], axis=1).astype(BF16), "row"
    ).astype(F32)

    grad_comb = mm("ct,cd->td", pick_ffn_any, grad_back[:, : width + 128])
    gg_back = grad_back[:, width + 128 : width + 130]
    grad_gates_part = jnp.stack(
        [jnp.sum(mm("ct,cx->tx", pick_ffn[k], gg_back), axis=1) for k in range(TOPK)], axis=1
    )
    grad_rank_inner = unspread(grad_comb[:, width:])
    grad_two_part = grad_comb[:, :width] + mm(
        "tr,rd->td", grad_rank_inner.astype(BF16), left_inner
    )
    down_comb = mm("ct,cd->td", pick_ffn_any, down_back)
    low_down_part = unspread(down_comb[:, width:])
    branch_ffn = down_comb[:, :width] + mm("tr,rd->td", low_down_part.astype(BF16), left_down)
    (grad_gates_ffn,) = lax.psum((grad_gates_part,), "col")
    logits_ffn_grad = router_back(gates_ffn, grad_gates_ffn, ffn_route, EXP_FF)
    grad_two = partials(grad_two_part) + exact(
        "te,de->td", logits_ffn_grad, own_columns(router_ffn).astype(F32)
    )
    scaled_two = grad_two * own_columns(norm_two)
    inner_sum, rank_inner_grad_full, low_down_full = lax.psum(
        (jnp.sum(scaled_two * middle, axis=1), grad_rank_inner, low_down_part), "col"
    )
    grad_middle = (
        masked_cot.astype(F32)
        + scale_two * scaled_two
        - middle * scale_two**3 * inner_sum[:, None] / width
    )
    output = ((middle + partials(branch_ffn)) * valid[:, None]).astype(BF16)

    grad_full = features(grad_middle.astype(BF16))
    grad_low_out = mm("td,rd->tr", grad_full, left_out)
    grad_middle_rows = mm(
        "ct,td->cd",
        pick_attn_any,
        jnp.concatenate([grad_full, grad_low_out.astype(BF16)], axis=1),
    ).astype(BF16)
    grad_att_rows = mm(
        "ecd,edw->ecw",
        grad_middle_rows[:, :width].reshape(EXP_ATT, CAP_ATT, width),
        out_full,
    ).reshape(EXP_ATT * CAP_ATT, query_width) + mm(
        "cr,rw->cw", grad_middle_rows[:, width:], right_out.astype(BF16)
    )
    gg_attn_rows = jnp.sum(attended_rows.astype(F32) * grad_att_rows, axis=1, keepdims=True)
    grad_gates_attn_part = jnp.concatenate(
        [exact("ct,cx->tx", pick_attn[k].astype(F32), gg_attn_rows) for k in range(TOPK)], axis=1
    )
    grad_att_rows = (grad_att_rows * gate_rows).astype(BF16)
    grad_attended = (
        mm("cx,cw->xw", pick_attn_both, grad_att_rows)
        .astype(BF16)
        .reshape(TOPK, count, heads, HEAD_DIM)
    )
    gated_low = (gates_attn.T[:, :, None] * grad_low_out[None]).reshape(TOPK * count, RANK)
    grad_right_out = mm("xr,xw->rw", gated_low.astype(BF16), attended)
    grad_prob = mm("kbhd,jhd->hkbj", grad_attended, values)
    centre = jnp.sum(probability * grad_prob, axis=-1, keepdims=True)
    grad_scores = (probability * (grad_prob - centre)).astype(BF16)
    grad_queries = mm("hkbj,jhd->kbhd", grad_scores, keys) * scaling
    grad_keys = mm("hkbj,kbhd->jhd", grad_scores, queries) * scaling
    grad_values = mm("hkbj,kbhd->jhd", probs, grad_attended)
    grad_query_raw = (
        rotate(grad_queries, cosine[None, :, None], -sine[None, :, None])
        .astype(BF16)
        .reshape(TOPK * count, query_width)
    )
    grad_key_raw = rotate(grad_keys, cosine[:, None], -sine[:, None])
    grad_kv = jnp.stack([grad_key_raw, grad_values]).astype(BF16).reshape(2, count, query_width)
    grad_query_rows = mm("cx,xw->cw", pick_attn_both, grad_query_raw).astype(BF16)
    grad_one_rows = (
        mm("ecw,edw->ecd", grad_query_rows.reshape(EXP_ATT, CAP_ATT, query_width), query_full)
        .astype(BF16)
        .reshape(EXP_ATT * CAP_ATT, width)
    )
    grad_query_sum = jnp.sum(
        grad_query_raw.astype(F32).reshape(TOPK, count, query_width), axis=0
    )
    grad_query_sum_low = grad_query_sum.astype(BF16)
    grad_rank_query = mm("tw,rw->tr", grad_query_sum_low, right_query.astype(BF16))
    grad_rank_kv = mm("stw,rsw->tr", grad_kv, right_kv.astype(BF16))
    grad_one_part = (
        mm("ct,cd->td", pick_attn_any, grad_one_rows)
        + mm("stw,sdw->td", grad_kv, kv_full)
        + mm(
            "tr,rd->td",
            jnp.concatenate([grad_rank_query, grad_rank_kv], axis=1).astype(BF16),
            jnp.concatenate([left_query, left_kv], axis=0),
        )
    )
    grad_right_query = mm("tr,tw->rw", rank_query.astype(BF16), grad_query_sum_low)
    grad_right_kv = mm("tr,stw->rsw", rank_kv.astype(BF16), grad_kv)
    grad_gates_attn, rank_query_grad_full, rank_kv_grad_full = lax.psum(
        (grad_gates_attn_part, grad_rank_query, grad_rank_kv), "col"
    )
    logits_attn_grad = router_back(gates_attn, grad_gates_attn, attn_route, EXP_ATT)
    grad_one = partials(grad_one_part) + exact(
        "te,de->td", logits_attn_grad, own_columns(router_attn).astype(F32)
    )
    scaled_one = grad_one * own_columns(norm_one)
    outer_sum = lax.psum(jnp.sum(scaled_one * x_local, axis=1), "col")
    grad_inputs = (
        grad_middle
        + scale_one * scaled_one
        - x_local * scale_one**3 * outer_sum[:, None] / width
    )

    hiddens = (hidden_one, hidden_one, grad_full, hidden_two, cot_full)
    lows = (
        rank_query_grad_full,
        rank_kv_grad_full,
        low_out_full,
        rank_inner_grad_full,
        low_down_full,
    )
    left_parts = jnp.concatenate(
        [mm("tr,td->rd", low.astype(BF16), hidden) for low, hidden in zip(lows, hiddens)]
    ).astype(BF16)
    left_parts = lax.all_to_all(
        left_parts.reshape(5 * RANK, rows_axis, depth), "row", 1, 0, tiled=False
    )
    left_grads = mm("ga,gx->ax", pick_onehot, left_parts.reshape(rows_axis, 5 * RANK * depth))
    left_grads = left_grads.reshape(ADAPT, 5, RANK, depth).swapaxes(2, 3)
    right_parts = jnp.concatenate(
        [grad_right_query, grad_right_kv[:, 0], grad_right_kv[:, 1], grad_right_out], axis=1
    ).astype(BF16)
    right_all = lax.all_gather(right_parts, "row", axis=0)
    right_grads = mm(
        "ga,gx->ax", pick_onehot, right_all.reshape(rows_axis, RANK * 4 * query_width)
    ).reshape(ADAPT, RANK, 4, query_width)
    return (
        output,
        grad_inputs,
        left_grads[:, 0],
        right_grads[:, :, 0],
        left_grads[:, 1],
        right_grads[:, :, 1:3],
        left_grads[:, 2],
        right_grads[:, :, 3],
        left_grads[:, 3],
        ffn_rights[:, : 2 * units].reshape(ADAPT, RANK, 2, units),
        left_grads[:, 4],
        ffn_rights[:, 2 * units :].reshape(ADAPT, RANK, units),
    )


def solution(mesh):
    placed = (
        P("row", "col"),
        P("row", "col"),
        P("row"),
        P("row"),
        P("row", None),
        P("row", None),
        P(),
        P(),
        P(),
        P(),
        P(None, "row", "col"),
        P(None, "row", "col"),
        P(None, "row", "col"),
        P(None, "row", None, "col"),
        P(None, "row", "col"),
        P(None, "row", None),
        P(None, None, "col"),
        P(None, "row", None),
        P(None, None, None, "col"),
        P(None, "row", None),
        P(None, None, "col"),
        P(None, "row", None),
        P(None, None, None, "col"),
        P(None, "row", None),
        P(None, None, "col"),
    )
    return jax.shard_map(
        on_device,
        mesh=mesh,
        in_specs=placed,
        out_specs=(
            P("row", "col"),
            P("row", "col"),
            P(None, "row", None),
            P(None, None, "col"),
            P(None, "row", None),
            P(None, None, None, "col"),
            P(None, "row", None),
            P(None, None, "col"),
            P(None, "row", None),
            P(None, None, None, "col"),
            P(None, "row", None),
            P(None, None, "col"),
        ),
        check_vma=False,
    )
```

time: 1610 us -> 1190 us (0.74)
  waiting for transfers between devices: 861 us -> 376 us
  local copies, waits for them, and re-layouts: 190 us -> 350 us
  other arithmetic: 206 us -> 145 us
  matrix products: 219 us -> 169 us
  starting transfers between devices: 1.3 us -> 50.5 us
  blocking collectives: 102 us -> 66.7 us
    all_gather x12 -> x3, waiting for transfers between devices: 514 us -> 197 us  [the longest x1 80.7 us: on_device(): query_full = lax.all_gather(query_weight, 'row', axis=1, tiled=True)]
    reduce_scatter x9 -> x4, waiting for transfers between devices: 251 us -> 30.1 us  [partials(): lax.psum_scatter(part.astype(BF16), 'col', scatter_dimension=1, tiled=True)]
    scatter-add x9 -> x0, other arithmetic: 131 us -> none  [the longest x4 98.8 us: on_device(): grad_inner_total.at[expert_rows].add(grad_gate_up.astype(jnp.float32))]
    concatenate x9 -> x25, local copies, waits for them, and re-layouts: 7.59 us -> 119 us  [the longest x20 114 us: xor_chunks(): flipped = jnp.concatenate([second, first], axis=axis + 1)]
    gather x41 -> x0, local copies, waits for them, and re-layouts: 99.9 us -> none  [the longest x4 24 us: on_device(): inner_pad[expert_rows]]
    ppermute x0 -> x19, waiting for transfers between devices: none -> 99.3 us  [swap(): lax.ppermute(value, 'row', [(i, i ^ offset) for i in range(rows_axis)])]
    concatenate x3 -> x28, other arithmetic: 0.16 us -> 93.9 us  [the longest x12 77.4 us: xor_chunks(): flipped = jnp.concatenate([second, first], axis=axis + 1)]
    psum x2 -> x1, waiting for transfers between devices: 89.4 us -> 2.27 us  [on_device(): lax.psum(jnp.concatenate([grad_right_inner, grad_right_down], axis=1).ast...]
  transfers between devices with their start and end apart: 26 -> 33, of which waited for: 21 -> 16; matrix products, arithmetic and copies ran while one was open for 20% -> 26% of each run, Pallas kernels for 0% -> 0%
where the time goes in v1:
time: 1190 us; the launch traced here: 1180 us
  waiting for transfers between devices  376 us (32%)
  local copies, waits for them, and re-layouts  350 us (29%)
  matrix products  169 us (14%)
  other arithmetic  145 us (12%)
  blocking collectives  66.7 us (6%)
  starting transfers between devices  50.5 us (4%)
  between operations  18.8 us (2%)
    dot_general x67, matrix products, mm(): return jnp.einsum(spec, a, b, preferred_element_type=F32)  161 us
    concatenate x20, local copies, waits for them, and re-layouts, xor_chunks(): flipped = jnp.concatenate([second, first], axis=axis + 1)  114 us
    ppermute x19, waiting for transfers between devices, swap(): lax.ppermute(value, 'row', [(i, i ^ offset) for i in range(rows_axis)])  99.3 us
    all_gather x1, waiting for transfers between devices, on_device(): query_full = lax.all_gather(query_weight, 'row', axis=1, tiled=True)  80.7 us
    concatenate x12, other arithmetic, xor_chunks(): flipped = jnp.concatenate([second, first], axis=axis + 1)  77.4 us
    all_gather x1, waiting for transfers between devices, on_device(): out_full = lax.all_gather(out_weight, 'row', axis=1, tiled=True)  69.2 us
    unnamed x368, local copies, waits for them, and re-layouts  69.2 us
    slice x12, local copies, waits for them, and re-layouts, xor_chunks(): second = lax.index_in_dim(view, 1, axis + 1, keepdims=True)  56.9 us
  transfers between devices with their start and end apart: 33, of which 16 were waited for; matrix products, arithmetic and copies ran while one was open for 26% of the time, Pallas kernels for 0%

profile of v1, /device:TPU:9, one launch (start us, length us, event | category | flops | bytes accessed | tf_op | source)
XLA Modules:
  0.0 1176.1 jit_solution(7412830858261269321)
XLA Ops:
  15.3 6.5 all-reduce.4
  27.2 6.1 all-to-all-start
  33.6 5.8 constant_dynamic-slice_fusion
  74.3 24.2 %collective-permute-done.4 = bf16[256,4224]{1,0:T(8,128)(2,1)} collective-permute-done((bf16[256,4224]{1,0:T(8,128)(2,1)}, bf16[256,4224]{1,0:T(8,128)(2,1)}, u32[]{:S(2)}, u32[]{:S(2)}) %collective-permute-start.4) | collective-permute-done | bytes 2162720 | tf_op jit(solution)/shard_map/ppermute | solution.py:128
  100.4 8.2 collective-permute-done.6
  108.6 6.1 collective-permute-start.7
  114.7 47.2 %all-gather.10.cloned.1.call-done = bf16[2,2048,512]{2,1,0:T(8,128)(2,1)} async-done(((bf16[2,256,512]{2,1,0:T(8,128)(2,1)}), bf16[2,2048,512]{2,1,0:T(8,128)(2,1)}) %all-gather.10.cloned.1.call-update) | async-done | bytes 4194320 | tf_op jit(solution)/shard_map/all_gather | solution.py:141
  173.0 80.7 %all-gather.12.cloned.1.call-done = bf16[8,2048,512]{2,1,0:T(8,128)(2,1)} async-done(((bf16[8,256,512]{2,1,0:T(8,128)(2,1)}), bf16[8,2048,512]{2,1,0:T(8,128)(2,1)}) %all-gather.12.cloned.1.call-update) | async-done | bytes 16777232 | tf_op jit(solution)/shard_map/all_gather | solution.py:142
  253.8 9.8 fusion.272
  276.2 69.2 %all-gather.14.cloned.1.call-done = bf16[8,2048,512]{2,1,0:T(8,128)(2,1)} async-done(((bf16[8,256,512]{2,1,0:T(8,128)(2,1)}), bf16[8,2048,512]{2,1,0:T(8,128)(2,1)}) %all-gather.14.cloned.1.call-update) | async-done | bytes 16777232 | tf_op jit(solution)/shard_map/all_gather | solution.py:143
  345.4 13.2 %fusion.275 = f32[8,80,2048]{2,1,0:T(8,128)} fusion(bf16[8,80,512]{2,1,0:T(8,128)(2,1)S(1)} %bitcast.394, bf16[8,2048,512]{2,1,0:T(8,128)(2,1)} %all-gather.14.cloned.1.call-done), kind=kOutput, calls=%fused_computation.491 | convolution fusion | flops 1342177280 | bytes 22675456 | tf_op jit(solution)/shard_map/ecw,edw->ecd/dot_general | solution.py:22
  379.4 11.9 %reduce-scatter.5.cloned.1.call-done = bf16[256,512]{0,1:T(8,128)(2,1)} async-done(((bf16[256,2048]{0,1:T(8,128)(2,1)}), bf16[256,512]{0,1:T(8,128)(2,1)}) %reduce-scatter.5.cloned.1.call-update) | async-done | bytes 262160 | tf_op jit(solution)/shard_map/reduce_scatter | solution.py:134
  392.4 8.7 psum.77
  412.9 19.6 %all-gather.16.cloned.1.call-done = bf16[256,2048]{0,1:T(8,128)(2,1)} async-done(((bf16[256,512]{0,1:T(8,128)(2,1)}), bf16[256,2048]{0,1:T(8,128)(2,1)}) %all-gather.16.cloned.1.call-update) | async-done | bytes 1048592 | tf_op jit(solution)/shard_map/all_gather | solution.py:131
  446.3 9.3 collective-permute-done.15
  456.8 16.2 %collective-permute-done.14 = bf16[160,2176]{1,0:T(8,128)(2,1)S(1)} collective-permute-done((bf16[160,2176]{1,0:T(8,128)(2,1)S(1)}, bf16[160,2176]{1,0:T(8,128)(2,1)S(1)}, u32[]{:S(2)}, u32[]{:S(2)}) %collective-permute-start.14) | collective-permute-done | bytes 696352 | tf_op jit(solution)/shard_map/ppermute | solution.py:128
  486.7 6.7 fusion.261
  493.4 6.0 pad_maximum_fusion.10
  506.3 5.5 reshape.872
  520.0 6.8 pad_maximum_fusion.11
  526.8 8.5 concatenate.262
  535.3 5.5 concatenate.266
  550.2 6.0 pad_maximum_fusion.12
  572.3 6.8 fusion.258
  579.1 6.0 pad_maximum_fusion.4
  592.0 5.9 reshape.863
  606.0 6.8 pad_maximum_fusion.5
  612.8 8.3 concatenate.235
  621.2 5.5 concatenate.239
  636.0 6.0 pad_maximum_fusion.6
  649.7 16.2 %fusion.12 = f32[640,2816]{1,0:T(8,128)} fusion(f32[640,2816]{1,0:T(8,128)} %fusion.277, bf16[2048,4224]{1,0:T(8,128)(2,1)} %constant_dynamic-update-slice_fusion, bf16[640,2048]{1,0:T(8,128)(2,1)} %bitcast.402, bf16[640,2048]{1,0:T(8,128)(2,1)} %concatenate.239, bf16[640,2048]{1,0:T(8,128)(2,1)} %concatenate.240, pred[]{:T(512)S(6)} %eq.192, ...), kind=kOutput, calls=%fused_computation.28 | convolution fusion | flops 7387709440 | bytes 36438020 | tf_op jit(solution)/shard_map/cd,df->cf/dot_general | solution.py:22
  667.8 13.0 %multiply_convert_fusion.2 = (bf16[640,1408]{1,0:T(8,128)(2,1)S(1)}, bf16[640,1408]{1,0:T(8,128)(2,1)S(1)}, f32[640]{0:T(1024)S(1)}, bf16[640,1408]{1,0:T(8,128)(2,1)}) fusion(f32[640,2816]{1,0:T(8,128)} %fusion.12, f32[640]{0:T(1024)S(1)} %add_reduce_fusion, f32[640,1408]{1,0:T(8,128)} %fusion.278, ...), kind=kOutput, calls=%fused_computation.39 | convolution fusion | flops 3713842688 | bytes 32479748 | tf_op jit(solution)/shard_map/cd,df->cf/dot_general | solution.py:22
  682.6 10.5 fusion.20
  700.2 6.9 fusion.252
  707.1 6.8 pad_maximum_fusion.13
  714.0 8.0 concatenate.270
  739.0 6.8 pad_maximum_fusion.14
  745.8 8.3 concatenate.272
  759.6 5.9 concatenate.277
  765.5 8.9 multiply_convert_fusion
  774.4 5.5 reshape.865
  779.9 5.5 reshape.866
  785.4 6.8 fusion.255
  792.1 6.9 pad_maximum_fusion.7
  799.0 8.0 concatenate.247
  812.4 5.5 reshape.867
  826.1 7.0 pad_maximum_fusion.8
  833.1 8.3 concatenate.249
  846.8 5.5 concatenate.254
  860.5 6.0 pad_maximum_fusion.15
  873.2 6.0 pad_maximum_fusion.9
  895.4 10.3 collective-permute-start.16
  905.7 11.4 collective-permute-done.11
  919.8 28.1 %collective-permute-done.17 = bf16[160,2304]{1,0:T(8,128)(2,1)S(1)} collective-permute-done((bf16[160,2304]{1,0:T(8,128)(2,1)}, bf16[160,2304]{1,0:T(8,128)(2,1)S(1)}, u32[]{:S(2)}, u32[]{:S(2)}) %collective-permute-start.17) | collective-permute-done | bytes 737312 | tf_op jit(solution)/shard_map/ppermute | solution.py:128
  960.1 6.7 psum.78
  966.9 18.3 %reduce-scatter.9.cloned.1.call-done = bf16[256,512]{0,1:T(8,128)(2,1)} async-done(((bf16[256,2048]{0,1:T(8,128)(2,1)}), bf16[256,512]{0,1:T(8,128)(2,1)}) %reduce-scatter.9.cloned.1.call-update) | async-done | bytes 262160 | tf_op jit(solution)/shard_map/reduce_scatter | solution.py:134
  986.6 8.7 psum.79
  1001.2 24.1 %all-gather.20.cloned.1.call-done = bf16[256,2048]{0,1:T(8,128)(2,1)} async-done(((bf16[256,512]{0,1:T(8,128)(2,1)}), bf16[256,2048]{0,1:T(8,128)(2,1)}) %all-gather.20.cloned.1.call-update) | async-done | bytes 1048592 | tf_op jit(solution)/shard_map/all_gather | solution.py:131
  1037.3 9.8 fusion.279
  1060.4 12.7 %convolution_convert_fusion.6 = bf16[8,80,2048]{2,1,0:T(8,128)(2,1)} fusion(bf16[8,80,512]{2,1,0:T(8,128)(2,1)S(1)} %bitcast.417, bf16[8,2048,512]{2,1,0:T(8,128)(2,1)} %all-gather.12.cloned.1.call-done), kind=kOutput, calls=%fused_computation.45 | convolution fusion | flops 1343488000 | bytes 20054016 | tf_op jit(solution)/shard_map/ecw,edw->ecd/dot_general | solution.py:22
  1100.4 10.4 all_gather.36
  1113.0 6.8 psum.80
  1127.0 18.9 %all-reduce.5 = (f32[256]{0:T(256)}, bf16[256,16]{0,1:T(8,128)(2,1)S(1)}, bf16[256,16]{0,1:T(8,128)(2,1)S(1)}, bf16[256,16]{0,1:T(8,128)(2,1)S(1)}, bf16[256,16]...) all-reduce(f32[256]{0:T(256)S(1)} %get-tuple-element.224, ...), channel_id=1, replica_groups=mesh['row'=8,'col'=4] {'col'}, use_global_device_ids=true, to_apply=%region_36.37 | all-reduce | flops 20736 | bytes 124928 | tf_op jit(solution)/shard_map/psum | solution.py:445
  1151.7 7.5 all-to-all-start.1
  (682 shorter events, 388.2 us)
Async XLA Ops:
  7.2 551.6 %copy-start = (bf16[8,16,1408]{2,1,0:T(8,128)(2,1)S(1)}, bf16[8,16,1408]{2,1,0:T(8,128)(2,1)}, u32[]{:S(2)}) copy-start(bf16[8,16,1408]{2,1,0:T(8,128)(2,1)} %param.49) | copy-start | bytes 1081348
  7.2 53.4 %all-gather.8.cloned.1.call-start = ((), (), s32[]{:S(2)}) async-start(), calls=%async_computation.6 | async-start | bytes 1310720 | tf_op jit(solution)/shard_map/all_gather | solution.py:131
  7.9 62.6 %all-gather.18.cloned.1.call-start = ((), (), s32[]{:S(2)}) async-start(), calls=%async_computation.13 | async-start | bytes 1310720 | tf_op jit(solution)/shard_map/all_gather | solution.py:131
  11.1 150.8 %all-gather.10.cloned.1.call-start = ((), (), s32[]{:S(2)}) async-start(), calls=%async_computation.7 | async-start | bytes 4718592 | tf_op jit(solution)/shard_map/all_gather | solution.py:141
  11.8 241.9 %all-gather.12.cloned.1.call-start = ((), (), s32[]{:S(2)}) async-start(), calls=%async_computation.8 | async-start | bytes 18874368 | tf_op jit(solution)/shard_map/all_gather | solution.py:142
  12.4 333.0 %all-gather.14.cloned.1.call-start = ((), (), s32[]{:S(2)}) async-start(), calls=%async_computation.9 | async-start | bytes 18874368 | tf_op jit(solution)/shard_map/all_gather | solution.py:143
  27.2 30.9 %all-to-all-start = ((bf16[8,80,256]{2,1,0:T(8,128)(2,1)}), bf16[8,80,256]{2,1,0:T(8,128)(2,1)}, u32[]{:S(2)}, u32[]{:S(2)}) async-start(bf16[8,80,256]{2,1,0:T(8,128)(2,1)} %copy.405), calls=%async_computation | async-start | bytes 655360 | tf_op jit(solution)/shard_map/all_to_all | solution.py:168
  33.4 357.9 %reduce-scatter.5.cloned.1.call-start = ((), (), s32[]{:S(2)}) async-start(), calls=%async_computation.10 | async-start | bytes 1310720 | tf_op jit(solution)/shard_map/reduce_scatter | solution.py:134
  42.3 324.2 %collective-permute-start.3 = (bf16[256,4224]{1,0:T(8,128)(2,1)}, bf16[256,4224]{1,0:T(8,128)(2,1)}, u32[]{:S(2)}, u32[]{:S(2)}) collective-permute-start(bf16[256,4224]{1,0:T(8,128)(2,1)} %get-tuple-element.155), channel_id=1, source_target_pairs={{0,4},{4,0},{8,12},{12,8},{16,20},{20,16},{24,28},{28,24},{1,5},{5... | collective-permute-start | bytes 6488072 | tf_op jit(solution)/shard_map/ppermute | solution.py:128
  44.1 54.4 %collective-permute-start.4 = (bf16[256,4224]{1,0:T(8,128)(2,1)}, bf16[256,4224]{1,0:T(8,128)(2,1)}, u32[]{:S(2)}, u32[]{:S(2)}) collective-permute-start(bf16[256,4224]{1,0:T(8,128)(2,1)} %pad_maximum_fusion.16), channel_id=1, source_target_pairs={{0,8},{4,12},{8,0},{12,4},{16,24},{20,28},{24,16},{28,20},{1,9},{5... | collective-permute-start | bytes 6488072 | tf_op jit(solution)/shard_map/ppermute | solution.py:128
  47.6 61.1 %collective-permute-start.6 = (bf16[256,4224]{1,0:T(8,128)(2,1)}, bf16[256,4224]{1,0:T(8,128)(2,1)}, u32[]{:S(2)}, u32[]{:S(2)}) collective-permute-start(bf16[256,4224]{1,0:T(8,128)(2,1)} %pad_maximum_fusion.17), channel_id=1, source_target_pairs={{0,16},{4,20},{8,24},{12,28},{16,0},{20,4},{24,8},{28,12},{1,17},{... | collective-permute-start | bytes 6488072 | tf_op jit(solution)/shard_map/ppermute | solution.py:128
  50.4 322.4 %collective-permute-start.8 = (bf16[256,4224]{1,0:T(8,128)(2,1)}, bf16[256,4224]{1,0:T(8,128)(2,1)}, u32[]{:S(2)}, u32[]{:S(2)}) collective-permute-start(bf16[256,4224]{1,0:T(8,128)(2,1)} %pad_maximum_fusion.18), channel_id=1, source_target_pairs={{0,24},{4,28},{8,16},{12,20},{16,8},{20,12},{24,0},{28,4},{1,25},{... | collective-permute-start | bytes 6488072 | tf_op jit(solution)/shard_map/ppermute | solution.py:128
  51.3 114.0 %copy-start.95 = (bf16[1,16,2,512]{3,2,1,0:T(2,128)(2,1)}, bf16[1,16,2,512]{3,2,1,0:T(2,128)(2,1)S(1)}, u32[]{:S(2)}) copy-start(bf16[1,16,2,512]{3,2,1,0:T(2,128)(2,1)S(1)} %constant_dynamic-slice_fusion.4) | copy-start | bytes 98308
  53.3 348.4 %copy-start.7 = (bf16[256,512]{0,1:T(8,128)(2,1)}, bf16[256,512]{0,1:T(8,128)(2,1)S(1)}, u32[]{:S(2)}) copy-start(bf16[256,512]{0,1:T(8,128)(2,1)S(1)} %copy.402) | copy-start | bytes 786436
  58.1 113.0 %copy-start.51 = (f32[256,64]{1,0:T(8,128)}, f32[256,64]{1,0:T(8,128)S(1)}, u32[]{:S(2)}) copy-start(f32[256,64]{1,0:T(8,128)S(1)} %get-tuple-element.199) | copy-start | bytes 196612
  64.8 97.1 %copy-start.1 = (bf16[256,2048]{1,0:T(8,128)(2,1)}, bf16[256,2048]{1,0:T(8,128)(2,1)S(1)}, u32[]{:S(2)}) copy-start(bf16[256,2048]{1,0:T(8,128)(2,1)S(1)} %fusion.54) | copy-start | bytes 3145732
  67.9 97.5 %copy-start.111 = (bf16[256,16,1]{0,1,2:T(8,128)(2,1)}, bf16[256,16,1]{0,1,2:T(8,128)(2,1)S(1)}, u32[]{:S(2)}) copy-start(bf16[256,16,1]{0,1,2:T(8,128)(2,1)S(1)} %fusion.73) | copy-start | bytes 24580
  98.5 274.6 %collective-permute-start.5 = (bf16[256,4224]{1,0:T(8,128)(2,1)}, bf16[256,4224]{1,0:T(8,128)(2,1)}, u32[]{:S(2)}, u32[]{:S(2)}) collective-permute-start(bf16[256,4224]{1,0:T(8,128)(2,1)} %collective-permute-done.4), channel_id=1, source_target_pairs={{0,4},{4,0},{8,12},{12,8},{16,20},{20,16},{24,28},{28,24},{1,5},{5... | collective-permute-start | bytes 6488072 | tf_op jit(solution)/shard_map/ppermute | solution.py:128
  108.6 294.9 %collective-permute-start.7 = (bf16[256,4224]{1,0:T(8,128)(2,1)}, bf16[256,4224]{1,0:T(8,128)(2,1)}, u32[]{:S(2)}, u32[]{:S(2)}) collective-permute-start(bf16[256,4224]{1,0:T(8,128)(2,1)} %collective-permute-done.6), channel_id=1, source_target_pairs={{0,4},{4,0},{8,12},{12,8},{16,20},{20,16},{24,28},{28,24},{1,5},{5... | collective-permute-start | bytes 6488072 | tf_op jit(solution)/shard_map/ppermute | solution.py:128
  167.4 86.4 %copy-start.6 = (bf16[640,2048]{1,0:T(8,128)(2,1)S(1)}, bf16[640,2048]{1,0:T(8,128)(2,1)}, u32[]{:S(2)}) copy-start(bf16[640,2048]{1,0:T(8,128)(2,1)} %convolution_convert_fusion.5) | copy-start | bytes 7864324
  274.4 84.2 %copy-start.56 = (bf16[2,256,4,128]{3,2,1,0:T(4,128)(2,1)}, bf16[2,256,4,128]{3,2,1,0:T(4,128)(2,1)S(1)}, u32[]{:S(2)}) copy-start(bf16[2,256,4,128]{3,2,1,0:T(4,128)(2,1)S(1)} %copy.417) | copy-start | bytes 1572868
  276.2 82.4 %copy-start.29 = (bf16[640,512]{1,0:T(8,128)(2,1)}, bf16[640,512]{1,0:T(8,128)(2,1)S(1)}, u32[]{:S(2)}) copy-start(bf16[640,512]{1,0:T(8,128)(2,1)S(1)} %convolution_convert_fusion.14) | copy-start | bytes 1966084
  366.4 66.2 %all-gather.16.cloned.1.call-start = ((), (), s32[]{:S(2)}) async-start(), calls=%async_computation.11 | async-start | bytes 1310720 | tf_op jit(solution)/shard_map/all_gather | solution.py:131
  372.8 36.9 %collective-permute-start.9 = (bf16[256,4224]{1,0:T(8,128)(2,1)}, bf16[256,4224]{1,0:T(8,128)(2,1)}, u32[]{:S(2)}, u32[]{:S(2)}) collective-permute-start(bf16[256,4224]{1,0:T(8,128)(2,1)} %collective-permute-done.8), channel_id=1, source_target_pairs={{0,4},{4,0},{8,12},{12,8},{16,20},{20,16},{24,28},{28,24},{1,5},{5... | collective-permute-start | bytes 6488072 | tf_op jit(solution)/shard_map/ppermute | solution.py:128
  403.4 581.7 %reduce-scatter.9.cloned.1.call-start = ((), (), s32[]{:S(2)}) async-start(), calls=%async_computation.14 | async-start | bytes 1310720 | tf_op jit(solution)/shard_map/reduce_scatter | solution.py:134
  409.7 27.3 %copy-start.155 = (f32[128]{0:T(128)S(1)}, f32[128]{0:T(128)}, u32[]{:S(2)}) copy-start(f32[128]{0:T(128)} %mul.649) | copy-start | bytes 1540
  409.7 27.4 %copy-start.36 = (bf16[256,2048]{0,1:T(8,128)(2,1)S(1)}, bf16[256,2048]{0,1:T(8,128)(2,1)}, u32[]{:S(2)}) copy-start(bf16[256,2048]{0,1:T(8,128)(2,1)} %all-gather.18.cloned.1.call-done) | copy-start | bytes 3145732
  438.3 34.7 %copy-start.27 = (bf16[160,2176]{1,0:T(8,128)(2,1)}, bf16[160,2176]{1,0:T(8,128)(2,1)S(1)}, u32[]{:S(2)}) copy-start(bf16[160,2176]{1,0:T(8,128)(2,1)S(1)} %get-tuple-element.127) | copy-start | bytes 2088964
  438.3 17.2 %collective-permute-start.15 = (bf16[160,2176]{1,0:T(8,128)(2,1)S(1)}, bf16[160,2176]{1,0:T(8,128)(2,1)S(1)}, u32[]{:S(2)}, u32[]{:S(2)}) collective-permute-start(bf16[160,2176]{1,0:T(8,128)(2,1)S(1)} %get-tuple-element.128), channel_id=1, source_target_pairs={{0,24},{4,28},{8,16},{12,20},{16,8},{20,12},{24,0},{28,4},{1,25},{... | collective-permute-start | bytes 2088968 | tf_op jit(solution)/shard_map/ppermute | solution.py:128
  440.5 32.5 %collective-permute-start.14 = (bf16[160,2176]{1,0:T(8,128)(2,1)S(1)}, bf16[160,2176]{1,0:T(8,128)(2,1)S(1)}, u32[]{:S(2)}, u32[]{:S(2)}) collective-permute-start(bf16[160,2176]{1,0:T(8,128)(2,1)S(1)} %get-tuple-element.129), channel_id=1, source_target_pairs={{0,16},{4,20},{8,24},{12,28},{16,0},{20,4},{24,8},{28,12},{1,17},{... | collective-permute-start | bytes 2088968 | tf_op jit(solution)/shard_map/ppermute | solution.py:128
  440.8 32.2 %collective-permute-start.13 = (bf16[160,2176]{1,0:T(8,128)(2,1)S(1)}, bf16[160,2176]{1,0:T(8,128)(2,1)S(1)}, u32[]{:S(2)}, u32[]{:S(2)}) collective-permute-start(bf16[160,2176]{1,0:T(8,128)(2,1)S(1)} %get-tuple-element.130), channel_id=1, source_target_pairs={{0,8},{4,12},{8,0},{12,4},{16,24},{20,28},{24,16},{28,20},{1,9},{5... | collective-permute-start | bytes 2088968 | tf_op jit(solution)/shard_map/ppermute | solution.py:128
  444.0 117.2 %collective-permute-start.2 = (bf16[160,2304]{1,0:T(8,128)(2,1)}, bf16[160,2304]{1,0:T(8,128)(2,1)}, u32[]{:S(2)}, u32[]{:S(2)}) collective-permute-start(bf16[160,2304]{1,0:T(8,128)(2,1)} %get-tuple-element.116), channel_id=1, source_target_pairs={{0,24},{4,28},{8,16},{12,20},{16,8},{20,12},{24,0},{28,4},{1,25},{... | collective-permute-start | bytes 2211848 | tf_op jit(solution)/shard_map/ppermute | solution.py:128
  446.0 115.1 %collective-permute-start.1 = (bf16[160,2304]{1,0:T(8,128)(2,1)}, bf16[160,2304]{1,0:T(8,128)(2,1)}, u32[]{:S(2)}, u32[]{:S(2)}) collective-permute-start(bf16[160,2304]{1,0:T(8,128)(2,1)} %get-tuple-element.117), channel_id=1, source_target_pairs={{0,16},{4,20},{8,24},{12,28},{16,0},{20,4},{24,8},{28,12},{1,17},{... | collective-permute-start | bytes 2211848 | tf_op jit(solution)/shard_map/ppermute | solution.py:128
  455.6 105.6 %collective-permute-start = (bf16[160,2304]{1,0:T(8,128)(2,1)}, bf16[160,2304]{1,0:T(8,128)(2,1)}, u32[]{:S(2)}, u32[]{:S(2)}) collective-permute-start(bf16[160,2304]{1,0:T(8,128)(2,1)} %get-tuple-element.118), channel_id=1, source_target_pairs={{0,8},{4,12},{8,0},{12,4},{16,24},{20,28},{24,16},{28,20},{1,9},{5... | collective-permute-start | bytes 2211848 | tf_op jit(solution)/shard_map/ppermute | solution.py:128
  667.1 185.2 %copy-start.128 = (f32[640]{0:T(1024)}, f32[640]{0:T(1024)S(1)}, u32[]{:S(2)}) copy-start(f32[640]{0:T(1024)S(1)} %add_reduce_fusion) | copy-start | bytes 7684
  882.5 12.9 %collective-permute-start.12 = (bf16[160,2176]{1,0:T(8,128)(2,1)S(1)}, bf16[160,2176]{1,0:T(8,128)(2,1)S(1)}, u32[]{:S(2)}, u32[]{:S(2)}) collective-permute-start(bf16[160,2176]{1,0:T(8,128)(2,1)S(1)} %get-tuple-element.125), channel_id=1, source_target_pairs={{0,24},{4,28},{8,16},{12,20},{16,8},{20,12},{24,0},{28,4},{1,25},{... | collective-permute-start | bytes 2088968 | tf_op jit(solution)/shard_map/ppermute | solution.py:128
  886.9 30.2 %collective-permute-start.11 = (bf16[160,2176]{1,0:T(8,128)(2,1)S(1)}, bf16[160,2176]{1,0:T(8,128)(2,1)S(1)}, u32[]{:S(2)}, u32[]{:S(2)}) collective-permute-start(bf16[160,2176]{1,0:T(8,128)(2,1)S(1)} %get-tuple-element.126), channel_id=1, source_target_pairs={{0,16},{4,20},{8,24},{12,28},{16,0},{20,4},{24,8},{28,12},{1,17},{... | collective-permute-start | bytes 2088968 | tf_op jit(solution)/shard_map/ppermute | solution.py:128
  888.4 28.7 %collective-permute-start.10 = (bf16[160,2176]{1,0:T(8,128)(2,1)S(1)}, bf16[160,2176]{1,0:T(8,128)(2,1)S(1)}, u32[]{:S(2)}, u32[]{:S(2)}) collective-permute-start(bf16[160,2176]{1,0:T(8,128)(2,1)S(1)} %get-tuple-element.124), channel_id=1, source_target_pairs={{0,8},{4,12},{8,0},{12,4},{16,24},{20,28},{24,16},{28,20},{1,9},{5... | collective-permute-start | bytes 2088968 | tf_op jit(solution)/shard_map/ppermute | solution.py:128
  889.4 27.7 %copy-start.107 = (s32[640]{0:T(1024)S(1)}, s32[640]{0:T(1024)}, u32[]{:S(2)}) copy-start(s32[640]{0:T(1024)} %add.246) | copy-start | bytes 7684
  889.4 27.7 %copy-start.136 = (s32[256,1]{0,1:T(1,128)S(1)}, s32[256,1]{0,1:T(1,128)}, u32[]{:S(2)}) copy-start(s32[256,1]{0,1:T(1,128)} %copy-done.135) | copy-start | bytes 3076
  889.4 27.7 %copy-start.139 = (s32[256,1]{0,1:T(1,128)S(1)}, s32[256,1]{0,1:T(1,128)}, u32[]{:S(2)}) copy-start(s32[256,1]{0,1:T(1,128)} %copy-done.138) | copy-start | bytes 3076
  890.8 29.0 %collective-permute-start.18 = (bf16[160,2304]{1,0:T(8,128)(2,1)}, bf16[160,2304]{1,0:T(8,128)(2,1)S(1)}, u32[]{:S(2)}, u32[]{:S(2)}) collective-permute-start(bf16[160,2304]{1,0:T(8,128)(2,1)} %get-tuple-element.112), channel_id=1, source_target_pairs={{0,24},{4,28},{8,16},{12,20},{16,8},{20,12},{24,0},{28,4},{1,25},{... | collective-permute-start | bytes 2211848 | tf_op jit(solution)/shard_map/ppermute | solution.py:128
  892.0 55.9 %collective-permute-start.17 = (bf16[160,2304]{1,0:T(8,128)(2,1)}, bf16[160,2304]{1,0:T(8,128)(2,1)S(1)}, u32[]{:S(2)}, u32[]{:S(2)}) collective-permute-start(bf16[160,2304]{1,0:T(8,128)(2,1)} %get-tuple-element.113), channel_id=1, source_target_pairs={{0,16},{4,20},{8,24},{12,28},{16,0},{20,4},{24,8},{28,12},{1,17},{... | collective-permute-start | bytes 2211848 | tf_op jit(solution)/shard_map/ppermute | solution.py:128
  895.4 52.5 %collective-permute-start.16 = (bf16[160,2304]{1,0:T(8,128)(2,1)}, bf16[160,2304]{1,0:T(8,128)(2,1)}, u32[]{:S(2)}, u32[]{:S(2)}) collective-permute-start(bf16[160,2304]{1,0:T(8,128)(2,1)} %get-tuple-element.114), channel_id=1, source_target_pairs={{0,8},{4,12},{8,0},{12,4},{16,24},{20,28},{24,16},{28,20},{1,9},{5... | collective-permute-start | bytes 2211848 | tf_op jit(solution)/shard_map/ppermute | solution.py:128
  919.8 29.6 %copy-start.39 = (bf16[160,2304]{1,0:T(8,128)(2,1)}, bf16[160,2304]{1,0:T(8,128)(2,1)S(1)}, u32[]{:S(2)}) copy-start(bf16[160,2304]{1,0:T(8,128)(2,1)S(1)} %collective-permute-done.18) | copy-start | bytes 2211844
  958.3 26.8 %copy-start.8 = (bf16[256,512]{0,1:T(8,128)(2,1)S(1)}, bf16[256,512]{0,1:T(8,128)(2,1)}, u32[]{:S(2)}) copy-start(bf16[256,512]{0,1:T(8,128)(2,1)} %copy-done.7) | copy-start | bytes 786436
  958.3 26.8 %copy-start.26 = (bf16[256,512]{0,1:T(8,128)(2,1)S(1)}, bf16[256,512]{0,1:T(8,128)(2,1)}, u32[]{:S(2)}) copy-start(bf16[256,512]{0,1:T(8,128)(2,1)} %reduce-scatter.5.cloned.1.call-done) | copy-start | bytes 786436
  958.3 26.8 %copy-start.123 = (f32[512]{0:T(512)S(1)}, f32[512]{0:T(512)}, u32[]{:S(2)}) copy-start(f32[512]{0:T(512)} %dynamic_slice.51) | copy-start | bytes 6148
  958.4 36.9 %copy-start.34 = (bf16[256,512]{0,1:T(8,128)(2,1)S(1)}, bf16[256,512]{0,1:T(8,128)(2,1)}, u32[]{:S(2)}) copy-start(bf16[256,512]{0,1:T(8,128)(2,1)} %copy-done.33) | copy-start | bytes 786436
  958.4 36.9 %copy-start.126 = (f32[256]{0:T(256)S(1)}, f32[256]{0:T(256)}, u32[]{:S(2)}) copy-start(f32[256]{0:T(256)} %copy-done.125) | copy-start | bytes 3076
  958.4 36.9 %copy-start.133 = (f32[256]{0:T(256)S(1)}, f32[256]{0:T(256)}, u32[]{:S(2)}) copy-start(f32[256]{0:T(256)} %get-tuple-element.202) | copy-start | bytes 3076
  958.4 36.9 %copy-start.145 = (bf16[256]{0:T(256)(128)(2,1)S(1)}, bf16[256]{0:T(256)(128)(2,1)}, u32[]{:S(2)}) copy-start(bf16[256]{0:T(256)(128)(2,1)} %copy-done.144) | copy-start | bytes 1540
  958.4 66.9 %all-gather.20.cloned.1.call-start = ((), (), s32[]{:S(2)}) async-start(), calls=%async_computation.15 | async-start | bytes 1310720 | tf_op jit(solution)/shard_map/all_gather | solution.py:131
  959.4 36.9 %copy-start.52 = (f32[256,64]{1,0:T(8,128)S(1)}, f32[256,64]{1,0:T(8,128)}, u32[]{:S(2)}) copy-start(f32[256,64]{1,0:T(8,128)} %copy-done.51) | copy-start | bytes 196612
  959.4 37.0 %copy-start.63 = (f32[256,64]{1,0:T(8,128)S(1)}, f32[256,64]{1,0:T(8,128)}, u32[]{:S(2)}) copy-start(f32[256,64]{1,0:T(8,128)} %get-tuple-element.197) | copy-start | bytes 196612
  959.4 37.0 %copy-start.65 = (bf16[640,128]{1,0:T(8,128)(2,1)S(1)}, bf16[640,128]{1,0:T(8,128)(2,1)}, u32[]{:S(2)}) copy-start(bf16[640,128]{1,0:T(8,128)(2,1)} %copy-done.64) | copy-start | bytes 491524
  996.2 88.5 %all-reduce.8.cloned.1.call-start = ((), (), s32[]{:S(2)}) async-start(), calls=%async_computation.17 | async-start | bytes 2162688 | tf_op jit(solution)/shard_map/psum | solution.py:343
  999.5 25.9 %copy-start.87 = (bf16[8,2,8,256]{3,2,0,1:T(8,128)(2,1)S(1)}, bf16[8,2,8,256]{3,2,0,1:T(8,128)(2,1)}, u32[]{:S(2)}) copy-start(bf16[8,2,8,256]{3,2,0,1:T(8,128)(2,1)} %copy.519) | copy-start | bytes 196612
  1000.1 26.7 %copy-start.116 = (s32[256,1]{0,1:T(1,128)S(1)}, s32[256,1]{0,1:T(1,128)}, u32[]{:S(2)}) copy-start(s32[256,1]{0,1:T(1,128)} %copy-done.114) | copy-start | bytes 3076
  1000.1 26.7 %copy-start.119 = (s32[256,1]{0,1:T(1,128)S(1)}, s32[256,1]{0,1:T(1,128)}, u32[]{:S(2)}) copy-start(s32[256,1]{0,1:T(1,128)} %copy-done.117) | copy-start | bytes 3076
  1001.2 123.6 %reduce-scatter.11.cloned.1.call-start = ((), (), s32[]{:S(2)}) async-start(), calls=%async_computation.16 | async-start | bytes 1310720 | tf_op jit(solution)/shard_map/reduce_scatter | solution.py:134
  1081.1 78.1 %reduce-scatter.7.cloned.1.call-start = ((), (), s32[]{:S(2)}) async-start(), calls=%async_computation.12 | async-start | bytes 1310720 | tf_op jit(solution)/shard_map/reduce_scatter | solution.py:134
  1111.4 34.5 %copy-start.2 = (bf16[256,2048]{1,0:T(8,128)(2,1)S(1)}, bf16[256,2048]{1,0:T(8,128)(2,1)}, u32[]{:S(2)}) copy-start(bf16[256,2048]{1,0:T(8,128)(2,1)} %copy-done.1) | copy-start | bytes 3145732
  1151.7 13.5 %all-to-all-start.1 = ((bf16[1,80,8,256]{3,1,0,2:T(8,128)(2,1)}), bf16[1,80,8,256]{3,1,0,2:T(8,128)(2,1)S(1)}, u32[]{:S(2)}, u32[]{:S(2)}) async-start(bf16[1,80,8,256]{3,1,0,2:T(8,128)(2,1)} %copy_dynamic-update-slice_fusion), calls=%async_computation.5 | async-start | bytes 655360 | tf_op jit(solution)/shard_map/all_to_all | solution.py:463
  (132 other events, 884.3 us)
Sparse Core Ops, SparseCore 0:
  9.6 28.8 all-gather.7
  40.6 27.4 all-gather.17
  70.0 91.8 all-gather.9
  163.7 90.0 all-gather.11
  255.5 89.8 all-gather.13
  366.5 24.6 reduce-scatter.4
  403.6 28.9 all-gather.15
  958.5 26.5 reduce-scatter.8
  996.3 28.9 all-gather.19
  1029.0 55.7 all-reduce.7
  1087.0 25.2 reduce-scatter.10
  1114.5 27.0 reduce-scatter.6

commit v2 on v1

--- a/solution.py
+++ b/solution.py
@@ -1,6 +1,10 @@
+import functools
+
 import jax
 import jax.numpy as jnp
 from jax import lax
+from jax.experimental import pallas as pl
+from jax.experimental.pallas import tpu as pltpu
 from jax.sharding import PartitionSpec as P
 
 HEAD_DIM = 128
@@ -16,6 +20,7 @@
 HIGHEST = lax.Precision.HIGHEST
 F32 = jnp.float32
 BF16 = jnp.bfloat16
+LANES = 128
 
 
 def mm(spec, a, b):
@@ -54,22 +59,6 @@
     return route * capacity + position.astype(jnp.int32)
 
 
-def xor_chunks(array, axis, parts, index):
-    shape = array.shape
-    size = shape[axis] // parts
-    step = 1
-    while step < parts:
-        view = array.reshape(
-            shape[:axis] + (parts // (2 * step), 2, step * size) + shape[axis + 1 :]
-        )
-        first = lax.index_in_dim(view, 0, axis + 1, keepdims=True)
-        second = lax.index_in_dim(view, 1, axis + 1, keepdims=True)
-        flipped = jnp.concatenate([second, first], axis=axis + 1)
-        array = jnp.where((index // step) % 2 == 1, flipped, view).reshape(shape)
-        step *= 2
-    return array
-
-
 def chosen_of(logits, route, experts):
     onehot = (route[:, :, None] == jnp.arange(experts, dtype=jnp.int32)).astype(F32)
     return jnp.sum(onehot * logits[:, None, :], axis=2)
@@ -79,6 +68,128 @@
     centred = gates * (grad_gates - jnp.sum(gates * grad_gates, axis=1, keepdims=True))
     onehot = (route[:, :, None] == jnp.arange(experts, dtype=jnp.int32)).astype(F32)
     return jnp.sum(centred[:, :, None] * onehot, axis=1)
+
+
+def ffn_kernel(parts, depth, width, units, *refs):
+    hids = refs[:EXP_FF]
+    cots = refs[EXP_FF : 2 * EXP_FF]
+    pieces = refs[2 * EXP_FF : 2 * EXP_FF + parts]
+    rights = refs[2 * EXP_FF + parts]
+    outs = refs[2 * EXP_FF + parts + 1 :]
+    grads = outs[:EXP_FF]
+    downs = outs[EXP_FF : 2 * EXP_FF]
+    adapt = outs[2 * EXP_FF]
+    hid, cot, block, act, product, sems = outs[2 * EXP_FF + 1 :]
+    row = lax.axis_index("row")
+    wide = width + LANES
+    copies = []
+    for j in range(EXP_FF):
+        where = pl.ds(j * CAP_FF, CAP_FF)
+        copies.append(pltpu.make_async_copy(hids[j], hid.at[where], sems.at[j]))
+        copies.append(pltpu.make_async_copy(cots[j], cot.at[where], sems.at[EXP_FF + j]))
+    copies.append(pltpu.make_async_copy(rights, block.at[pl.ds(width, LANES)], sems.at[2 * EXP_FF]))
+    for m in range(parts):
+        owner = jnp.bitwise_xor(row, m)
+        where = pl.ds(pl.multiple_of(owner * depth, depth), depth)
+        copies.append(pltpu.make_async_copy(pieces[m], block.at[where], sems.at[2 * EXP_FF + 1 + m]))
+    for copy in copies:
+        copy.start()
+    for copy in copies:
+        copy.wait()
+    gate_scale = hid[:, wide : wide + 1].astype(F32) + hid[:, wide + 1 : wide + 2].astype(F32)
+    product[...] = jnp.zeros_like(product)
+
+    def forward(start, size):
+        here = pl.ds(start, size)
+        up_here = pl.ds(units + start, size)
+        down_here = pl.ds(2 * units + start, size)
+        gate = jnp.dot(hid[:, :wide], block[:, here], preferred_element_type=F32)
+        up = jnp.dot(hid[:, :wide], block[:, up_here], preferred_element_type=F32)
+        grad = jnp.dot(cot[...], block[:, down_here], preferred_element_type=F32)
+        sig = 1.0 / (1.0 + jnp.exp(-gate))
+        mixed = (gate * sig * up).astype(BF16)
+        act[:, down_here] = mixed
+        product[...] += jnp.sum(mixed.astype(F32) * grad, axis=1, keepdims=True)
+        grad = grad * gate_scale
+        act[:, here] = (grad * up * sig * (1.0 + gate * (1.0 - sig))).astype(BF16)
+        act[:, up_here] = (grad * gate * sig).astype(BF16)
+
+    step = 2 * LANES
+    full = units // step
+
+    @pl.loop(0, full)
+    def _(i):
+        forward(pl.multiple_of(i * step, step), step)
+
+    if units % step:
+        forward(full * step, units % step)
+
+    def backward(start, size):
+        here = pl.ds(start, size)
+        result = lax.dot_general(
+            act[:, : 2 * units], block[here, : 2 * units], (((1,), (1,)), ((), ())),
+            preferred_element_type=F32,
+        ).astype(BF16)
+        for j in range(EXP_FF):
+            grads[j][:, here] = result[j * CAP_FF : (j + 1) * CAP_FF]
+        result = lax.dot_general(
+            act[:, 2 * units :], block[here, 2 * units :], (((1,), (1,)), ((), ())),
+            preferred_element_type=F32,
+        )
+        result = (result * gate_scale).astype(BF16)
+        for j in range(EXP_FF):
+            downs[j][:, here] = result[j * CAP_FF : (j + 1) * CAP_FF]
+
+    full_rows = wide // step
+
+    @pl.loop(0, full_rows)
+    def _(i):
+        backward(pl.multiple_of(i * step, step), step)
+
+    if wide % step:
+        backward(full_rows * step, wide % step)
+    total = product[...]
+    high = total.astype(BF16)
+    low = (total - high.astype(F32)).astype(BF16)
+    lane = lax.broadcasted_iota(jnp.int32, (EXP_FF * CAP_FF, LANES), 1)
+    packed = jnp.where(lane == 0, high.astype(F32), jnp.where(lane == 1, low.astype(F32), 0.0)).astype(BF16)
+    for j in range(EXP_FF):
+        grads[j][:, wide:] = packed[j * CAP_FF : (j + 1) * CAP_FF]
+    ext = hid[:, width:wide]
+    low_ext = (cot[:, width:].astype(F32) * gate_scale).astype(BF16)
+    adapt[:, : 2 * units] = lax.dot_general(
+        ext, act[:, : 2 * units], (((0,), (0,)), ((), ())), preferred_element_type=F32
+    ).astype(BF16)
+    adapt[:, 2 * units :] = lax.dot_general(
+        low_ext, act[:, 2 * units :], (((0,), (0,)), ((), ())), preferred_element_type=F32
+    ).astype(BF16)
+
+def feed_forward(hids, cots, pieces, rights):
+    parts = len(pieces)
+    depth, triple = pieces[0].shape
+    units = triple // 3
+    width = depth * parts
+    rows = EXP_FF * CAP_FF
+    hbm = pl.BlockSpec(memory_space=pl.ANY)
+    vmem = pl.BlockSpec(memory_space=pltpu.VMEM)
+    wide = width + LANES
+    return pl.pallas_call(
+        functools.partial(ffn_kernel, parts, depth, width, units),
+        out_shape=[jax.ShapeDtypeStruct((CAP_FF, wide + LANES), BF16)] * EXP_FF
+        + [jax.ShapeDtypeStruct((CAP_FF, wide), BF16)] * EXP_FF
+        + [jax.ShapeDtypeStruct((LANES, triple), BF16)],
+        in_specs=[hbm] * (2 * EXP_FF + parts + 1),
+        out_specs=[vmem] * (2 * EXP_FF + 1),
+        scratch_shapes=[
+            pltpu.VMEM((rows, wide + LANES), BF16),
+            pltpu.VMEM((rows, wide), BF16),
+            pltpu.VMEM((wide, triple), BF16),
+            pltpu.VMEM((rows, triple), BF16),
+            pltpu.VMEM((rows, 1), F32),
+            pltpu.SemaphoreType.DMA((2 * EXP_FF + 1 + parts,)),
+        ],
+        compiler_params=pltpu.CompilerParams(vmem_limit_bytes=56 * 2**20),
+    )(*hids, *cots, *pieces, rights)
 
 
 def on_device(
@@ -142,20 +253,28 @@
     query_full = lax.all_gather(query_weight, "row", axis=1, tiled=True)
     out_full = lax.all_gather(out_weight, "row", axis=1, tiled=True)
 
+    def later(value, *earlier):
+        return lax.optimization_barrier((value, *earlier))[0]
+
+    padding = -units % LANES
+
+    def padded(value):
+        return jnp.pad(value, ((0, 0), (0, padding))) if padding else value
+
+    inner_later, down_later = later((inner_weight, down_weight), out_full)
     near = []
     for j in range(EXP_FF):
         which = expert ^ j
-        inner_own = lax.dynamic_index_in_dim(inner_weight, which, 0, keepdims=False)
-        down_own = lax.dynamic_index_in_dim(down_weight, which, 0, keepdims=False)
-        piece = jnp.concatenate([inner_own[:, 0], inner_own[:, 1], down_own], axis=1)
+        inner_own = lax.dynamic_index_in_dim(inner_later, which, 0, keepdims=False)
+        down_own = lax.dynamic_index_in_dim(down_later, which, 0, keepdims=False)
+        piece = jnp.concatenate(
+            [padded(inner_own[:, 0]), padded(inner_own[:, 1]), padded(down_own)], axis=1
+        )
         near.append(swap(piece, j * replicas) if j else piece)
     chunks = []
     for j in range(EXP_FF):
         for i in range(replicas):
             chunks.append(swap(near[j], i) if i else near[j])
-    expert_block = jnp.concatenate(chunks, axis=0)
-    gate_up_block = expert_block[:, : 2 * units]
-    down_block = expert_block[:, 2 * units :]
 
     picks = lax.all_gather(adapter_pick, "row", axis=0, tiled=True)
     pick_onehot = (picks[:, None] == jnp.arange(ADAPT, dtype=jnp.int32)[None, :]).astype(BF16)
@@ -173,8 +292,12 @@
     right_query = query_right[adapter].astype(F32)
     right_kv = kv_right[adapter].astype(F32)
     right_out = out_right[adapter].astype(F32)
-    right_inner_all = inner_right.reshape(ADAPT * RANK, 2 * units)
+    right_inner_all = inner_right.reshape(ADAPT * RANK, 2, units)
     right_down_all = down_right.reshape(ADAPT * RANK, units)
+    ffn_right = jnp.concatenate(
+        [padded(right_inner_all[:, 0]), padded(right_inner_all[:, 1]), padded(right_down_all)],
+        axis=1,
+    )
     own_adapter = (jnp.arange(ADAPT, dtype=jnp.int32) == adapter).astype(F32)
 
     def spread(low):
@@ -198,22 +321,18 @@
     pick_ffn = [(rows_ffn[:, None] == slots_ffn[None, :, k]).astype(BF16) for k in range(TOPK)]
     pick_ffn_any = pick_ffn[0] + pick_ffn[1]
 
-    def trade(rows):
+    def blocks_of(rows):
         blocks = rows.reshape(EXP_FF, CAP_FF, rows.shape[1])
-        return jnp.concatenate(
-            [blocks[j] if j == 0 else swap(blocks[j], j * replicas) for j in range(EXP_FF)]
-        )
+        return [blocks[j] for j in range(EXP_FF)]
+
+    def trade(blocks):
+        return [swap(block, j * replicas) if j else block for j, block in enumerate(blocks)]
 
     masked_cot = cotangent * valid.astype(BF16)[:, None]
     cot_full = features(masked_cot)
     grad_low_down = mm("td,rd->tr", cot_full, left_down)
-    cot_rows = trade(
-        mm(
-            "ct,td->cd",
-            pick_ffn_any,
-            jnp.concatenate([cot_full, spread(grad_low_down).astype(BF16)], axis=1),
-        ).astype(BF16)
-    )
+    cot_ext = jnp.concatenate([cot_full, spread(grad_low_down).astype(BF16)], axis=1)
+    cot_rows = trade(blocks_of(mm("ct,td->cd", pick_ffn_any, cot_ext).astype(BF16)))
 
     x_full = features(inputs)
     x_wide = x_full.astype(F32)
@@ -297,52 +416,12 @@
         for k in range(TOPK)
     )
     gate_out = jnp.pad(gate_out, ((0, 0), (0, 126))).astype(BF16)
-    hidden_in = trade(jnp.concatenate([hidden_out, gate_out], axis=1))
-    gate_in = (
-        hidden_in[:, width + 128].astype(F32) + hidden_in[:, width + 129].astype(F32)
-    )[:, None]
-    hidden_in_ext = hidden_in[:, width : width + 128]
-    hidden_in = xor_chunks(hidden_in[:, :width], 1, rows_axis, row)
-    cot_in_ext = cot_rows[:, width:]
-    cot_in = xor_chunks(cot_rows[:, :width], 1, rows_axis, row)
-    grad_mixed = mm("cd,df->cf", cot_in, down_block) + mm("cr,rf->cf", cot_in_ext, right_down_all)
-    gate_up = mm("cd,df->cf", hidden_in, gate_up_block) + mm(
-        "cr,rf->cf", hidden_in_ext, right_inner_all
-    )
-    gate_part = gate_up[:, :units]
-    up_part = gate_up[:, units:]
-    sig = jax.nn.sigmoid(gate_part)
-    mixed = (gate_part * sig * up_part).astype(BF16)
-    gate_grad_rows = jnp.sum(mixed.astype(F32) * grad_mixed, axis=1, keepdims=True)
-    grad_mixed = grad_mixed * gate_in
-    grad_gate_up = jnp.concatenate(
-        [
-            grad_mixed * up_part * sig * (1.0 + gate_part * (1.0 - sig)),
-            grad_mixed * gate_part * sig,
-        ],
-        axis=1,
-    ).astype(BF16)
-    grad_rows = xor_chunks(
-        mm("cf,df->cd", grad_gate_up, gate_up_block).astype(BF16), 1, rows_axis, row
-    )
-    grad_rank_rows = mm("cf,rf->cr", grad_gate_up, right_inner_all).astype(BF16)
-    gg_high = gate_grad_rows.astype(BF16)
-    gg_low = (gate_grad_rows - gg_high.astype(F32)).astype(BF16)
-    grad_msg = jnp.concatenate(
-        [grad_rows, grad_rank_rows, jnp.pad(jnp.concatenate([gg_high, gg_low], 1), ((0, 0), (0, 126)))],
-        axis=1,
-    )
-    grad_back = trade(grad_msg)
-    down_rows = xor_chunks(
-        (mm("cf,df->cd", mixed, down_block) * gate_in).astype(BF16), 1, rows_axis, row
-    )
-    down_low_rows = (mm("cf,rf->cr", mixed, right_down_all) * gate_in).astype(BF16)
-    down_back = trade(jnp.concatenate([down_rows, down_low_rows], axis=1))
-    grad_right_inner = mm("cr,cf->rf", hidden_in_ext, grad_gate_up)
-    grad_right_down = mm("cr,cf->rf", (cot_in_ext.astype(F32) * gate_in).astype(BF16), mixed)
-    ffn_rights = lax.psum(
-        jnp.concatenate([grad_right_inner, grad_right_down], axis=1).astype(BF16), "row"
-    ).astype(F32)
+    hidden_in = trade(blocks_of(jnp.concatenate([hidden_out, gate_out], axis=1)))
+    results = feed_forward(hidden_in, cot_rows, chunks, ffn_right)
+    grad_back = jnp.concatenate(trade(results[:EXP_FF]))
+    down_back = jnp.concatenate(trade(results[EXP_FF : 2 * EXP_FF]))
+    ffn_rights = lax.optimization_barrier(lax.psum(results[2 * EXP_FF], "row")).astype(F32)
+    ffn_rights = ffn_rights.reshape(ADAPT, RANK, 3, units + padding)[..., :units]
 
     grad_comb = mm("ct,cd->td", pick_ffn_any, grad_back[:, : width + 128])
     gg_back = grad_back[:, width + 128 : width + 130]
@@ -482,9 +561,9 @@
         left_grads[:, 2],
         right_grads[:, :, 3],
         left_grads[:, 3],
-        ffn_rights[:, : 2 * units].reshape(ADAPT, RANK, 2, units),
+        ffn_rights[:, :, :2],
         left_grads[:, 4],
-        ffn_rights[:, 2 * units :].reshape(ADAPT, RANK, units),
+        ffn_rights[:, :, 2],
     )
 
 

time: 1190 us -> 845 us (0.71)
  local copies, waits for them, and re-layouts: 350 us -> 101 us
  other arithmetic: 145 us -> 37.8 us
  matrix products: 169 us -> 124 us
  Pallas kernels: 0 us -> 42.7 us
  waiting for transfers between devices: 376 us -> 408 us
  starting transfers between devices: 50.5 us -> 32.4 us
    concatenate x22 -> x1, local copies, waits for them, and re-layouts: 118 us -> 2.04 us  [on_device(): grad_back = jnp.concatenate(trade(results[:EXP_FF]))]
    concatenate x24 -> x6, other arithmetic: 93.7 us -> 7.36 us  [the longest x4 6.08 us: on_device(): jnp.concatenate([padded(inner_own[:, 0]), padded(inner_own[:, 1]), padded...]
    slice x19 -> x4, local copies, waits for them, and re-layouts: 63.9 us -> 8.28 us  [the longest x1 3.57 us: on_device(): ffn_rights[:, :, :2]]
    ppermute x19, waiting for transfers between devices: 99.3 us -> 153 us  [swap(): lax.ppermute(value, 'row', [(i, i ^ offset) for i in range(rows_axis)])]
    reshape x13 -> x1, local copies, waits for them, and re-layouts: 55.3 us -> 4.01 us  [on_device(): ffn_rights.reshape(ADAPT, RANK, 3, units + padding)[..., :units]]
    dot_general x67 -> x57, matrix products: 161 us -> 114 us  [mm(): return jnp.einsum(spec, a, b, preferred_element_type=F32)]
    pallas_call x0 -> x1, Pallas kernels: none -> 42.7 us  [feed_forward(): pl.pallas_call(functools.partial(ffn_kernel, parts, depth, width, units),...]
    unnamed x368 -> x269, local copies, waits for them, and re-layouts: 69.2 us -> 39.1 us
  transfers between devices with their start and end apart: 33 -> 33, of which waited for: 16 -> 21; matrix products, arithmetic and copies ran while one was open for 26% -> 25% of each run, Pallas kernels for 0% -> 0%
where the time goes in v2:
time: 845 us; the launch traced here: 828 us
  waiting for transfers between devices  408 us (48%)
  matrix products  124 us (15%)
  local copies, waits for them, and re-layouts  101 us (12%)
  blocking collectives  64.8 us (8%)
  Pallas kernels  42.7 us (5%)
  other arithmetic  37.8 us (4%)
  starting transfers between devices  32.4 us (4%)
  between operations  17.9 us (2%)
    ppermute x19, waiting for transfers between devices, swap(): lax.ppermute(value, 'row', [(i, i ^ offset) for i in range(rows_axis)])  153 us
    dot_general x57, matrix products, mm(): return jnp.einsum(spec, a, b, preferred_element_type=F32)  114 us
    all_gather x1, waiting for transfers between devices, on_device(): query_full = lax.all_gather(query_weight, 'row', axis=1, tiled=True)  85.7 us
    all_gather x1, waiting for transfers between devices, on_device(): out_full = lax.all_gather(out_weight, 'row', axis=1, tiled=True)  66.1 us
    all_gather x4, waiting for transfers between devices, features(): return lax.all_gather(part, 'col', axis=1, tiled=True)  48.8 us
    pallas_call x1, Pallas kernels, feed_forward(): pl.pallas_call(functools.partial(ffn_kernel, parts, depth, width, units),...  42.7 us
    unnamed x269, local copies, waits for them, and re-layouts  39.1 us
    all_gather x1, waiting for transfers between devices, on_device(): kv_full = lax.all_gather(kv_weight, 'row', axis=1, tiled=True)  27.9 us
  transfers between devices with their start and end apart: 33, of which 21 were waited for; matrix products, arithmetic and copies ran while one was open for 25% of the time, Pallas kernels for 0%

profile of v2, /device:TPU:9, one launch (start us, length us, event | category | flops | bytes accessed | tf_op | source)
XLA Modules:
  0.0 828.4 jit_solution(902865794309652633)
XLA Ops:
  12.1 6.5 all-reduce.3
  19.9 5.6 all-to-all-start
  28.4 3.2 all-to-all-done
  32.3 6.2 all-gather.8.cloned.1.call-done
  47.1 2.4 convolution_convert_fusion.4
  49.4 27.9 %all-gather.10.cloned.1.call-done = bf16[2,2048,512]{2,1,0:T(8,128)(2,1)} async-done(((bf16[2,256,512]{2,1,0:T(8,128)(2,1)}), bf16[2,2048,512]{2,1,0:T(8,128)(2,1)}) %all-gather.10.cloned.1.call-update) | async-done | bytes 4194320 | tf_op jit(solution)/shard_map/all_gather | solution.py:252
  77.3 3.4 convolution_bitcast_fusion.2
  83.4 85.7 %all-gather.12.cloned.1.call-done = bf16[8,2048,512]{2,1,0:T(8,128)(2,1)} async-done(((bf16[8,256,512]{2,1,0:T(8,128)(2,1)}), bf16[8,2048,512]{2,1,0:T(8,128)(2,1)}) %all-gather.12.cloned.1.call-update) | async-done | bytes 16777232 | tf_op jit(solution)/shard_map/all_gather | solution.py:253
  169.1 9.6 %fusion.217 = f32[8,80,512]{2,1,0:T(8,128)S(1)} fusion(bf16[8,80,2048]{2,1,0:T(8,128)(2,1)} %bitcast.327, bf16[8,2048,512]{2,1,0:T(8,128)(2,1)} %all-gather.12.cloned.1.call-done), kind=kOutput, calls=%fused_computation.385 | convolution fusion | flops 1342177280 | bytes 20709376 | tf_op jit(solution)/shard_map/ecd,edw->ecw/dot_general | solution.py:27
  180.2 1.8 convolution_add_fusion.4
  185.1 2.0 fusion.213
  187.1 2.3 fusion.25
  189.4 2.1 copy.412
  194.7 66.1 %all-gather.14.cloned.1.call-done = bf16[8,2048,512]{2,1,0:T(8,128)(2,1)} async-done(((bf16[8,256,512]{2,1,0:T(8,128)(2,1)}), bf16[8,2048,512]{2,1,0:T(8,128)(2,1)}) %all-gather.14.cloned.1.call-update) | async-done | bytes 16777232 | tf_op jit(solution)/shard_map/all_gather | solution.py:254
  260.8 13.2 %fusion.220 = f32[8,80,2048]{2,1,0:T(8,128)} fusion(bf16[8,80,512]{2,1,0:T(8,128)(2,1)S(1)} %bitcast.330, bf16[8,2048,512]{2,1,0:T(8,128)(2,1)} %all-gather.14.cloned.1.call-done), kind=kOutput, calls=%fused_computation.388 | convolution fusion | flops 1342177280 | bytes 22675456 | tf_op jit(solution)/shard_map/ecw,edw->ecd/dot_general | solution.py:27
  274.0 3.9 fusion.4
  284.6 2.0 dynamic-slice_bitcast_fusion
  286.6 5.7 constant_dynamic-slice_fusion
  296.5 1.8 collective-permute-start.11
  301.7 3.8 reduce-scatter.5.cloned.1.call-done
  306.6 9.1 %psum.77 = f32[256]{0:T(256)S(1)} all-reduce(f32[256]{0:T(256)S(1)} %multiply_reduce_fusion.3), channel_id=1, replica_groups=mesh['row'=8,'col'=4] {'col'}, use_global_device_ids=true, to_apply=%region_12.13 | all-reduce | flops 256 | bytes 2048 | tf_op jit(solution)/shard_map/psum | solution.py:402
  318.4 17.0 %all-gather.18.cloned.1.call-done = bf16[256,2048]{0,1:T(8,128)(2,1)} async-done(((bf16[256,512]{0,1:T(8,128)(2,1)}), bf16[256,2048]{0,1:T(8,128)(2,1)}) %all-gather.18.cloned.1.call-update) | async-done | bytes 1048592 | tf_op jit(solution)/shard_map/all_gather | solution.py:242
  340.8 48.7 %collective-permute-done.9.refs_12_ = bf16[256,4224]{1,0:T(8,128)(2,1)} collective-permute-done((bf16[256,4224]{1,0:T(8,128)(2,1)}, bf16[256,4224]{1,0:T(8,128)(2,1)}, u32[]{:S(2)}, u32[]{:S(2)}) %collective-permute-start.9) | collective-permute-done | bytes 2162720 | tf_op jit(solution)/shard_map/ppermute | solution.py:239
  408.7 10.8 %collective-permute-done.5.refs_7_ = bf16[160,2176]{1,0:T(8,128)(2,1)S(1)} collective-permute-done((bf16[160,2176]{1,0:T(8,128)(2,1)S(1)}, bf16[160,2176]{1,0:T(8,128)(2,1)S(1)}, u32[]{:S(2)}, u32[]{:S(2)}) %collective-permute-start.5) | collective-permute-done | bytes 696352 | tf_op jit(solution)/shard_map/ppermute | solution.py:239
  421.9 13.2 %collective-permute-done.4.refs_6_ = bf16[160,2176]{1,0:T(8,128)(2,1)S(1)} collective-permute-done((bf16[160,2176]{1,0:T(8,128)(2,1)S(1)}, bf16[160,2176]{1,0:T(8,128)(2,1)S(1)}, u32[]{:S(2)}, u32[]{:S(2)}) %collective-permute-start.4) | collective-permute-done | bytes 696352 | tf_op jit(solution)/shard_map/ppermute | solution.py:239
  435.0 15.3 %collective-permute-done.2.refs_3_ = bf16[160,2304]{1,0:T(8,128)(2,1)S(1)} collective-permute-done((bf16[160,2304]{1,0:T(8,128)(2,1)S(1)}, bf16[160,2304]{1,0:T(8,128)(2,1)S(1)}, u32[]{:S(2)}, u32[]{:S(2)}) %collective-permute-start.2) | collective-permute-done | bytes 737312 | tf_op jit(solution)/shard_map/ppermute | solution.py:239
  450.3 16.0 %collective-permute-done.1.refs_2_ = bf16[160,2304]{1,0:T(8,128)(2,1)S(1)} collective-permute-done((bf16[160,2304]{1,0:T(8,128)(2,1)S(1)}, bf16[160,2304]{1,0:T(8,128)(2,1)S(1)}, u32[]{:S(2)}, u32[]{:S(2)}) %collective-permute-start.1) | collective-permute-done | bytes 737312 | tf_op jit(solution)/shard_map/ppermute | solution.py:239
  467.5 42.7 %shard_map.328 = (bf16[160,2304]{1,0:T(8,128)(2,1)}, bf16[160,2304]{1,0:T(8,128)(2,1)}, bf16[160,2304]{1,0:T(8,128)(2,1)}, bf16[160,2304]{1,0:T(8,128)(2,1)}, bf...) custom-call(bf16[160,2304]{1,0:T(8,128)(2,1)} %get-tuple-element.130, ...), custom_call_target="tpu_custom_call" | custom-call | tf_op jit(solution)/shard_map/pallas_call | solution.py:176
  514.4 2.0 constant_dynamic-update-slice_fusion.3
  516.4 10.8 %collective-permute-done.13 = bf16[160,2176]{1,0:T(8,128)(2,1)S(1)} collective-permute-done((bf16[160,2176]{1,0:T(8,128)(2,1)}, bf16[160,2176]{1,0:T(8,128)(2,1)S(1)}, u32[]{:S(2)}, u32[]{:S(2)}) %collective-permute-start.13) | collective-permute-done | bytes 696352 | tf_op jit(solution)/shard_map/ppermute | solution.py:239
  528.6 13.9 %collective-permute-done.15 = bf16[160,2176]{1,0:T(8,128)(2,1)S(1)} collective-permute-done((bf16[160,2176]{1,0:T(8,128)(2,1)}, bf16[160,2176]{1,0:T(8,128)(2,1)S(1)}, u32[]{:S(2)}, u32[]{:S(2)}) %collective-permute-start.15) | collective-permute-done | bytes 696352 | tf_op jit(solution)/shard_map/ppermute | solution.py:239
  542.5 2.3 fusion.8
  547.8 10.3 %collective-permute-done.16 = bf16[160,2304]{1,0:T(8,128)(2,1)} collective-permute-done((bf16[160,2304]{1,0:T(8,128)(2,1)}, bf16[160,2304]{1,0:T(8,128)(2,1)}, u32[]{:S(2)}, u32[]{:S(2)}) %collective-permute-start.16) | collective-permute-done | bytes 737312 | tf_op jit(solution)/shard_map/ppermute | solution.py:239
  558.1 2.1 constant_dynamic-update-slice_fusion.2
  560.2 2.0 constant_dynamic-update-slice_fusion.1
  562.2 12.1 %collective-permute-done.18 = bf16[160,2304]{1,0:T(8,128)(2,1)} collective-permute-done((bf16[160,2304]{1,0:T(8,128)(2,1)}, bf16[160,2304]{1,0:T(8,128)(2,1)}, u32[]{:S(2)}, u32[]{:S(2)}) %collective-permute-start.18) | collective-permute-done | bytes 737312 | tf_op jit(solution)/shard_map/ppermute | solution.py:239
  574.3 2.0 constant_dynamic-update-slice_fusion
  576.3 3.0 fusion.6
  581.5 2.9 copy.503
  593.3 7.7 psum.78
  603.7 14.4 %reduce-scatter.9.cloned.1.call-done = bf16[256,512]{0,1:T(8,128)(2,1)} async-done(((bf16[256,2048]{0,1:T(8,128)(2,1)}), bf16[256,512]{0,1:T(8,128)(2,1)}) %reduce-scatter.9.cloned.1.call-update) | async-done | bytes 262160 | tf_op jit(solution)/shard_map/reduce_scatter | solution.py:245
  618.2 2.8 multiply_reduce_fusion.2
  621.0 9.4 %psum.79 = f32[256]{0:T(256)} all-reduce(f32[256]{0:T(256)} %get-tuple-element.196), channel_id=1, replica_groups=mesh['row'=8,'col'=4] {'col'}, use_global_device_ids=true, to_apply=%region_26.27 | all-reduce | flops 256 | bytes 2048 | tf_op jit(solution)/shard_map/psum | solution.py:444
  630.4 2.0 fusion.125
  635.7 25.6 %all-gather.20.cloned.1.call-done = bf16[256,2048]{0,1:T(8,128)(2,1)} async-done(((bf16[256,512]{0,1:T(8,128)(2,1)}), bf16[256,2048]{0,1:T(8,128)(2,1)}) %all-gather.20.cloned.1.call-update) | async-done | bytes 1048592 | tf_op jit(solution)/shard_map/all_gather | solution.py:242
  661.3 2.1 fusion.214
  663.4 2.3 convolution_convert_fusion.1
  669.0 4.7 copy.432
  673.7 9.8 %fusion.222 = f32[8,80,512]{2,1,0:T(8,128)S(1)} fusion(bf16[8,80,2048]{2,1,0:T(8,128)(2,1)} %bitcast.329, bf16[8,2048,512]{2,1,0:T(8,128)(2,1)} %all-gather.14.cloned.1.call-done), kind=kOutput, calls=%fused_computation.390 | convolution fusion | flops 1342177280 | bytes 20709376 | tf_op jit(solution)/shard_map/ecd,edw->ecw/dot_general | solution.py:27
  683.5 1.8 multiply_reduce_fusion.1
  689.1 3.1 fusion.30
  702.6 2.1 copy.440
  704.7 2.6 convolution_convert_fusion.11
  707.2 12.9 %convolution_convert_fusion.5 = bf16[8,80,2048]{2,1,0:T(8,128)(2,1)} fusion(bf16[8,80,512]{2,1,0:T(8,128)(2,1)} %bitcast.350, bf16[8,2048,512]{2,1,0:T(8,128)(2,1)} %all-gather.12.cloned.1.call-done), kind=kOutput, calls=%fused_computation.10 | convolution fusion | flops 1343488000 | bytes 20054016 | tf_op jit(solution)/shard_map/ecw,edw->ecd/dot_general | solution.py:27
  720.2 3.8 convolution_bitcast_fusion
  732.1 4.0 reshape.616
  736.1 2.6 slice.366
  738.7 3.6 slice.364
  744.8 3.0 copy.502
  755.2 10.6 %all_gather.36 = bf16[8,16,2048]{2,1,0:T(8,128)(2,1)S(1)} all-gather(bf16[1,16,2048]{2,1,0:T(8,128)(2,1)S(1)} %pad_maximum_fusion.12), channel_id=1, replica_groups=mesh['row'=8,'col'=4] {'row'}, dimensions={0}, use_global_device_ids=true | all-gather | bytes 589824 | tf_op jit(solution)/shard_map/all_gather | solution.py:550
  768.1 7.8 psum.80
  782.3 13.7 %all-reduce.4 = (f32[256]{0:T(256)}, bf16[256,16]{0,1:T(8,128)(2,1)}, bf16[256,16]{0,1:T(8,128)(2,1)}, bf16[256,16]{0,1:T(8,128)(2,1)S(1)}, bf16[256,16]{0,1:T(8,128)(2,1)S(1)}, /*index=5*/bf16[256,16]{0,1:T(8,128)(2,1)S(1)}) all-reduce(f32[256]{0:T(256)S(1)} %get-tuple-element.208, ...), channel_id=1, replica_groups=mesh['row'=8,'col'=4] {'col'}, use_global_device_ids=true, to_apply=%region_35.36 | all-reduce | flops 20736 | bytes 124928 | tf_op jit(solution)/shard_map/psum | solution.py:524
  802.4 8.8 %all-to-all-start.1 = ((bf16[1,80,8,256]{3,1,0,2:T(8,128)(2,1)}), bf16[1,80,8,256]{3,1,0,2:T(8,128)(2,1)S(1)}, u32[]{:S(2)}, u32[]{:S(2)}) async-start(bf16[1,80,8,256]{3,1,0,2:T(8,128)(2,1)} %copy_dynamic-update-slice_fusion), calls=%async_computation.5 | async-start | bytes 655360 | tf_op jit(solution)/shard_map/all_to_all | solution.py:542
  814.4 2.8 all-to-all-done.1
  (494 shorter events, 155.3 us)
Async XLA Ops:
  7.2 19.0 %copy-start = (bf16[8,16,2,512]{3,2,1,0:T(2,128)(2,1)S(1)}, bf16[8,16,2,512]{3,2,1,0:T(2,128)(2,1)}, u32[]{:S(2)}) copy-start(bf16[8,16,2,512]{3,2,1,0:T(2,128)(2,1)} %param.43) | copy-start | bytes 786436
  7.2 31.3 %all-gather.8.cloned.1.call-start = ((), (), s32[]{:S(2)}) async-start(), calls=%async_computation.6 | async-start | bytes 1310720 | tf_op jit(solution)/shard_map/all_gather | solution.py:242
  7.9 69.4 %all-gather.10.cloned.1.call-start = ((), (), s32[]{:S(2)}) async-start(), calls=%async_computation.7 | async-start | bytes 4718592 | tf_op jit(solution)/shard_map/all_gather | solution.py:252
  8.7 160.4 %all-gather.12.cloned.1.call-start = ((), (), s32[]{:S(2)}) async-start(), calls=%async_computation.8 | async-start | bytes 18874368 | tf_op jit(solution)/shard_map/all_gather | solution.py:253
  9.5 251.3 %all-gather.14.cloned.1.call-start = ((), (), s32[]{:S(2)}) async-start(), calls=%async_computation.9 | async-start | bytes 18874368 | tf_op jit(solution)/shard_map/all_gather | solution.py:254
  10.1 16.1 %copy-start.66 = (s32[256,2]{0,1:T(2,128)S(1)}, s32[256,2]{0,1:T(2,128)}, u32[]{:S(2)}) copy-start(s32[256,2]{0,1:T(2,128)} %param.29) | copy-start | bytes 6148
  19.1 21.5 %copy-start.90 = (f32[2048]{0:T(1024)S(1)}, f32[2048]{0:T(1024)}, u32[]{:S(2)}) copy-start(f32[2048]{0:T(1024)} %param.31) | copy-start | bytes 24580
  19.9 11.7 %all-to-all-start = ((bf16[8,80,256]{2,1,0:T(8,128)(2,1)}), bf16[8,80,256]{2,1,0:T(8,128)(2,1)S(1)}, u32[]{:S(2)}, u32[]{:S(2)}) async-start(bf16[8,80,256]{2,1,0:T(8,128)(2,1)} %copy.400), calls=%async_computation | async-start | bytes 655360 | tf_op jit(solution)/shard_map/all_to_all | solution.py:287
  25.5 280.1 %reduce-scatter.5.cloned.1.call-start = ((), (), s32[]{:S(2)}) async-start(), calls=%async_computation.10 | async-start | bytes 1310720 | tf_op jit(solution)/shard_map/reduce_scatter | solution.py:245
  26.2 54.5 %copy-start.53 = (bf16[1,16,2,512]{3,2,1,0:T(2,128)(2,1)}, bf16[1,16,2,512]{3,2,1,0:T(2,128)(2,1)S(1)}, u32[]{:S(2)}) copy-start(bf16[1,16,2,512]{3,2,1,0:T(2,128)(2,1)S(1)} %constant_dynamic-slice_fusion.4) | copy-start | bytes 98308
  28.4 54.1 %copy-start.14 = (f32[256,64]{1,0:T(8,128)}, f32[256,64]{1,0:T(8,128)S(1)}, u32[]{:S(2)}) copy-start(f32[256,64]{1,0:T(8,128)S(1)} %get-tuple-element.183) | copy-start | bytes 196612
  28.4 13.8 %copy-start.65 = (bf16[2048,8]{0,1:T(8,128)(2,1)S(1)}, bf16[2048,8]{0,1:T(8,128)(2,1)}, u32[]{:S(2)}) copy-start(bf16[2048,8]{0,1:T(8,128)(2,1)} %param.33) | copy-start | bytes 98308
  32.2 245.7 %copy-start.42 = (bf16[8,2,8,256]{3,2,0,1:T(8,128)(2,1)}, bf16[8,2,8,256]{3,2,0,1:T(8,128)(2,1)S(1)}, u32[]{:S(2)}) copy-start(bf16[8,2,8,256]{3,2,0,1:T(8,128)(2,1)S(1)} %copy.506) | copy-start | bytes 196612
  43.3 230.6 %copy-start.76 = (s32[256,1]{0,1:T(1,128)}, s32[256,1]{0,1:T(1,128)S(1)}, u32[]{:S(2)}) copy-start(s32[256,1]{0,1:T(1,128)S(1)} %get-tuple-element.180) | copy-start | bytes 3076
  45.2 35.6 %copy-start.73 = (bf16[256,16,1]{0,1,2:T(8,128)(2,1)}, bf16[256,16,1]{0,1,2:T(8,128)(2,1)S(1)}, u32[]{:S(2)}) copy-start(bf16[256,16,1]{0,1,2:T(8,128)(2,1)S(1)} %fusion.39) | copy-start | bytes 24580
  280.7 54.7 %all-gather.18.cloned.1.call-start = ((), (), s32[]{:S(2)}) async-start(), calls=%async_computation.12 | async-start | bytes 1310720 | tf_op jit(solution)/shard_map/all_gather | solution.py:242
  281.7 111.7 %all-gather.16.cloned.1.call-start = ((), (), s32[]{:S(2)}) async-start(), calls=%async_computation.11 | async-start | bytes 1310720 | tf_op jit(solution)/shard_map/all_gather | solution.py:242
  282.1 113.7 %copy-start.69 = (s32[640]{0:T(1024)}, s32[640]{0:T(1024)S(1)}, u32[]{:S(2)}) copy-start(s32[640]{0:T(1024)S(1)} %add.207) | copy-start | bytes 7684
  284.6 31.7 %copy-start.85 = (f32[512]{0:T(512)}, f32[512]{0:T(512)S(1)}, u32[]{:S(2)}) copy-start(f32[512]{0:T(512)S(1)} %dynamic_slice.51) | copy-start | bytes 6148
  294.4 95.0 %collective-permute-start.9 = (bf16[256,4224]{1,0:T(8,128)(2,1)}, bf16[256,4224]{1,0:T(8,128)(2,1)}, u32[]{:S(2)}, u32[]{:S(2)}) collective-permute-start(bf16[256,4224]{1,0:T(8,128)(2,1)} %pad_maximum_fusion.2), channel_id=1, source_target_pairs={{0,16},{4,20},{8,24},{12,28},{16,0},{20,4},{24,8},{28,12},{1,17},{... | collective-permute-start | bytes 6488072 | tf_op jit(solution)/shard_map/ppermute | solution.py:239
  296.5 94.0 %collective-permute-start.11 = (bf16[256,4224]{1,0:T(8,128)(2,1)}, bf16[256,4224]{1,0:T(8,128)(2,1)}, u32[]{:S(2)}, u32[]{:S(2)}) collective-permute-start(bf16[256,4224]{1,0:T(8,128)(2,1)} %pad_maximum_fusion.3), channel_id=1, source_target_pairs={{0,24},{4,28},{8,16},{12,20},{16,8},{20,12},{24,0},{28,4},{1,25},{... | collective-permute-start | bytes 6488072 | tf_op jit(solution)/shard_map/ppermute | solution.py:239
  299.9 18.4 %copy-start.44 = (bf16[8,2,8,256]{3,2,1,0:T(8,128)(2,1)S(1)}, bf16[8,2,8,256]{3,2,1,0:T(8,128)(2,1)}, u32[]{:S(2)}) copy-start(bf16[8,2,8,256]{3,2,1,0:T(8,128)(2,1)} %get-tuple-element.170) | copy-start | bytes 196612
  299.9 18.4 %copy-start.43 = (bf16[8,2,8,256]{3,2,1,0:T(8,128)(2,1)S(1)}, bf16[8,2,8,256]{3,2,1,0:T(8,128)(2,1)}, u32[]{:S(2)}) copy-start(bf16[8,2,8,256]{3,2,1,0:T(8,128)(2,1)} %get-tuple-element.171) | copy-start | bytes 196612
  301.4 90.6 %collective-permute-start.7 = (bf16[256,4224]{1,0:T(8,128)(2,1)}, bf16[256,4224]{1,0:T(8,128)(2,1)}, u32[]{:S(2)}, u32[]{:S(2)}) collective-permute-start(bf16[256,4224]{1,0:T(8,128)(2,1)} %pad_maximum_fusion.1), channel_id=1, source_target_pairs={{0,8},{4,12},{8,0},{12,4},{16,24},{20,28},{24,16},{28,20},{1,9},{5... | collective-permute-start | bytes 6488072 | tf_op jit(solution)/shard_map/ppermute | solution.py:239
  316.3 22.0 %copy-start.86 = (f32[256]{0:T(256)}, f32[256]{0:T(256)S(1)}, u32[]{:S(2)}) copy-start(f32[256]{0:T(256)S(1)} %get-tuple-element.187) | copy-start | bytes 3076
  318.1 300.1 %reduce-scatter.9.cloned.1.call-start = ((), (), s32[]{:S(2)}) async-start(), calls=%async_computation.14 | async-start | bytes 1310720 | tf_op jit(solution)/shard_map/reduce_scatter | solution.py:245
  318.4 20.0 %copy-start.34 = (bf16[8,2,8,256]{3,2,0,1:T(8,128)(2,1)}, bf16[8,2,8,256]{3,2,0,1:T(8,128)(2,1)S(1)}, u32[]{:S(2)}) copy-start(bf16[8,2,8,256]{3,2,0,1:T(8,128)(2,1)S(1)} %copy.508) | copy-start | bytes 196612
  338.3 55.0 %copy-start.75 = (bf16[2048,4]{0,1:T(4,128)(2,1)S(1)}, bf16[2048,4]{0,1:T(4,128)(2,1)}, u32[]{:S(2)}) copy-start(bf16[2048,4]{0,1:T(4,128)(2,1)} %param.34) | copy-start | bytes 49156
  338.4 56.5 %slice-start.1 = ((bf16[256,2,4]{0,2,1:T(4,128)(2,1)}), bf16[256,1,4]{0,2,1:T(4,128)(2,1)S(1)}, s32[]{:S(2)}) async-start(bf16[256,2,4]{0,2,1:T(4,128)(2,1)} %copy-done.99), calls=%async_computation.19 | async-start | bytes 4096 | tf_op jit(solution)/shard_map/slice | solution.py:57
  339.9 58.7 %copy-start.8 = (bf16[256,2048]{0,1:T(8,128)(2,1)S(1)}, bf16[256,2048]{0,1:T(8,128)(2,1)}, u32[]{:S(2)}) copy-start(bf16[256,2048]{0,1:T(8,128)(2,1)} %all-gather.18.cloned.1.call-done) | copy-start | bytes 3145732
  339.9 65.0 %collective-permute-start.6 = (bf16[256,4224]{1,0:T(8,128)(2,1)}, bf16[256,4224]{1,0:T(8,128)(2,1)}, u32[]{:S(2)}, u32[]{:S(2)}) collective-permute-start(bf16[256,4224]{1,0:T(8,128)(2,1)} %pad_maximum_fusion.refs_8_), channel_id=1, source_target_pairs={{0,4},{4,0},{8,12},{12,8},{16,20},{20,16},{24,28},{28,24},{1,5},{5... | collective-permute-start | bytes 6488072 | tf_op jit(solution)/shard_map/ppermute | solution.py:239
  389.5 16.6 %collective-permute-start.10 = (bf16[256,4224]{1,0:T(8,128)(2,1)}, bf16[256,4224]{1,0:T(8,128)(2,1)}, u32[]{:S(2)}, u32[]{:S(2)}) collective-permute-start(bf16[256,4224]{1,0:T(8,128)(2,1)} %collective-permute-done.9.refs_12_), channel_id=1, source_target_pairs={{0,4},{4,0},{8,12},{12,8},{16,20},{20,16},{24,28},{28,24},{1,5},{5... | collective-permute-start | bytes 6488072 | tf_op jit(solution)/shard_map/ppermute | solution.py:239
  390.6 15.8 %collective-permute-start.12 = (bf16[256,4224]{1,0:T(8,128)(2,1)}, bf16[256,4224]{1,0:T(8,128)(2,1)}, u32[]{:S(2)}, u32[]{:S(2)}) collective-permute-start(bf16[256,4224]{1,0:T(8,128)(2,1)} %collective-permute-done.11.refs_14_), channel_id=1, source_target_pairs={{0,4},{4,0},{8,12},{12,8},{16,20},{20,16},{24,28},{28,24},{1,5},{5... | collective-permute-start | bytes 6488072 | tf_op jit(solution)/shard_map/ppermute | solution.py:239
  392.0 15.5 %collective-permute-start.8 = (bf16[256,4224]{1,0:T(8,128)(2,1)}, bf16[256,4224]{1,0:T(8,128)(2,1)}, u32[]{:S(2)}, u32[]{:S(2)}) collective-permute-start(bf16[256,4224]{1,0:T(8,128)(2,1)} %collective-permute-done.7.refs_10_), channel_id=1, source_target_pairs={{0,4},{4,0},{8,12},{12,8},{16,20},{20,16},{24,28},{28,24},{1,5},{5... | collective-permute-start | bytes 6488072 | tf_op jit(solution)/shard_map/ppermute | solution.py:239
  401.4 18.2 %collective-permute-start.5 = (bf16[160,2176]{1,0:T(8,128)(2,1)S(1)}, bf16[160,2176]{1,0:T(8,128)(2,1)S(1)}, u32[]{:S(2)}, u32[]{:S(2)}) collective-permute-start(bf16[160,2176]{1,0:T(8,128)(2,1)S(1)} %get-tuple-element.135), channel_id=1, source_target_pairs={{0,24},{4,28},{8,16},{12,20},{16,8},{20,12},{24,0},{28,4},{1,25},{... | collective-permute-start | bytes 2088968 | tf_op jit(solution)/shard_map/ppermute | solution.py:239
  403.8 17.0 %copy-start.10 = (bf16[8,16,2,1408]{3,1,0,2:T(8,128)(2,1)S(1)}, bf16[8,16,2,1408]{3,1,0,2:T(8,128)(2,1)}, u32[]{:S(2)}) copy-start(bf16[8,16,2,1408]{3,1,0,2:T(8,128)(2,1)} %copy.424) | copy-start | bytes 2162692
  403.8 17.0 %copy-start.37 = (bf16[8,16,1408]{2,1,0:T(8,128)(2,1)S(1)}, bf16[8,16,1408]{2,1,0:T(8,128)(2,1)}, u32[]{:S(2)}) copy-start(bf16[8,16,1408]{2,1,0:T(8,128)(2,1)} %param.49) | copy-start | bytes 1081348
  404.9 30.2 %collective-permute-start.4 = (bf16[160,2176]{1,0:T(8,128)(2,1)S(1)}, bf16[160,2176]{1,0:T(8,128)(2,1)S(1)}, u32[]{:S(2)}, u32[]{:S(2)}) collective-permute-start(bf16[160,2176]{1,0:T(8,128)(2,1)S(1)} %get-tuple-element.136), channel_id=1, source_target_pairs={{0,16},{4,20},{8,24},{12,28},{16,0},{20,4},{24,8},{28,12},{1,17},{... | collective-permute-start | bytes 2088968 | tf_op jit(solution)/shard_map/ppermute | solution.py:239
  406.1 28.9 %collective-permute-start.3 = (bf16[160,2176]{1,0:T(8,128)(2,1)S(1)}, bf16[160,2176]{1,0:T(8,128)(2,1)S(1)}, u32[]{:S(2)}, u32[]{:S(2)}) collective-permute-start(bf16[160,2176]{1,0:T(8,128)(2,1)S(1)} %get-tuple-element.137), channel_id=1, source_target_pairs={{0,8},{4,12},{8,0},{12,4},{16,24},{20,28},{24,16},{28,20},{1,9},{5... | collective-permute-start | bytes 2088968 | tf_op jit(solution)/shard_map/ppermute | solution.py:239
  406.4 43.9 %collective-permute-start.2 = (bf16[160,2304]{1,0:T(8,128)(2,1)S(1)}, bf16[160,2304]{1,0:T(8,128)(2,1)S(1)}, u32[]{:S(2)}, u32[]{:S(2)}) collective-permute-start(bf16[160,2304]{1,0:T(8,128)(2,1)S(1)} %get-tuple-element.127), channel_id=1, source_target_pairs={{0,24},{4,28},{8,16},{12,20},{16,8},{20,12},{24,0},{28,4},{1,25},{... | collective-permute-start | bytes 2211848 | tf_op jit(solution)/shard_map/ppermute | solution.py:239
  407.5 58.8 %collective-permute-start.1 = (bf16[160,2304]{1,0:T(8,128)(2,1)S(1)}, bf16[160,2304]{1,0:T(8,128)(2,1)S(1)}, u32[]{:S(2)}, u32[]{:S(2)}) collective-permute-start(bf16[160,2304]{1,0:T(8,128)(2,1)S(1)} %get-tuple-element.128), channel_id=1, source_target_pairs={{0,16},{4,20},{8,24},{12,28},{16,0},{20,4},{24,8},{28,12},{1,17},{... | collective-permute-start | bytes 2211848 | tf_op jit(solution)/shard_map/ppermute | solution.py:239
  419.6 46.8 %copy-start.27 = (bf16[160,2176]{1,0:T(8,128)(2,1)}, bf16[160,2176]{1,0:T(8,128)(2,1)S(1)}, u32[]{:S(2)}) copy-start(bf16[160,2176]{1,0:T(8,128)(2,1)S(1)} %collective-permute-done.5.refs_7_) | copy-start | bytes 2088964
  419.6 46.8 %collective-permute-start = (bf16[160,2304]{1,0:T(8,128)(2,1)S(1)}, bf16[160,2304]{1,0:T(8,128)(2,1)S(1)}, u32[]{:S(2)}, u32[]{:S(2)}) collective-permute-start(bf16[160,2304]{1,0:T(8,128)(2,1)S(1)} %get-tuple-element.129), channel_id=1, source_target_pairs={{0,8},{4,12},{8,0},{12,4},{16,24},{20,28},{24,16},{28,20},{1,9},{5... | collective-permute-start | bytes 2211848 | tf_op jit(solution)/shard_map/ppermute | solution.py:239
  435.0 31.3 %copy-start.28 = (bf16[160,2176]{1,0:T(8,128)(2,1)}, bf16[160,2176]{1,0:T(8,128)(2,1)S(1)}, u32[]{:S(2)}) copy-start(bf16[160,2176]{1,0:T(8,128)(2,1)S(1)} %collective-permute-done.4.refs_6_) | copy-start | bytes 2088964
  435.0 31.3 %copy-start.29 = (bf16[160,2176]{1,0:T(8,128)(2,1)}, bf16[160,2176]{1,0:T(8,128)(2,1)S(1)}, u32[]{:S(2)}) copy-start(bf16[160,2176]{1,0:T(8,128)(2,1)S(1)} %collective-permute-done.3.refs_5_) | copy-start | bytes 2088964
  450.3 16.1 %copy-start.23 = (bf16[160,2304]{1,0:T(8,128)(2,1)}, bf16[160,2304]{1,0:T(8,128)(2,1)S(1)}, u32[]{:S(2)}) copy-start(bf16[160,2304]{1,0:T(8,128)(2,1)S(1)} %collective-permute-done.2.refs_3_) | copy-start | bytes 2211844
  510.2 17.0 %collective-permute-start.13 = (bf16[160,2176]{1,0:T(8,128)(2,1)}, bf16[160,2176]{1,0:T(8,128)(2,1)S(1)}, u32[]{:S(2)}, u32[]{:S(2)}) collective-permute-start(bf16[160,2176]{1,0:T(8,128)(2,1)} %get-tuple-element.26), channel_id=1, source_target_pairs={{0,8},{4,12},{8,0},{12,4},{16,24},{20,28},{24,16},{28,20},{1,9},{5... | collective-permute-start | bytes 2088968 | tf_op jit(solution)/shard_map/ppermute | solution.py:239
  511.5 17.2 %collective-permute-start.14 = (bf16[160,2176]{1,0:T(8,128)(2,1)}, bf16[160,2176]{1,0:T(8,128)(2,1)S(1)}, u32[]{:S(2)}, u32[]{:S(2)}) collective-permute-start(bf16[160,2176]{1,0:T(8,128)(2,1)} %get-tuple-element.27), channel_id=1, source_target_pairs={{0,16},{4,20},{8,24},{12,28},{16,0},{20,4},{24,8},{28,12},{1,17},{... | collective-permute-start | bytes 2088968 | tf_op jit(solution)/shard_map/ppermute | solution.py:239
  511.7 30.8 %collective-permute-start.15 = (bf16[160,2176]{1,0:T(8,128)(2,1)}, bf16[160,2176]{1,0:T(8,128)(2,1)S(1)}, u32[]{:S(2)}, u32[]{:S(2)}) collective-permute-start(bf16[160,2176]{1,0:T(8,128)(2,1)} %get-tuple-element.28), channel_id=1, source_target_pairs={{0,24},{4,28},{8,16},{12,20},{16,8},{20,12},{24,0},{28,4},{1,25},{... | collective-permute-start | bytes 2088968 | tf_op jit(solution)/shard_map/ppermute | solution.py:239
  513.0 45.2 %collective-permute-start.16 = (bf16[160,2304]{1,0:T(8,128)(2,1)}, bf16[160,2304]{1,0:T(8,128)(2,1)}, u32[]{:S(2)}, u32[]{:S(2)}) collective-permute-start(bf16[160,2304]{1,0:T(8,128)(2,1)} %get-tuple-element.30), channel_id=1, source_target_pairs={{0,8},{4,12},{8,0},{12,4},{16,24},{20,28},{24,16},{28,20},{1,9},{5... | collective-permute-start | bytes 2211848 | tf_op jit(solution)/shard_map/ppermute | solution.py:239
  514.1 46.0 %collective-permute-start.17 = (bf16[160,2304]{1,0:T(8,128)(2,1)}, bf16[160,2304]{1,0:T(8,128)(2,1)}, u32[]{:S(2)}, u32[]{:S(2)}) collective-permute-start(bf16[160,2304]{1,0:T(8,128)(2,1)} %get-tuple-element.31), channel_id=1, source_target_pairs={{0,16},{4,20},{8,24},{12,28},{16,0},{20,4},{24,8},{28,12},{1,17},{... | collective-permute-start | bytes 2211848 | tf_op jit(solution)/shard_map/ppermute | solution.py:239
  527.2 47.0 %collective-permute-start.18 = (bf16[160,2304]{1,0:T(8,128)(2,1)}, bf16[160,2304]{1,0:T(8,128)(2,1)}, u32[]{:S(2)}, u32[]{:S(2)}) collective-permute-start(bf16[160,2304]{1,0:T(8,128)(2,1)} %get-tuple-element.32), channel_id=1, source_target_pairs={{0,24},{4,28},{8,16},{12,20},{16,8},{20,12},{24,0},{28,4},{1,25},{... | collective-permute-start | bytes 2211848 | tf_op jit(solution)/shard_map/ppermute | solution.py:239
  588.9 29.2 %copy-start.6 = (bf16[256,512]{0,1:T(8,128)(2,1)S(1)}, bf16[256,512]{0,1:T(8,128)(2,1)}, u32[]{:S(2)}) copy-start(bf16[256,512]{0,1:T(8,128)(2,1)} %reduce-scatter.5.cloned.1.call-done) | copy-start | bytes 786436
  590.2 71.1 %all-gather.20.cloned.1.call-start = ((), (), s32[]{:S(2)}) async-start(), calls=%async_computation.15 | async-start | bytes 1310720 | tf_op jit(solution)/shard_map/all_gather | solution.py:242
  632.4 99.8 %all-reduce.7.cloned.1.call-start = ((), (), s32[]{:S(2)}) async-start(), calls=%async_computation.17 | async-start | bytes 2162688 | tf_op jit(solution)/shard_map/psum | solution.py:423
  635.7 145.1 %reduce-scatter.11.cloned.1.call-start = ((), (), s32[]{:S(2)}) async-start(), calls=%async_computation.16 | async-start | bytes 1310720 | tf_op jit(solution)/shard_map/reduce_scatter | solution.py:245
  729.2 82.0 %reduce-scatter.7.cloned.1.call-start = ((), (), s32[]{:S(2)}) async-start(), calls=%async_computation.13 | async-start | bytes 1310720 | tf_op jit(solution)/shard_map/reduce_scatter | solution.py:245
  767.1 13.7 %copy-start.104 = (f32[512]{0:T(512)S(1)}, f32[512]{0:T(512)}, u32[]{:S(2)}) copy-start(f32[512]{0:T(512)} %dynamic_slice.62) | copy-start | bytes 6148
  767.2 15.0 %copy-start.50 = (f32[256,16]{0,1:T(8,128)S(1)}, f32[256,16]{0,1:T(8,128)}, u32[]{:S(2)}) copy-start(f32[256,16]{0,1:T(8,128)} %copy-done.49) | copy-start | bytes 49156
  767.2 15.0 %copy-start.52 = (f32[256,16]{0,1:T(8,128)S(1)}, f32[256,16]{0,1:T(8,128)}, u32[]{:S(2)}) copy-start(f32[256,16]{0,1:T(8,128)} %get-tuple-element.111) | copy-start | bytes 49156
  767.2 15.0 %copy-start.63 = (f32[256,16]{0,1:T(8,128)S(1)}, f32[256,16]{0,1:T(8,128)}, u32[]{:S(2)}) copy-start(f32[256,16]{0,1:T(8,128)} %get-tuple-element.207) | copy-start | bytes 49156
  767.2 15.0 %slice-start = ((f32[256,2064]{0,1:T(8,128)}), f32[256,16]{0,1:T(8,128)S(1)}, s32[]{:S(2)}) async-start(f32[256,2064]{0,1:T(8,128)} %copy-done.64), calls=%async_computation.18 | async-start | bytes 32768 | tf_op jit(solution)/shard_map/slice | solution.py:398
  767.2 15.0 %copy-start.89 = (f32[256,16]{0,1:T(8,128)S(1)}, f32[256,16]{0,1:T(8,128)}, u32[]{:S(2)}) copy-start(f32[256,16]{0,1:T(8,128)} %get-tuple-element.205) | copy-start | bytes 49156
  802.4 14.8 %all-to-all-start.1 = ((bf16[1,80,8,256]{3,1,0,2:T(8,128)(2,1)}), bf16[1,80,8,256]{3,1,0,2:T(8,128)(2,1)S(1)}, u32[]{:S(2)}, u32[]{:S(2)}) async-start(bf16[1,80,8,256]{3,1,0,2:T(8,128)(2,1)} %copy_dynamic-update-slice_fusion), calls=%async_computation.5 | async-start | bytes 655360 | tf_op jit(solution)/shard_map/all_to_all | solution.py:542
  (86 other events, 397.5 us)
Sparse Core Ops, SparseCore 0:
  9.6 28.8 all-gather.7
  40.4 36.8 all-gather.9
  79.2 89.8 all-gather.11
  170.9 89.8 all-gather.13
  280.8 24.6 reduce-scatter.4
  307.1 28.3 all-gather.17
  337.6 27.4 all-gather.15
  590.3 27.8 reduce-scatter.8
  632.5 28.7 all-gather.19
  664.4 55.7 all-reduce.6
  729.3 24.8 reduce-scatter.10
  756.5 26.0 reduce-scatter.6

commit v3 on v2

--- a/solution.py
+++ b/solution.py
@@ -70,12 +70,256 @@
     return jnp.sum(centred[:, :, None] * onehot, axis=1)
 
 
+def opposite(axis, offset):
+    index = jnp.bitwise_xor(lax.axis_index(axis), offset)
+    if axis == "row":
+        return (index, lax.axis_index("col"))
+    return (lax.axis_index("row"), index)
+
+
+def greet(partners):
+    barrier = pltpu.get_barrier_semaphore()
+    for partner in partners:
+        pl.semaphore_signal(
+            barrier, inc=1, device_id=partner, device_id_type=pl.DeviceIdType.MESH
+        )
+    pl.semaphore_wait(barrier, len(partners))
+
+
+def gather_kernel(parts, cols, counts, *refs):
+    blocks = refs[: len(counts)]
+    tokens = refs[len(counts) : len(counts) + 2]
+    wholes = refs[len(counts) + 2 : 2 * len(counts) + 2]
+    token_wholes = refs[2 * len(counts) + 2 : 2 * len(counts) + 4]
+    send, recv, local = refs[2 * len(counts) + 4 :]
+    row = lax.axis_index("row")
+    col = lax.axis_index("col")
+    depth = blocks[0].shape[1]
+    wide = tokens[0].shape[1]
+    partners = {offset: opposite("row", offset) for offset in (1, 2, 4)}
+    greet(list(partners.values()) + [opposite("col", i) for i in range(1, cols)])
+    chunks = [(a, i) for a, count in enumerate(counts) for i in range(count)]
+    total = len(chunks)
+    used = [0]
+    started = []
+
+    def place(chunk, offset):
+        array, i = chunk
+        owner = jnp.bitwise_xor(row, offset)
+        return wholes[array].at[i, pl.ds(pl.multiple_of(owner * depth, depth), depth)]
+
+    def push(source, chunk, target, offset):
+        n = used[0]
+        used[0] += 1
+        copy = pltpu.make_async_remote_copy(
+            src_ref=source,
+            dst_ref=place(chunk, offset),
+            send_sem=send.at[n],
+            recv_sem=recv.at[n],
+            device_id=partners[target],
+            device_id_type=pl.DeviceIdType.MESH,
+        )
+        copy.start()
+        started.append(copy)
+        return copy
+
+    copies = []
+    for k in range(2):
+        here = pl.ds(pl.multiple_of(col * wide, wide), wide)
+        copy = pltpu.make_async_copy(tokens[k], token_wholes[k].at[:, here], local.at[k])
+        copy.start()
+        copies.append(copy)
+        for i in range(1, cols):
+            n = used[0]
+            used[0] += 1
+            copy = pltpu.make_async_remote_copy(
+                src_ref=tokens[k],
+                dst_ref=token_wholes[k].at[:, here],
+                send_sem=send.at[n],
+                recv_sem=recv.at[n],
+                device_id=opposite("col", i),
+                device_id_type=pl.DeviceIdType.MESH,
+            )
+            copy.start()
+            started.append(copy)
+    for a in range(len(counts)):
+        where = pl.ds(pl.multiple_of(row * depth, depth), depth)
+        copy = pltpu.make_async_copy(blocks[a], wholes[a].at[:, where], local.at[2 + a])
+        copy.start()
+        copies.append(copy)
+    first = {}
+    for number, chunk in enumerate(chunks):
+        source = blocks[chunk[0]].at[chunk[1]]
+        for target in (2, 4):
+            first[number, target] = push(source, chunk, target, 0)
+    for number, chunk in enumerate(chunks):
+        push(blocks[chunk[0]].at[chunk[1]], chunk, 1, 0)
+    relayed = {}
+    for number, chunk in enumerate(chunks):
+        first[number, 2].wait_recv()
+        first[number, 4].wait_recv()
+        if number % 2 == 0:
+            relayed[number] = push(place(chunk, 2), chunk, 4, 2)
+        else:
+            relayed[number] = push(place(chunk, 4), chunk, 2, 4)
+        for offset in (2, 4):
+            push(place(chunk, offset), chunk, 1, offset)
+    for number, chunk in enumerate(chunks):
+        relayed[number].wait_recv()
+        push(place(chunk, 6), chunk, 1, 6)
+    waited = {id(copy) for copy in first.values()} | {id(copy) for copy in relayed.values()}
+    for copy in started:
+        if id(copy) not in waited:
+            copy.wait_recv()
+    for copy in started:
+        copy.wait_send()
+    for copy in copies:
+        copy.wait()
+
+
+def gather_all(blocks, tokens, parts, cols):
+    counts = [block.shape[0] for block in blocks]
+    hbm = pl.BlockSpec(memory_space=pl.ANY)
+    remote = 7 * sum(counts) + 2 * (cols - 1)
+    return pl.pallas_call(
+        functools.partial(gather_kernel, parts, cols, counts),
+        out_shape=[
+            jax.ShapeDtypeStruct((b.shape[0], b.shape[1] * parts, b.shape[2]), b.dtype)
+            for b in blocks
+        ]
+        + [jax.ShapeDtypeStruct((t.shape[0], t.shape[1] * cols), t.dtype) for t in tokens],
+        in_specs=[hbm] * (len(blocks) + 2),
+        out_specs=[hbm] * (len(blocks) + 2),
+        scratch_shapes=[
+            pltpu.SemaphoreType.DMA((remote,)),
+            pltpu.SemaphoreType.DMA((remote,)),
+            pltpu.SemaphoreType.DMA((2 + len(blocks),)),
+        ],
+        compiler_params=pltpu.CompilerParams(collective_id=1, has_side_effects=True),
+    )(*blocks, *tokens)
+
+
+def cot_kernel(cols, replicas, *refs):
+    blocks, exts = refs[:EXP_FF], refs[EXP_FF : 2 * EXP_FF]
+    wholes, ext_wholes = refs[2 * EXP_FF : 3 * EXP_FF], refs[3 * EXP_FF : 4 * EXP_FF]
+    landed, send, recv, local = refs[4 * EXP_FF :]
+    col = lax.axis_index("col")
+    wide = blocks[0].shape[1]
+    here = pl.ds(pl.multiple_of(col * wide, wide), wide)
+    along = [opposite("col", i) for i in range(1, cols)]
+    across = [opposite("row", j * replicas) for j in range(1, EXP_FF)]
+    greet(along + across)
+    copies = []
+
+    def push(source, target, n, device):
+        copy = pltpu.make_async_remote_copy(
+            src_ref=source,
+            dst_ref=target,
+            send_sem=send.at[n],
+            recv_sem=recv.at[n],
+            device_id=device,
+            device_id_type=pl.DeviceIdType.MESH,
+        )
+        copy.start()
+        copies.append(copy)
+        return copy
+
+    def keep(source, target, n):
+        copy = pltpu.make_async_copy(source, target, local.at[n])
+        copy.start()
+        return copy
+
+    first = [
+        push(blocks[j], landed.at[j - 1], j - 1, across[j - 1]) for j in range(1, EXP_FF)
+    ]
+    base = EXP_FF - 1
+    for j in range(1, EXP_FF):
+        push(exts[j], ext_wholes[j], base + j - 1, across[j - 1])
+    base += EXP_FF - 1
+    kept = [keep(exts[0], ext_wholes[0], 0)]
+    for j in range(EXP_FF):
+        if j:
+            first[j - 1].wait_recv()
+            source = landed.at[j - 1]
+        else:
+            source = blocks[0]
+        kept.append(keep(source, wholes[j].at[:, here], 1 + j))
+        for i in range(cols - 1):
+            push(source, wholes[j].at[:, here], base + j * (cols - 1) + i, along[i])
+    for copy in copies[EXP_FF - 1 :]:
+        copy.wait_recv()
+    for copy in copies:
+        copy.wait_send()
+    for copy in kept:
+        copy.wait()
+
+
+def spread_cot(blocks, exts, cols, replicas):
+    hbm = pl.BlockSpec(memory_space=pl.ANY)
+    wide = blocks[0].shape[1]
+    remote = 2 * (EXP_FF - 1) + EXP_FF * (cols - 1)
+    return pl.pallas_call(
+        functools.partial(cot_kernel, cols, replicas),
+        out_shape=[jax.ShapeDtypeStruct((CAP_FF, wide * cols), BF16)] * EXP_FF
+        + [jax.ShapeDtypeStruct((CAP_FF, LANES), BF16)] * EXP_FF,
+        in_specs=[hbm] * (2 * EXP_FF),
+        out_specs=[hbm] * (2 * EXP_FF),
+        scratch_shapes=[
+            pltpu.VMEM((EXP_FF - 1, CAP_FF, wide), BF16),
+            pltpu.SemaphoreType.DMA((remote,)),
+            pltpu.SemaphoreType.DMA((remote,)),
+            pltpu.SemaphoreType.DMA((1 + EXP_FF,)),
+        ],
+        compiler_params=pltpu.CompilerParams(collective_id=2, has_side_effects=True),
+    )(*blocks, *exts)
+
+
+def trade_kernel(replicas, *refs):
+    count = EXP_FF - 1
+    blocks, arrived = refs[:count], refs[count : 2 * count]
+    send, recv = refs[2 * count :]
+    across = [opposite("row", j * replicas) for j in range(1, EXP_FF)]
+    greet(across)
+    copies = []
+    for j in (2, 1, 0):
+        copy = pltpu.make_async_remote_copy(
+            src_ref=blocks[j],
+            dst_ref=arrived[j],
+            send_sem=send.at[j],
+            recv_sem=recv.at[j],
+            device_id=across[j],
+            device_id_type=pl.DeviceIdType.MESH,
+        )
+        copy.start()
+        copies.append(copy)
+    for copy in copies:
+        copy.wait()
+
+
+def trade_rows(blocks, replicas, number):
+    hbm = pl.BlockSpec(memory_space=pl.ANY)
+    count = EXP_FF - 1
+    arrived = pl.pallas_call(
+        functools.partial(trade_kernel, replicas),
+        out_shape=[jax.ShapeDtypeStruct(b.shape, b.dtype) for b in blocks[1:]],
+        in_specs=[hbm] * count,
+        out_specs=[hbm] * count,
+        scratch_shapes=[
+            pltpu.SemaphoreType.DMA((count,)),
+            pltpu.SemaphoreType.DMA((count,)),
+        ],
+        compiler_params=pltpu.CompilerParams(collective_id=number, has_side_effects=True),
+    )(*blocks[1:])
+    return [blocks[0], *arrived]
+
+
 def ffn_kernel(parts, depth, width, units, *refs):
     hids = refs[:EXP_FF]
     cots = refs[EXP_FF : 2 * EXP_FF]
-    pieces = refs[2 * EXP_FF : 2 * EXP_FF + parts]
-    rights = refs[2 * EXP_FF + parts]
-    outs = refs[2 * EXP_FF + parts + 1 :]
+    cot_exts = refs[2 * EXP_FF : 3 * EXP_FF]
+    pieces = refs[3 * EXP_FF : 3 * EXP_FF + parts]
+    rights = refs[3 * EXP_FF + parts]
+    outs = refs[3 * EXP_FF + parts + 1 :]
     grads = outs[:EXP_FF]
     downs = outs[EXP_FF : 2 * EXP_FF]
     adapt = outs[2 * EXP_FF]
@@ -86,12 +330,15 @@
     for j in range(EXP_FF):
         where = pl.ds(j * CAP_FF, CAP_FF)
         copies.append(pltpu.make_async_copy(hids[j], hid.at[where], sems.at[j]))
-        copies.append(pltpu.make_async_copy(cots[j], cot.at[where], sems.at[EXP_FF + j]))
-    copies.append(pltpu.make_async_copy(rights, block.at[pl.ds(width, LANES)], sems.at[2 * EXP_FF]))
+        near = cot.at[where, pl.ds(0, width)]
+        copies.append(pltpu.make_async_copy(cots[j], near, sems.at[EXP_FF + j]))
+        near = cot.at[where, pl.ds(width, LANES)]
+        copies.append(pltpu.make_async_copy(cot_exts[j], near, sems.at[2 * EXP_FF + j]))
+    copies.append(pltpu.make_async_copy(rights, block.at[pl.ds(width, LANES)], sems.at[3 * EXP_FF]))
     for m in range(parts):
         owner = jnp.bitwise_xor(row, m)
         where = pl.ds(pl.multiple_of(owner * depth, depth), depth)
-        copies.append(pltpu.make_async_copy(pieces[m], block.at[where], sems.at[2 * EXP_FF + 1 + m]))
+        copies.append(pltpu.make_async_copy(pieces[m], block.at[where], sems.at[3 * EXP_FF + 1 + m]))
     for copy in copies:
         copy.start()
     for copy in copies:
@@ -164,7 +411,7 @@
         low_ext, act[:, 2 * units :], (((0,), (0,)), ((), ())), preferred_element_type=F32
     ).astype(BF16)
 
-def feed_forward(hids, cots, pieces, rights):
+def feed_forward(hids, cots, cot_exts, pieces, rights):
     parts = len(pieces)
     depth, triple = pieces[0].shape
     units = triple // 3
@@ -178,7 +425,7 @@
         out_shape=[jax.ShapeDtypeStruct((CAP_FF, wide + LANES), BF16)] * EXP_FF
         + [jax.ShapeDtypeStruct((CAP_FF, wide), BF16)] * EXP_FF
         + [jax.ShapeDtypeStruct((LANES, triple), BF16)],
-        in_specs=[hbm] * (2 * EXP_FF + parts + 1),
+        in_specs=[hbm] * (3 * EXP_FF + parts + 1),
         out_specs=[vmem] * (2 * EXP_FF + 1),
         scratch_shapes=[
             pltpu.VMEM((rows, wide + LANES), BF16),
@@ -186,10 +433,10 @@
             pltpu.VMEM((wide, triple), BF16),
             pltpu.VMEM((rows, triple), BF16),
             pltpu.VMEM((rows, 1), F32),
-            pltpu.SemaphoreType.DMA((2 * EXP_FF + 1 + parts,)),
+            pltpu.SemaphoreType.DMA((3 * EXP_FF + 1 + parts,)),
         ],
         compiler_params=pltpu.CompilerParams(vmem_limit_bytes=56 * 2**20),
-    )(*hids, *cots, *pieces, rights)
+    )(*hids, *cots, *cot_exts, *pieces, rights)
 
 
 def on_device(
@@ -249,28 +496,35 @@
     def own_columns(table):
         return lax.dynamic_slice_in_dim(table, col * slice_width, slice_width, 0)
 
-    kv_full = lax.all_gather(kv_weight, "row", axis=1, tiled=True)
-    query_full = lax.all_gather(query_weight, "row", axis=1, tiled=True)
-    out_full = lax.all_gather(out_weight, "row", axis=1, tiled=True)
-
     def later(value, *earlier):
         return lax.optimization_barrier((value, *earlier))[0]
 
+    cols = lax.axis_size("col")
+    if rows_axis == 8:
+        kv_full, query_full, x_full, cot_full = gather_all(
+            [kv_weight, query_weight], [inputs, cotangent], rows_axis, cols
+        )
+    else:
+        kv_full = lax.all_gather(kv_weight, "row", axis=1, tiled=True)
+        query_full = lax.all_gather(query_weight, "row", axis=1, tiled=True)
+        x_full = features(inputs)
+        cot_full = features(cotangent)
+    out_full = lax.all_gather(later(out_weight, query_full), "row", axis=1, tiled=True)
+
     padding = -units % LANES
 
     def padded(value):
         return jnp.pad(value, ((0, 0), (0, padding))) if padding else value
 
-    inner_later, down_later = later((inner_weight, down_weight), out_full)
     near = []
     for j in range(EXP_FF):
         which = expert ^ j
-        inner_own = lax.dynamic_index_in_dim(inner_later, which, 0, keepdims=False)
-        down_own = lax.dynamic_index_in_dim(down_later, which, 0, keepdims=False)
+        inner_own = lax.dynamic_index_in_dim(inner_weight, which, 0, keepdims=False)
+        down_own = lax.dynamic_index_in_dim(down_weight, which, 0, keepdims=False)
         piece = jnp.concatenate(
             [padded(inner_own[:, 0]), padded(inner_own[:, 1]), padded(down_own)], axis=1
         )
-        near.append(swap(piece, j * replicas) if j else piece)
+        near.append(swap(later(piece, query_full), j * replicas) if j else piece)
     chunks = []
     for j in range(EXP_FF):
         for i in range(replicas):
@@ -329,12 +583,15 @@
         return [swap(block, j * replicas) if j else block for j, block in enumerate(blocks)]
 
     masked_cot = cotangent * valid.astype(BF16)[:, None]
-    cot_full = features(masked_cot)
+    cot_full = cot_full * valid.astype(BF16)[:, None]
     grad_low_down = mm("td,rd->tr", cot_full, left_down)
-    cot_ext = jnp.concatenate([cot_full, spread(grad_low_down).astype(BF16)], axis=1)
-    cot_rows = trade(blocks_of(mm("ct,td->cd", pick_ffn_any, cot_ext).astype(BF16)))
-
-    x_full = features(inputs)
+    cot_rows = spread_cot(
+        blocks_of(mm("ct,td->cd", pick_ffn_any, masked_cot).astype(BF16)),
+        blocks_of(mm("ct,td->cd", pick_ffn_any, spread(grad_low_down).astype(BF16)).astype(BF16)),
+        cols,
+        replicas,
+    )
+
     x_wide = x_full.astype(F32)
     scale_one = lax.rsqrt(jnp.mean(x_wide * x_wide, axis=1, keepdims=True) + EPSILON)
     hidden_one = (x_wide * scale_one * norm_one).astype(BF16)
@@ -416,10 +673,11 @@
         for k in range(TOPK)
     )
     gate_out = jnp.pad(gate_out, ((0, 0), (0, 126))).astype(BF16)
-    hidden_in = trade(blocks_of(jnp.concatenate([hidden_out, gate_out], axis=1)))
-    results = feed_forward(hidden_in, cot_rows, chunks, ffn_right)
-    grad_back = jnp.concatenate(trade(results[:EXP_FF]))
-    down_back = jnp.concatenate(trade(results[EXP_FF : 2 * EXP_FF]))
+    hidden_in = trade_rows(blocks_of(jnp.concatenate([hidden_out, gate_out], axis=1)), replicas, 3)
+    results = feed_forward(hidden_in, cot_rows[:EXP_FF], cot_rows[EXP_FF:], chunks, ffn_right)
+    grad_back = jnp.concatenate(trade_rows(results[:EXP_FF], replicas, 4))
+    down_back = trade(list(later(tuple(results[EXP_FF : 2 * EXP_FF]), grad_back)))
+    down_back = jnp.concatenate(down_back)
     ffn_rights = lax.optimization_barrier(lax.psum(results[2 * EXP_FF], "row")).astype(F32)
     ffn_rights = ffn_rights.reshape(ADAPT, RANK, 3, units + padding)[..., :units]
 

time: 845 us -> 802 us (0.949)
  waiting for transfers between devices: 408 us -> 97.7 us
  Pallas kernels: 42.7 us -> 272 us
  starting transfers between devices: 32.4 us -> 68.7 us
  local copies, waits for them, and re-layouts: 101 us -> 110 us
    pallas_call x0 -> x4, Pallas kernels: none -> 230 us  [the longest x1 100 us: gather_all(): pl.pallas_call(functools.partial(gather_kernel, parts, cols, counts), out...]
    all_gather x3 -> x1, waiting for transfers between devices: 180 us -> 9.22 us  [on_device(): lax.all_gather(later(out_weight, query_full), 'row', axis=1, tiled=True)]
    ppermute x19 -> x10, waiting for transfers between devices: 153 us -> 32.2 us  [swap(): lax.ppermute(value, 'row', [(i, i ^ offset) for i in range(rows_axis)])]
    ppermute x19 -> x10, starting transfers between devices: 17.4 us -> 54.1 us  [swap(): lax.ppermute(value, 'row', [(i, i ^ offset) for i in range(rows_axis)])]
    all_gather x4 -> x2, waiting for transfers between devices: 48.8 us -> 25.6 us  [features(): return lax.all_gather(part, 'col', axis=1, tiled=True)]
    reduce_scatter x4, waiting for transfers between devices: 18.3 us -> 27.8 us  [partials(): lax.psum_scatter(part.astype(BF16), 'col', scatter_dimension=1, tiled=True)]
    unnamed x269 -> x287, local copies, waits for them, and re-layouts: 39.1 us -> 43 us
    dot_general x57 -> x58, matrix products: 114 us -> 113 us  [mm(): return jnp.einsum(spec, a, b, preferred_element_type=F32)]
  transfers between devices with their start and end apart: 33 -> 20, of which waited for: 21 -> 8; matrix products, arithmetic and copies ran while one was open for 25% -> 29% of each run, Pallas kernels for 0% -> 12%
where the time goes in v3:
time: 802 us; the launch traced here: 791 us
  Pallas kernels  272 us (34%)
  matrix products  124 us (15%)
  local copies, waits for them, and re-layouts  110 us (14%)
  waiting for transfers between devices  97.7 us (12%)
  starting transfers between devices  68.7 us (9%)
  blocking collectives  65.5 us (8%)
  other arithmetic  35.6 us (4%)
  between operations  17.7 us (2%)
    dot_general x58, matrix products, mm(): return jnp.einsum(spec, a, b, preferred_element_type=F32)  113 us
    pallas_call x1, Pallas kernels, gather_all(): pl.pallas_call(functools.partial(gather_kernel, parts, cols, counts), out...  100 us
    pallas_call x2, Pallas kernels, trade_rows(): pl.pallas_call(functools.partial(trade_kernel, replicas), out_shape=[jax....  69.1 us
    pallas_call x1, Pallas kernels, spread_cot(): pl.pallas_call(functools.partial(cot_kernel, cols, replicas), out_shape=[...  60.5 us
    ppermute x10, starting transfers between devices, swap(): lax.ppermute(value, 'row', [(i, i ^ offset) for i in range(rows_axis)])  54.1 us
    unnamed x287, local copies, waits for them, and re-layouts  43 us
    pallas_call x1, Pallas kernels, feed_forward(): pl.pallas_call(functools.partial(ffn_kernel, parts, depth, width, units),...  42.2 us
    ppermute x10, waiting for transfers between devices, swap(): lax.ppermute(value, 'row', [(i, i ^ offset) for i in range(rows_axis)])  32.2 us
  transfers between devices with their start and end apart: 20, of which 8 were waited for; matrix products, arithmetic and copies ran while one was open for 29% of the time, Pallas kernels for 12%

profile of v3, /device:TPU:9, one launch (start us, length us, event | category | flops | bytes accessed | tf_op | source)
XLA Modules:
  0.0 791.1 jit_solution(17792323646353155520)
XLA Ops:
  7.3 100.2 %shard_map.328 = (bf16[2,2048,512]{2,1,0:T(8,128)(2,1)}, bf16[8,2048,512]{2,1,0:T(8,128)(2,1)}, bf16[256,2048]{1,0:T(8,128)(2,1)}, bf16[256,2048]{1,0:T(8,128)(2,1)}) custom-call(bf16[2,256,512]{2,1,0:T(8,128)(2,1)} %refs_0_.1, bf16[8,256,512]{2,1,0:T(8,128)(2,1)} %refs_1_.1, bf16[256,512]{1,0:T(8,128)(2,1)} %refs_2_.1, bf16[256,512]{1,0:T(8,128)(2,1)} %refs_3_.1), custom_call_target="tpu_custom_call" | custom-call | tf_op jit(solution)/shard_map/pallas_call | solution.py:184
  109.5 6.7 all-reduce.3
  117.6 5.6 all-to-all-start
  123.2 3.3 dynamic-slice_bitcast_fusion
  127.4 5.0 constant_dynamic-slice_fusion
  136.5 2.6 copy.544
  149.3 2.3 fusion.41
  155.1 8.9 %fusion.223 = f32[8,80,512]{2,1,0:T(8,128)S(1)} fusion(bf16[8,80,2048]{2,1,0:T(8,128)(2,1)S(1)} %bitcast.333, bf16[8,2048,512]{2,1,0:T(8,128)(2,1)} %get-tuple-element.49), kind=kOutput, calls=%fused_computation.389 | convolution fusion | flops 1342177280 | bytes 20709376 | tf_op jit(solution)/shard_map/ecd,edw->ecw/dot_general | solution.py:27
  173.2 1.8 fusion.104
  181.9 2.6 fusion.219
  184.5 2.3 fusion.26
  186.8 2.1 copy.406
  188.9 1.7 convolution_convert_fusion.12
  191.7 9.2 %all-gather.4.cloned.1.call-done = bf16[8,2048,512]{2,1,0:T(8,128)(2,1)} async-done(((bf16[8,256,512]{2,1,0:T(8,128)(2,1)}), bf16[8,2048,512]{2,1,0:T(8,128)(2,1)}) %all-gather.4.cloned.1.call-update) | async-done | bytes 16777232 | tf_op jit(solution)/shard_map/all_gather | solution.py:512
  200.9 13.3 %fusion.226 = f32[8,80,2048]{2,1,0:T(8,128)} fusion(bf16[8,80,512]{2,1,0:T(8,128)(2,1)S(1)} %bitcast.336, bf16[8,2048,512]{2,1,0:T(8,128)(2,1)} %all-gather.4.cloned.1.call-done), kind=kOutput, calls=%fused_computation.392 | convolution fusion | flops 1342177280 | bytes 22675456 | tf_op jit(solution)/shard_map/ecw,edw->ecd/dot_general | solution.py:27
  214.2 3.9 fusion.4
  221.1 3.8 pad_maximum_fusion.1
  230.3 15.6 %reduce-scatter.5.cloned.1.call-done = bf16[256,512]{0,1:T(8,128)(2,1)} async-done(((bf16[256,2048]{0,1:T(8,128)(2,1)}), bf16[256,512]{0,1:T(8,128)(2,1)}) %reduce-scatter.5.cloned.1.call-update) | async-done | bytes 262160 | tf_op jit(solution)/shard_map/reduce_scatter | solution.py:492
  247.0 9.1 %psum.77 = f32[256]{0:T(256)S(1)} all-reduce(f32[256]{0:T(256)S(1)} %multiply_reduce_fusion.3), channel_id=1, replica_groups=mesh['row'=8,'col'=4] {'col'}, use_global_device_ids=true, to_apply=%region_12.13 | all-reduce | flops 256 | bytes 2048 | tf_op jit(solution)/shard_map/psum | solution.py:659
  256.6 1.8 multiply_convert_fusion.4
  262.6 11.1 %collective-permute-done.1.refs_14_ = bf16[256,4224]{1,0:T(8,128)(2,1)} collective-permute-done((bf16[256,4224]{1,0:T(8,128)(2,1)}, bf16[256,4224]{1,0:T(8,128)(2,1)}, u32[]{:S(2)}, u32[]{:S(2)}) %collective-permute-start.1) | collective-permute-done | bytes 2162720 | tf_op jit(solution)/shard_map/ppermute | solution.py:486
  275.4 46.9 %collective-permute-start.4 = (bf16[256,4224]{1,0:T(8,128)(2,1)}, bf16[256,4224]{1,0:T(8,128)(2,1)}, u32[]{:S(2)}, u32[]{:S(2)}) collective-permute-start(bf16[256,4224]{1,0:T(8,128)(2,1)} %collective-permute-done.3.refs_16_), channel_id=1, source_target_pairs={{0,4},{4,0},{8,12},{12,8},{16,20},{20,16},{24,28},{28,24},{1,5},{5... | collective-permute-start | bytes 6488072 | tf_op jit(solution)/shard_map/ppermute | solution.py:486
  331.2 33.8 %shard_map.329 = (bf16[160,2304]{1,0:T(8,128)(2,1)}, bf16[160,2304]{1,0:T(8,128)(2,1)}, bf16[160,2304]{1,0:T(8,128)(2,1)}) custom-call(bf16[160,2304]{1,0:T(8,128)(2,1)} %get-tuple-element.177.refs_0_, bf16[160,2304]{1,0:T(8,128)(2,1)} %get-tuple-element.176.refs_1_, bf16[160,2304]{1,0:T(8,128)(2,1)} %get-tuple-element.175.refs_2_), custom_call_target="tpu_custom_call" | custom-call | tf_op jit(solution)/shard_map/pallas_call | solution.py:302
  367.2 60.5 %shard_map.330 = (bf16[160,2048]{1,0:T(8,128)(2,1)}, bf16[160,2048]{1,0:T(8,128)(2,1)}, bf16[160,2048]{1,0:T(8,128)(2,1)}, bf16[160,2048]{1,0:T(8,128)(2,1)}, bf...) custom-call(bf16[160,512]{1,0:T(8,128)(2,1)} %get-tuple-element.211.refs, ...), custom_call_target="tpu_custom_call" | custom-call | tf_op jit(solution)/shard_map/pallas_call | solution.py:261
  427.8 42.2 %shard_map.331 = (bf16[160,2304]{1,0:T(8,128)(2,1)}, bf16[160,2304]{1,0:T(8,128)(2,1)}, bf16[160,2304]{1,0:T(8,128)(2,1)}, bf16[160,2304]{1,0:T(8,128)(2,1)}, bf...) custom-call(bf16[160,2304]{1,0:T(8,128)(2,1)} %get-tuple-element.178, ...), custom_call_target="tpu_custom_call" | custom-call | tf_op jit(solution)/shard_map/pallas_call | solution.py:423
  470.0 2.1 constant_dynamic-update-slice_fusion.3
  472.1 35.3 %shard_map.332 = (bf16[160,2304]{1,0:T(8,128)(2,1)}, bf16[160,2304]{1,0:T(8,128)(2,1)}, bf16[160,2304]{1,0:T(8,128)(2,1)}) custom-call(bf16[160,2304]{1,0:T(8,128)(2,1)} %get-tuple-element.71.refs_0_, bf16[160,2304]{1,0:T(8,128)(2,1)} %get-tuple-element.72.refs_1_, bf16[160,2304]{1,0:T(8,128)(2,1)} %get-tuple-element.73.refs_2_), custom_call_target="tpu_custom_call" | custom-call | tf_op jit(solution)/shard_map/pallas_call | solution.py:302
  507.4 2.1 constant_dynamic-update-slice_fusion.2
  509.5 2.1 constant_dynamic-update-slice_fusion.1
  515.2 3.0 fusion.6
  519.8 2.9 copy.495
  522.8 6.5 collective-permute-done.7
  529.3 14.6 %collective-permute-done.9 = bf16[160,2176]{1,0:T(8,128)(2,1)} collective-permute-done((bf16[160,2176]{1,0:T(8,128)(2,1)}, bf16[160,2176]{1,0:T(8,128)(2,1)}, u32[]{:S(2)}, u32[]{:S(2)}) %collective-permute-start.9) | collective-permute-done | bytes 696352 | tf_op jit(solution)/shard_map/ppermute | solution.py:486
  543.9 2.9 fusion.8
  551.8 3.1 fusion.18
  558.1 8.2 %psum.78 = f32[256,2]{0,1:T(2,128)} all-reduce(f32[256,2]{0,1:T(2,128)} %pad_maximum_fusion.13), channel_id=1, replica_groups=mesh['row'=8,'col'=4] {'col'}, use_global_device_ids=true, to_apply=%region_22.23 | all-reduce | flops 512 | bytes 4096 | tf_op jit(solution)/shard_map/psum | solution.py:696
  569.0 12.2 %reduce-scatter.9.cloned.1.call-done = bf16[256,512]{0,1:T(8,128)(2,1)} async-done(((bf16[256,2048]{0,1:T(8,128)(2,1)}), bf16[256,512]{0,1:T(8,128)(2,1)}) %reduce-scatter.9.cloned.1.call-update) | async-done | bytes 262160 | tf_op jit(solution)/shard_map/reduce_scatter | solution.py:492
  581.2 2.8 multiply_reduce_fusion.2
  584.0 9.4 %psum.79 = f32[256]{0:T(256)} all-reduce(f32[256]{0:T(256)} %get-tuple-element.248), channel_id=1, replica_groups=mesh['row'=8,'col'=4] {'col'}, use_global_device_ids=true, to_apply=%region_26.27 | all-reduce | flops 256 | bytes 2048 | tf_op jit(solution)/shard_map/psum | solution.py:702
  593.3 2.0 fusion.152
  598.7 25.6 %all-gather.8.cloned.1.call-done = bf16[256,2048]{0,1:T(8,128)(2,1)} async-done(((bf16[256,512]{0,1:T(8,128)(2,1)}), bf16[256,2048]{0,1:T(8,128)(2,1)}) %all-gather.8.cloned.1.call-update) | async-done | bytes 1048592 | tf_op jit(solution)/shard_map/all_gather | solution.py:489
  624.3 2.1 fusion.220
  626.4 2.3 convolution_convert_fusion.1
  630.2 1.7 slice.373
  631.9 4.6 copy.426
  636.6 9.8 %fusion.228 = f32[8,80,512]{2,1,0:T(8,128)S(1)} fusion(bf16[8,80,2048]{2,1,0:T(8,128)(2,1)} %bitcast.335, bf16[8,2048,512]{2,1,0:T(8,128)(2,1)} %all-gather.4.cloned.1.call-done), kind=kOutput, calls=%fused_computation.394 | convolution fusion | flops 1342177280 | bytes 20709376 | tf_op jit(solution)/shard_map/ecd,edw->ecw/dot_general | solution.py:27
  646.4 1.8 multiply_reduce_fusion.1
  652.0 3.1 fusion.31
  659.2 1.8 copy.442
  665.5 2.1 copy.434
  667.6 2.6 convolution_convert_fusion.11
  670.2 13.0 %convolution_convert_fusion.4 = bf16[8,80,2048]{2,1,0:T(8,128)(2,1)} fusion(bf16[8,80,512]{2,1,0:T(8,128)(2,1)} %bitcast.359, bf16[8,2048,512]{2,1,0:T(8,128)(2,1)} %get-tuple-element.49), kind=kOutput, calls=%fused_computation.9 | convolution fusion | flops 1343488000 | bytes 20054016 | tf_op jit(solution)/shard_map/ecw,edw->ecd/dot_general | solution.py:27
  683.2 3.8 convolution_bitcast_fusion
  695.1 4.0 reshape.625
  699.0 2.6 slice.390
  701.6 3.6 slice.388
  707.6 2.9 copy.494
  718.1 10.6 %all_gather.20 = bf16[8,16,2048]{2,1,0:T(8,128)(2,1)S(1)} all-gather(bf16[1,16,2048]{2,1,0:T(8,128)(2,1)S(1)} %pad_maximum_fusion.12), channel_id=1, replica_groups=mesh['row'=8,'col'=4] {'row'}, dimensions={0}, use_global_device_ids=true | all-gather | bytes 589824 | tf_op jit(solution)/shard_map/all_gather | solution.py:808
  731.0 8.2 %psum.80 = f32[256,2]{0,1:T(2,128)S(1)} all-reduce(f32[256,2]{0,1:T(2,128)S(1)} %pad_maximum_fusion.14), channel_id=1, replica_groups=mesh['row'=8,'col'=4] {'col'}, use_global_device_ids=true, to_apply=%region_31.32 | all-reduce | flops 512 | bytes 4096 | tf_op jit(solution)/shard_map/psum | solution.py:774
  739.2 1.8 copy.460
  742.2 1.8 copy.456
  745.5 13.3 %all-reduce.4 = (f32[256]{0:T(256)}, bf16[256,16]{0,1:T(8,128)(2,1)}, bf16[256,16]{0,1:T(8,128)(2,1)}, bf16[256,16]{0,1:T(8,128)(2,1)S(1)}, bf16[256,16]{0,1:T(8,128)(2,1)S(1)}, /*index=5*/bf16[256,16]{0,1:T(8,128)(2,1)S(1)}) all-reduce(f32[256]{0:T(256)S(1)} %get-tuple-element.260, ...), channel_id=1, replica_groups=mesh['row'=8,'col'=4] {'col'}, use_global_device_ids=true, to_apply=%region_35.36 | all-reduce | flops 20736 | bytes 124928 | tf_op jit(solution)/shard_map/psum | solution.py:782
  765.2 8.7 %all-to-all-start.1 = ((bf16[1,80,8,256]{3,1,0,2:T(8,128)(2,1)}), bf16[1,80,8,256]{3,1,0,2:T(8,128)(2,1)S(1)}, u32[]{:S(2)}, u32[]{:S(2)}) async-start(bf16[1,80,8,256]{3,1,0,2:T(8,128)(2,1)} %copy_dynamic-update-slice_fusion), calls=%async_computation.5 | async-start | bytes 655360 | tf_op jit(solution)/shard_map/all_to_all | solution.py:800
  777.2 2.8 all-to-all-done.1
  (485 shorter events, 133.5 us)
Async XLA Ops:
  7.2 156.8 %copy-start = (bf16[8,16,2,512]{3,2,1,0:T(2,128)(2,1)S(1)}, bf16[8,16,2,512]{3,2,1,0:T(2,128)(2,1)}, u32[]{:S(2)}) copy-start(bf16[8,16,2,512]{3,2,1,0:T(2,128)(2,1)} %param.43) | copy-start | bytes 786436
  7.2 101.0 %copy-start.122 = (u32[32]{0:T(128)S(1)}, u32[32]{0:T(128)}, u32[]{:S(2)}) copy-start(u32[32]{0:T(128)} %constant.109) | copy-start | bytes 388
  7.2 109.0 %copy-start.62 = (bf16[8,256,16]{1,2,0:T(8,128)(2,1)S(1)}, bf16[8,256,16]{1,2,0:T(8,128)(2,1)}, u32[]{:S(2)}) copy-start(bf16[8,256,16]{1,2,0:T(8,128)(2,1)} %param.40) | copy-start | bytes 196612
  7.2 109.0 %copy-start.63 = (bf16[8,256,16]{1,2,0:T(8,128)(2,1)S(1)}, bf16[8,256,16]{1,2,0:T(8,128)(2,1)}, u32[]{:S(2)}) copy-start(bf16[8,256,16]{1,2,0:T(8,128)(2,1)} %param.42) | copy-start | bytes 196612
  7.2 109.1 %copy-start.64 = (bf16[8,256,16]{1,2,0:T(8,128)(2,1)S(1)}, bf16[8,256,16]{1,2,0:T(8,128)(2,1)}, u32[]{:S(2)}) copy-start(bf16[8,256,16]{1,2,0:T(8,128)(2,1)} %param.44) | copy-start | bytes 196612
  7.2 109.1 %copy-start.65 = (bf16[8,256,16]{1,2,0:T(8,128)(2,1)S(1)}, bf16[8,256,16]{1,2,0:T(8,128)(2,1)}, u32[]{:S(2)}) copy-start(bf16[8,256,16]{1,2,0:T(8,128)(2,1)} %param.46) | copy-start | bytes 196612
  7.2 109.1 %copy-start.66 = (bf16[8,256,16]{1,2,0:T(8,128)(2,1)S(1)}, bf16[8,256,16]{1,2,0:T(8,128)(2,1)}, u32[]{:S(2)}) copy-start(bf16[8,256,16]{1,2,0:T(8,128)(2,1)} %param.48) | copy-start | bytes 196612
  7.3 193.6 %all-gather.4.cloned.1.call-start = ((), (), s32[]{:S(2)}) async-start(), calls=%async_computation.6 | async-start | bytes 18874368 | tf_op jit(solution)/shard_map/all_gather | solution.py:512
  117.6 50.4 %all-to-all-start = ((bf16[8,80,256]{2,1,0:T(8,128)(2,1)}), bf16[8,80,256]{2,1,0:T(8,128)(2,1)S(1)}, u32[]{:S(2)}, u32[]{:S(2)}) async-start(bf16[8,80,256]{2,1,0:T(8,128)(2,1)} %copy.396), calls=%async_computation | async-start | bytes 655360 | tf_op jit(solution)/shard_map/all_to_all | solution.py:541
  123.1 122.8 %reduce-scatter.5.cloned.1.call-start = ((), (), s32[]{:S(2)}) async-start(), calls=%async_computation.7 | async-start | bytes 1310720 | tf_op jit(solution)/shard_map/reduce_scatter | solution.py:492
  135.6 292.2 %collective-permute-start = (bf16[256,4224]{1,0:T(8,128)(2,1)}, bf16[256,4224]{1,0:T(8,128)(2,1)}, u32[]{:S(2)}, u32[]{:S(2)}) collective-permute-start(bf16[256,4224]{1,0:T(8,128)(2,1)} %pad_maximum_fusion.refs_12_), channel_id=1, source_target_pairs={{0,4},{4,0},{8,12},{12,8},{16,20},{20,16},{24,28},{28,24},{1,5},{5... | collective-permute-start | bytes 6488072 | tf_op jit(solution)/shard_map/ppermute | solution.py:486
  144.2 22.7 %copy-start.81 = (s32[256,1]{0,1:T(1,128)}, s32[256,1]{0,1:T(1,128)S(1)}, u32[]{:S(2)}) copy-start(s32[256,1]{0,1:T(1,128)S(1)} %get-tuple-element.232) | copy-start | bytes 3076
  144.2 22.6 %copy-start.85 = (s32[256,1]{0,1:T(1,128)}, s32[256,1]{0,1:T(1,128)S(1)}, u32[]{:S(2)}) copy-start(s32[256,1]{0,1:T(1,128)S(1)} %get-tuple-element.231) | copy-start | bytes 3076
  147.1 33.9 %copy-start.19 = (f32[256,64]{1,0:T(8,128)}, f32[256,64]{1,0:T(8,128)S(1)}, u32[]{:S(2)}) copy-start(f32[256,64]{1,0:T(8,128)S(1)} %get-tuple-element.235) | copy-start | bytes 196612
  200.9 13.3 %copy-start.82 = (s32[256,1]{0,1:T(1,128)S(1)}, s32[256,1]{0,1:T(1,128)}, u32[]{:S(2)}) copy-start(s32[256,1]{0,1:T(1,128)} %copy-done.81) | copy-start | bytes 3076
  200.9 13.3 %copy-start.86 = (s32[256,1]{0,1:T(1,128)S(1)}, s32[256,1]{0,1:T(1,128)}, u32[]{:S(2)}) copy-start(s32[256,1]{0,1:T(1,128)} %copy-done.85) | copy-start | bytes 3076
  200.9 13.3 %copy-start.112 = (f32[640]{0:T(1024)S(1)}, f32[640]{0:T(1024)}, u32[]{:S(2)}) copy-start(f32[640]{0:T(1024)} %add.205) | copy-start | bytes 7684
  221.0 101.2 %all-gather.6.cloned.1.call-start = ((), (), s32[]{:S(2)}) async-start(), calls=%async_computation.8 | async-start | bytes 1310720 | tf_op jit(solution)/shard_map/all_gather | solution.py:489
  224.9 48.7 %collective-permute-start.1 = (bf16[256,4224]{1,0:T(8,128)(2,1)}, bf16[256,4224]{1,0:T(8,128)(2,1)}, u32[]{:S(2)}, u32[]{:S(2)}) collective-permute-start(bf16[256,4224]{1,0:T(8,128)(2,1)} %get-tuple-element.63), channel_id=1, source_target_pairs={{0,8},{4,12},{8,0},{12,4},{16,24},{20,28},{24,16},{28,20},{1,9},{5... | collective-permute-start | bytes 6488072 | tf_op jit(solution)/shard_map/ppermute | solution.py:486
  226.1 49.2 %collective-permute-start.3 = (bf16[256,4224]{1,0:T(8,128)(2,1)}, bf16[256,4224]{1,0:T(8,128)(2,1)}, u32[]{:S(2)}, u32[]{:S(2)}) collective-permute-start(bf16[256,4224]{1,0:T(8,128)(2,1)} %get-tuple-element.64), channel_id=1, source_target_pairs={{0,16},{4,20},{8,24},{12,28},{16,0},{20,4},{24,8},{28,12},{1,17},{... | collective-permute-start | bytes 6488072 | tf_op jit(solution)/shard_map/ppermute | solution.py:486
  226.6 31.9 %copy-start.29 = (bf16[256,512]{1,0:T(8,128)(2,1)S(1)}, bf16[256,512]{1,0:T(8,128)(2,1)}, u32[]{:S(2)}) copy-start(bf16[256,512]{1,0:T(8,128)(2,1)} %refs_3_.1) | copy-start | bytes 786436
  228.1 31.4 %copy-start.32 = (bf16[8,16,2,1408]{3,2,1,0:T(2,128)(2,1)S(1)}, bf16[8,16,2,1408]{3,2,1,0:T(2,128)(2,1)}, u32[]{:S(2)}) copy-start(bf16[8,16,2,1408]{3,2,1,0:T(2,128)(2,1)} %param.47) | copy-start | bytes 2162692
  228.1 94.2 %collective-permute-start.5 = (bf16[256,4224]{1,0:T(8,128)(2,1)}, bf16[256,4224]{1,0:T(8,128)(2,1)}, u32[]{:S(2)}, u32[]{:S(2)}) collective-permute-start(bf16[256,4224]{1,0:T(8,128)(2,1)} %pad_maximum_fusion.3), channel_id=1, source_target_pairs={{0,24},{4,28},{8,16},{12,20},{16,8},{20,12},{24,0},{28,4},{1,25},{... | collective-permute-start | bytes 6488072 | tf_op jit(solution)/shard_map/ppermute | solution.py:486
  230.2 29.6 %copy-start.91 = (f32[512]{0:T(512)}, f32[512]{0:T(512)S(1)}, u32[]{:S(2)}) copy-start(f32[512]{0:T(512)S(1)} %dynamic_slice.51) | copy-start | bytes 6148
  230.2 30.8 %copy-start.114 = (bf16[256]{0:T(256)(128)(2,1)}, bf16[256]{0:T(256)(128)(2,1)S(1)}, u32[]{:S(2)}) copy-start(bf16[256]{0:T(256)(128)(2,1)S(1)} %convert_convert_fusion) | copy-start | bytes 1540
  230.3 29.5 %copy-start.104 = (bf16[256,2,4]{0,2,1:T(4,128)(2,1)}, bf16[256,2,4]{0,2,1:T(4,128)(2,1)S(1)}, u32[]{:S(2)}) copy-start(bf16[256,2,4]{0,2,1:T(4,128)(2,1)S(1)} %fusion.163) | copy-start | bytes 12292
  258.4 322.7 %reduce-scatter.9.cloned.1.call-start = ((), (), s32[]{:S(2)}) async-start(), calls=%async_computation.10 | async-start | bytes 1310720 | tf_op jit(solution)/shard_map/reduce_scatter | solution.py:492
  258.7 256.4 %copy-start.75 = (s32[640]{0:T(1024)}, s32[640]{0:T(1024)S(1)}, u32[]{:S(2)}) copy-start(s32[640]{0:T(1024)S(1)} %add.211) | copy-start | bytes 7684
  259.8 62.5 %copy-start.80 = (bf16[2048,4]{0,1:T(4,128)(2,1)S(1)}, bf16[2048,4]{0,1:T(4,128)(2,1)}, u32[]{:S(2)}) copy-start(bf16[2048,4]{0,1:T(4,128)(2,1)} %param.34) | copy-start | bytes 49156
  259.8 64.0 %slice-start.2 = ((bf16[256,2,4]{0,2,1:T(4,128)(2,1)}), bf16[256,1,4]{0,2,1:T(4,128)(2,1)S(1)}, s32[]{:S(2)}) async-start(bf16[256,2,4]{0,2,1:T(4,128)(2,1)} %copy-done.104), calls=%async_computation.16 | async-start | bytes 4096 | tf_op jit(solution)/shard_map/slice | solution.py:57
  260.9 67.3 %copy-start.37 = (bf16[8,2,8,256]{3,2,0,1:T(8,128)(2,1)}, bf16[8,2,8,256]{3,2,0,1:T(8,128)(2,1)S(1)}, u32[]{:S(2)}) copy-start(bf16[8,2,8,256]{3,2,0,1:T(8,128)(2,1)S(1)} %copy.499) | copy-start | bytes 196612
  273.6 154.1 %collective-permute-start.2 = (bf16[256,4224]{1,0:T(8,128)(2,1)}, bf16[256,4224]{1,0:T(8,128)(2,1)}, u32[]{:S(2)}, u32[]{:S(2)}) collective-permute-start(bf16[256,4224]{1,0:T(8,128)(2,1)} %collective-permute-done.1.refs_14_), channel_id=1, source_target_pairs={{0,4},{4,0},{8,12},{12,8},{16,20},{20,16},{24,28},{28,24},{1,5},{5... | collective-permute-start | bytes 6488072 | tf_op jit(solution)/shard_map/ppermute | solution.py:486
  275.4 152.4 %collective-permute-start.4 = (bf16[256,4224]{1,0:T(8,128)(2,1)}, bf16[256,4224]{1,0:T(8,128)(2,1)}, u32[]{:S(2)}, u32[]{:S(2)}) collective-permute-start(bf16[256,4224]{1,0:T(8,128)(2,1)} %collective-permute-done.3.refs_16_), channel_id=1, source_target_pairs={{0,4},{4,0},{8,12},{12,8},{16,20},{20,16},{24,28},{28,24},{1,5},{5... | collective-permute-start | bytes 6488072 | tf_op jit(solution)/shard_map/ppermute | solution.py:486
  322.3 105.5 %collective-permute-start.6 = (bf16[256,4224]{1,0:T(8,128)(2,1)}, bf16[256,4224]{1,0:T(8,128)(2,1)}, u32[]{:S(2)}, u32[]{:S(2)}) collective-permute-start(bf16[256,4224]{1,0:T(8,128)(2,1)} %collective-permute-done.5.refs_18_), channel_id=1, source_target_pairs={{0,4},{4,0},{8,12},{12,8},{16,20},{20,16},{24,28},{28,24},{1,5},{5... | collective-permute-start | bytes 6488072 | tf_op jit(solution)/shard_map/ppermute | solution.py:486
  323.9 191.3 %copy-start.102 = (s32[256,1]{0,1:T(1,128)}, s32[256,1]{0,1:T(1,128)S(1)}, u32[]{:S(2)}) copy-start(s32[256,1]{0,1:T(1,128)S(1)} %get-tuple-element.230) | copy-start | bytes 3076
  323.9 191.3 %copy-start.103 = (s32[256,1]{0,1:T(1,128)}, s32[256,1]{0,1:T(1,128)S(1)}, u32[]{:S(2)}) copy-start(s32[256,1]{0,1:T(1,128)S(1)} %get-tuple-element.229) | copy-start | bytes 3076
  331.2 33.8 %copy-start.68 = (bf16[256,128]{0,1:T(8,128)(2,1)S(1)}, bf16[256,128]{0,1:T(8,128)(2,1)}, u32[]{:S(2)}) copy-start(bf16[256,128]{0,1:T(8,128)(2,1)} %get-tuple-element.244) | copy-start | bytes 196612
  331.2 34.8 %copy-start.115 = (bf16[256]{0:T(256)(128)(2,1)S(1)}, bf16[256]{0:T(256)(128)(2,1)}, u32[]{:S(2)}) copy-start(bf16[256]{0:T(256)(128)(2,1)} %copy-done.114) | copy-start | bytes 1540
  512.5 16.8 %collective-permute-start.7 = (bf16[160,2176]{1,0:T(8,128)(2,1)}, bf16[160,2176]{1,0:T(8,128)(2,1)}, u32[]{:S(2)}, u32[]{:S(2)}) collective-permute-start(bf16[160,2176]{1,0:T(8,128)(2,1)} %get-tuple-element.78), channel_id=1, source_target_pairs={{0,8},{4,12},{8,0},{12,4},{16,24},{20,28},{24,16},{28,20},{1,9},{5... | collective-permute-start | bytes 2088968 | tf_op jit(solution)/shard_map/ppermute | solution.py:486
  512.5 16.8 %collective-permute-start.8 = (bf16[160,2176]{1,0:T(8,128)(2,1)}, bf16[160,2176]{1,0:T(8,128)(2,1)}, u32[]{:S(2)}, u32[]{:S(2)}) collective-permute-start(bf16[160,2176]{1,0:T(8,128)(2,1)} %get-tuple-element.79), channel_id=1, source_target_pairs={{0,16},{4,20},{8,24},{12,28},{16,0},{20,4},{24,8},{28,12},{1,17},{... | collective-permute-start | bytes 2088968 | tf_op jit(solution)/shard_map/ppermute | solution.py:486
  514.1 29.8 %collective-permute-start.9 = (bf16[160,2176]{1,0:T(8,128)(2,1)}, bf16[160,2176]{1,0:T(8,128)(2,1)}, u32[]{:S(2)}, u32[]{:S(2)}) collective-permute-start(bf16[160,2176]{1,0:T(8,128)(2,1)} %get-tuple-element.80), channel_id=1, source_target_pairs={{0,24},{4,28},{8,16},{12,20},{16,8},{20,12},{24,0},{28,4},{1,25},{... | collective-permute-start | bytes 2088968 | tf_op jit(solution)/shard_map/ppermute | solution.py:486
  551.8 29.3 %copy-start.5 = (bf16[256,512]{0,1:T(8,128)(2,1)S(1)}, bf16[256,512]{0,1:T(8,128)(2,1)}, u32[]{:S(2)}) copy-start(bf16[256,512]{0,1:T(8,128)(2,1)} %reduce-scatter.5.cloned.1.call-done) | copy-start | bytes 786436
  555.0 69.3 %all-gather.8.cloned.1.call-start = ((), (), s32[]{:S(2)}) async-start(), calls=%async_computation.11 | async-start | bytes 1310720 | tf_op jit(solution)/shard_map/all_gather | solution.py:489
  595.3 99.7 %all-reduce.7.cloned.1.call-start = ((), (), s32[]{:S(2)}) async-start(), calls=%async_computation.13 | async-start | bytes 2162688 | tf_op jit(solution)/shard_map/psum | solution.py:681
  598.6 145.4 %reduce-scatter.11.cloned.1.call-start = ((), (), s32[]{:S(2)}) async-start(), calls=%async_computation.12 | async-start | bytes 1310720 | tf_op jit(solution)/shard_map/reduce_scatter | solution.py:492
  670.2 13.0 %copy-start.51 = (bf16[1,256,512]{2,1,0:T(8,128)(2,1)S(1)}, bf16[1,256,512]{2,1,0:T(8,128)(2,1)}, u32[]{:S(2)}) copy-start(bf16[1,256,512]{2,1,0:T(8,128)(2,1)} %copy.442) | copy-start | bytes 786436
  692.4 81.6 %reduce-scatter.7.cloned.1.call-start = ((), (), s32[]{:S(2)}) async-start(), calls=%async_computation.9 | async-start | bytes 1310720 | tf_op jit(solution)/shard_map/reduce_scatter | solution.py:492
  728.7 10.4 %copy-start.60 = (f32[256,2]{0,1:T(2,128)S(1)}, f32[256,2]{0,1:T(2,128)}, u32[]{:S(2)}) copy-start(f32[256,2]{0,1:T(2,128)} %copy-done.59) | copy-start | bytes 6148
  728.7 10.4 %copy-start.77 = (f32[256]{0:T(256)S(1)}, f32[256]{0:T(256)}, u32[]{:S(2)}) copy-start(f32[256]{0:T(256)} %copy-done.76) | copy-start | bytes 3076
  728.7 10.4 %copy-start.90 = (f32[256]{0:T(256)S(1)}, f32[256]{0:T(256)}, u32[]{:S(2)}) copy-start(f32[256]{0:T(256)} %copy-done.89) | copy-start | bytes 3076
  728.8 10.4 %copy-start.73 = (s32[256,2]{0,1:T(2,128)S(1)}, s32[256,2]{0,1:T(2,128)}, u32[]{:S(2)}) copy-start(s32[256,2]{0,1:T(2,128)} %param.29) | copy-start | bytes 6148
  730.0 14.0 %copy-start.109 = (f32[512]{0:T(512)S(1)}, f32[512]{0:T(512)}, u32[]{:S(2)}) copy-start(f32[512]{0:T(512)} %dynamic_slice.62) | copy-start | bytes 6148
  730.1 15.4 %copy-start.54 = (f32[256,16]{0,1:T(8,128)S(1)}, f32[256,16]{0,1:T(8,128)}, u32[]{:S(2)}) copy-start(f32[256,16]{0,1:T(8,128)} %copy-done.53) | copy-start | bytes 49156
  730.1 15.4 %copy-start.56 = (f32[256,16]{0,1:T(8,128)S(1)}, f32[256,16]{0,1:T(8,128)}, u32[]{:S(2)}) copy-start(f32[256,16]{0,1:T(8,128)} %get-tuple-element.159) | copy-start | bytes 49156
  730.1 15.4 %copy-start.69 = (f32[256,16]{0,1:T(8,128)S(1)}, f32[256,16]{0,1:T(8,128)}, u32[]{:S(2)}) copy-start(f32[256,16]{0,1:T(8,128)} %get-tuple-element.259) | copy-start | bytes 49156
  730.1 15.4 %slice-start = ((f32[256,2064]{0,1:T(8,128)}), f32[256,16]{0,1:T(8,128)S(1)}, s32[]{:S(2)}) async-start(f32[256,2064]{0,1:T(8,128)} %copy-done.70), calls=%async_computation.14 | async-start | bytes 32768 | tf_op jit(solution)/shard_map/slice | solution.py:655
  730.1 15.4 %copy-start.96 = (f32[256,16]{0,1:T(8,128)S(1)}, f32[256,16]{0,1:T(8,128)}, u32[]{:S(2)}) copy-start(f32[256,16]{0,1:T(8,128)} %get-tuple-element.257) | copy-start | bytes 49156
  730.1 28.7 %copy-start.116 = (bf16[256]{0:T(256)(128)(2,1)S(1)}, bf16[256]{0:T(256)(128)(2,1)}, u32[]{:S(2)}) copy-start(bf16[256]{0:T(256)(128)(2,1)} %copy-done.114) | copy-start | bytes 1540
  761.3 12.7 %copy-start.11 = (f32[256,512]{0,1:T(8,128)S(1)}, f32[256,512]{0,1:T(8,128)}, u32[]{:S(2)}) copy-start(f32[256,512]{0,1:T(8,128)} %get-tuple-element.249) | copy-start | bytes 1572868
  761.3 12.7 %copy-start.94 = (f32[256]{0:T(256)S(1)}, f32[256]{0:T(256)}, u32[]{:S(2)}) copy-start(f32[256]{0:T(256)} %copy-done.93) | copy-start | bytes 3076
  761.3 12.7 %copy-start.99 = (f32[256]{0:T(256)S(1)}, f32[256]{0:T(256)}, u32[]{:S(2)}) copy-start(f32[256]{0:T(256)} %copy-done.98) | copy-start | bytes 3076
  761.3 12.7 %copy-start.100 = (f32[256]{0:T(256)S(1)}, f32[256]{0:T(256)}, u32[]{:S(2)}) copy-start(f32[256]{0:T(256)} %get-tuple-element.238) | copy-start | bytes 3076
  761.3 12.7 %copy-start.101 = (f32[256]{0:T(256)S(1)}, f32[256]{0:T(256)}, u32[]{:S(2)}) copy-start(f32[256]{0:T(256)} %psum.79) | copy-start | bytes 3076
  765.2 14.7 %all-to-all-start.1 = ((bf16[1,80,8,256]{3,1,0,2:T(8,128)(2,1)}), bf16[1,80,8,256]{3,1,0,2:T(8,128)(2,1)S(1)}, u32[]{:S(2)}, u32[]{:S(2)}) async-start(bf16[1,80,8,256]{3,1,0,2:T(8,128)(2,1)} %copy_dynamic-update-slice_fusion), calls=%async_computation.5 | async-start | bytes 655360 | tf_op jit(solution)/shard_map/all_to_all | solution.py:800
  (82 other events, 225.2 us)
Sparse Core Ops, SparseCore 0:
  107.6 93.2 all-gather.3
  221.2 24.6 reduce-scatter.4
  258.5 28.5 all-gather.5
  555.1 26.0 reduce-scatter.8
  595.4 28.7 all-gather.7
  627.3 55.7 all-reduce.6
  692.5 24.8 reduce-scatter.10
  719.8 26.0 reduce-scatter.6

commit v4 on v3

--- a/solution.py
+++ b/solution.py
@@ -64,12 +64,6 @@
     return jnp.sum(onehot * logits[:, None, :], axis=2)
 
 
-def router_back(gates, grad_gates, route, experts):
-    centred = gates * (grad_gates - jnp.sum(gates * grad_gates, axis=1, keepdims=True))
-    onehot = (route[:, :, None] == jnp.arange(experts, dtype=jnp.int32)).astype(F32)
-    return jnp.sum(centred[:, :, None] * onehot, axis=1)
-
-
 def opposite(axis, offset):
     index = jnp.bitwise_xor(lax.axis_index(axis), offset)
     if axis == "row":
@@ -86,22 +80,72 @@
     pl.semaphore_wait(barrier, len(partners))
 
 
-def gather_kernel(parts, cols, counts, *refs):
-    blocks = refs[: len(counts)]
-    tokens = refs[len(counts) : len(counts) + 2]
-    wholes = refs[len(counts) + 2 : 2 * len(counts) + 2]
-    token_wholes = refs[2 * len(counts) + 2 : 2 * len(counts) + 4]
-    send, recv, local = refs[2 * len(counts) + 4 :]
+def dispatch_matrix(route, flip, experts, capacity):
+    count = route.shape[0]
+    lane = lax.broadcasted_iota(jnp.int32, (count, LANES), 1)
+    chosen = [(route[:, k : k + 1] == lane).astype(F32) for k in range(TOPK)]
+    place = lax.broadcasted_iota(jnp.int32, (count, count), 0)
+    other = lax.broadcasted_iota(jnp.int32, (count, count), 1)
+    before = (other < place).astype(F32).astype(BF16)
+    earlier = jnp.dot(
+        before, (chosen[0] + chosen[1]).astype(BF16), preferred_element_type=F32
+    )
+    rows = lax.broadcasted_iota(jnp.int32, (count, experts * capacity), 1)
+    result = None
+    for k in range(TOPK):
+        position = jnp.sum(earlier * chosen[k], axis=1, keepdims=True).astype(jnp.int32)
+        mine = jnp.bitwise_xor(route[:, k : k + 1], flip) * capacity + position
+        found = (rows == mine).astype(F32)
+        result = found if result is None else result + found
+    return result.astype(BF16)
+
+
+def gather_kernel(parts, cols, replicas, counts, *refs):
+    n_blocks = len(counts)
+    lengths, route, tokens, cot = refs[:4]
+    blocks = refs[4 : 4 + n_blocks]
+    outs = refs[4 + n_blocks :]
+    wholes = outs[:n_blocks]
+    tokens_whole = outs[n_blocks]
+    cot_wholes = outs[n_blocks + 1 : n_blocks + 1 + EXP_FF]
+    own_rows, landed, send, recv, local = outs[n_blocks + 1 + EXP_FF :]
     row = lax.axis_index("row")
     col = lax.axis_index("col")
     depth = blocks[0].shape[1]
-    wide = tokens[0].shape[1]
+    count, wide = tokens.shape
     partners = {offset: opposite("row", offset) for offset in (1, 2, 4)}
-    greet(list(partners.values()) + [opposite("col", i) for i in range(1, cols)])
-    chunks = [(a, i) for a, count in enumerate(counts) for i in range(count)]
-    total = len(chunks)
+    along = [opposite("col", i) for i in range(1, cols)]
+    greet(list(partners.values()) + [opposite("row", 6)] + along)
+    chunks = [(a, i) for a, number in enumerate(counts) for i in range(number)]
     used = [0]
     started = []
+    received = set()
+    kept = []
+    here = pl.ds(pl.multiple_of(col * wide, wide), wide)
+
+    def send_to(source, target, device):
+        n = used[0]
+        used[0] += 1
+        copy = pltpu.make_async_remote_copy(
+            src_ref=source,
+            dst_ref=target,
+            send_sem=send.at[n],
+            recv_sem=recv.at[n],
+            device_id=device,
+            device_id_type=pl.DeviceIdType.MESH,
+        )
+        copy.start()
+        started.append(copy)
+        return copy
+
+    def arrive(copy):
+        copy.wait_recv()
+        received.add(id(copy))
+
+    def keep(source, target):
+        copy = pltpu.make_async_copy(source, target, local.at[len(kept)])
+        copy.start()
+        kept.append(copy)
 
     def place(chunk, offset):
         array, i = chunk
@@ -109,100 +153,95 @@
         return wholes[array].at[i, pl.ds(pl.multiple_of(owner * depth, depth), depth)]
 
     def push(source, chunk, target, offset):
-        n = used[0]
-        used[0] += 1
-        copy = pltpu.make_async_remote_copy(
-            src_ref=source,
-            dst_ref=place(chunk, offset),
-            send_sem=send.at[n],
-            recv_sem=recv.at[n],
-            device_id=partners[target],
-            device_id_type=pl.DeviceIdType.MESH,
-        )
-        copy.start()
-        started.append(copy)
-        return copy
-
-    copies = []
-    for k in range(2):
-        here = pl.ds(pl.multiple_of(col * wide, wide), wide)
-        copy = pltpu.make_async_copy(tokens[k], token_wholes[k].at[:, here], local.at[k])
-        copy.start()
-        copies.append(copy)
-        for i in range(1, cols):
-            n = used[0]
-            used[0] += 1
-            copy = pltpu.make_async_remote_copy(
-                src_ref=tokens[k],
-                dst_ref=token_wholes[k].at[:, here],
-                send_sem=send.at[n],
-                recv_sem=recv.at[n],
-                device_id=opposite("col", i),
-                device_id_type=pl.DeviceIdType.MESH,
-            )
-            copy.start()
-            started.append(copy)
-    for a in range(len(counts)):
-        where = pl.ds(pl.multiple_of(row * depth, depth), depth)
-        copy = pltpu.make_async_copy(blocks[a], wholes[a].at[:, where], local.at[2 + a])
-        copy.start()
-        copies.append(copy)
+        return send_to(source, place(chunk, offset), partners[target])
+
+    for device in along:
+        send_to(tokens, tokens_whole.at[:, here], device)
+    keep(tokens, tokens_whole.at[:, here])
     first = {}
     for number, chunk in enumerate(chunks):
         source = blocks[chunk[0]].at[chunk[1]]
         for target in (2, 4):
             first[number, target] = push(source, chunk, target, 0)
+    for a in range(n_blocks):
+        where = pl.ds(pl.multiple_of(row * depth, depth), depth)
+        keep(blocks[a], wholes[a].at[:, where])
+    for chunk in chunks:
+        push(blocks[chunk[0]].at[chunk[1]], chunk, 1, 0)
+    valid = lax.broadcasted_iota(jnp.int32, (count, 1), 0) < lengths[0]
+    matrix = dispatch_matrix(route[...], row // replicas, EXP_FF, CAP_FF)
+    masked = jnp.where(valid, cot[...].astype(F32), 0.0).astype(BF16)
+    dispatched = lax.dot_general(
+        matrix, masked, (((0,), (0,)), ((), ())), preferred_element_type=F32
+    ).astype(BF16)
+    for j in range(EXP_FF):
+        own_rows[j] = dispatched[j * CAP_FF : (j + 1) * CAP_FF]
+    traded = [
+        send_to(own_rows.at[j], landed.at[j - 1], opposite("row", j * replicas))
+        for j in range(1, EXP_FF)
+    ]
+    for j in range(EXP_FF):
+        if j:
+            arrive(traded[j - 1])
+            source = landed.at[j - 1]
+        else:
+            source = own_rows.at[0]
+        keep(source, cot_wholes[j].at[:, here])
+        for device in along:
+            send_to(source, cot_wholes[j].at[:, here], device)
+    relayed = []
     for number, chunk in enumerate(chunks):
-        push(blocks[chunk[0]].at[chunk[1]], chunk, 1, 0)
-    relayed = {}
-    for number, chunk in enumerate(chunks):
-        first[number, 2].wait_recv()
-        first[number, 4].wait_recv()
+        arrive(first[number, 2])
+        arrive(first[number, 4])
         if number % 2 == 0:
-            relayed[number] = push(place(chunk, 2), chunk, 4, 2)
+            relayed.append(push(place(chunk, 2), chunk, 4, 2))
         else:
-            relayed[number] = push(place(chunk, 4), chunk, 2, 4)
+            relayed.append(push(place(chunk, 4), chunk, 2, 4))
         for offset in (2, 4):
             push(place(chunk, offset), chunk, 1, offset)
     for number, chunk in enumerate(chunks):
-        relayed[number].wait_recv()
+        arrive(relayed[number])
         push(place(chunk, 6), chunk, 1, 6)
-    waited = {id(copy) for copy in first.values()} | {id(copy) for copy in relayed.values()}
     for copy in started:
-        if id(copy) not in waited:
+        if id(copy) not in received:
             copy.wait_recv()
     for copy in started:
         copy.wait_send()
-    for copy in copies:
+    for copy in kept:
         copy.wait()
 
 
-def gather_all(blocks, tokens, parts, cols):
+def gather_all(lengths, route, tokens, cot, blocks, parts, cols, replicas):
     counts = [block.shape[0] for block in blocks]
     hbm = pl.BlockSpec(memory_space=pl.ANY)
-    remote = 7 * sum(counts) + 2 * (cols - 1)
+    vmem = pl.BlockSpec(memory_space=pltpu.VMEM)
+    smem = pl.BlockSpec(memory_space=pltpu.SMEM)
+    count, wide = tokens.shape
+    remote = 7 * sum(counts) + (cols - 1) * (1 + EXP_FF) + EXP_FF - 1
     return pl.pallas_call(
-        functools.partial(gather_kernel, parts, cols, counts),
+        functools.partial(gather_kernel, parts, cols, replicas, counts),
         out_shape=[
             jax.ShapeDtypeStruct((b.shape[0], b.shape[1] * parts, b.shape[2]), b.dtype)
             for b in blocks
         ]
-        + [jax.ShapeDtypeStruct((t.shape[0], t.shape[1] * cols), t.dtype) for t in tokens],
-        in_specs=[hbm] * (len(blocks) + 2),
-        out_specs=[hbm] * (len(blocks) + 2),
+        + [jax.ShapeDtypeStruct((count, wide * cols), tokens.dtype)]
+        + [jax.ShapeDtypeStruct((CAP_FF, wide * cols), BF16)] * EXP_FF,
+        in_specs=[smem, vmem, hbm, vmem] + [hbm] * len(blocks),
+        out_specs=[hbm] * (len(blocks) + 1 + EXP_FF),
         scratch_shapes=[
+            pltpu.VMEM((EXP_FF, CAP_FF, wide), BF16),
+            pltpu.VMEM((EXP_FF - 1, CAP_FF, wide), BF16),
             pltpu.SemaphoreType.DMA((remote,)),
             pltpu.SemaphoreType.DMA((remote,)),
-            pltpu.SemaphoreType.DMA((2 + len(blocks),)),
+            pltpu.SemaphoreType.DMA((1 + EXP_FF + len(blocks),)),
         ],
         compiler_params=pltpu.CompilerParams(collective_id=1, has_side_effects=True),
-    )(*blocks, *tokens)
+    )(lengths, route, tokens, cot, *blocks)
 
 
 def cot_kernel(cols, replicas, *refs):
-    blocks, exts = refs[:EXP_FF], refs[EXP_FF : 2 * EXP_FF]
-    wholes, ext_wholes = refs[2 * EXP_FF : 3 * EXP_FF], refs[3 * EXP_FF : 4 * EXP_FF]
-    landed, send, recv, local = refs[4 * EXP_FF :]
+    blocks, wholes = refs[:EXP_FF], refs[EXP_FF : 2 * EXP_FF]
+    landed, send, recv, local = refs[2 * EXP_FF :]
     col = lax.axis_index("col")
     wide = blocks[0].shape[1]
     here = pl.ds(pl.multiple_of(col * wide, wide), wide)
@@ -233,17 +272,14 @@
         push(blocks[j], landed.at[j - 1], j - 1, across[j - 1]) for j in range(1, EXP_FF)
     ]
     base = EXP_FF - 1
-    for j in range(1, EXP_FF):
-        push(exts[j], ext_wholes[j], base + j - 1, across[j - 1])
-    base += EXP_FF - 1
-    kept = [keep(exts[0], ext_wholes[0], 0)]
+    kept = []
     for j in range(EXP_FF):
         if j:
             first[j - 1].wait_recv()
             source = landed.at[j - 1]
         else:
             source = blocks[0]
-        kept.append(keep(source, wholes[j].at[:, here], 1 + j))
+        kept.append(keep(source, wholes[j].at[:, here], j))
         for i in range(cols - 1):
             push(source, wholes[j].at[:, here], base + j * (cols - 1) + i, along[i])
     for copy in copies[EXP_FF - 1 :]:
@@ -254,24 +290,413 @@
         copy.wait()
 
 
-def spread_cot(blocks, exts, cols, replicas):
+def spread_cot(blocks, cols, replicas):
     hbm = pl.BlockSpec(memory_space=pl.ANY)
     wide = blocks[0].shape[1]
-    remote = 2 * (EXP_FF - 1) + EXP_FF * (cols - 1)
+    remote = EXP_FF - 1 + EXP_FF * (cols - 1)
     return pl.pallas_call(
         functools.partial(cot_kernel, cols, replicas),
-        out_shape=[jax.ShapeDtypeStruct((CAP_FF, wide * cols), BF16)] * EXP_FF
-        + [jax.ShapeDtypeStruct((CAP_FF, LANES), BF16)] * EXP_FF,
-        in_specs=[hbm] * (2 * EXP_FF),
-        out_specs=[hbm] * (2 * EXP_FF),
+        out_shape=[jax.ShapeDtypeStruct((CAP_FF, wide * cols), BF16)] * EXP_FF,
+        in_specs=[hbm] * EXP_FF,
+        out_specs=[hbm] * EXP_FF,
         scratch_shapes=[
             pltpu.VMEM((EXP_FF - 1, CAP_FF, wide), BF16),
             pltpu.SemaphoreType.DMA((remote,)),
             pltpu.SemaphoreType.DMA((remote,)),
-            pltpu.SemaphoreType.DMA((1 + EXP_FF,)),
+            pltpu.SemaphoreType.DMA((EXP_FF,)),
         ],
         compiler_params=pltpu.CompilerParams(collective_id=2, has_side_effects=True),
-    )(*blocks, *exts)
+    )(*blocks)
+
+
+def split(value):
+    high = value.astype(BF16).astype(F32)
+    return high, value - high
+
+
+def pack(columns, lanes):
+    lane = lax.broadcasted_iota(jnp.int32, (columns[0].shape[0], LANES), 1)
+    result = jnp.zeros((columns[0].shape[0], LANES), F32)
+    for column, n in zip(columns, lanes):
+        result = jnp.where(lane == n, column, result)
+    return result
+
+
+def route_term(stat, grads, router, start, size):
+    gates = [stat[:, k : k + 1] for k in range(TOPK)]
+    mean = gates[0] * grads[0] + gates[1] * grads[1]
+    product = 0.0
+    term = 0.0
+    weights = [gates[k] * (grads[k] - mean) for k in range(TOPK)]
+    for k in range(TOPK):
+        product += weights[k] * stat[:, 2 + k : 3 + k]
+    for e in range(router.shape[0]):
+        weight = 0.0
+        for k in range(TOPK):
+            weight += jnp.where(stat[:, 5 + k : 6 + k] == float(e), weights[k], 0.0)
+        term += weight * router[e : e + 1, pl.ds(start, size)].astype(F32)
+    return term, product
+
+
+def fetch(sources, targets, sems):
+    copies = []
+    for n, (source, target) in enumerate(zip(sources, targets)):
+        copies.append(pltpu.make_async_copy(source, target, sems.at[n]))
+        copies[-1].start()
+    return copies
+
+
+def remote(source, target, send, recv, n, device):
+    copy = pltpu.make_async_remote_copy(
+        src_ref=source,
+        dst_ref=target,
+        send_sem=send.at[n],
+        recv_sem=recv.at[n],
+        device_id=device,
+        device_id_type=pl.DeviceIdType.MESH,
+    )
+    copy.start()
+    return copy
+
+
+def middle_back_kernel(cols, replicas, *refs):
+    blocks, downs = refs[:EXP_FF], refs[EXP_FF : 2 * EXP_FF]
+    adapter, norm, router, stat = refs[2 * EXP_FF : 2 * EXP_FF + 4]
+    sources = refs[2 * EXP_FF + 4 : 2 * EXP_FF + 10]
+    grad_middle, grad_whole, totals, branch, low_down = refs[2 * EXP_FF + 10 : 2 * EXP_FF + 15]
+    scratch = refs[2 * EXP_FF + 15 :]
+    pick_0, pick_1, lefts, hidden, middle, cot = scratch[:6]
+    rows, down_rows, exact_part, parts, extra, parts_in, extra_in, low, send, recv, local = (
+        scratch[6:]
+    )
+    col = lax.axis_index("col")
+    count, wide = middle.shape
+    width = hidden.shape[1]
+    across = [opposite("row", j * replicas) for j in range(1, EXP_FF)]
+    along = [opposite("col", i) for i in range(1, cols)]
+    greet(across + along)
+    copies = [
+        remote(
+            blocks[j], rows.at[pl.ds(j * CAP_FF, CAP_FF)], send, recv, j - 1, across[j - 1]
+        )
+        for j in range(1, EXP_FF)
+    ]
+    near = fetch(
+        [blocks[0], downs[0], *sources],
+        [rows.at[pl.ds(0, CAP_FF)], down_rows.at[pl.ds(0, CAP_FF)], *scratch[:6]],
+        local,
+    )
+    for copy in near:
+        copy.wait()
+    for copy in copies:
+        copy.wait_recv()
+    base = EXP_FF - 1
+    down_copies = [
+        remote(
+            downs[j],
+            down_rows.at[pl.ds(j * CAP_FF, CAP_FF)],
+            send,
+            recv,
+            base + j - 1,
+            across[j - 1],
+        )
+        for j in range(1, EXP_FF)
+    ]
+    picks = [pick_0[...], pick_1[...]]
+    any_pick = picks[0] + picks[1]
+
+    def back(pick, source, start, size):
+        return lax.dot_general(
+            pick,
+            source[:, start : start + size],
+            (((0,), (0,)), ((), ())),
+            preferred_element_type=F32,
+        )
+
+    sub = lax.broadcasted_iota(jnp.int32, (LANES, LANES), 0)
+    lane = lax.broadcasted_iota(jnp.int32, (LANES, LANES), 1)
+    mine = lax.broadcasted_iota(jnp.int32, (count, LANES), 1) // RANK == adapter[0]
+    place_rank = (lane == RANK + sub % RANK).astype(F32).astype(BF16)
+
+    def own_rank(value):
+        value = jnp.where(mine, value, 0.0).astype(BF16)
+        return jnp.dot(value, place_rank, preferred_element_type=F32)
+
+    gate_grads = []
+    for k in range(TOPK):
+        pair = back(picks[k], rows, width + LANES, LANES)
+        gate_grads.append(pair[:, 0:1] + pair[:, 1:2])
+    rank = own_rank(back(any_pick, rows, width, LANES))
+    rank_low = rank[:, RANK : 2 * RANK].astype(BF16)
+    product = jnp.zeros((count, 1), F32)
+    for q in range(cols):
+        here = slice(q * wide, (q + 1) * wide)
+        part = back(any_pick, rows, q * wide, wide) + jnp.dot(
+            rank_low, lefts[3 * RANK : 4 * RANK, here], preferred_element_type=F32
+        )
+        product += jnp.sum(part * hidden[:, here].astype(F32), axis=1, keepdims=True)
+        exact_part[q] = part
+        parts[q] = part.astype(BF16)
+    columns = [*split(gate_grads[0]), *split(gate_grads[1]), *split(product)]
+    small = pack(columns, range(6)) + rank
+    extra[...] = small.astype(BF16)
+    base += EXP_FF - 1
+    arrivals = []
+    for i in range(1, cols):
+        target = jnp.bitwise_xor(col, i)
+        n = base + 2 * (i - 1)
+        arrivals.append(remote(extra, extra_in.at[i - 1], send, recv, n + 1, along[i - 1]))
+        arrivals.append(
+            remote(parts.at[target], parts_in.at[i - 1], send, recv, n, along[i - 1])
+        )
+    for copy in arrivals:
+        copy.wait_recv()
+    grad = exact_part[col]
+    total = small
+    for i in range(cols - 1):
+        grad += parts_in[i].astype(F32)
+        total += extra_in[i].astype(F32)
+    totals[...] = total
+    gate_grads = [total[:, 0:1] + total[:, 1:2], total[:, 2:3] + total[:, 3:4]]
+    first = pl.multiple_of(col * wide, wide)
+    term, more = route_term(stat, gate_grads, router, first, wide)
+    inner = total[:, 4:5] + total[:, 5:6] + more
+    scaled = (grad + term) * norm[:, pl.ds(first, wide)]
+    factor = stat[:, 4:5]
+    valid = stat[:, 7:8]
+    result = (
+        cot[...].astype(F32) * valid
+        + factor * scaled
+        - middle[...] * (factor * factor * inner * (1.0 / width))
+    )
+    grad_middle[...] = result
+    low[...] = result.astype(BF16)
+    here = pl.ds(first, wide)
+    kept = pltpu.make_async_copy(low, grad_whole.at[:, here], local.at[8])
+    kept.start()
+    base += 2 * (cols - 1)
+    last = [
+        remote(low, grad_whole.at[:, here], send, recv, base + i, along[i])
+        for i in range(cols - 1)
+    ]
+    for copy in down_copies:
+        copy.wait_recv()
+    rank = own_rank(back(any_pick, down_rows, width, LANES))
+    rank_low = rank[:, RANK : 2 * RANK].astype(BF16)
+    low_down[...] = rank
+    for q in range(cols):
+        here = slice(q * wide, (q + 1) * wide)
+        part = back(any_pick, down_rows, q * wide, wide) + jnp.dot(
+            rank_low, lefts[4 * RANK : 5 * RANK, here], preferred_element_type=F32
+        )
+        branch[:, here] = part.astype(BF16)
+    for copy in last:
+        copy.wait_recv()
+    for copy in copies + down_copies + arrivals + last:
+        copy.wait_send()
+    kept.wait()
+
+
+def middle_back(blocks, downs, adapter, norm, router, stat, sources, cols, replicas):
+    hbm = pl.BlockSpec(memory_space=pl.ANY)
+    vmem = pl.BlockSpec(memory_space=pltpu.VMEM)
+    smem = pl.BlockSpec(memory_space=pltpu.SMEM)
+    count, wide = sources[-1].shape
+    total = 2 * (EXP_FF - 1) + 3 * (cols - 1)
+    rows = EXP_FF * CAP_FF
+    return pl.pallas_call(
+        functools.partial(middle_back_kernel, cols, replicas),
+        out_shape=[
+            jax.ShapeDtypeStruct((count, wide), F32),
+            jax.ShapeDtypeStruct((count, wide * cols), BF16),
+            jax.ShapeDtypeStruct((count, LANES), F32),
+            jax.ShapeDtypeStruct((count, wide * cols), BF16),
+            jax.ShapeDtypeStruct((count, LANES), F32),
+        ],
+        in_specs=[hbm] * (2 * EXP_FF) + [smem, vmem, vmem, vmem] + [hbm] * 6,
+        out_specs=[vmem, hbm, vmem, vmem, vmem],
+        scratch_shapes=[pltpu.VMEM(source.shape, source.dtype) for source in sources]
+        + [
+            pltpu.VMEM((rows, blocks[0].shape[1]), BF16),
+            pltpu.VMEM((rows, downs[0].shape[1]), BF16),
+            pltpu.VMEM((cols, count, wide), F32),
+            pltpu.VMEM((cols, count, wide), BF16),
+            pltpu.VMEM((count, LANES), BF16),
+            pltpu.VMEM((cols - 1, count, wide), BF16),
+            pltpu.VMEM((cols - 1, count, LANES), BF16),
+            pltpu.VMEM((count, wide), BF16),
+            pltpu.SemaphoreType.DMA((total,)),
+            pltpu.SemaphoreType.DMA((total,)),
+            pltpu.SemaphoreType.DMA((9,)),
+        ],
+        compiler_params=pltpu.CompilerParams(
+            collective_id=4, has_side_effects=True, vmem_limit_bytes=48 * 2**20
+        ),
+    )(*blocks, *downs, adapter, norm, router, stat, *sources)
+
+
+def input_back_kernel(parts_axis, cols, *refs):
+    adapters, part, small_in, norm, router, stat, lows, rights = refs[:8]
+    sources = refs[8:14]
+    grad_inputs = refs[14]
+    left_outs = refs[15:20]
+    right_outs = refs[20:24]
+    hidden_one, grad_whole, hidden_two, cot_whole, tokens, grad_middle = refs[24:30]
+    parts, extra, parts_in, extra_in, lefts, lefts_in, rights_in, send, recv, local = refs[30:]
+    row = lax.axis_index("row")
+    col = lax.axis_index("col")
+    count, wide = tokens.shape
+    width = hidden_one.shape[1]
+    depth = width // parts_axis
+    right_width = rights.shape[1] // 4
+    along = [opposite("col", i) for i in range(1, cols)]
+    across = [opposite("row", m) for m in range(1, parts_axis)]
+    greet(across + along)
+    near = fetch(sources, refs[24:30], local)
+    near[0].wait()
+    product = jnp.zeros((count, 1), F32)
+    for q in range(cols):
+        value = part[:, q * wide : (q + 1) * wide]
+        product += jnp.sum(
+            value * hidden_one[:, q * wide : (q + 1) * wide].astype(F32), axis=1, keepdims=True
+        )
+        parts[q] = value.astype(BF16)
+    lane = lax.broadcasted_iota(jnp.int32, (count, LANES), 1)
+    columns = [*split(small_in[:, 0:1]), *split(small_in[:, 2:3]), *split(product)]
+    small = jnp.where(lane < RANK, 0.0, small_in[...]) + pack(columns, range(6))
+    extra[...] = small.astype(BF16)
+    arrivals = []
+    for i in range(1, cols):
+        target = jnp.bitwise_xor(col, i)
+        n = 2 * (i - 1)
+        arrivals.append(remote(extra, extra_in.at[i - 1], send, recv, n + 1, along[i - 1]))
+        arrivals.append(
+            remote(parts.at[target], parts_in.at[i - 1], send, recv, n, along[i - 1])
+        )
+    base = 2 * (cols - 1)
+    right_copies = [
+        remote(rights, rights_in.at[m], send, recv, base + m, across[m])
+        for m in range(parts_axis - 1)
+    ]
+    base += parts_axis - 1
+    total = small
+    for i in range(cols - 1):
+        arrivals[2 * i].wait_recv()
+        total += extra_in[i].astype(F32)
+    ranks = total.astype(BF16)
+
+    def outer(left, right):
+        return lax.dot_general(
+            left, right, (((0,), (0,)), ((), ())), preferred_element_type=F32
+        ).astype(BF16)
+
+    for copy in near[1:]:
+        copy.wait()
+    whole = outer(ranks, hidden_one[...])
+    for m in range(parts_axis):
+        lefts[m, : 2 * RANK] = whole[RANK : 3 * RANK, m * depth : (m + 1) * depth]
+    whole = outer(lows[...], grad_whole[...])
+    for m in range(parts_axis):
+        lefts[m, 2 * RANK : 3 * RANK] = whole[:RANK, m * depth : (m + 1) * depth]
+    whole = outer(lows[...], hidden_two[...])
+    for m in range(parts_axis):
+        lefts[m, 3 * RANK : 4 * RANK] = whole[RANK : 2 * RANK, m * depth : (m + 1) * depth]
+    whole = outer(ranks, cot_whole[...])
+    for m in range(parts_axis):
+        lefts[m, 4 * RANK :] = whole[3 * RANK : 4 * RANK, m * depth : (m + 1) * depth]
+    left_copies = [
+        remote(
+            lefts.at[jnp.bitwise_xor(row, m)],
+            lefts_in.at[m - 1],
+            send,
+            recv,
+            base + m - 1,
+            across[m - 1],
+        )
+        for m in range(1, parts_axis)
+    ]
+    first = pl.multiple_of(col * wide, wide)
+    grad = part[:, pl.ds(first, wide)]
+    for i in range(cols - 1):
+        arrivals[2 * i + 1].wait_recv()
+        grad += parts_in[i].astype(F32)
+    gate_grads = [total[:, 0:1] + total[:, 1:2], total[:, 2:3] + total[:, 3:4]]
+    term, more = route_term(stat, gate_grads, router, first, wide)
+    inner = total[:, 4:5] + total[:, 5:6] + more
+    factor = stat[:, 4:5]
+    grad_inputs[...] = (
+        grad_middle[...]
+        + factor * ((grad + term) * norm[:, pl.ds(first, wide)])
+        - tokens[...].astype(F32) * (factor * factor * inner * (1.0 / width))
+    )
+    chosen_by = [
+        [
+            jnp.where(adapters[jnp.bitwise_xor(row, m)] == a, 1.0, 0.0).astype(F32)
+            for a in range(ADAPT)
+        ]
+        for m in range(parts_axis)
+    ]
+    for copy in right_copies:
+        copy.wait_recv()
+    for p in range(4):
+        here = slice(p * right_width, (p + 1) * right_width)
+        values = [rights[:, here].astype(F32)] + [
+            rights_in[m, :, here].astype(F32) for m in range(parts_axis - 1)
+        ]
+        for a in range(ADAPT):
+            result = chosen_by[0][a] * values[0]
+            for m in range(1, parts_axis):
+                result += chosen_by[m][a] * values[m]
+            right_outs[p][a] = result
+    for copy in left_copies:
+        copy.wait_recv()
+    for p in range(5):
+        here = slice(p * RANK, (p + 1) * RANK)
+        values = [lefts[row, here].astype(F32)] + [
+            lefts_in[m, here].astype(F32) for m in range(parts_axis - 1)
+        ]
+        for a in range(ADAPT):
+            result = chosen_by[0][a] * values[0]
+            for m in range(1, parts_axis):
+                result += chosen_by[m][a] * values[m]
+            left_outs[p][a] = result
+    for copy in arrivals + right_copies + left_copies:
+        copy.wait_send()
+
+
+def input_back(adapters, part, small, norm, router, stat, lows, rights, sources, parts_axis, cols):
+    hbm = pl.BlockSpec(memory_space=pl.ANY)
+    vmem = pl.BlockSpec(memory_space=pltpu.VMEM)
+    smem = pl.BlockSpec(memory_space=pltpu.SMEM)
+    count, width = part.shape
+    wide = width // cols
+    depth = width // parts_axis
+    right_width = rights.shape[1] // 4
+    total = 2 * (cols - 1) + 2 * (parts_axis - 1)
+    return pl.pallas_call(
+        functools.partial(input_back_kernel, parts_axis, cols),
+        out_shape=[jax.ShapeDtypeStruct((count, wide), F32)]
+        + [jax.ShapeDtypeStruct((ADAPT, RANK, depth), F32)] * 5
+        + [jax.ShapeDtypeStruct((ADAPT, RANK, right_width), F32)] * 4,
+        in_specs=[smem] + [vmem] * 7 + [hbm] * 6,
+        out_specs=[vmem] * 10,
+        scratch_shapes=[pltpu.VMEM(source.shape, source.dtype) for source in sources]
+        + [
+            pltpu.VMEM((cols, count, wide), BF16),
+            pltpu.VMEM((count, LANES), BF16),
+            pltpu.VMEM((cols - 1, count, wide), BF16),
+            pltpu.VMEM((cols - 1, count, LANES), BF16),
+            pltpu.VMEM((parts_axis, 5 * RANK, depth), BF16),
+            pltpu.VMEM((parts_axis - 1, 5 * RANK, depth), BF16),
+            pltpu.VMEM((parts_axis - 1, RANK, 4 * right_width), BF16),
+            pltpu.SemaphoreType.DMA((total,)),
+            pltpu.SemaphoreType.DMA((total,)),
+            pltpu.SemaphoreType.DMA((6,)),
+        ],
+        compiler_params=pltpu.CompilerParams(
+            collective_id=5, has_side_effects=True, vmem_limit_bytes=48 * 2**20
+        ),
+    )(adapters, part, small, norm, router, stat, lows, rights, *sources)
 
 
 def trade_kernel(replicas, *refs):
@@ -316,24 +741,25 @@
 def ffn_kernel(parts, depth, width, units, *refs):
     hids = refs[:EXP_FF]
     cots = refs[EXP_FF : 2 * EXP_FF]
-    cot_exts = refs[2 * EXP_FF : 3 * EXP_FF]
-    pieces = refs[3 * EXP_FF : 3 * EXP_FF + parts]
-    rights = refs[3 * EXP_FF + parts]
-    outs = refs[3 * EXP_FF + parts + 1 :]
+    pieces = refs[2 * EXP_FF : 2 * EXP_FF + parts]
+    rights = refs[2 * EXP_FF + parts]
+    outs = refs[2 * EXP_FF + parts + 1 :]
     grads = outs[:EXP_FF]
     downs = outs[EXP_FF : 2 * EXP_FF]
-    adapt = outs[2 * EXP_FF]
-    hid, cot, block, act, product, sems = outs[2 * EXP_FF + 1 :]
+    adapt = outs[2 * EXP_FF : 2 * EXP_FF + 3]
+    hid, cot, block, act, product, sems = outs[2 * EXP_FF + 3 :]
     row = lax.axis_index("row")
     wide = width + LANES
     copies = []
     for j in range(EXP_FF):
         where = pl.ds(j * CAP_FF, CAP_FF)
-        copies.append(pltpu.make_async_copy(hids[j], hid.at[where], sems.at[j]))
+        near = hids[j].at[:, pl.ds(0, wide + LANES)]
+        copies.append(pltpu.make_async_copy(near, hid.at[where], sems.at[j]))
         near = cot.at[where, pl.ds(0, width)]
         copies.append(pltpu.make_async_copy(cots[j], near, sems.at[EXP_FF + j]))
         near = cot.at[where, pl.ds(width, LANES)]
-        copies.append(pltpu.make_async_copy(cot_exts[j], near, sems.at[2 * EXP_FF + j]))
+        low = hids[j].at[:, pl.ds(wide + LANES, LANES)]
+        copies.append(pltpu.make_async_copy(low, near, sems.at[2 * EXP_FF + j]))
     copies.append(pltpu.make_async_copy(rights, block.at[pl.ds(width, LANES)], sems.at[3 * EXP_FF]))
     for m in range(parts):
         owner = jnp.bitwise_xor(row, m)
@@ -404,14 +830,16 @@
         grads[j][:, wide:] = packed[j * CAP_FF : (j + 1) * CAP_FF]
     ext = hid[:, width:wide]
     low_ext = (cot[:, width:].astype(F32) * gate_scale).astype(BF16)
-    adapt[:, : 2 * units] = lax.dot_general(
-        ext, act[:, : 2 * units], (((0,), (0,)), ((), ())), preferred_element_type=F32
-    ).astype(BF16)
-    adapt[:, 2 * units :] = lax.dot_general(
-        low_ext, act[:, 2 * units :], (((0,), (0,)), ((), ())), preferred_element_type=F32
-    ).astype(BF16)
-
-def feed_forward(hids, cots, cot_exts, pieces, rights):
+    for n, low_rows in enumerate((ext, ext, low_ext)):
+        adapt[n][...] = lax.dot_general(
+            low_rows,
+            act[:, n * units : (n + 1) * units],
+            (((0,), (0,)), ((), ())),
+            preferred_element_type=F32,
+        ).astype(BF16)
+
+
+def feed_forward(hids, cots, pieces, rights):
     parts = len(pieces)
     depth, triple = pieces[0].shape
     units = triple // 3
@@ -424,9 +852,9 @@
         functools.partial(ffn_kernel, parts, depth, width, units),
         out_shape=[jax.ShapeDtypeStruct((CAP_FF, wide + LANES), BF16)] * EXP_FF
         + [jax.ShapeDtypeStruct((CAP_FF, wide), BF16)] * EXP_FF
-        + [jax.ShapeDtypeStruct((LANES, triple), BF16)],
-        in_specs=[hbm] * (3 * EXP_FF + parts + 1),
-        out_specs=[vmem] * (2 * EXP_FF + 1),
+        + [jax.ShapeDtypeStruct((LANES, units), BF16)] * 3,
+        in_specs=[hbm] * (2 * EXP_FF + parts + 1),
+        out_specs=[vmem] * (2 * EXP_FF + 3),
         scratch_shapes=[
             pltpu.VMEM((rows, wide + LANES), BF16),
             pltpu.VMEM((rows, wide), BF16),
@@ -436,7 +864,7 @@
             pltpu.SemaphoreType.DMA((3 * EXP_FF + 1 + parts,)),
         ],
         compiler_params=pltpu.CompilerParams(vmem_limit_bytes=56 * 2**20),
-    )(*hids, *cots, *cot_exts, *pieces, rights)
+    )(*hids, *cots, *pieces, rights)
 
 
 def on_device(
@@ -499,16 +927,25 @@
     def later(value, *earlier):
         return lax.optimization_barrier((value, *earlier))[0]
 
+    lanes = lax.broadcasted_iota(jnp.int32, (count, LANES), 1)
+
+    def table_of(*columns):
+        result = jnp.zeros((count, LANES), F32)
+        for n, column in enumerate(columns):
+            if column is not None:
+                result = jnp.where(lanes == n, column, result)
+        return result
+
     cols = lax.axis_size("col")
     if rows_axis == 8:
-        kv_full, query_full, x_full, cot_full = gather_all(
-            [kv_weight, query_weight], [inputs, cotangent], rows_axis, cols
+        kv_full, query_full, x_full, *cot_rows = gather_all(
+            lengths, ffn_route, inputs, cotangent, [kv_weight, query_weight], rows_axis, cols, replicas
         )
     else:
         kv_full = lax.all_gather(kv_weight, "row", axis=1, tiled=True)
         query_full = lax.all_gather(query_weight, "row", axis=1, tiled=True)
         x_full = features(inputs)
-        cot_full = features(cotangent)
+        cot_rows = None
     out_full = lax.all_gather(later(out_weight, query_full), "row", axis=1, tiled=True)
 
     padding = -units % LANES
@@ -524,7 +961,7 @@
         piece = jnp.concatenate(
             [padded(inner_own[:, 0]), padded(inner_own[:, 1]), padded(down_own)], axis=1
         )
-        near.append(swap(later(piece, query_full), j * replicas) if j else piece)
+        near.append(swap(later(piece, out_full), j * replicas) if j else piece)
     chunks = []
     for j in range(EXP_FF):
         for i in range(replicas):
@@ -579,25 +1016,19 @@
         blocks = rows.reshape(EXP_FF, CAP_FF, rows.shape[1])
         return [blocks[j] for j in range(EXP_FF)]
 
-    def trade(blocks):
-        return [swap(block, j * replicas) if j else block for j, block in enumerate(blocks)]
-
     masked_cot = cotangent * valid.astype(BF16)[:, None]
-    cot_full = cot_full * valid.astype(BF16)[:, None]
-    grad_low_down = mm("td,rd->tr", cot_full, left_down)
-    cot_rows = spread_cot(
-        blocks_of(mm("ct,td->cd", pick_ffn_any, masked_cot).astype(BF16)),
-        blocks_of(mm("ct,td->cd", pick_ffn_any, spread(grad_low_down).astype(BF16)).astype(BF16)),
-        cols,
-        replicas,
-    )
+    left_down_own = lax.dynamic_slice_in_dim(left_down, col * slice_width, slice_width, 1)
+    grad_low_down_part = mm("td,rd->tr", masked_cot, left_down_own)
+    if cot_rows is None:
+        cot_rows = spread_cot(
+            blocks_of(mm("ct,td->cd", pick_ffn_any, masked_cot).astype(BF16)), cols, replicas
+        )
 
     x_wide = x_full.astype(F32)
     scale_one = lax.rsqrt(jnp.mean(x_wide * x_wide, axis=1, keepdims=True) + EPSILON)
     hidden_one = (x_wide * scale_one * norm_one).astype(BF16)
-    gates_attn = jax.nn.softmax(
-        chosen_of(mm("td,de->te", hidden_one, router_attn), attn_route, EXP_ATT), axis=1
-    )
+    chosen_attn = chosen_of(mm("td,de->te", hidden_one, router_attn), attn_route, EXP_ATT)
+    gates_attn = jax.nn.softmax(chosen_attn, axis=1)
     rank_query = mm("td,rd->tr", hidden_one, left_query)
     rank_kv = mm("td,rd->tr", hidden_one, left_kv)
     kv_raw = mm("td,sdw->stw", hidden_one, kv_full) + mm(
@@ -656,72 +1087,64 @@
     branch_attn = combined[:, :width] + mm("tr,rd->td", low_out_part.astype(BF16), left_out)
     x_local = inputs.astype(F32)
     middle = x_local + partials(branch_attn)
-    square_sum, low_out_full = lax.psum((jnp.sum(middle * middle, axis=1), low_out_part), "col")
+    square_sum, low_out_full, grad_low_down = lax.psum(
+        (jnp.sum(middle * middle, axis=1), low_out_part, grad_low_down_part), "col"
+    )
     scale_two = lax.rsqrt(square_sum[:, None] / width + EPSILON)
     hidden_two = features((middle * scale_two * own_columns(norm_two)).astype(BF16))
 
-    gates_ffn = jax.nn.softmax(
-        chosen_of(mm("td,de->te", hidden_two, router_ffn), ffn_route, EXP_FF), axis=1
-    )
+    chosen_ffn = chosen_of(mm("td,de->te", hidden_two, router_ffn), ffn_route, EXP_FF)
+    gates_ffn = jax.nn.softmax(chosen_ffn, axis=1)
     rank_inner = mm("td,rd->tr", hidden_two, left_inner)
     hidden_ext = jnp.concatenate([hidden_two, spread(rank_inner).astype(BF16)], axis=1)
     hidden_out = mm("ct,td->cd", pick_ffn_any, hidden_ext).astype(BF16)
-    gate_high = gates_ffn.astype(BF16)
-    gate_low = (gates_ffn - gate_high.astype(F32)).astype(BF16)
+    gate_high = lax.reduce_precision(gates_ffn, 8, 7)
+    gate_low = (gates_ffn - gate_high).astype(BF16)
+    gate_high = gate_high.astype(BF16)
     gate_out = sum(
         mm("ct,tx->cx", pick_ffn[k], jnp.stack([gate_high[:, k], gate_low[:, k]], axis=1))
         for k in range(TOPK)
     )
     gate_out = jnp.pad(gate_out, ((0, 0), (0, 126))).astype(BF16)
-    hidden_in = trade_rows(blocks_of(jnp.concatenate([hidden_out, gate_out], axis=1)), replicas, 3)
-    results = feed_forward(hidden_in, cot_rows[:EXP_FF], cot_rows[EXP_FF:], chunks, ffn_right)
-    grad_back = jnp.concatenate(trade_rows(results[:EXP_FF], replicas, 4))
-    down_back = trade(list(later(tuple(results[EXP_FF : 2 * EXP_FF]), grad_back)))
-    down_back = jnp.concatenate(down_back)
-    ffn_rights = lax.optimization_barrier(lax.psum(results[2 * EXP_FF], "row")).astype(F32)
-    ffn_rights = ffn_rights.reshape(ADAPT, RANK, 3, units + padding)[..., :units]
-
-    grad_comb = mm("ct,cd->td", pick_ffn_any, grad_back[:, : width + 128])
-    gg_back = grad_back[:, width + 128 : width + 130]
-    grad_gates_part = jnp.stack(
-        [jnp.sum(mm("ct,cx->tx", pick_ffn[k], gg_back), axis=1) for k in range(TOPK)], axis=1
-    )
-    grad_rank_inner = unspread(grad_comb[:, width:])
-    grad_two_part = grad_comb[:, :width] + mm(
-        "tr,rd->td", grad_rank_inner.astype(BF16), left_inner
-    )
-    down_comb = mm("ct,cd->td", pick_ffn_any, down_back)
-    low_down_part = unspread(down_comb[:, width:])
-    branch_ffn = down_comb[:, :width] + mm("tr,rd->td", low_down_part.astype(BF16), left_down)
-    (grad_gates_ffn,) = lax.psum((grad_gates_part,), "col")
-    logits_ffn_grad = router_back(gates_ffn, grad_gates_ffn, ffn_route, EXP_FF)
-    grad_two = partials(grad_two_part) + exact(
-        "te,de->td", logits_ffn_grad, own_columns(router_ffn).astype(F32)
-    )
-    scaled_two = grad_two * own_columns(norm_two)
-    inner_sum, rank_inner_grad_full, low_down_full = lax.psum(
-        (jnp.sum(scaled_two * middle, axis=1), grad_rank_inner, low_down_part), "col"
-    )
-    grad_middle = (
-        masked_cot.astype(F32)
-        + scale_two * scaled_two
-        - middle * scale_two**3 * inner_sum[:, None] / width
-    )
+    cot_ext = mm("ct,td->cd", pick_ffn_any, spread(grad_low_down).astype(BF16)).astype(BF16)
+    hidden_in = trade_rows(
+        blocks_of(jnp.concatenate([hidden_out, gate_out, cot_ext], axis=1)), replicas, 3
+    )
+    results = feed_forward(hidden_in, cot_rows, chunks, ffn_right)
+    grad_middle, grad_full, totals, branch_ffn, low_down_part = middle_back(
+        results[:EXP_FF],
+        results[EXP_FF : 2 * EXP_FF],
+        adapter_pick,
+        norm_two[None, :],
+        router_ffn.T,
+        table_of(
+            gates_ffn[:, 0:1],
+            gates_ffn[:, 1:2],
+            chosen_ffn[:, 0:1],
+            chosen_ffn[:, 1:2],
+            scale_two,
+            ffn_route[:, 0:1].astype(F32),
+            ffn_route[:, 1:2].astype(F32),
+            valid[:, None],
+        ),
+        [pick_ffn[0], pick_ffn[1], lefts.reshape(5 * RANK, width), hidden_two, middle, cotangent],
+        cols,
+        replicas,
+    )
+    rights_ffn = lax.optimization_barrier(lax.psum(tuple(results[2 * EXP_FF :]), "row"))
+    rights_ffn = [
+        value[:, :units].reshape(ADAPT, RANK, units).astype(F32) for value in rights_ffn
+    ]
+
     output = ((middle + partials(branch_ffn)) * valid[:, None]).astype(BF16)
 
-    grad_full = features(grad_middle.astype(BF16))
     grad_low_out = mm("td,rd->tr", grad_full, left_out)
-    grad_middle_rows = mm(
-        "ct,td->cd",
-        pick_attn_any,
-        jnp.concatenate([grad_full, grad_low_out.astype(BF16)], axis=1),
-    ).astype(BF16)
+    grad_middle_rows = mm("ct,td->cd", pick_attn_any, grad_full).astype(BF16)
+    grad_low_rows = mm("ct,tr->cr", pick_attn_any, grad_low_out.astype(BF16)).astype(BF16)
     grad_att_rows = mm(
-        "ecd,edw->ecw",
-        grad_middle_rows[:, :width].reshape(EXP_ATT, CAP_ATT, width),
-        out_full,
+        "ecd,edw->ecw", grad_middle_rows.reshape(EXP_ATT, CAP_ATT, width), out_full
     ).reshape(EXP_ATT * CAP_ATT, query_width) + mm(
-        "cr,rw->cw", grad_middle_rows[:, width:], right_out.astype(BF16)
+        "cr,rw->cw", grad_low_rows, right_out.astype(BF16)
     )
     gg_attn_rows = jnp.sum(attended_rows.astype(F32) * grad_att_rows, axis=1, keepdims=True)
     grad_gates_attn_part = jnp.concatenate(
@@ -771,57 +1194,54 @@
     )
     grad_right_query = mm("tr,tw->rw", rank_query.astype(BF16), grad_query_sum_low)
     grad_right_kv = mm("tr,stw->rsw", rank_kv.astype(BF16), grad_kv)
-    grad_gates_attn, rank_query_grad_full, rank_kv_grad_full = lax.psum(
-        (grad_gates_attn_part, grad_rank_query, grad_rank_kv), "col"
-    )
-    logits_attn_grad = router_back(gates_attn, grad_gates_attn, attn_route, EXP_ATT)
-    grad_one = partials(grad_one_part) + exact(
-        "te,de->td", logits_attn_grad, own_columns(router_attn).astype(F32)
-    )
-    scaled_one = grad_one * own_columns(norm_one)
-    outer_sum = lax.psum(jnp.sum(scaled_one * x_local, axis=1), "col")
-    grad_inputs = (
-        grad_middle
-        + scale_one * scaled_one
-        - x_local * scale_one**3 * outer_sum[:, None] / width
-    )
-
-    hiddens = (hidden_one, hidden_one, grad_full, hidden_two, cot_full)
-    lows = (
-        rank_query_grad_full,
-        rank_kv_grad_full,
-        low_out_full,
-        rank_inner_grad_full,
-        low_down_full,
-    )
-    left_parts = jnp.concatenate(
-        [mm("tr,td->rd", low.astype(BF16), hidden) for low, hidden in zip(lows, hiddens)]
-    ).astype(BF16)
-    left_parts = lax.all_to_all(
-        left_parts.reshape(5 * RANK, rows_axis, depth), "row", 1, 0, tiled=False
-    )
-    left_grads = mm("ga,gx->ax", pick_onehot, left_parts.reshape(rows_axis, 5 * RANK * depth))
-    left_grads = left_grads.reshape(ADAPT, 5, RANK, depth).swapaxes(2, 3)
+    cot_full = features(masked_cot)
+    small = table_of(grad_gates_attn_part[:, 0:1], None, grad_gates_attn_part[:, 1:2])
+    small += jnp.pad(
+        jnp.concatenate([grad_rank_query, grad_rank_kv, low_down_part[:, RANK : 2 * RANK]], axis=1),
+        ((0, 0), (RANK, LANES - 4 * RANK)),
+    )
+    lows = (jnp.pad(low_out_full, ((0, 0), (0, LANES - RANK))) + jnp.where(
+        (lanes >= RANK) & (lanes < 2 * RANK), totals, 0.0
+    )).astype(BF16)
     right_parts = jnp.concatenate(
         [grad_right_query, grad_right_kv[:, 0], grad_right_kv[:, 1], grad_right_out], axis=1
     ).astype(BF16)
-    right_all = lax.all_gather(right_parts, "row", axis=0)
-    right_grads = mm(
-        "ga,gx->ax", pick_onehot, right_all.reshape(rows_axis, RANK * 4 * query_width)
-    ).reshape(ADAPT, RANK, 4, query_width)
+    grad_inputs, *grads = input_back(
+        picks,
+        grad_one_part,
+        small,
+        norm_one[None, :],
+        router_attn.T,
+        table_of(
+            gates_attn[:, 0:1],
+            gates_attn[:, 1:2],
+            chosen_attn[:, 0:1],
+            chosen_attn[:, 1:2],
+            scale_one,
+            attn_route[:, 0:1].astype(F32),
+            attn_route[:, 1:2].astype(F32),
+        ),
+        lows,
+        right_parts,
+        [hidden_one, grad_full, hidden_two, cot_full, inputs, grad_middle],
+        rows_axis,
+        cols,
+    )
+    lefts_back = [grad.swapaxes(1, 2) for grad in grads[:5]]
+    rights_back = grads[5:]
     return (
         output,
         grad_inputs,
-        left_grads[:, 0],
-        right_grads[:, :, 0],
-        left_grads[:, 1],
-        right_grads[:, :, 1:3],
-        left_grads[:, 2],
-        right_grads[:, :, 3],
-        left_grads[:, 3],
-        ffn_rights[:, :, :2],
-        left_grads[:, 4],
-        ffn_rights[:, :, 2],
+        lefts_back[0],
+        rights_back[0],
+        lefts_back[1],
+        jnp.stack(rights_back[1:3], axis=2),
+        lefts_back[2],
+        rights_back[3],
+        lefts_back[3],
+        jnp.stack(rights_ffn[:2], axis=2),
+        lefts_back[4],
+        rights_ffn[2],
     )
 
 

time: 802 us -> 746 us (0.930)
  waiting for transfers between devices: 97.7 us -> 156 us
  starting transfers between devices: 68.7 us -> 16.4 us
  Pallas kernels: 272 us -> 317 us
  blocking collectives: 65.5 us -> 23.7 us
  local copies, waits for them, and re-layouts: 110 us -> 70 us
  matrix products: 124 us -> 106 us
    pallas_call x2 -> x3, Pallas kernels: 161 us -> 237 us  [the longest x1 107 us: gather_all(): pl.pallas_call(functools.partial(gather_kernel, parts, cols, replicas, co...]
    ppermute x10 -> x7, waiting for transfers between devices: 32.2 us -> 87.7 us  [swap(): lax.ppermute(value, 'row', [(i, i ^ offset) for i in range(rows_axis)])]
    ppermute x10 -> x7, starting transfers between devices: 54.1 us -> 10.1 us  [swap(): lax.ppermute(value, 'row', [(i, i ^ offset) for i in range(rows_axis)])]
    psum x5 -> x1, blocking collectives: 48.1 us -> 15.3 us  [on_device(): lax.psum((jnp.sum(middle * middle, axis=1), low_out_part, grad_low_down_p...]
    pallas_call x2 -> x1, Pallas kernels: 69.1 us -> 36.7 us  [trade_rows(): pl.pallas_call(functools.partial(trade_kernel, replicas), out_shape=[jax....]
    all_gather x1, waiting for transfers between devices: 9.22 us -> 41.1 us  [on_device(): lax.all_gather(later(out_weight, query_full), 'row', axis=1, tiled=True)]
    all_gather x2, waiting for transfers between devices: 25.6 us -> 0.01 us  [features(): return lax.all_gather(part, 'col', axis=1, tiled=True)]
    unnamed x287 -> x296, local copies, waits for them, and re-layouts: 43 us -> 25.3 us
  transfers between devices with their start and end apart: 20 -> 14, of which waited for: 8 -> 5; matrix products, arithmetic and copies ran while one was open for 29% -> 22% of each run, Pallas kernels for 12% -> 28%
where the time goes in v4:
time: 746 us; the launch traced here: 738 us
  Pallas kernels  317 us (42%)
  waiting for transfers between devices  156 us (21%)
  matrix products  106 us (14%)
  local copies, waits for them, and re-layouts  70 us (9%)
  other arithmetic  31.2 us (4%)
  blocking collectives  23.7 us (3%)
  between operations  17.9 us (2%)
  starting transfers between devices  16.4 us (2%)
    pallas_call x1, Pallas kernels, gather_all(): pl.pallas_call(functools.partial(gather_kernel, parts, cols, replicas, co...  107 us
    dot_general x44, matrix products, mm(): return jnp.einsum(spec, a, b, preferred_element_type=F32)  99.2 us
    pallas_call x1, Pallas kernels, middle_back(): pl.pallas_call(functools.partial(middle_back_kernel, cols, replicas), out...  91.5 us
    ppermute x7, waiting for transfers between devices, swap(): lax.ppermute(value, 'row', [(i, i ^ offset) for i in range(rows_axis)])  87.7 us
    pallas_call x1, Pallas kernels, feed_forward(): pl.pallas_call(functools.partial(ffn_kernel, parts, depth, width, units),...  42.7 us
    all_gather x1, waiting for transfers between devices, on_device(): lax.all_gather(later(out_weight, query_full), 'row', axis=1, tiled=True)  41.1 us
    pallas_call x1, Pallas kernels, input_back(): pl.pallas_call(functools.partial(input_back_kernel, parts_axis, cols), ou...  38.4 us
    pallas_call x1, Pallas kernels, trade_rows(): pl.pallas_call(functools.partial(trade_kernel, replicas), out_shape=[jax....  36.7 us
  transfers between devices with their start and end apart: 14, of which 5 were waited for; matrix products, arithmetic and copies ran while one was open for 22% of the time, Pallas kernels for 28%

profile of v4, /device:TPU:9, one launch (start us, length us, event | category | flops | bytes accessed | tf_op | source)
XLA Modules:
  0.0 738.0 jit_solution(15014877654051741611)
XLA Ops:
  7.9 1.5 copy.305.refs_1_
  9.4 107.1 %shard_map.328 = (bf16[2,2048,512]{2,1,0:T(8,128)(2,1)}, bf16[8,2048,512]{2,1,0:T(8,128)(2,1)}, bf16[256,2048]{1,0:T(8,128)(2,1)}, bf16[160,2048]{1,0:T(8,128)(2...) custom-call(s32[1]{0:T(128)} %copy.433.refs_0_, s32[256,2]{1,0:T(8,128)} %copy.305.refs_1_, ...), custom_call_target="tpu_custom_call" | custom-call | tf_op jit(solution)/shard_map/pallas_call | solution.py:221
  118.7 8.4 %all-reduce.5.refs_0_ = s32[8]{0:T(128)S(1)} all-reduce(s32[8]{0:T(128)S(1)} %dynamic-update-slice), channel_id=1, replica_groups=mesh['row'=8,'col'=4] {'row'}, use_global_device_ids=true, to_apply=%add.5 | all-reduce | flops 8 | bytes 64
  128.5 5.9 all-to-all-start
  140.0 5.2 fusion.24
  145.2 3.0 fusion.162
  148.5 1.5 copy.314
  157.7 1.4 convolution_convert_fusion.9
  161.1 1.8 subtract_convert_fusion.2
  162.8 3.4 fusion.155
  166.2 2.0 fusion.16
  168.5 1.7 convolution_convert_fusion.6
  171.5 41.1 %all-gather.4.cloned.1.call-done = bf16[8,2048,512]{2,1,0:T(8,128)(2,1)} async-done(((bf16[8,256,512]{2,1,0:T(8,128)(2,1)}), bf16[8,2048,512]{2,1,0:T(8,128)(2,1)}) %all-gather.4.cloned.1.call-update) | async-done | bytes 16777232 | tf_op jit(solution)/shard_map/all_gather | solution.py:949
  212.6 13.2 %fusion.165 = f32[8,80,2048]{2,1,0:T(8,128)} fusion(bf16[8,80,512]{2,1,0:T(8,128)(2,1)S(1)} %bitcast.285, bf16[8,2048,512]{2,1,0:T(8,128)(2,1)} %all-gather.4.cloned.1.call-done), kind=kOutput, calls=%fused_computation.309 | convolution fusion | flops 1342177280 | bytes 22675456 | tf_op jit(solution)/shard_map/ecw,edw->ecd/dot_general | solution.py:27
  225.9 3.7 fusion.6
  230.9 1.4 fusion.9
  232.6 7.7 %constant_dynamic-slice_fusion = (bf16[1,256,2,1408]{3,2,1,0:T(2,128)(2,1)}, bf16[1,256,2,1408]{3,2,1,0:T(2,128)(2,1)}, bf16[1,256,2,1408]{3,2,1,0:T(2,128)(2,1)}, bf16[1,256,2,1408]{3,2,1,0:T(2,128)(2,1)}) fusion(bf16[4,256,2,1408]{3,2,1,0:T(2,128)(2,1)} %param.38, s32[]{:T(128)S(6)} %select_n.99, s32[]{:T(128)S(6)} %select_n.97, s32[]{:T(128)S(6)} %select_n.96, ...), kind=kLoop, calls=%fused_computation.227 | loop fusion | bytes 11534352 | tf_op jit(solution)/shard_map/jit(dynamic_index_in_dim)/dynamic_slice | solution.py:959
  240.6 16.6 %reduce-scatter.3.cloned.1.call-done = bf16[256,512]{1,0:T(8,128)(2,1)} async-done(((bf16[256,2048]{1,0:T(8,128)(2,1)}), bf16[256,512]{1,0:T(8,128)(2,1)}) %reduce-scatter.3.cloned.1.call-update) | async-done | bytes 262160 | tf_op jit(solution)/shard_map/reduce_scatter | solution.py:920
  258.3 15.3 %all-reduce.6 = (f32[256]{0:T(256)S(1)}, f32[256,16]{0,1:T(8,128)S(1)}, f32[256,16]{1,0:T(8,128)}) all-reduce(f32[256]{0:T(256)S(1)} %get-tuple-element.215, f32[256,16]{0,1:T(8,128)S(1)} %fusion.97, f32[256,16]{1,0:T(8,128)S(1)} %slice-done.1), channel_id=1, replica_groups=mesh['row'=8,'col'=4] {'col'}, use_global_device_ids=true, to_apply=%region_12.13 | all-reduce | flops 8448 | bytes 67584 | tf_op jit(solution)/shard_map/psum | solution.py:1090
  273.6 1.8 multiply_convert_fusion.4
  275.5 3.4 copy_bitcast_fusion
  278.9 1.4 dynamic-slice_bitcast_fusion
  280.5 1.5 pad_maximum_fusion.refs_8_
  281.9 4.1 collective-permute-start
  287.6 1.6 copy.415
  292.7 2.6 slice_bitcast_fusion.1
  295.3 2.1 copy.334
  298.1 3.2 pad_maximum_fusion.3
  301.4 2.6 pad_maximum_fusion.1
  304.0 1.4 collective-permute-start.1
  310.4 42.6 %collective-permute-done.1.refs_10_ = bf16[256,4224]{1,0:T(8,128)(2,1)} collective-permute-done((bf16[256,4224]{1,0:T(8,128)(2,1)}, bf16[256,4224]{1,0:T(8,128)(2,1)}, u32[]{:S(2)}, u32[]{:S(2)}) %collective-permute-start.1) | collective-permute-done | bytes 2162720 | tf_op jit(solution)/shard_map/ppermute | solution.py:914
  354.2 45.1 %collective-permute-done.3.refs_12_ = bf16[256,4224]{1,0:T(8,128)(2,1)} collective-permute-done((bf16[256,4224]{1,0:T(8,128)(2,1)}, bf16[256,4224]{1,0:T(8,128)(2,1)}, u32[]{:S(2)}, u32[]{:S(2)}) %collective-permute-start.3) | collective-permute-done | bytes 2162720 | tf_op jit(solution)/shard_map/ppermute | solution.py:914
  399.3 2.2 collective-permute-start.4
  401.5 1.6 fusion.166
  403.3 1.6 fusion.167
  406.2 2.2 convolution_convert_fusion.1
  408.7 1.7 fusion.144
  410.4 36.7 %shard_map.329 = (bf16[160,2432]{1,0:T(8,128)(2,1)}, bf16[160,2432]{1,0:T(8,128)(2,1)}, bf16[160,2432]{1,0:T(8,128)(2,1)}) custom-call(bf16[160,2432]{1,0:T(8,128)(2,1)} %get-tuple-element.190.refs_0_, bf16[160,2432]{1,0:T(8,128)(2,1)} %get-tuple-element.189.refs_1_, bf16[160,2432]{1,0:T(8,128)(2,1)} %get-tuple-element.188.refs_2_), custom_call_target="tpu_custom_call" | custom-call | tf_op jit(solution)/shard_map/pallas_call | solution.py:727
  447.8 42.7 %shard_map.330 = (bf16[160,2304]{1,0:T(8,128)(2,1)}, bf16[160,2304]{1,0:T(8,128)(2,1)}, bf16[160,2304]{1,0:T(8,128)(2,1)}, bf16[160,2304]{1,0:T(8,128)(2,1)}, bf...) custom-call(bf16[160,2432]{1,0:T(8,128)(2,1)} %get-tuple-element.191, ...), custom_call_target="tpu_custom_call" | custom-call | tf_op jit(solution)/shard_map/pallas_call | solution.py:851
  494.9 91.5 %shard_map.331 = (f32[256,512]{1,0:T(8,128)S(1)}, bf16[256,2048]{1,0:T(8,128)(2,1)}, f32[256,128]{1,0:T(8,128)S(1)}, bf16[256,2048]{1,0:T(8,128)(2,1)}, f32[256,128]{1,0:T(8,128)S(1)}) custom-call(bf16[160,2304]{1,0:T(8,128)(2,1)} %get-tuple-element.69.refs_0_, bf16[160,2304]{1,0:T(8,128)(2,1)} %get-tuple-element.70.refs_1_, ...), custom_call_target="tpu_custom_call" | custom-call | tf_op jit(solution)/shard_map/pallas_call | solution.py:507
  586.5 2.2 convolution_convert_fusion.2
  589.1 9.9 %fusion.168 = f32[8,80,512]{2,1,0:T(8,128)} fusion(bf16[8,80,2048]{2,1,0:T(8,128)(2,1)S(1)} %bitcast.282, bf16[8,2048,512]{2,1,0:T(8,128)(2,1)} %all-gather.4.cloned.1.call-done), kind=kOutput, calls=%fused_computation.312 | convolution fusion | flops 1342177280 | bytes 20709376 | tf_op jit(solution)/shard_map/ecd,edw->ecw/dot_general | solution.py:27
  599.0 3.8 multiply_reduce_fusion.1
  602.8 2.9 convolution_convert_fusion.7
  605.6 2.0 reshape.459
  607.6 2.1 copy.348
  609.7 2.3 multiply_reduce_fusion
  613.1 1.5 fusion.15
  617.8 1.4 subtract_convert_fusion.1
  622.2 1.8 fusion.156
  627.1 1.5 fusion.157
  630.1 2.1 copy.343
  635.9 1.6 convolution_convert_fusion.5
  638.5 5.1 convolution_bitcast_fusion
  643.7 1.6 select_select_fusion
  645.3 12.8 %convolution_convert_fusion.4 = bf16[8,80,2048]{2,1,0:T(8,128)(2,1)} fusion(bf16[8,80,512]{2,1,0:T(8,128)(2,1)} %bitcast.304, bf16[8,2048,512]{2,1,0:T(8,128)(2,1)} %get-tuple-element.57), kind=kOutput, calls=%fused_computation.11 | convolution fusion | flops 1343488000 | bytes 20054016 | tf_op jit(solution)/shard_map/ecw,edw->ecd/dot_general | solution.py:27
  658.1 3.4 convolution_add_fusion
  661.6 1.7 convolution_add_fusion.1.refs_1_
  663.4 38.4 %shard_map.332 = (f32[256,512]{1,0:T(8,128)S(1)}, f32[8,16,256]{2,1,0:T(8,128)S(1)}, f32[8,16,256]{2,1,0:T(8,128)S(1)}, f32[8,16,256]{2,1,0:T(8,128)S(1)}, f32[8...) custom-call(s32[8]{0:T(128)S(1)} %all-reduce.5.refs_0_, ...), custom_call_target="tpu_custom_call" | custom-call | tf_op jit(solution)/shard_map/pallas_call | solution.py:676
  705.9 1.6 copy.355
  707.5 1.5 copy.356
  710.0 2.8 maximum_convert_fusion.1
  712.8 10.9 %reduce-scatter.5.cloned.1.call-done = bf16[256,512]{1,0:T(8,128)(2,1)} async-done(((bf16[256,2048]{1,0:T(8,128)(2,1)}), bf16[256,512]{1,0:T(8,128)(2,1)}) %reduce-scatter.5.cloned.1.call-update) | async-done | bytes 262160 | tf_op jit(solution)/shard_map/reduce_scatter | solution.py:920
  723.7 1.8 multiply_convert_fusion.3
  (459 shorter events, 68.2 us)
Async XLA Ops:
  7.2 141.1 %copy-start = (bf16[8,16,2,512]{3,2,1,0:T(2,128)(2,1)S(1)}, bf16[8,16,2,512]{3,2,1,0:T(2,128)(2,1)}, u32[]{:S(2)}) copy-start(bf16[8,16,2,512]{3,2,1,0:T(2,128)(2,1)} %param.43) | copy-start | bytes 786436
  7.2 205.4 %all-gather.4.cloned.1.call-start = ((), (), s32[]{:S(2)}) async-start(), calls=%async_computation.3 | async-start | bytes 18874368 | tf_op jit(solution)/shard_map/all_gather | solution.py:949
  9.4 108.0 %copy-start.136 = (u32[32]{0:T(128)S(1)}, u32[32]{0:T(128)}, u32[]{:S(2)}) copy-start(u32[32]{0:T(128)} %constant.124) | copy-start | bytes 388
  9.4 117.7 %copy-start.93 = (bf16[8,256,16]{1,2,0:T(8,128)(2,1)S(1)}, bf16[8,256,16]{1,2,0:T(8,128)(2,1)}, u32[]{:S(2)}) copy-start(bf16[8,256,16]{1,2,0:T(8,128)(2,1)} %param.40) | copy-start | bytes 196612
  9.4 117.7 %copy-start.94 = (bf16[8,256,16]{1,2,0:T(8,128)(2,1)S(1)}, bf16[8,256,16]{1,2,0:T(8,128)(2,1)}, u32[]{:S(2)}) copy-start(bf16[8,256,16]{1,2,0:T(8,128)(2,1)} %param.42) | copy-start | bytes 196612
  9.4 117.7 %copy-start.95 = (bf16[8,256,16]{1,2,0:T(8,128)(2,1)S(1)}, bf16[8,256,16]{1,2,0:T(8,128)(2,1)}, u32[]{:S(2)}) copy-start(bf16[8,256,16]{1,2,0:T(8,128)(2,1)} %param.44) | copy-start | bytes 196612
  9.4 117.7 %copy-start.96 = (bf16[8,256,16]{1,2,0:T(8,128)(2,1)S(1)}, bf16[8,256,16]{1,2,0:T(8,128)(2,1)}, u32[]{:S(2)}) copy-start(bf16[8,256,16]{1,2,0:T(8,128)(2,1)} %param.46) | copy-start | bytes 196612
  9.4 117.8 %copy-start.97 = (bf16[8,256,16]{1,2,0:T(8,128)(2,1)S(1)}, bf16[8,256,16]{1,2,0:T(8,128)(2,1)}, u32[]{:S(2)}) copy-start(bf16[8,256,16]{1,2,0:T(8,128)(2,1)} %param.48) | copy-start | bytes 196612
  116.6 17.9 %copy-start.99 = (s32[256,2]{0,1:T(2,128)S(1)}, s32[256,2]{0,1:T(2,128)}, u32[]{:S(2)}) copy-start(s32[256,2]{0,1:T(2,128)} %param.29) | copy-start | bytes 6148
  116.6 17.9 %copy-start.35 = (bf16[256,2048]{1,0:T(8,128)(2,1)S(1)}, bf16[256,2048]{1,0:T(8,128)(2,1)}, u32[]{:S(2)}) copy-start(bf16[256,2048]{1,0:T(8,128)(2,1)} %get-tuple-element.56) | copy-start | bytes 3145732
  127.2 8.2 %copy-start.29 = (f32[2048]{0:T(1024)S(1)}, f32[2048]{0:T(1024)}, u32[]{:S(2)}) copy-start(f32[2048]{0:T(1024)} %param.31) | copy-start | bytes 24580
  127.7 8.1 %copy-start.15 = (bf16[2048,8]{0,1:T(8,128)(2,1)S(1)}, bf16[2048,8]{0,1:T(8,128)(2,1)}, u32[]{:S(2)}) copy-start(bf16[2048,8]{0,1:T(8,128)(2,1)} %param.33) | copy-start | bytes 98308
  128.5 22.5 %all-to-all-start = ((bf16[8,80,256]{2,1,0:T(8,128)(2,1)}), bf16[8,80,256]{2,1,0:T(8,128)(2,1)S(1)}, u32[]{:S(2)}, u32[]{:S(2)}) async-start(bf16[8,80,256]{2,1,0:T(8,128)(2,1)} %copy.309), calls=%async_computation | async-start | bytes 655360 | tf_op jit(solution)/shard_map/all_to_all | solution.py:978
  134.3 122.8 %reduce-scatter.3.cloned.1.call-start = ((), (), s32[]{:S(2)}) async-start(), calls=%async_computation.4 | async-start | bytes 1310720 | tf_op jit(solution)/shard_map/reduce_scatter | solution.py:920
  136.3 450.2 %copy-start.89 = (s32[256,1]{0,1:T(1,128)}, s32[256,1]{0,1:T(1,128)S(1)}, u32[]{:S(2)}) copy-start(s32[256,1]{0,1:T(1,128)S(1)} %get-tuple-element.244) | copy-start | bytes 3076
  136.3 12.0 %copy-start.103 = (f32[256,2]{0,1:T(2,128)}, f32[256,2]{0,1:T(2,128)S(1)}, u32[]{:S(2)}) copy-start(f32[256,2]{0,1:T(2,128)S(1)} %fusion.116) | copy-start | bytes 6148
  137.9 7.3 copy-start.31
  139.1 15.5 %copy-start.63 = (f32[256,64]{1,0:T(8,128)}, f32[256,64]{1,0:T(8,128)S(1)}, u32[]{:S(2)}) copy-start(f32[256,64]{1,0:T(8,128)S(1)} %get-tuple-element.246) | copy-start | bytes 196612
  139.1 147.1 %copy-start.47 = (f32[256,64]{1,0:T(8,128)}, f32[256,64]{1,0:T(8,128)S(1)}, u32[]{:S(2)}) copy-start(f32[256,64]{1,0:T(8,128)S(1)} %get-tuple-element.247) | copy-start | bytes 196612
  149.9 75.9 %copy-start.125 = (f32[640]{0:T(1024)}, f32[640]{0:T(1024)S(1)}, u32[]{:S(2)}) copy-start(f32[640]{0:T(1024)S(1)} %add.177) | copy-start | bytes 7684
  168.5 57.4 %copy-start.50 = (bf16[2,256,4,128]{3,2,1,0:T(4,128)(2,1)}, bf16[2,256,4,128]{3,2,1,0:T(4,128)(2,1)S(1)}, u32[]{:S(2)}) copy-start(bf16[2,256,4,128]{3,2,1,0:T(4,128)(2,1)S(1)} %copy.319) | copy-start | bytes 1572868
  168.5 61.1 %copy-start.77 = (bf16[8,2,8,256]{3,2,0,1:T(8,128)(2,1)}, bf16[8,2,8,256]{3,2,0,1:T(8,128)(2,1)S(1)}, u32[]{:S(2)}) copy-start(bf16[8,2,8,256]{3,2,0,1:T(8,128)(2,1)S(1)} %copy.382) | copy-start | bytes 196612
  170.2 55.7 %copy-start.32 = (bf16[640,512]{1,0:T(8,128)(2,1)}, bf16[640,512]{1,0:T(8,128)(2,1)S(1)}, u32[]{:S(2)}) copy-start(bf16[640,512]{1,0:T(8,128)(2,1)S(1)} %convolution_convert_fusion.6) | copy-start | bytes 1966084
  232.3 169.2 %all-gather.6.cloned.1.call-start = ((), (), s32[]{:S(2)}) async-start(), calls=%async_computation.5 | async-start | bytes 1310720 | tf_op jit(solution)/shard_map/all_gather | solution.py:917
  232.6 7.8 %copy-start.46 = (bf16[256,512]{1,0:T(8,128)(2,1)}, bf16[256,512]{1,0:T(8,128)(2,1)S(1)}, u32[]{:S(2)}) copy-start(bf16[256,512]{1,0:T(8,128)(2,1)S(1)} %broadcast_multiply_fusion) | copy-start | bytes 786436
  232.6 7.8 %copy-start.80 = (bf16[8,2,8,256]{3,2,1,0:T(8,128)(2,1)S(1)}, bf16[8,2,8,256]{3,2,1,0:T(8,128)(2,1)}, u32[]{:S(2)}) copy-start(bf16[8,2,8,256]{3,2,1,0:T(8,128)(2,1)} %get-tuple-element.221) | copy-start | bytes 196612
  232.6 24.6 %copy-start.3 = (bf16[256,512]{1,0:T(8,128)(2,1)S(1)}, bf16[256,512]{1,0:T(8,128)(2,1)}, u32[]{:S(2)}) copy-start(bf16[256,512]{1,0:T(8,128)(2,1)} %refs_12_.1) | copy-start | bytes 786436
  232.6 25.7 %slice-start.1 = ((f32[256,2064]{1,0:T(8,128)}), f32[256,16]{1,0:T(8,128)S(1)}, s32[]{:S(2)}) async-start(f32[256,2064]{1,0:T(8,128)} %copy-done.67), calls=%async_computation.10 | async-start | bytes 262144 | tf_op jit(solution)/shard_map/slice | solution.py:1086
  275.4 388.0 %all-gather.8.cloned.1.call-start = ((), (), s32[]{:S(2)}) async-start(), calls=%async_computation.7 | async-start | bytes 1310720 | tf_op jit(solution)/shard_map/all_gather | solution.py:917
  281.9 165.8 %collective-permute-start = (bf16[256,4224]{1,0:T(8,128)(2,1)}, bf16[256,4224]{1,0:T(8,128)(2,1)}, u32[]{:S(2)}, u32[]{:S(2)}) collective-permute-start(bf16[256,4224]{1,0:T(8,128)(2,1)} %pad_maximum_fusion.refs_8_), channel_id=1, source_target_pairs={{0,4},{4,0},{8,12},{12,8},{16,20},{20,16},{24,28},{28,24},{1,5},{5... | collective-permute-start | bytes 6488072 | tf_op jit(solution)/shard_map/ppermute | solution.py:914
  286.0 419.9 %all-reduce.10.cloned.1.call-start = ((), (), s32[]{:S(2)}) async-start(), calls=%async_computation.8 | async-start | bytes 2162688 | tf_op jit(solution)/shard_map/psum | solution.py:1134
  286.1 161.0 %copy-start.128 = (pred[128]{0:T(512)(128)(4,1)}, pred[128]{0:T(512)(128)(4,1)S(1)}, u32[]{:S(2)}) copy-start(pred[128]{0:T(512)(128)(4,1)S(1)} %get-tuple-element.270) | copy-start | bytes 388
  286.2 161.0 %copy-start.129 = (pred[128]{0:T(512)(128)(4,1)}, pred[128]{0:T(512)(128)(4,1)S(1)}, u32[]{:S(2)}) copy-start(pred[128]{0:T(512)(128)(4,1)S(1)} %get-tuple-element.271) | copy-start | bytes 388
  286.2 161.0 %copy-start.130 = (pred[128]{0:T(512)(128)(4,1)}, pred[128]{0:T(512)(128)(4,1)S(1)}, u32[]{:S(2)}) copy-start(pred[128]{0:T(512)(128)(4,1)S(1)} %get-tuple-element.272) | copy-start | bytes 388
  286.2 161.0 %copy-start.131 = (pred[128]{0:T(512)(128)(4,1)}, pred[128]{0:T(512)(128)(4,1)S(1)}, u32[]{:S(2)}) copy-start(pred[128]{0:T(512)(128)(4,1)S(1)} %get-tuple-element.273) | copy-start | bytes 388
  286.2 161.0 %copy-start.132 = (pred[128]{0:T(512)(128)(4,1)}, pred[128]{0:T(512)(128)(4,1)S(1)}, u32[]{:S(2)}) copy-start(pred[128]{0:T(512)(128)(4,1)S(1)} %get-tuple-element.274) | copy-start | bytes 388
  286.2 161.0 %copy-start.133 = (pred[128]{0:T(512)(128)(4,1)}, pred[128]{0:T(512)(128)(4,1)S(1)}, u32[]{:S(2)}) copy-start(pred[128]{0:T(512)(128)(4,1)S(1)} %get-tuple-element.275) | copy-start | bytes 388
  286.2 160.9 %copy-start.134 = (pred[128]{0:T(512)(128)(4,1)}, pred[128]{0:T(512)(128)(4,1)S(1)}, u32[]{:S(2)}) copy-start(pred[128]{0:T(512)(128)(4,1)S(1)} %get-tuple-element.276) | copy-start | bytes 388
  297.4 149.8 %copy-start.117 = (f32[256]{0:T(256)}, f32[256]{0:T(256)S(1)}, u32[]{:S(2)}) copy-start(f32[256]{0:T(256)S(1)} %fusion.140) | copy-start | bytes 3076
  301.4 7.7 %copy-start.37 = (bf16[8,16,2,1408]{3,1,0,2:T(8,128)(2,1)S(1)}, bf16[8,16,2,1408]{3,1,0,2:T(8,128)(2,1)}, u32[]{:S(2)}) copy-start(bf16[8,16,2,1408]{3,1,0,2:T(8,128)(2,1)} %copy.334) | copy-start | bytes 2162692
  301.4 7.8 %copy-start.70 = (bf16[8,16,1408]{2,1,0:T(8,128)(2,1)S(1)}, bf16[8,16,1408]{2,1,0:T(8,128)(2,1)}, u32[]{:S(2)}) copy-start(bf16[8,16,1408]{2,1,0:T(8,128)(2,1)} %param.49) | copy-start | bytes 1081348
  304.0 49.0 %collective-permute-start.1 = (bf16[256,4224]{1,0:T(8,128)(2,1)}, bf16[256,4224]{1,0:T(8,128)(2,1)}, u32[]{:S(2)}, u32[]{:S(2)}) collective-permute-start(bf16[256,4224]{1,0:T(8,128)(2,1)} %get-tuple-element.66), channel_id=1, source_target_pairs={{0,8},{4,12},{8,0},{12,4},{16,24},{20,28},{24,16},{28,20},{1,9},{5... | collective-permute-start | bytes 6488072 | tf_op jit(solution)/shard_map/ppermute | solution.py:914
  305.4 93.9 %collective-permute-start.3 = (bf16[256,4224]{1,0:T(8,128)(2,1)}, bf16[256,4224]{1,0:T(8,128)(2,1)}, u32[]{:S(2)}, u32[]{:S(2)}) collective-permute-start(bf16[256,4224]{1,0:T(8,128)(2,1)} %get-tuple-element.67), channel_id=1, source_target_pairs={{0,16},{4,20},{8,24},{12,28},{16,0},{20,4},{24,8},{28,12},{1,17},{... | collective-permute-start | bytes 6488072 | tf_op jit(solution)/shard_map/ppermute | solution.py:914
  306.6 94.9 %collective-permute-start.5 = (bf16[256,4224]{1,0:T(8,128)(2,1)}, bf16[256,4224]{1,0:T(8,128)(2,1)}, u32[]{:S(2)}, u32[]{:S(2)}) collective-permute-start(bf16[256,4224]{1,0:T(8,128)(2,1)} %pad_maximum_fusion.3), channel_id=1, source_target_pairs={{0,24},{4,28},{8,16},{12,20},{16,8},{20,12},{24,0},{28,4},{1,25},{... | collective-permute-start | bytes 6488072 | tf_op jit(solution)/shard_map/ppermute | solution.py:914
  309.2 94.1 %copy-start.28 = (bf16[2048,4]{0,1:T(4,128)(2,1)S(1)}, bf16[2048,4]{0,1:T(4,128)(2,1)}, u32[]{:S(2)}) copy-start(bf16[2048,4]{0,1:T(4,128)(2,1)} %param.34) | copy-start | bytes 49156
  310.2 94.6 %slice-start.2 = ((bf16[256,2,4]{0,2,1:T(4,128)(2,1)}), bf16[256,1,4]{0,2,1:T(4,128)(2,1)S(1)}, s32[]{:S(2)}) async-start(bf16[256,2,4]{0,2,1:T(4,128)(2,1)} %copy-done.110), calls=%async_computation.11 | async-start | bytes 4096 | tf_op jit(solution)/shard_map/slice | solution.py:57
  353.0 94.7 %collective-permute-start.2 = (bf16[256,4224]{1,0:T(8,128)(2,1)}, bf16[256,4224]{1,0:T(8,128)(2,1)}, u32[]{:S(2)}, u32[]{:S(2)}) collective-permute-start(bf16[256,4224]{1,0:T(8,128)(2,1)} %collective-permute-done.1.refs_10_), channel_id=1, source_target_pairs={{0,4},{4,0},{8,12},{12,8},{16,20},{20,16},{24,28},{28,24},{1,5},{5... | collective-permute-start | bytes 6488072 | tf_op jit(solution)/shard_map/ppermute | solution.py:914
  399.3 48.5 %collective-permute-start.4 = (bf16[256,4224]{1,0:T(8,128)(2,1)}, bf16[256,4224]{1,0:T(8,128)(2,1)}, u32[]{:S(2)}, u32[]{:S(2)}) collective-permute-start(bf16[256,4224]{1,0:T(8,128)(2,1)} %collective-permute-done.3.refs_12_), channel_id=1, source_target_pairs={{0,4},{4,0},{8,12},{12,8},{16,20},{20,16},{24,28},{28,24},{1,5},{5... | collective-permute-start | bytes 6488072 | tf_op jit(solution)/shard_map/ppermute | solution.py:914
  401.5 46.3 %collective-permute-start.6 = (bf16[256,4224]{1,0:T(8,128)(2,1)}, bf16[256,4224]{1,0:T(8,128)(2,1)}, u32[]{:S(2)}, u32[]{:S(2)}) collective-permute-start(bf16[256,4224]{1,0:T(8,128)(2,1)} %collective-permute-done.5.refs_14_), channel_id=1, source_target_pairs={{0,4},{4,0},{8,12},{12,8},{16,20},{20,16},{24,28},{28,24},{1,5},{5... | collective-permute-start | bytes 6488072 | tf_op jit(solution)/shard_map/ppermute | solution.py:914
  589.1 9.9 %copy-start.90 = (s32[256,1]{0,1:T(1,128)S(1)}, s32[256,1]{0,1:T(1,128)}, u32[]{:S(2)}) copy-start(s32[256,1]{0,1:T(1,128)} %copy-done.89) | copy-start | bytes 3076
  622.2 7.1 copy-start.19
  626.1 8.1 %copy-start.66 = (f32[256,16]{1,0:T(8,128)S(1)}, f32[256,16]{1,0:T(8,128)}, u32[]{:S(2)}) copy-start(f32[256,16]{1,0:T(8,128)} %copy.354) | copy-start | bytes 49156
  626.1 8.1 %copy-start.116 = (f32[2,256]{1,0:T(2,128)S(1)}, f32[2,256]{1,0:T(2,128)}, u32[]{:S(2)}) copy-start(f32[2,256]{1,0:T(2,128)} %fusion.217) | copy-start | bytes 6148
  637.5 86.2 %reduce-scatter.5.cloned.1.call-start = ((), (), s32[]{:S(2)}) async-start(), calls=%async_computation.6 | async-start | bytes 1310720 | tf_op jit(solution)/shard_map/reduce_scatter | solution.py:920
  709.1 14.6 %copy-start.45 = (bf16[256,512]{1,0:T(8,128)(2,1)S(1)}, bf16[256,512]{1,0:T(8,128)(2,1)}, u32[]{:S(2)}) copy-start(bf16[256,512]{1,0:T(8,128)(2,1)} %reduce-scatter.3.cloned.1.call-done) | copy-start | bytes 786436
  709.1 14.6 %copy-start.118 = (f32[256]{0:T(256)S(1)}, f32[256]{0:T(256)}, u32[]{:S(2)}) copy-start(f32[256]{0:T(256)} %copy-done.117) | copy-start | bytes 3076
  710.0 15.4 %copy-start.10 = (f32[256,512]{1,0:T(8,128)S(1)}, f32[256,512]{1,0:T(8,128)}, u32[]{:S(2)}) copy-start(f32[256,512]{1,0:T(8,128)} %copy-done.9) | copy-start | bytes 1572868
  710.0 16.2 %copy-start.27 = (f32[8,16,256]{2,1,0:T(8,128)S(1)}, f32[8,16,256]{2,1,0:T(8,128)}, u32[]{:S(2)}) copy-start(f32[8,16,256]{2,1,0:T(8,128)} %copy-done.26) | copy-start | bytes 393220
  710.0 16.9 %copy-start.14 = (f32[8,16,512]{2,1,0:T(8,128)S(1)}, f32[8,16,512]{2,1,0:T(8,128)}, u32[]{:S(2)}) copy-start(f32[8,16,512]{2,1,0:T(8,128)} %copy-done.13) | copy-start | bytes 786436
  710.0 20.9 %copy-start.1 = (bf16[8,16,2,512]{3,2,1,0:T(2,128)(2,1)S(1)}, bf16[8,16,2,512]{3,2,1,0:T(2,128)(2,1)}, u32[]{:S(2)}) copy-start(bf16[8,16,2,512]{3,2,1,0:T(2,128)(2,1)} %param.43) | copy-start | bytes 786436
  712.8 14.8 %copy-start.25 = (f32[8,16,256]{2,1,0:T(8,128)S(1)}, f32[8,16,256]{2,1,0:T(8,128)}, u32[]{:S(2)}) copy-start(f32[8,16,256]{2,1,0:T(8,128)} %copy-done.24) | copy-start | bytes 393220
  712.8 15.5 %copy-start.23 = (f32[8,16,256]{2,1,0:T(8,128)S(1)}, f32[8,16,256]{2,1,0:T(8,128)}, u32[]{:S(2)}) copy-start(f32[8,16,256]{2,1,0:T(8,128)} %copy-done.22) | copy-start | bytes 393220
  712.8 16.1 %copy-start.12 = (f32[8,16,512]{2,1,0:T(8,128)S(1)}, f32[8,16,512]{2,1,0:T(8,128)}, u32[]{:S(2)}) copy-start(f32[8,16,512]{2,1,0:T(8,128)} %copy-done.11) | copy-start | bytes 786436
  712.8 16.8 %copy-start.21 = (f32[8,16,256]{2,1,0:T(8,128)S(1)}, f32[8,16,256]{2,1,0:T(8,128)}, u32[]{:S(2)}) copy-start(f32[8,16,256]{2,1,0:T(8,128)} %copy-done.20) | copy-start | bytes 393220
  (90 other events, 293.0 us)
Sparse Core Ops, SparseCore 0:
  116.7 95.8 all-gather.3
  232.4 24.6 reduce-scatter.2
  275.6 32.6 all-gather.5
  309.8 27.4 all-gather.7
  637.6 58.0 all-reduce.9
  697.9 25.6 reduce-scatter.4

commit v5 on v4

--- a/solution.py
+++ b/solution.py
@@ -699,51 +699,249 @@
     )(adapters, part, small, norm, router, stat, lows, rights, *sources)
 
 
-def trade_kernel(replicas, *refs):
-    count = EXP_FF - 1
-    blocks, arrived = refs[:count], refs[count : 2 * count]
-    send, recv = refs[2 * count :]
+def middle_kernel(parts_axis, cols, replicas, *refs):
+    adapter, norm, router, route, low_rows, low_in = refs[:6]
+    sources = refs[6:12]
+    weights = refs[12:14]
+    outs = refs[14:]
+    extra_chunks = parts_axis - 1
+    chunks = [(None,) + tuple(outs[n * extra_chunks : (n + 1) * extra_chunks]) for n in (0, 1)]
+    outs = outs[2 * extra_chunks :]
+    hids = outs[:EXP_FF]
+    hidden_out, middle, stat, totals = outs[EXP_FF : EXP_FF + 4]
+    scratch = outs[EXP_FF + 4 :]
+    out_rows, pick_attn, pick_0, pick_1, lefts, tokens = scratch[:6]
+    (
+        exact_part,
+        parts,
+        extra,
+        parts_in,
+        extra_in,
+        square,
+        square_in,
+        low,
+        hidden,
+        message,
+        send,
+        recv,
+        local,
+    ) = scratch[6:]
+    col = lax.axis_index("col")
+    count, wide = tokens.shape
+    width = hidden.shape[1]
     across = [opposite("row", j * replicas) for j in range(1, EXP_FF)]
-    greet(across)
-    copies = []
-    for j in (2, 1, 0):
-        copy = pltpu.make_async_remote_copy(
-            src_ref=blocks[j],
-            dst_ref=arrived[j],
-            send_sem=send.at[j],
-            recv_sem=recv.at[j],
-            device_id=across[j],
-            device_id_type=pl.DeviceIdType.MESH,
-        )
-        copy.start()
-        copies.append(copy)
-    for copy in copies:
+    beside = [opposite("row", i) for i in range(1, replicas)]
+    along = [opposite("col", i) for i in range(1, cols)]
+    greet(across + beside + along)
+    near = fetch(sources, scratch[:6], local)
+    used = [0]
+    started = []
+
+    def send_to(source, target, device):
+        copy = remote(source, target, send, recv, used[0], device)
+        used[0] += 1
+        started.append(copy)
+        return copy
+
+    expert = lax.axis_index("row") // replicas
+    piece_copies = [
+        [
+            send_to(weights[n].at[jnp.bitwise_xor(expert, j)], chunks[n][j * replicas], across[j - 1])
+            for n in (0, 1)
+        ]
+        for j in range(1, EXP_FF)
+    ]
+    sibling_copies = [
+        send_to(weights[n].at[expert], chunks[n][i], beside[i - 1])
+        for i in range(1, replicas)
+        for n in (0, 1)
+    ]
+    for copy in near:
         copy.wait()
 
-
-def trade_rows(blocks, replicas, number):
+    def back(source):
+        return lax.dot_general(
+            pick_attn[...], source, (((0,), (0,)), ((), ())), preferred_element_type=F32
+        )
+
+    sub = lax.broadcasted_iota(jnp.int32, (LANES, LANES), 0)
+    lane = lax.broadcasted_iota(jnp.int32, (LANES, LANES), 1)
+    lanes = lax.broadcasted_iota(jnp.int32, (count, LANES), 1)
+    low_out = back(low_rows[...])
+    small = low_in[...] + low_out
+    low_out = low_out[:, RANK : 2 * RANK].astype(BF16)
+    for q in range(cols):
+        here = slice(q * wide, (q + 1) * wide)
+        part = back(out_rows[:, here]) + jnp.dot(
+            low_out, lefts[2 * RANK : 3 * RANK, here], preferred_element_type=F32
+        )
+        exact_part[q] = part
+        parts[q] = part.astype(BF16)
+    extra[...] = small.astype(BF16)
+    part_copies = []
+    extra_copies = []
+    for i in range(1, cols):
+        target = jnp.bitwise_xor(col, i)
+        part_copies.append(send_to(parts.at[target], parts_in.at[i - 1], along[i - 1]))
+        extra_copies.append(send_to(extra, extra_in.at[i - 1], along[i - 1]))
+    value = tokens[...].astype(F32) + exact_part[col]
+    total = small
+    for i in range(cols - 1):
+        part_copies[i].wait_recv()
+        value += parts_in[i].astype(F32)
+    middle[...] = value
+    square[...] = lax.dot_general(
+        jnp.ones((8, wide), F32),
+        value * value,
+        (((1,), (1,)), ((), ())),
+        precision=HIGHEST,
+        preferred_element_type=F32,
+    )
+    square_copies = [
+        send_to(square, square_in.at[i], along[i]) for i in range(cols - 1)
+    ]
+    for i in range(cols - 1):
+        extra_copies[i].wait_recv()
+        total += extra_in[i].astype(F32)
+    totals[...] = total
+    squares = square[...]
+    for i in range(cols - 1):
+        square_copies[i].wait_recv()
+        squares += square_in[i]
+    squares = lax.dot_general(
+        squares,
+        jnp.full((8, LANES), 0.125, F32),
+        (((0,), (0,)), ((), ())),
+        precision=HIGHEST,
+        preferred_element_type=F32,
+    )
+    scale = lax.rsqrt(squares[:, 0:1] * (1.0 / width) + EPSILON)
+    first = pl.multiple_of(col * wide, wide)
+    here = pl.ds(first, wide)
+    low[...] = (value * scale * norm[:, here]).astype(BF16)
+    hidden[:, here] = low[...]
+    hidden_copies = [send_to(low, hidden.at[:, here], along[i]) for i in range(cols - 1)]
+    mine = lanes // RANK == adapter[0]
+
+    def own_adapter(value, start):
+        spread = (sub - start == lane % RANK).astype(F32).astype(BF16)
+        value = jnp.dot(value.astype(BF16), spread, preferred_element_type=F32)
+        return jnp.where(mine, value, 0.0).astype(BF16)
+
+    picks = [pick_0[...], pick_1[...]]
+    any_pick = picks[0] + picks[1]
+    message[:, width + 2 * LANES :] = jnp.dot(
+        any_pick, own_adapter(total, 2 * RANK), preferred_element_type=F32
+    ).astype(BF16)
+    for copy in hidden_copies:
+        copy.wait_recv()
+    kept = pltpu.make_async_copy(hidden, hidden_out, local.at[6])
+    kept.start()
+
+    def times(right):
+        return lax.dot_general(
+            hidden[...], right, (((1,), (1,)), ((), ())), preferred_element_type=F32
+        )
+
+    logits = times(router[...])
+    routes = [route[:, k : k + 1] for k in range(TOPK)]
+    chosen = []
+    for k in range(TOPK):
+        score = 0.0
+        for e in range(EXP_FF):
+            score += jnp.where(routes[k] == float(e), logits[:, e : e + 1], 0.0)
+        chosen.append(score)
+    top = jnp.maximum(chosen[0], chosen[1])
+    powers = [jnp.exp(score - top) for score in chosen]
+    gates = [power / (powers[0] + powers[1]) for power in powers]
+    stat[...] = pack(
+        [*gates, *chosen, scale, *routes, route[:, 2:3]], range(8)
+    )
+    gate_rows = 0.0
+    for k in range(TOPK):
+        columns = pack([*split(gates[k])], range(2)).astype(BF16)
+        gate_rows += jnp.dot(picks[k], columns, preferred_element_type=F32)
+    message[:, width + LANES : width + 2 * LANES] = gate_rows.astype(BF16)
+    rank = times(lefts[3 * RANK : 4 * RANK])
+    rank = jnp.concatenate([rank, jnp.zeros((count, LANES - RANK), F32)], axis=1)
+    message[:, width : width + LANES] = jnp.dot(
+        any_pick, own_adapter(rank, 0), preferred_element_type=F32
+    ).astype(BF16)
+    traded = []
+    for j in range(EXP_FF - 1, -1, -1):
+        rows = slice(j * CAP_FF, (j + 1) * CAP_FF)
+        message[rows, :width] = jnp.dot(
+            any_pick[rows], hidden[...], preferred_element_type=F32
+        ).astype(BF16)
+        if j:
+            traded.append(send_to(message.at[pl.ds(j * CAP_FF, CAP_FF)], hids[j], across[j - 1]))
+    own = pltpu.make_async_copy(message.at[pl.ds(0, CAP_FF)], hids[0], local.at[7])
+    own.start()
+    for j in range(1, EXP_FF):
+        for n in (0, 1):
+            piece_copies[j - 1][n].wait_recv()
+            for i in range(1, replicas):
+                m = j * replicas
+                sibling_copies.append(send_to(chunks[n][m], chunks[n][m + i], beside[i - 1]))
+    for copy in traded + sibling_copies:
+        copy.wait_recv()
+    for copy in started:
+        copy.wait_send()
+    kept.wait()
+    own.wait()
+
+
+def middle_forward(adapter, norm, router, route, low_rows, low_in, sources, weights, parts_axis, cols, replicas):
     hbm = pl.BlockSpec(memory_space=pl.ANY)
-    count = EXP_FF - 1
-    arrived = pl.pallas_call(
-        functools.partial(trade_kernel, replicas),
-        out_shape=[jax.ShapeDtypeStruct(b.shape, b.dtype) for b in blocks[1:]],
-        in_specs=[hbm] * count,
-        out_specs=[hbm] * count,
-        scratch_shapes=[
-            pltpu.SemaphoreType.DMA((count,)),
-            pltpu.SemaphoreType.DMA((count,)),
+    vmem = pl.BlockSpec(memory_space=pltpu.VMEM)
+    smem = pl.BlockSpec(memory_space=pltpu.SMEM)
+    count, wide = sources[-1].shape
+    width = wide * cols
+    rows = EXP_FF * CAP_FF
+    full = width + 3 * LANES
+    total = 2 * (parts_axis - 1) + 4 * (cols - 1) + EXP_FF - 1
+    return pl.pallas_call(
+        functools.partial(middle_kernel, parts_axis, cols, replicas),
+        out_shape=[jax.ShapeDtypeStruct(weights[0].shape[1:], BF16)] * (parts_axis - 1)
+        + [jax.ShapeDtypeStruct(weights[1].shape[1:], BF16)] * (parts_axis - 1)
+        + [jax.ShapeDtypeStruct((CAP_FF, full), BF16)] * EXP_FF
+        + [
+            jax.ShapeDtypeStruct((count, width), BF16),
+            jax.ShapeDtypeStruct((count, wide), F32),
+            jax.ShapeDtypeStruct((count, LANES), F32),
+            jax.ShapeDtypeStruct((count, LANES), F32),
         ],
-        compiler_params=pltpu.CompilerParams(collective_id=number, has_side_effects=True),
-    )(*blocks[1:])
-    return [blocks[0], *arrived]
+        in_specs=[smem] + [vmem] * 5 + [hbm] * 8,
+        out_specs=[hbm] * (2 * parts_axis - 1 + EXP_FF) + [vmem] * 3,
+        scratch_shapes=[pltpu.VMEM(source.shape, source.dtype) for source in sources]
+        + [
+            pltpu.VMEM((cols, count, wide), F32),
+            pltpu.VMEM((cols, count, wide), BF16),
+            pltpu.VMEM((count, LANES), BF16),
+            pltpu.VMEM((cols - 1, count, wide), BF16),
+            pltpu.VMEM((cols - 1, count, LANES), BF16),
+            pltpu.VMEM((8, count), F32),
+            pltpu.VMEM((cols - 1, 8, count), F32),
+            pltpu.VMEM((count, wide), BF16),
+            pltpu.VMEM((count, width), BF16),
+            pltpu.VMEM((rows, full), BF16),
+            pltpu.SemaphoreType.DMA((total,)),
+            pltpu.SemaphoreType.DMA((total,)),
+            pltpu.SemaphoreType.DMA((8,)),
+        ],
+        compiler_params=pltpu.CompilerParams(
+            collective_id=3, has_side_effects=True, vmem_limit_bytes=48 * 2**20
+        ),
+    )(adapter, norm, router, route, low_rows, low_in, *sources, *weights)
 
 
 def ffn_kernel(parts, depth, width, units, *refs):
     hids = refs[:EXP_FF]
     cots = refs[EXP_FF : 2 * EXP_FF]
-    pieces = refs[2 * EXP_FF : 2 * EXP_FF + parts]
-    rights = refs[2 * EXP_FF + parts]
-    outs = refs[2 * EXP_FF + parts + 1 :]
+    inners = refs[2 * EXP_FF : 2 * EXP_FF + parts]
+    lasts = refs[2 * EXP_FF + parts : 2 * EXP_FF + 2 * parts]
+    rights = refs[2 * EXP_FF + 2 * parts]
+    outs = refs[2 * EXP_FF + 2 * parts + 1 :]
     grads = outs[:EXP_FF]
     downs = outs[EXP_FF : 2 * EXP_FF]
     adapt = outs[2 * EXP_FF : 2 * EXP_FF + 3]
@@ -761,10 +959,16 @@
         low = hids[j].at[:, pl.ds(wide + LANES, LANES)]
         copies.append(pltpu.make_async_copy(low, near, sems.at[2 * EXP_FF + j]))
     copies.append(pltpu.make_async_copy(rights, block.at[pl.ds(width, LANES)], sems.at[3 * EXP_FF]))
+    expert = row // (parts // EXP_FF)
     for m in range(parts):
         owner = jnp.bitwise_xor(row, m)
         where = pl.ds(pl.multiple_of(owner * depth, depth), depth)
-        copies.append(pltpu.make_async_copy(pieces[m], block.at[where], sems.at[3 * EXP_FF + 1 + m]))
+        inner = inners[m] if m else inners[0].at[expert]
+        last = lasts[m] if m else lasts[0].at[expert]
+        near = block.at[where, pl.ds(0, 2 * units)]
+        copies.append(pltpu.make_async_copy(inner, near, sems.at[3 * EXP_FF + 1 + m]))
+        near = block.at[where, pl.ds(2 * units, units)]
+        copies.append(pltpu.make_async_copy(last, near, sems.at[3 * EXP_FF + 1 + parts + m]))
     for copy in copies:
         copy.start()
     for copy in copies:
@@ -839,10 +1043,10 @@
         ).astype(BF16)
 
 
-def feed_forward(hids, cots, pieces, rights):
-    parts = len(pieces)
-    depth, triple = pieces[0].shape
-    units = triple // 3
+def feed_forward(hids, cots, inners, lasts, rights):
+    parts = len(inners)
+    depth, units = lasts[1].shape
+    triple = 3 * units
     width = depth * parts
     rows = EXP_FF * CAP_FF
     hbm = pl.BlockSpec(memory_space=pl.ANY)
@@ -853,7 +1057,7 @@
         out_shape=[jax.ShapeDtypeStruct((CAP_FF, wide + LANES), BF16)] * EXP_FF
         + [jax.ShapeDtypeStruct((CAP_FF, wide), BF16)] * EXP_FF
         + [jax.ShapeDtypeStruct((LANES, units), BF16)] * 3,
-        in_specs=[hbm] * (2 * EXP_FF + parts + 1),
+        in_specs=[hbm] * (2 * EXP_FF + 2 * parts + 1),
         out_specs=[vmem] * (2 * EXP_FF + 3),
         scratch_shapes=[
             pltpu.VMEM((rows, wide + LANES), BF16),
@@ -861,10 +1065,10 @@
             pltpu.VMEM((wide, triple), BF16),
             pltpu.VMEM((rows, triple), BF16),
             pltpu.VMEM((rows, 1), F32),
-            pltpu.SemaphoreType.DMA((3 * EXP_FF + 1 + parts,)),
+            pltpu.SemaphoreType.DMA((3 * EXP_FF + 1 + 2 * parts,)),
         ],
         compiler_params=pltpu.CompilerParams(vmem_limit_bytes=56 * 2**20),
-    )(*hids, *cots, *pieces, rights)
+    )(*hids, *cots, *inners, *lasts, rights)
 
 
 def on_device(
@@ -910,9 +1114,6 @@
     cosine, sine = tables(count, HEAD_DIM)
     scaling = HEAD_DIM ** (-0.5)
 
-    def swap(value, offset):
-        return lax.ppermute(value, "row", [(i, i ^ offset) for i in range(rows_axis)])
-
     def features(part):
         return lax.all_gather(part, "col", axis=1, tiled=True)
 
@@ -951,21 +1152,12 @@
     padding = -units % LANES
 
     def padded(value):
-        return jnp.pad(value, ((0, 0), (0, padding))) if padding else value
-
-    near = []
-    for j in range(EXP_FF):
-        which = expert ^ j
-        inner_own = lax.dynamic_index_in_dim(inner_weight, which, 0, keepdims=False)
-        down_own = lax.dynamic_index_in_dim(down_weight, which, 0, keepdims=False)
-        piece = jnp.concatenate(
-            [padded(inner_own[:, 0]), padded(inner_own[:, 1]), padded(down_own)], axis=1
-        )
-        near.append(swap(later(piece, out_full), j * replicas) if j else piece)
-    chunks = []
-    for j in range(EXP_FF):
-        for i in range(replicas):
-            chunks.append(swap(near[j], i) if i else near[j])
+        if not padding:
+            return value
+        return jnp.pad(value, [(0, 0)] * (value.ndim - 1) + [(0, padding)])
+
+    inner_flat = padded(inner_weight).reshape(EXP_FF, depth, 2 * (units + padding))
+    down_flat = padded(down_weight)
 
     picks = lax.all_gather(adapter_pick, "row", axis=0, tiled=True)
     pick_onehot = (picks[:, None] == jnp.arange(ADAPT, dtype=jnp.int32)[None, :]).astype(BF16)
@@ -989,15 +1181,6 @@
         [padded(right_inner_all[:, 0]), padded(right_inner_all[:, 1]), padded(right_down_all)],
         axis=1,
     )
-    own_adapter = (jnp.arange(ADAPT, dtype=jnp.int32) == adapter).astype(F32)
-
-    def spread(low):
-        return (own_adapter[None, :, None] * low[:, None, :]).reshape(count, ADAPT * RANK)
-
-    def unspread(high):
-        return jnp.sum(
-            own_adapter[None, :, None] * high.reshape(count, ADAPT, RANK), axis=1
-        )
 
     slots_attn = slot_rows(attn_route, EXP_ATT, CAP_ATT)
     slots_ffn = slot_rows(ffn_route, EXP_FF, CAP_FF)
@@ -1077,57 +1260,40 @@
     probs = probability.astype(BF16)
     attended = mm("hkbj,jhd->kbhd", probs, values).astype(BF16).reshape(TOPK * count, query_width)
     attended_rows = mm("cx,xw->cw", pick_attn_both, attended).astype(BF16)
+    attended_rows = later(attended_rows, inner_flat)
     out_rows = mm(
         "ecw,edw->ecd", attended_rows.reshape(EXP_ATT, CAP_ATT, query_width), out_full
     ).reshape(EXP_ATT * CAP_ATT, width)
-    low_rows = mm("cw,rw->cr", attended_rows, right_out.astype(BF16))
-    out_ext = (jnp.concatenate([out_rows, low_rows], axis=1) * gate_rows).astype(BF16)
-    combined = mm("ct,cd->td", pick_attn_any, out_ext)
-    low_out_part = combined[:, width:]
-    branch_attn = combined[:, :width] + mm("tr,rd->td", low_out_part.astype(BF16), left_out)
-    x_local = inputs.astype(F32)
-    middle = x_local + partials(branch_attn)
-    square_sum, low_out_full, grad_low_down = lax.psum(
-        (jnp.sum(middle * middle, axis=1), low_out_part, grad_low_down_part), "col"
-    )
-    scale_two = lax.rsqrt(square_sum[:, None] / width + EPSILON)
-    hidden_two = features((middle * scale_two * own_columns(norm_two)).astype(BF16))
-
-    chosen_ffn = chosen_of(mm("td,de->te", hidden_two, router_ffn), ffn_route, EXP_FF)
-    gates_ffn = jax.nn.softmax(chosen_ffn, axis=1)
-    rank_inner = mm("td,rd->tr", hidden_two, left_inner)
-    hidden_ext = jnp.concatenate([hidden_two, spread(rank_inner).astype(BF16)], axis=1)
-    hidden_out = mm("ct,td->cd", pick_ffn_any, hidden_ext).astype(BF16)
-    gate_high = lax.reduce_precision(gates_ffn, 8, 7)
-    gate_low = (gates_ffn - gate_high).astype(BF16)
-    gate_high = gate_high.astype(BF16)
-    gate_out = sum(
-        mm("ct,tx->cx", pick_ffn[k], jnp.stack([gate_high[:, k], gate_low[:, k]], axis=1))
-        for k in range(TOPK)
-    )
-    gate_out = jnp.pad(gate_out, ((0, 0), (0, 126))).astype(BF16)
-    cot_ext = mm("ct,td->cd", pick_ffn_any, spread(grad_low_down).astype(BF16)).astype(BF16)
-    hidden_in = trade_rows(
-        blocks_of(jnp.concatenate([hidden_out, gate_out, cot_ext], axis=1)), replicas, 3
-    )
-    results = feed_forward(hidden_in, cot_rows, chunks, ffn_right)
+    out_rows = (out_rows * gate_rows).astype(BF16)
+    low_rows = mm("cw,rw->cr", attended_rows, right_out.astype(BF16)) * gate_rows
+    low_rows = jnp.pad(low_rows.astype(BF16), ((0, 0), (RANK, LANES - 2 * RANK)))
+    lefts_flat = lefts.reshape(5 * RANK, width)
+
+    *outs, hidden_two, middle, stat_ffn, totals_attn = middle_forward(
+        adapter_pick,
+        norm_two[None, :],
+        router_ffn.T,
+        table_of(ffn_route[:, 0:1].astype(F32), ffn_route[:, 1:2].astype(F32), valid[:, None]),
+        low_rows,
+        jnp.pad(grad_low_down_part, ((0, 0), (2 * RANK, LANES - 3 * RANK))),
+        [out_rows, pick_attn_any, pick_ffn[0], pick_ffn[1], lefts_flat, inputs],
+        [inner_flat, down_flat],
+        rows_axis,
+        cols,
+        replicas,
+    )
+    inners = [inner_flat, *outs[: rows_axis - 1]]
+    lasts = [down_flat, *outs[rows_axis - 1 : 2 * rows_axis - 2]]
+    hidden_in = outs[2 * rows_axis - 2 :]
+    results = feed_forward(hidden_in, cot_rows, inners, lasts, ffn_right)
     grad_middle, grad_full, totals, branch_ffn, low_down_part = middle_back(
         results[:EXP_FF],
         results[EXP_FF : 2 * EXP_FF],
         adapter_pick,
         norm_two[None, :],
         router_ffn.T,
-        table_of(
-            gates_ffn[:, 0:1],
-            gates_ffn[:, 1:2],
-            chosen_ffn[:, 0:1],
-            chosen_ffn[:, 1:2],
-            scale_two,
-            ffn_route[:, 0:1].astype(F32),
-            ffn_route[:, 1:2].astype(F32),
-            valid[:, None],
-        ),
-        [pick_ffn[0], pick_ffn[1], lefts.reshape(5 * RANK, width), hidden_two, middle, cotangent],
+        stat_ffn,
+        [pick_ffn[0], pick_ffn[1], lefts_flat, hidden_two, middle, cotangent],
         cols,
         replicas,
     )
@@ -1136,7 +1302,8 @@
         value[:, :units].reshape(ADAPT, RANK, units).astype(F32) for value in rights_ffn
     ]
 
-    output = ((middle + partials(branch_ffn)) * valid[:, None]).astype(BF16)
+    branch_own = partials(branch_ffn)
+    output = ((middle + branch_own) * valid[:, None]).astype(BF16)
 
     grad_low_out = mm("td,rd->tr", grad_full, left_out)
     grad_middle_rows = mm("ct,td->cd", pick_attn_any, grad_full).astype(BF16)
@@ -1200,15 +1367,16 @@
         jnp.concatenate([grad_rank_query, grad_rank_kv, low_down_part[:, RANK : 2 * RANK]], axis=1),
         ((0, 0), (RANK, LANES - 4 * RANK)),
     )
-    lows = (jnp.pad(low_out_full, ((0, 0), (0, LANES - RANK))) + jnp.where(
+    lows = jnp.where(lanes < RANK, jnp.roll(totals_attn, -RANK, axis=1), 0.0) + jnp.where(
         (lanes >= RANK) & (lanes < 2 * RANK), totals, 0.0
-    )).astype(BF16)
+    )
+    lows = lows.astype(BF16)
     right_parts = jnp.concatenate(
         [grad_right_query, grad_right_kv[:, 0], grad_right_kv[:, 1], grad_right_out], axis=1
     ).astype(BF16)
     grad_inputs, *grads = input_back(
         picks,
-        grad_one_part,
+        later(grad_one_part, output, *rights_ffn),
         small,
         norm_one[None, :],
         router_attn.T,

time: 746 us -> 666 us (0.89)
  waiting for transfers between devices: 156 us -> 5.5 us
  Pallas kernels: 317 us -> 418 us
  blocking collectives: 23.7 us -> 8.37 us
  matrix products: 106 us -> 91.1 us
  local copies, waits for them, and re-layouts: 70 us -> 81.7 us
  starting transfers between devices: 16.4 us -> 6.4 us
    pallas_call x1, Pallas kernels: 36.7 us -> 132 us  [middle_forward(): pl.pallas_call(functools.partial(middle_kernel, parts_axis, cols, replica...]
    ppermute x7 -> x0, waiting for transfers between devices: 87.7 us -> none  [swap(): lax.ppermute(value, 'row', [(i, i ^ offset) for i in range(rows_axis)])]
    all_gather x1, waiting for transfers between devices: 41.1 us -> 5.33 us  [on_device(): lax.all_gather(later(out_weight, query_full), 'row', axis=1, tiled=True)]
    reduce_scatter x2 -> x1, waiting for transfers between devices: 27.5 us -> 0.01 us  [partials(): lax.psum_scatter(part.astype(BF16), 'col', scatter_dimension=1, tiled=True)]
    psum x1 -> x0, blocking collectives: 15.3 us -> none  [on_device(): lax.psum((jnp.sum(middle * middle, axis=1), low_out_part, grad_low_down_p...]
    dot_general x44 -> x36, matrix products: 99.2 us -> 84.3 us  [mm(): return jnp.einsum(spec, a, b, preferred_element_type=F32)]
    reshape x0 -> x1, local copies, waits for them, and re-layouts: none -> 14 us  [on_device(): padded(inner_weight).reshape(EXP_FF, depth, 2 * (units + padding))]
    ppermute x7 -> x0, starting transfers between devices: 10.1 us -> none  [swap(): lax.ppermute(value, 'row', [(i, i ^ offset) for i in range(rows_axis)])]
  transfers between devices with their start and end apart: 14 -> 5, of which waited for: 5 -> 1; matrix products, arithmetic and copies ran while one was open for 22% -> 24% of each run, Pallas kernels for 28% -> 15%
where the time goes in v5:
time: 666 us; the launch traced here: 656 us
  Pallas kernels  418 us (63%)
  matrix products  91.1 us (14%)
  local copies, waits for them, and re-layouts  81.7 us (12%)
  other arithmetic  27.9 us (4%)
  between operations  16.8 us (3%)
  blocking collectives  8.37 us (1%)
    pallas_call x1, Pallas kernels, middle_forward(): pl.pallas_call(functools.partial(middle_kernel, parts_axis, cols, replica...  132 us
    pallas_call x1, Pallas kernels, gather_all(): pl.pallas_call(functools.partial(gather_kernel, parts, cols, replicas, co...  107 us
    pallas_call x1, Pallas kernels, middle_back(): pl.pallas_call(functools.partial(middle_back_kernel, cols, replicas), out...  98.7 us
    dot_general x36, matrix products, mm(): return jnp.einsum(spec, a, b, preferred_element_type=F32)  84.3 us
    pallas_call x1, Pallas kernels, feed_forward(): pl.pallas_call(functools.partial(ffn_kernel, parts, depth, width, units),...  42.3 us
    pallas_call x1, Pallas kernels, input_back(): pl.pallas_call(functools.partial(input_back_kernel, parts_axis, cols), ou...  37.4 us
    unnamed x248, local copies, waits for them, and re-layouts  31.8 us
    reshape x1, local copies, waits for them, and re-layouts, on_device(): padded(inner_weight).reshape(EXP_FF, depth, 2 * (units + padding))  14 us
  transfers between devices with their start and end apart: 5, of which 1 were waited for; matrix products, arithmetic and copies ran while one was open for 24% of the time, Pallas kernels for 15%

profile of v5, /device:TPU:9, one launch (start us, length us, event | category | flops | bytes accessed | tf_op | source)
XLA Modules:
  0.0 655.5 jit_solution(12734845809766615324)
XLA Ops:
  7.9 1.5 copy.251.refs_1_
  9.4 107.1 %shard_map.328 = (bf16[2,2048,512]{2,1,0:T(8,128)(2,1)}, bf16[8,2048,512]{2,1,0:T(8,128)(2,1)}, bf16[256,2048]{1,0:T(8,128)(2,1)}, bf16[160,2048]{1,0:T(8,128)(2...) custom-call(s32[1]{0:T(128)} %copy.362.refs_0_, s32[256,2]{1,0:T(8,128)} %copy.251.refs_1_, ...), custom_call_target="tpu_custom_call" | custom-call | tf_op jit(solution)/shard_map/pallas_call | solution.py:221
  118.6 8.4 %all-reduce.5.refs_0_ = s32[8]{0:T(128)S(1)} all-reduce(s32[8]{0:T(128)S(1)} %dynamic-update-slice), channel_id=1, replica_groups=mesh['row'=8,'col'=4] {'row'}, use_global_device_ids=true, to_apply=%add.5 | all-reduce | flops 8 | bytes 64
  128.4 5.9 all-to-all-start
  134.3 2.0 copy.271
  136.9 1.6 fusion.4.refs_8_
  141.1 1.1 select_select_fusion
  142.4 1.2 fusion.63
  144.4 1.1 fusion.21
  146.4 4.8 fusion.14
  151.3 1.1 pad_maximum_fusion.refs_24_
  153.4 4.1 fusion.121
  158.3 2.8 copy.260
  161.1 14.0 %reshape.422.refs_12_.refs_8_ = bf16[4,256,2816]{2,1,0:T(8,128)(2,1)} reshape(bf16[4,256,2,1408]{3,2,1,0:T(2,128)(2,1)} %param.38) | data formatting | bytes 11534336 | tf_op jit(solution)/shard_map/reshape | solution.py:1159
  180.9 1.1 convolution_add_fusion.3
  183.1 1.4 convolution_convert_fusion.8
  184.6 2.0 reshape.420
  186.5 2.1 copy.281
  189.4 1.1 copy.314
  191.5 1.9 subtract_convert_fusion.2
  193.4 3.5 fusion.114
  196.9 2.7 fusion.8
  199.7 2.2 copy.265
  201.9 1.7 convolution_convert_fusion.5
  207.2 5.3 all-gather.3.cloned.1.call-done
  212.5 13.4 %fusion.124 = f32[8,80,2048]{2,1,0:T(8,128)} fusion(bf16[8,80,512]{2,1,0:T(8,128)(2,1)} %bitcast.244, bf16[8,2048,512]{2,1,0:T(8,128)(2,1)} %all-gather.3.cloned.1.call-done), kind=kOutput, calls=%fused_computation.230 | convolution fusion | flops 1342177280 | bytes 22675456 | tf_op jit(solution)/shard_map/ecw,edw->ecd/dot_general | solution.py:27
  226.0 4.4 fusion.1.refs_6_
  230.4 132.2 %shard_map.329 = (bf16[256,2816]{1,0:T(8,128)(2,1)}, bf16[256,2816]{1,0:T(8,128)(2,1)}, bf16[256,2816]{1,0:T(8,128)(2,1)}, bf16[256,2816]{1,0:T(8,128)(2,1)}, bf...) custom-call(s32[1]{0:T(128)} %copy.363.refs_0_.refs_8_, ...), custom_call_target="tpu_custom_call" | custom-call | tf_op jit(solution)/shard_map/pallas_call | solution.py:903
  367.4 42.3 %shard_map.330 = (bf16[160,2304]{1,0:T(8,128)(2,1)}, bf16[160,2304]{1,0:T(8,128)(2,1)}, bf16[160,2304]{1,0:T(8,128)(2,1)}, bf16[160,2304]{1,0:T(8,128)(2,1)}, bf...) custom-call(bf16[160,2432]{1,0:T(8,128)(2,1)} %get-tuple-element.79., ...), custom_call_target="tpu_custom_call" | custom-call | tf_op jit(solution)/shard_map/pallas_call | solution.py:1055
  409.8 1.1 copy-done.9
  410.9 1.1 copy-done.10
  412.0 1.1 copy-done.11
  413.1 1.1 copy-done.12
  414.2 98.7 %shard_map.331 = (f32[256,512]{1,0:T(8,128)S(1)}, bf16[256,2048]{1,0:T(8,128)(2,1)}, f32[256,128]{1,0:T(8,128)S(1)}, bf16[256,2048]{1,0:T(8,128)(2,1)}, f32[256,128]{1,0:T(8,128)S(1)}) custom-call(bf16[160,2304]{1,0:T(8,128)(2,1)} %get-tuple-element.101.refs_0_, bf16[160,2304]{1,0:T(8,128)(2,1)} %get-tuple-element.102.refs_1_, ...), custom_call_target="tpu_custom_call" | custom-call | tf_op jit(solution)/shard_map/pallas_call | solution.py:507
  517.2 1.6 copy.279
  519.7 1.5 convolution_convert_fusion.1
  521.6 10.0 %fusion.125 = f32[8,80,512]{2,1,0:T(8,128)} fusion(bf16[8,80,2048]{2,1,0:T(8,128)(2,1)S(1)} %bitcast.242, bf16[8,2048,512]{2,1,0:T(8,128)(2,1)} %all-gather.3.cloned.1.call-done), kind=kOutput, calls=%fused_computation.231 | convolution fusion | flops 1342177280 | bytes 20709376 | tf_op jit(solution)/shard_map/ecd,edw->ecw/dot_general | solution.py:27
  531.5 3.2 multiply_reduce_fusion.1
  534.7 3.0 convolution_convert_fusion.6
  537.7 2.0 reshape.431
  539.7 2.1 copy.285
  541.8 2.5 multiply_reduce_fusion
  545.3 1.5 fusion.7
  546.8 1.2 fusion.10
  548.0 1.2 fusion.11
  551.7 1.5 subtract_convert_fusion.1
  554.1 1.8 copy.284
  555.9 1.8 copy.287
  557.7 1.8 copy.288
  559.5 1.3 convolution_convert_fusion.9
  560.8 1.9 fusion.115
  568.3 2.1 copy.280
  570.4 2.6 convolution_convert_fusion.4
  573.0 12.7 %convolution_convert_fusion.3 = bf16[8,80,2048]{2,1,0:T(8,128)(2,1)} fusion(bf16[8,80,512]{2,1,0:T(8,128)(2,1)} %bitcast.260, bf16[8,2048,512]{2,1,0:T(8,128)(2,1)} %get-tuple-element.75), kind=kOutput, calls=%fused_computation.6 | convolution fusion | flops 1343488000 | bytes 20054016 | tf_op jit(solution)/shard_map/ecw,edw->ecd/dot_general | solution.py:27
  586.8 1.3 fusion.49.refs_2_
  588.1 3.9 convolution_bitcast_fusion
  593.2 1.8 convolution_add_fusion.1.refs_1_
  595.0 1.6 copy.292
  596.5 1.5 copy.293
  599.0 2.8 maximum_convert_fusion.1
  601.8 1.8 multiply_convert_fusion.3
  603.6 1.0 copy-done.17
  604.6 37.4 %shard_map.332 = (f32[256,512]{1,0:T(8,128)S(1)}, f32[8,16,256]{2,1,0:T(8,128)S(1)}, f32[8,16,256]{2,1,0:T(8,128)S(1)}, f32[8,16,256]{2,1,0:T(8,128)S(1)}, f32[8...) custom-call(s32[8]{0:T(128)S(1)} %copy-done.32, ...), custom_call_target="tpu_custom_call" | custom-call | tf_op jit(solution)/shard_map/pallas_call | solution.py:676
  642.1 1.2 copy.294
  (349 shorter events, 50.2 us)
Async XLA Ops:
  7.2 150.3 %copy-start = (bf16[8,16,2,512]{3,2,1,0:T(2,128)(2,1)S(1)}, bf16[8,16,2,512]{3,2,1,0:T(2,128)(2,1)}, u32[]{:S(2)}) copy-start(bf16[8,16,2,512]{3,2,1,0:T(2,128)(2,1)} %param.43) | copy-start | bytes 786436
  7.2 205.3 %all-gather.3.cloned.1.call-start = ((), (), s32[]{:S(2)}) async-start(), calls=%async_computation.2 | async-start | bytes 18874368 | tf_op jit(solution)/shard_map/all_gather | solution.py:1150
  9.4 107.9 %copy-start.112 = (u32[32]{0:T(128)S(1)}, u32[32]{0:T(128)}, u32[]{:S(2)}) copy-start(u32[32]{0:T(128)} %constant.98) | copy-start | bytes 388
  9.4 117.6 %copy-start.82 = (bf16[8,256,16]{1,2,0:T(8,128)(2,1)S(1)}, bf16[8,256,16]{1,2,0:T(8,128)(2,1)}, u32[]{:S(2)}) copy-start(bf16[8,256,16]{1,2,0:T(8,128)(2,1)} %param.40) | copy-start | bytes 196612
  9.4 117.6 %copy-start.83 = (bf16[8,256,16]{1,2,0:T(8,128)(2,1)S(1)}, bf16[8,256,16]{1,2,0:T(8,128)(2,1)}, u32[]{:S(2)}) copy-start(bf16[8,256,16]{1,2,0:T(8,128)(2,1)} %param.42) | copy-start | bytes 196612
  9.4 117.6 %copy-start.84 = (bf16[8,256,16]{1,2,0:T(8,128)(2,1)S(1)}, bf16[8,256,16]{1,2,0:T(8,128)(2,1)}, u32[]{:S(2)}) copy-start(bf16[8,256,16]{1,2,0:T(8,128)(2,1)} %param.44) | copy-start | bytes 196612
  9.4 117.7 %copy-start.85 = (bf16[8,256,16]{1,2,0:T(8,128)(2,1)S(1)}, bf16[8,256,16]{1,2,0:T(8,128)(2,1)}, u32[]{:S(2)}) copy-start(bf16[8,256,16]{1,2,0:T(8,128)(2,1)} %param.46) | copy-start | bytes 196612
  116.6 10.5 %copy-start.86 = (bf16[8,256,16]{1,2,0:T(8,128)(2,1)S(1)}, bf16[8,256,16]{1,2,0:T(8,128)(2,1)}, u32[]{:S(2)}) copy-start(bf16[8,256,16]{1,2,0:T(8,128)(2,1)} %param.48) | copy-start | bytes 196612
  116.6 17.7 %copy-start.88 = (s32[256,2]{0,1:T(2,128)S(1)}, s32[256,2]{0,1:T(2,128)}, u32[]{:S(2)}) copy-start(s32[256,2]{0,1:T(2,128)} %param.29) | copy-start | bytes 6148
  116.6 17.7 %copy-start.79 = (s32[256,2]{0,1:T(2,128)S(1)}, s32[256,2]{0,1:T(2,128)}, u32[]{:S(2)}) copy-start(s32[256,2]{0,1:T(2,128)} %param.30) | copy-start | bytes 6148
  127.0 9.4 %copy-start.31 = (s32[8]{0:T(128)}, s32[8]{0:T(128)S(1)}, u32[]{:S(2)}) copy-start(s32[8]{0:T(128)S(1)} %all-reduce.5.refs_0_) | copy-start | bytes 100
  127.1 9.2 %copy-start.37 = (bf16[256,2048]{1,0:T(8,128)(2,1)S(1)}, bf16[256,2048]{1,0:T(8,128)(2,1)}, u32[]{:S(2)}) copy-start(bf16[256,2048]{1,0:T(8,128)(2,1)} %get-tuple-element.74) | copy-start | bytes 3145732
  127.6 9.3 %copy-start.27 = (f32[2048]{0:T(1024)S(1)}, f32[2048]{0:T(1024)}, u32[]{:S(2)}) copy-start(f32[2048]{0:T(1024)} %param.31) | copy-start | bytes 24580
  128.4 47.0 %all-to-all-start = ((bf16[8,80,256]{2,1,0:T(8,128)(2,1)}), bf16[8,80,256]{2,1,0:T(8,128)(2,1)S(1)}, u32[]{:S(2)}, u32[]{:S(2)}) async-start(bf16[8,80,256]{2,1,0:T(8,128)(2,1)} %copy.255), calls=%async_computation | async-start | bytes 655360 | tf_op jit(solution)/shard_map/all_to_all | solution.py:1170
  134.2 460.7 %all-reduce.9.cloned.1.call-start = ((), (), s32[]{:S(2)}) async-start(), calls=%async_computation.5 | async-start | bytes 2162688 | tf_op jit(solution)/shard_map/psum | solution.py:1300
  136.9 6.7 %copy-start.3 = (bf16[256,512]{1,0:T(8,128)(2,1)S(1)}, bf16[256,512]{1,0:T(8,128)(2,1)}, u32[]{:S(2)}) copy-start(bf16[256,512]{1,0:T(8,128)(2,1)} %refs_17_.1) | copy-start | bytes 786436
  138.9 7.4 %copy-start.80 = (f32[256,2]{0,1:T(2,128)}, f32[256,2]{0,1:T(2,128)S(1)}, u32[]{:S(2)}) copy-start(f32[256,2]{0,1:T(2,128)S(1)} %get-tuple-element.206) | copy-start | bytes 6148
  138.9 7.4 %copy-start.94 = (f32[256]{0:T(256)}, f32[256]{0:T(256)S(1)}, u32[]{:S(2)}) copy-start(f32[256]{0:T(256)S(1)} %reduce_max.18) | copy-start | bytes 3076
  139.0 7.3 %copy-start.104 = (pred[128]{0:T(512)(128)(4,1)}, pred[128]{0:T(512)(128)(4,1)S(1)}, u32[]{:S(2)}) copy-start(pred[128]{0:T(512)(128)(4,1)S(1)} %get-tuple-element.266) | copy-start | bytes 388
  139.0 7.3 %copy-start.106 = (pred[128]{0:T(512)(128)(4,1)}, pred[128]{0:T(512)(128)(4,1)S(1)}, u32[]{:S(2)}) copy-start(pred[128]{0:T(512)(128)(4,1)S(1)} %get-tuple-element.267) | copy-start | bytes 388
  139.1 7.3 %copy-start.102 = (f32[256]{0:T(256)}, f32[256]{0:T(256)S(1)}, u32[]{:S(2)}) copy-start(f32[256]{0:T(256)S(1)} %fusion.106) | copy-start | bytes 3076
  139.1 7.3 %copy-start.96 = (f32[256]{0:T(256)}, f32[256]{0:T(256)S(1)}, u32[]{:S(2)}) copy-start(f32[256]{0:T(256)S(1)} %fusion.90) | copy-start | bytes 3076
  139.4 40.2 %copy-start.73 = (s32[256,1]{0,1:T(1,128)}, s32[256,1]{0,1:T(1,128)S(1)}, u32[]{:S(2)}) copy-start(s32[256,1]{0,1:T(1,128)S(1)} %get-tuple-element.243) | copy-start | bytes 3076
  139.4 40.2 %copy-start.76 = (s32[256,1]{0,1:T(1,128)}, s32[256,1]{0,1:T(1,128)S(1)}, u32[]{:S(2)}) copy-start(s32[256,1]{0,1:T(1,128)S(1)} %get-tuple-element.244) | copy-start | bytes 3076
  143.6 48.0 %copy-start.44 = (f32[256,64]{1,0:T(8,128)}, f32[256,64]{1,0:T(8,128)S(1)}, u32[]{:S(2)}) copy-start(f32[256,64]{1,0:T(8,128)S(1)} %get-tuple-element.251) | copy-start | bytes 196612
  144.4 6.9 %copy-start.40 = (bf16[8,16,2,1408]{3,1,0,2:T(8,128)(2,1)S(1)}, bf16[8,16,2,1408]{3,1,0,2:T(8,128)(2,1)}, u32[]{:S(2)}) copy-start(bf16[8,16,2,1408]{3,1,0,2:T(8,128)(2,1)} %copy.271) | copy-start | bytes 2162692
  145.5 7.9 %copy-start.33 = (bf16[8,2048,512]{2,1,0:T(8,128)(2,1)S(1)}, bf16[8,2048,512]{2,1,0:T(8,128)(2,1)}, u32[]{:S(2)}) copy-start(bf16[8,2048,512]{2,1,0:T(8,128)(2,1)} %get-tuple-element.75) | copy-start | bytes 50331652
  146.4 4.9 copy-start.61
  157.5 18.9 %copy-start.70 = (bf16[1,16,2,512]{3,2,1,0:T(2,128)(2,1)}, bf16[1,16,2,512]{3,2,1,0:T(2,128)(2,1)S(1)}, u32[]{:S(2)}) copy-start(bf16[1,16,2,512]{3,2,1,0:T(2,128)(2,1)S(1)} %constant_dynamic-slice_fusion) | copy-start | bytes 98308
  175.1 28.5 %copy-start.89 = (f32[640]{0:T(1024)}, f32[640]{0:T(1024)S(1)}, u32[]{:S(2)}) copy-start(f32[640]{0:T(1024)S(1)} %add.138) | copy-start | bytes 7684
  183.1 5.5 slice-start
  188.6 4.8 copy-start.87
  196.9 4.9 copy-start.63
  212.5 13.4 %copy-start.90 = (f32[640]{0:T(1024)S(1)}, f32[640]{0:T(1024)}, u32[]{:S(2)}) copy-start(f32[640]{0:T(1024)} %copy-done.89) | copy-start | bytes 7684
  225.9 4.4 copy-start.4
  226.0 4.4 copy-start.13
  226.0 4.4 copy-start.14
  226.0 4.4 copy-start.15
  226.0 4.4 copy-start.26
  367.4 42.4 %copy-start.21 = (f32[256,128]{1,0:T(8,128)S(1)}, f32[256,128]{1,0:T(8,128)}, u32[]{:S(2)}) copy-start(f32[256,128]{1,0:T(8,128)} %copy-done.20) | copy-start | bytes 393220
  367.4 42.4 %copy-start.30 = (f32[2048]{0:T(1024)S(1)}, f32[2048]{0:T(1024)}, u32[]{:S(2)}) copy-start(f32[2048]{0:T(1024)} %param.32) | copy-start | bytes 24580
  409.8 192.0 %reduce-scatter.2.cloned.1.call-start = ((), (), s32[]{:S(2)}) async-start(), calls=%async_computation.3 | async-start | bytes 1310720 | tf_op jit(solution)/shard_map/reduce_scatter | solution.py:1121
  414.2 101.8 %copy-start.81 = (f32[256,2]{0,1:T(2,128)S(1)}, f32[256,2]{0,1:T(2,128)}, u32[]{:S(2)}) copy-start(f32[256,2]{0,1:T(2,128)} %copy-done.80) | copy-start | bytes 6148
  414.2 101.8 %copy-start.95 = (f32[256]{0:T(256)S(1)}, f32[256]{0:T(256)}, u32[]{:S(2)}) copy-start(f32[256]{0:T(256)} %copy-done.94) | copy-start | bytes 3076
  414.2 101.8 %copy-start.97 = (f32[256]{0:T(256)S(1)}, f32[256]{0:T(256)}, u32[]{:S(2)}) copy-start(f32[256]{0:T(256)} %copy-done.96) | copy-start | bytes 3076
  514.4 5.3 copy-start.2
  514.4 89.1 %all-gather.5.cloned.1.call-start = ((), (), s32[]{:S(2)}) async-start(), calls=%async_computation.4 | async-start | bytes 1310720 | tf_op jit(solution)/shard_map/all_gather | solution.py:1118
  521.6 10.0 %copy-start.74 = (s32[256,1]{0,1:T(1,128)S(1)}, s32[256,1]{0,1:T(1,128)}, u32[]{:S(2)}) copy-start(s32[256,1]{0,1:T(1,128)} %copy-done.73) | copy-start | bytes 3076
  521.6 10.0 %copy-start.77 = (s32[256,1]{0,1:T(1,128)S(1)}, s32[256,1]{0,1:T(1,128)}, u32[]{:S(2)}) copy-start(s32[256,1]{0,1:T(1,128)} %copy-done.76) | copy-start | bytes 3076
  534.7 7.1 %copy-start.99 = (f32[4,2,256]{2,1,0:T(2,128)S(1)}, f32[4,2,256]{2,1,0:T(2,128)}, u32[]{:S(2)}) copy-start(f32[4,2,256]{2,1,0:T(2,128)} %copy-done.98) | copy-start | bytes 24580
  551.7 7.7 %copy-start.93 = (bf16[256,16,1]{0,1,2:T(8,128)(2,1)S(1)}, bf16[256,16,1]{0,1,2:T(8,128)(2,1)}, u32[]{:S(2)}) copy-start(bf16[256,16,1]{0,1,2:T(8,128)(2,1)} %copy-done.92) | copy-start | bytes 24580
  553.2 7.6 %copy-start.71 = (bf16[1,16,2,512]{3,2,1,0:T(2,128)(2,1)S(1)}, bf16[1,16,2,512]{3,2,1,0:T(2,128)(2,1)}, u32[]{:S(2)}) copy-start(bf16[1,16,2,512]{3,2,1,0:T(2,128)(2,1)} %copy-done.70) | copy-start | bytes 98308
  553.2 9.5 %copy-start.67 = (f32[256,64]{0,1:T(8,128)S(1)}, f32[256,64]{0,1:T(8,128)}, u32[]{:S(2)}) copy-start(f32[256,64]{0,1:T(8,128)} %copy.279) | copy-start | bytes 196612
  562.9 4.6 copy-start.25
  573.0 12.7 %copy-start.110 = (pred[128]{0:T(512)(128)(4,1)S(1)}, pred[128]{0:T(512)(128)(4,1)}, u32[]{:S(2)}) copy-start(pred[128]{0:T(512)(128)(4,1)} %get-tuple-element.270) | copy-start | bytes 388
  573.0 12.7 %copy-start.111 = (pred[128]{0:T(512)(128)(4,1)S(1)}, pred[128]{0:T(512)(128)(4,1)}, u32[]{:S(2)}) copy-start(pred[128]{0:T(512)(128)(4,1)} %get-tuple-element.271) | copy-start | bytes 388
  573.0 13.7 %copy-start.105 = (pred[128]{0:T(512)(128)(4,1)S(1)}, pred[128]{0:T(512)(128)(4,1)}, u32[]{:S(2)}) copy-start(pred[128]{0:T(512)(128)(4,1)} %copy-done.104) | copy-start | bytes 388
  573.0 13.8 %copy-start.107 = (pred[128]{0:T(512)(128)(4,1)S(1)}, pred[128]{0:T(512)(128)(4,1)}, u32[]{:S(2)}) copy-start(pred[128]{0:T(512)(128)(4,1)} %copy-done.106) | copy-start | bytes 388
  573.0 13.8 %copy-start.108 = (f32[1,256]{1,0:T(1,128)S(1)}, f32[1,256]{1,0:T(1,128)}, u32[]{:S(2)}) copy-start(f32[1,256]{1,0:T(1,128)} %fusion.20) | copy-start | bytes 3076
  573.0 13.8 %copy-start.109 = (f32[1,256]{1,0:T(1,128)S(1)}, f32[1,256]{1,0:T(1,128)}, u32[]{:S(2)}) copy-start(f32[1,256]{1,0:T(1,128)} %fusion.22) | copy-start | bytes 3076
  599.0 4.5 copy-start.23
  599.0 4.5 copy-start.28
  599.0 4.5 copy-start.32
  642.0 6.7 %copy-start.1 = (bf16[8,16,2,512]{3,2,1,0:T(2,128)(2,1)S(1)}, bf16[8,16,2,512]{3,2,1,0:T(2,128)(2,1)}, u32[]{:S(2)}) copy-start(bf16[8,16,2,512]{3,2,1,0:T(2,128)(2,1)} %param.43) | copy-start | bytes 786436
  (55 other events, 121.5 us)
Sparse Core Ops, SparseCore 0:
  116.7 95.7 all-gather.2
  409.9 65.6 all-reduce.8
  514.6 24.6 reduce-scatter.1
  540.8 28.2 all-gather.4

commit v6 on v5

--- a/solution.py
+++ b/solution.py
@@ -47,23 +47,6 @@
     )
 
 
-def slot_rows(route, experts, capacity):
-    count = route.shape[0]
-    chosen = (route[:, :, None] == jnp.arange(experts, dtype=jnp.int32)).astype(BF16)
-    per_token = jnp.sum(chosen, axis=1)
-    place = jnp.arange(count)
-    before = (place[None, :] < place[:, None]).astype(BF16)
-    earlier = mm("tu,ue->te", before, per_token)
-    inside = jnp.stack([jnp.zeros_like(chosen[:, 0]), chosen[:, 0]], axis=1).astype(F32)
-    position = jnp.sum((earlier[:, None, :] + inside) * chosen.astype(F32), axis=2)
-    return route * capacity + position.astype(jnp.int32)
-
-
-def chosen_of(logits, route, experts):
-    onehot = (route[:, :, None] == jnp.arange(experts, dtype=jnp.int32)).astype(F32)
-    return jnp.sum(onehot * logits[:, None, :], axis=2)
-
-
 def opposite(axis, offset):
     index = jnp.bitwise_xor(lax.axis_index(axis), offset)
     if axis == "row":
@@ -78,235 +61,6 @@
             barrier, inc=1, device_id=partner, device_id_type=pl.DeviceIdType.MESH
         )
     pl.semaphore_wait(barrier, len(partners))
-
-
-def dispatch_matrix(route, flip, experts, capacity):
-    count = route.shape[0]
-    lane = lax.broadcasted_iota(jnp.int32, (count, LANES), 1)
-    chosen = [(route[:, k : k + 1] == lane).astype(F32) for k in range(TOPK)]
-    place = lax.broadcasted_iota(jnp.int32, (count, count), 0)
-    other = lax.broadcasted_iota(jnp.int32, (count, count), 1)
-    before = (other < place).astype(F32).astype(BF16)
-    earlier = jnp.dot(
-        before, (chosen[0] + chosen[1]).astype(BF16), preferred_element_type=F32
-    )
-    rows = lax.broadcasted_iota(jnp.int32, (count, experts * capacity), 1)
-    result = None
-    for k in range(TOPK):
-        position = jnp.sum(earlier * chosen[k], axis=1, keepdims=True).astype(jnp.int32)
-        mine = jnp.bitwise_xor(route[:, k : k + 1], flip) * capacity + position
-        found = (rows == mine).astype(F32)
-        result = found if result is None else result + found
-    return result.astype(BF16)
-
-
-def gather_kernel(parts, cols, replicas, counts, *refs):
-    n_blocks = len(counts)
-    lengths, route, tokens, cot = refs[:4]
-    blocks = refs[4 : 4 + n_blocks]
-    outs = refs[4 + n_blocks :]
-    wholes = outs[:n_blocks]
-    tokens_whole = outs[n_blocks]
-    cot_wholes = outs[n_blocks + 1 : n_blocks + 1 + EXP_FF]
-    own_rows, landed, send, recv, local = outs[n_blocks + 1 + EXP_FF :]
-    row = lax.axis_index("row")
-    col = lax.axis_index("col")
-    depth = blocks[0].shape[1]
-    count, wide = tokens.shape
-    partners = {offset: opposite("row", offset) for offset in (1, 2, 4)}
-    along = [opposite("col", i) for i in range(1, cols)]
-    greet(list(partners.values()) + [opposite("row", 6)] + along)
-    chunks = [(a, i) for a, number in enumerate(counts) for i in range(number)]
-    used = [0]
-    started = []
-    received = set()
-    kept = []
-    here = pl.ds(pl.multiple_of(col * wide, wide), wide)
-
-    def send_to(source, target, device):
-        n = used[0]
-        used[0] += 1
-        copy = pltpu.make_async_remote_copy(
-            src_ref=source,
-            dst_ref=target,
-            send_sem=send.at[n],
-            recv_sem=recv.at[n],
-            device_id=device,
-            device_id_type=pl.DeviceIdType.MESH,
-        )
-        copy.start()
-        started.append(copy)
-        return copy
-
-    def arrive(copy):
-        copy.wait_recv()
-        received.add(id(copy))
-
-    def keep(source, target):
-        copy = pltpu.make_async_copy(source, target, local.at[len(kept)])
-        copy.start()
-        kept.append(copy)
-
-    def place(chunk, offset):
-        array, i = chunk
-        owner = jnp.bitwise_xor(row, offset)
-        return wholes[array].at[i, pl.ds(pl.multiple_of(owner * depth, depth), depth)]
-
-    def push(source, chunk, target, offset):
-        return send_to(source, place(chunk, offset), partners[target])
-
-    for device in along:
-        send_to(tokens, tokens_whole.at[:, here], device)
-    keep(tokens, tokens_whole.at[:, here])
-    first = {}
-    for number, chunk in enumerate(chunks):
-        source = blocks[chunk[0]].at[chunk[1]]
-        for target in (2, 4):
-            first[number, target] = push(source, chunk, target, 0)
-    for a in range(n_blocks):
-        where = pl.ds(pl.multiple_of(row * depth, depth), depth)
-        keep(blocks[a], wholes[a].at[:, where])
-    for chunk in chunks:
-        push(blocks[chunk[0]].at[chunk[1]], chunk, 1, 0)
-    valid = lax.broadcasted_iota(jnp.int32, (count, 1), 0) < lengths[0]
-    matrix = dispatch_matrix(route[...], row // replicas, EXP_FF, CAP_FF)
-    masked = jnp.where(valid, cot[...].astype(F32), 0.0).astype(BF16)
-    dispatched = lax.dot_general(
-        matrix, masked, (((0,), (0,)), ((), ())), preferred_element_type=F32
-    ).astype(BF16)
-    for j in range(EXP_FF):
-        own_rows[j] = dispatched[j * CAP_FF : (j + 1) * CAP_FF]
-    traded = [
-        send_to(own_rows.at[j], landed.at[j - 1], opposite("row", j * replicas))
-        for j in range(1, EXP_FF)
-    ]
-    for j in range(EXP_FF):
-        if j:
-            arrive(traded[j - 1])
-            source = landed.at[j - 1]
-        else:
-            source = own_rows.at[0]
-        keep(source, cot_wholes[j].at[:, here])
-        for device in along:
-            send_to(source, cot_wholes[j].at[:, here], device)
-    relayed = []
-    for number, chunk in enumerate(chunks):
-        arrive(first[number, 2])
-        arrive(first[number, 4])
-        if number % 2 == 0:
-            relayed.append(push(place(chunk, 2), chunk, 4, 2))
-        else:
-            relayed.append(push(place(chunk, 4), chunk, 2, 4))
-        for offset in (2, 4):
-            push(place(chunk, offset), chunk, 1, offset)
-    for number, chunk in enumerate(chunks):
-        arrive(relayed[number])
-        push(place(chunk, 6), chunk, 1, 6)
-    for copy in started:
-        if id(copy) not in received:
-            copy.wait_recv()
-    for copy in started:
-        copy.wait_send()
-    for copy in kept:
-        copy.wait()
-
-
-def gather_all(lengths, route, tokens, cot, blocks, parts, cols, replicas):
-    counts = [block.shape[0] for block in blocks]
-    hbm = pl.BlockSpec(memory_space=pl.ANY)
-    vmem = pl.BlockSpec(memory_space=pltpu.VMEM)
-    smem = pl.BlockSpec(memory_space=pltpu.SMEM)
-    count, wide = tokens.shape
-    remote = 7 * sum(counts) + (cols - 1) * (1 + EXP_FF) + EXP_FF - 1
-    return pl.pallas_call(
-        functools.partial(gather_kernel, parts, cols, replicas, counts),
-        out_shape=[
-            jax.ShapeDtypeStruct((b.shape[0], b.shape[1] * parts, b.shape[2]), b.dtype)
-            for b in blocks
-        ]
-        + [jax.ShapeDtypeStruct((count, wide * cols), tokens.dtype)]
-        + [jax.ShapeDtypeStruct((CAP_FF, wide * cols), BF16)] * EXP_FF,
-        in_specs=[smem, vmem, hbm, vmem] + [hbm] * len(blocks),
-        out_specs=[hbm] * (len(blocks) + 1 + EXP_FF),
-        scratch_shapes=[
-            pltpu.VMEM((EXP_FF, CAP_FF, wide), BF16),
-            pltpu.VMEM((EXP_FF - 1, CAP_FF, wide), BF16),
-            pltpu.SemaphoreType.DMA((remote,)),
-            pltpu.SemaphoreType.DMA((remote,)),
-            pltpu.SemaphoreType.DMA((1 + EXP_FF + len(blocks),)),
-        ],
-        compiler_params=pltpu.CompilerParams(collective_id=1, has_side_effects=True),
-    )(lengths, route, tokens, cot, *blocks)
-
-
-def cot_kernel(cols, replicas, *refs):
-    blocks, wholes = refs[:EXP_FF], refs[EXP_FF : 2 * EXP_FF]
-    landed, send, recv, local = refs[2 * EXP_FF :]
-    col = lax.axis_index("col")
-    wide = blocks[0].shape[1]
-    here = pl.ds(pl.multiple_of(col * wide, wide), wide)
-    along = [opposite("col", i) for i in range(1, cols)]
-    across = [opposite("row", j * replicas) for j in range(1, EXP_FF)]
-    greet(along + across)
-    copies = []
-
-    def push(source, target, n, device):
-        copy = pltpu.make_async_remote_copy(
-            src_ref=source,
-            dst_ref=target,
-            send_sem=send.at[n],
-            recv_sem=recv.at[n],
-            device_id=device,
-            device_id_type=pl.DeviceIdType.MESH,
-        )
-        copy.start()
-        copies.append(copy)
-        return copy
-
-    def keep(source, target, n):
-        copy = pltpu.make_async_copy(source, target, local.at[n])
-        copy.start()
-        return copy
-
-    first = [
-        push(blocks[j], landed.at[j - 1], j - 1, across[j - 1]) for j in range(1, EXP_FF)
-    ]
-    base = EXP_FF - 1
-    kept = []
-    for j in range(EXP_FF):
-        if j:
-            first[j - 1].wait_recv()
-            source = landed.at[j - 1]
-        else:
-            source = blocks[0]
-        kept.append(keep(source, wholes[j].at[:, here], j))
-        for i in range(cols - 1):
-            push(source, wholes[j].at[:, here], base + j * (cols - 1) + i, along[i])
-    for copy in copies[EXP_FF - 1 :]:
-        copy.wait_recv()
-    for copy in copies:
-        copy.wait_send()
-    for copy in kept:
-        copy.wait()
-
-
-def spread_cot(blocks, cols, replicas):
-    hbm = pl.BlockSpec(memory_space=pl.ANY)
-    wide = blocks[0].shape[1]
-    remote = EXP_FF - 1 + EXP_FF * (cols - 1)
-    return pl.pallas_call(
-        functools.partial(cot_kernel, cols, replicas),
-        out_shape=[jax.ShapeDtypeStruct((CAP_FF, wide * cols), BF16)] * EXP_FF,
-        in_specs=[hbm] * EXP_FF,
-        out_specs=[hbm] * EXP_FF,
-        scratch_shapes=[
-            pltpu.VMEM((EXP_FF - 1, CAP_FF, wide), BF16),
-            pltpu.SemaphoreType.DMA((remote,)),
-            pltpu.SemaphoreType.DMA((remote,)),
-            pltpu.SemaphoreType.DMA((EXP_FF,)),
-        ],
-        compiler_params=pltpu.CompilerParams(collective_id=2, has_side_effects=True),
-    )(*blocks)
 
 
 def split(value):
@@ -359,15 +113,469 @@
     return copy
 
 
+def dispatch_matrices(route, flip, experts, capacity):
+    count = route.shape[0]
+    lane = lax.broadcasted_iota(jnp.int32, (count, LANES), 1)
+    chosen = [(route[:, k : k + 1] == lane).astype(F32) for k in range(TOPK)]
+    place = lax.broadcasted_iota(jnp.int32, (count, count), 0)
+    other = lax.broadcasted_iota(jnp.int32, (count, count), 1)
+    before = (other < place).astype(F32).astype(BF16)
+    earlier = jnp.dot(
+        before, (chosen[0] + chosen[1]).astype(BF16), preferred_element_type=F32
+    )
+    rows = lax.broadcasted_iota(jnp.int32, (count, experts * capacity), 1)
+    results = []
+    for k in range(TOPK):
+        position = jnp.sum(earlier * chosen[k], axis=1, keepdims=True).astype(jnp.int32)
+        mine = jnp.bitwise_xor(route[:, k : k + 1], flip) * capacity + position
+        results.append((rows == mine).astype(F32).astype(BF16))
+    return results
+
+
+def turn(value, cosine, sine):
+    half = HEAD_DIM // 2
+    heads = []
+    for h in range(value.shape[1] // HEAD_DIM):
+        head = value[:, h * HEAD_DIM : (h + 1) * HEAD_DIM]
+        heads.append(head * cosine + pltpu.roll(head, half, axis=1) * sine)
+    return jnp.concatenate(heads, axis=1)
+
+
+def scores_of(stat_route, logits, experts):
+    chosen = []
+    for k in range(TOPK):
+        score = 0.0
+        for e in range(experts):
+            score += jnp.where(stat_route[k] == float(e), logits[:, e : e + 1], 0.0)
+        chosen.append(score)
+    top = jnp.maximum(chosen[0], chosen[1])
+    powers = [jnp.exp(score - top) for score in chosen]
+    return chosen, [power / (powers[0] + powers[1]) for power in powers]
+
+
+def front_kernel(parts, cols, replicas, *refs):
+    lengths, pick, route_attn, route_ffn, cot, norm, router, cosine, sine, rights = refs[:10]
+    left_refs = refs[10:15]
+    tokens = refs[15]
+    blocks = refs[16:19]
+    pairs = refs[19]
+    outs = refs[20:]
+    flat = outs[0]
+    outs = outs[1:]
+    wholes = outs[:3]
+    cot_wholes = outs[3 : 3 + EXP_FF]
+    (
+        hidden,
+        lefts,
+        stat,
+        low_in,
+        keys,
+        values,
+        queries,
+        attended,
+        probability,
+        att_rows,
+        low_rows,
+        out_rows,
+        picks_attn,
+        picks_ffn,
+        ranks,
+        gate_rows,
+        picks,
+    ) = outs[3 + EXP_FF : 20 + EXP_FF]
+    (
+        x_all,
+        own_rows,
+        landed,
+        hidden_rows,
+        buffer,
+        query_rows,
+        pick_out,
+        lefts_out,
+        pair_in,
+        pair_out,
+        send,
+        recv,
+        local,
+        load,
+    ) = outs[20 + EXP_FF :]
+    row = lax.axis_index("row")
+    col = lax.axis_index("col")
+    depth = blocks[0].shape[1]
+    count, wide = tokens.shape
+    width = hidden.shape[1]
+    head_width = keys.shape[1]
+    heads = head_width // HEAD_DIM
+    across = [None] + [opposite("row", m) for m in range(1, parts)]
+    along = [opposite("col", i) for i in range(1, cols)]
+    greet(across[1:] + along)
+    started, kept = [], []
+    received = set()
+    here = pl.ds(pl.multiple_of(col * wide, wide), wide)
+    own = pl.ds(pl.multiple_of(row * depth, depth), depth)
+
+    def send_to(source, target, device):
+        copy = remote(source, target, send, recv, len(started), device)
+        started.append(copy)
+        return copy
+
+    def arrive(copy):
+        copy.wait_recv()
+        received.add(id(copy))
+
+    def keep(source, target):
+        copy = pltpu.make_async_copy(source, target, local.at[len(kept)])
+        copy.start()
+        kept.append(copy)
+        return copy
+
+    pair = 2
+    chunks = [
+        (a, start) for a in range(3) for start in range(0, blocks[a].shape[0], pair)
+    ]
+
+    def place(n, offset, item=None):
+        array, start = chunks[n]
+        owner = jnp.bitwise_xor(row, offset)
+        owner_rows = pl.ds(pl.multiple_of(owner * depth, depth), depth)
+        if item is None:
+            return wholes[array].at[pl.ds(start, pair), owner_rows]
+        return wholes[array].at[start + item, owner_rows]
+
+    first, direct, relayed, beside = {}, {}, {}, {}
+
+    def push_own(n):
+        if n >= len(chunks):
+            return
+        array, start = chunks[n]
+        source = blocks[array].at[pl.ds(start, pair)]
+        if parts == 8:
+            first[n] = [send_to(source, place(n, 0), across[m]) for m in (2, 4)]
+            beside[n] = [send_to(source, place(n, 0), across[1])]
+        else:
+            direct[n] = [send_to(source, place(n, 0), across[m]) for m in range(1, parts)]
+
+    def relay(n):
+        if parts == 8:
+            for copy in first[n]:
+                arrive(copy)
+            relayed[n] = [
+                send_to(place(n, 2, 0), place(n, 2, 0), across[4]),
+                send_to(place(n, 4, 1), place(n, 4, 1), across[2]),
+            ]
+            for offset in (2, 4):
+                beside[n].append(send_to(place(n, offset), place(n, offset), across[1]))
+
+    def finish(n):
+        if parts == 8:
+            for copy in relayed[n]:
+                arrive(copy)
+            beside[n].append(send_to(place(n, 6), place(n, 6), across[1]))
+            for copy in beside[n]:
+                arrive(copy)
+        else:
+            for copy in direct[n]:
+                arrive(copy)
+
+    token_copies = [send_to(tokens, x_all.at[:, here], device) for device in along]
+    token_kept = keep(tokens, x_all.at[:, here])
+    block_kept = [keep(blocks[a], wholes[a].at[:, own]) for a in range(3)]
+    pick_out[...] = jnp.full(pick_out.shape, 1.0, F32) * pick[0].astype(F32)
+    picks[0] = pick_out[...]
+    pick_copies = [
+        send_to(pick_out, picks.at[m], across[m]) for m in range(1, parts)
+    ]
+    window, behind = 9, 5
+    for n in range(window):
+        push_own(n)
+
+    position = lax.broadcasted_iota(jnp.int32, (count, 1), 0)
+    valid = position < lengths[0]
+    matrices = dispatch_matrices(route_ffn[...], row // replicas, EXP_FF, CAP_FF)
+    for k in range(TOPK):
+        picks_ffn[k] = matrices[k]
+    masked = jnp.where(valid, cot[...].astype(F32), 0.0).astype(BF16)
+
+    def rows_of(matrix, value):
+        return lax.dot_general(
+            matrix, value, (((0,), (0,)), ((), ())), preferred_element_type=F32
+        )
+
+    def times(left, right):
+        return lax.dot_general(
+            left, right, (((1,), (1,)), ((), ())), preferred_element_type=F32
+        )
+
+    dispatched = rows_of(matrices[0] + matrices[1], masked).astype(BF16)
+    for j in range(EXP_FF):
+        own_rows[j] = dispatched[j * CAP_FF : (j + 1) * CAP_FF]
+    traded = [
+        send_to(own_rows.at[j], landed.at[j - 1], across[j * replicas])
+        for j in range(1, EXP_FF)
+    ]
+    attn = dispatch_matrices(route_attn[...], 0, EXP_ATT, CAP_ATT)
+    for k in range(TOPK):
+        picks_attn[k] = attn[k]
+    attn_any = attn[0] + attn[1]
+    picks_attn[TOPK] = attn_any
+
+    left_copies = []
+    for m in range(parts):
+        if m:
+            arrive(pick_copies[m - 1])
+        theirs = picks[m, 0:1, 0:1]
+        for p in range(5):
+            value = jnp.zeros((RANK, depth), F32)
+            for a in range(ADAPT):
+                value += jnp.where(theirs == float(a), left_refs[p][a].astype(F32), 0.0)
+            lefts_out[m, p * RANK : (p + 1) * RANK] = value.astype(BF16)
+        if m:
+            left_copies.append(send_to(lefts_out.at[m], lefts.at[:, own], across[m]))
+        else:
+            lefts[:, own] = lefts_out[0]
+    for j in range(EXP_FF):
+        if j:
+            arrive(traded[j - 1])
+            source = landed.at[j - 1]
+        else:
+            source = own_rows.at[0]
+        keep(source, cot_wholes[j].at[:, here])
+        for device in along:
+            send_to(source, cot_wholes[j].at[:, here], device)
+    relay(0)
+    push_own(window)
+
+    for copy in token_copies:
+        arrive(copy)
+    token_kept.wait()
+    square = jnp.zeros((count, 1), F32)
+    for q in range(cols):
+        value = x_all[:, q * wide : (q + 1) * wide].astype(F32)
+        square += jnp.sum(value * value, axis=1, keepdims=True)
+    scale = lax.rsqrt(square * (1.0 / width) + EPSILON)
+    for q in range(cols):
+        span = slice(q * wide, (q + 1) * wide)
+        value = x_all[:, span].astype(F32)
+        hidden[:, span] = (value * scale * norm[:, span]).astype(BF16)
+    for copy in left_copies:
+        arrive(copy)
+    relay(1)
+    push_own(window + 1)
+    logits = times(hidden[...], router[...])
+    routes = [route_attn[:, k : k + 1].astype(F32) for k in range(TOPK)]
+    chosen, gates = scores_of(routes, logits, EXP_ATT)
+    extras = [valid.astype(F32), *(route_ffn[:, k : k + 1].astype(F32) for k in range(TOPK))]
+    stat[...] = pack([*gates, *chosen, scale, *routes, *extras], range(10))
+    rank_both = times(hidden[...], lefts[: 2 * RANK])
+    ranks[...] = rank_both
+    rank_query = rank_both[:, :RANK].astype(BF16)
+    rank_kv = rank_both[:, RANK:].astype(BF16)
+    low_down = times(masked, lefts[4 * RANK : 5 * RANK, here])
+    low_in[...] = jnp.concatenate(
+        [
+            jnp.zeros((count, 2 * RANK), F32),
+            low_down,
+            jnp.zeros((count, LANES - 3 * RANK), F32),
+        ],
+        axis=1,
+    )
+    gate_wide = 0.0
+    for k in range(TOPK):
+        columns = pack([*split(gates[k])], range(2)).astype(BF16)
+        gate_wide += rows_of(attn[k], columns)
+    gate_row = gate_wide[:, 0:1] + gate_wide[:, 1:2]
+    gate_rows[...] = gate_row
+    rank_rows = rows_of(attn_any, rank_query).astype(BF16)
+    for q in range(cols):
+        span = slice(q * wide, (q + 1) * wide)
+        hidden_rows[:, span] = rows_of(attn_any, hidden[:, span]).astype(BF16)
+
+    def attend():
+        value = query_rows[...]
+        high = value.astype(BF16)
+        low = (value - high.astype(F32)).astype(BF16)
+        for k in range(TOPK):
+            query = jnp.dot(attn[k], high, preferred_element_type=F32) + jnp.dot(
+                attn[k], low, preferred_element_type=F32
+            )
+            queries[k] = turn(query, cosine[...], sine[...]).astype(BF16)
+        other = lax.broadcasted_iota(jnp.int32, (count, count), 1)
+        place_row = lax.broadcasted_iota(jnp.int32, (count, count), 0)
+        allowed = (other <= place_row) & (other < lengths[0])
+        for h in range(heads):
+            span = slice(h * HEAD_DIM, (h + 1) * HEAD_DIM)
+            for k in range(TOPK):
+                scores = times(queries[k, :, span], keys[:, span]) * HEAD_DIM ** (-0.5)
+                scores = jnp.where(allowed, scores, -1e30)
+                power = jnp.exp(scores - jnp.max(scores, axis=1, keepdims=True))
+                probs = power / jnp.sum(power, axis=1, keepdims=True)
+                probability[h, k] = probs
+                attended[k, :, span] = jnp.dot(
+                    probs.astype(BF16), values[:, span], preferred_element_type=F32
+                ).astype(BF16)
+        rows = rows_of(attn[0], attended[0]) + rows_of(attn[1], attended[1])
+        att_rows[...] = rows.astype(BF16)
+        low = times(att_rows[...], rights[3 * RANK :]) * gate_row
+        low_rows[...] = jnp.concatenate(
+            [
+                jnp.zeros((low.shape[0], RANK), F32),
+                low,
+                jnp.zeros((low.shape[0], LANES - 2 * RANK), F32),
+            ],
+            axis=1,
+        ).astype(BF16)
+
+    def compute(n):
+        array, start = chunks[n]
+        weight = buffer.at[n % 2]
+        if array == 0:
+            key = jnp.dot(hidden[...], weight[0], preferred_element_type=F32) + jnp.dot(
+                rank_kv, rights[RANK : 2 * RANK], preferred_element_type=F32
+            )
+            keys[...] = turn(key, cosine[...], sine[...]).astype(BF16)
+            value = jnp.dot(hidden[...], weight[1], preferred_element_type=F32) + jnp.dot(
+                rank_kv, rights[2 * RANK : 3 * RANK], preferred_element_type=F32
+            )
+            values[...] = value.astype(BF16)
+            return
+        for item in range(pair):
+            e = start + item
+            span = slice(e * CAP_ATT, (e + 1) * CAP_ATT)
+            if array == 1:
+                query_rows[span] = jnp.dot(
+                    hidden_rows[span], weight[item], preferred_element_type=F32
+                ) + jnp.dot(rank_rows[span], rights[:RANK], preferred_element_type=F32)
+            else:
+                out_rows[span] = (times(att_rows[span], weight[item]) * gate_row[span]).astype(
+                    BF16
+                )
+        if array == 1 and start + pair == EXP_ATT:
+            attend()
+
+    def flatten(e):
+        copy = pltpu.make_async_copy(pairs.at[e], pair_in, load.at[2])
+        copy.start()
+        copy.wait()
+        step = 64
+
+        @pl.loop(0, pair_in.shape[0] // step)
+        def _(i):
+            span = pl.ds(pl.multiple_of(i * step, step), step)
+            pair_out[span] = pair_in[span].reshape(step, pair_out.shape[1])
+
+        copy = pltpu.make_async_copy(pair_out, flat.at[e], load.at[3])
+        copy.start()
+        copy.wait()
+
+    loads = {}
+    total = len(chunks)
+    for n in range(2, total + behind + 1):
+        if n < total:
+            relay(n)
+            push_own(n + window)
+        if n - 2 < EXP_FF:
+            flatten(n - 2)
+        for m in range(n - behind + 1) if n == 2 else [n - behind]:
+            if 0 <= m < total:
+                if m == 0:
+                    for copy in block_kept:
+                        copy.wait()
+                finish(m)
+                loads[m] = pltpu.make_async_copy(
+                    place_whole(wholes, chunks[m], pair), buffer.at[m % 2], load.at[m % 2]
+                )
+                loads[m].start()
+            if 0 <= m - 1 < total:
+                loads[m - 1].wait()
+                compute(m - 1)
+    for copy in started:
+        if id(copy) not in received:
+            copy.wait_recv()
+    for copy in started:
+        copy.wait_send()
+    for copy in kept[1 + len(block_kept) :]:
+        copy.wait()
+
+
+def place_whole(wholes, chunk, pair):
+    array, start = chunk
+    return wholes[array].at[pl.ds(start, pair)]
+
+
+def front(smalls, lefts, tokens, blocks, pairs, parts, cols, replicas):
+    hbm = pl.BlockSpec(memory_space=pl.ANY)
+    vmem = pl.BlockSpec(memory_space=pltpu.VMEM)
+    smem = pl.BlockSpec(memory_space=pltpu.SMEM)
+    count, wide = tokens.shape
+    width = wide * cols
+    depth, head_width = blocks[0].shape[1:]
+    heads = head_width // HEAD_DIM
+    rows = EXP_ATT * CAP_ATT
+    rows_ffn = EXP_FF * CAP_FF
+    shape = jax.ShapeDtypeStruct
+    flat = (pairs.shape[0], pairs.shape[1], 2 * pairs.shape[3])
+    n_chunks = sum(block.shape[0] for block in blocks) // 2
+    per_chunk = 8 if parts == 8 else parts - 1
+    remotes = (
+        n_chunks * per_chunk + (cols - 1) * (1 + EXP_FF) + EXP_FF - 1 + 2 * (parts - 1)
+    )
+    return pl.pallas_call(
+        functools.partial(front_kernel, parts, cols, replicas),
+        out_shape=[shape(flat, BF16)]
+        + [shape((b.shape[0], width, head_width), BF16) for b in blocks]
+        + [shape((CAP_FF, width), BF16)] * EXP_FF
+        + [
+            shape((count, width), BF16),
+            shape((5 * RANK, width), BF16),
+            shape((count, LANES), F32),
+            shape((count, LANES), F32),
+            shape((count, head_width), BF16),
+            shape((count, head_width), BF16),
+            shape((TOPK, count, head_width), BF16),
+            shape((TOPK, count, head_width), BF16),
+            shape((heads, TOPK, count, count), F32),
+            shape((rows, head_width), BF16),
+            shape((rows, LANES), BF16),
+            shape((rows, width), BF16),
+            shape((TOPK + 1, count, rows), BF16),
+            shape((TOPK, count, rows_ffn), BF16),
+            shape((count, 2 * RANK), F32),
+            shape((rows, 1), F32),
+            shape((parts, 8, LANES), F32),
+        ],
+        in_specs=[smem] * 2 + [vmem] * 13 + [hbm] * 5,
+        out_specs=[hbm] * (4 + EXP_FF) + [vmem] * 17,
+        scratch_shapes=[
+            pltpu.VMEM((count, width), BF16),
+            pltpu.VMEM((EXP_FF, CAP_FF, wide), BF16),
+            pltpu.VMEM((EXP_FF - 1, CAP_FF, wide), BF16),
+            pltpu.VMEM((rows, width), BF16),
+            pltpu.VMEM((2, 2, width, head_width), BF16),
+            pltpu.VMEM((rows, head_width), F32),
+            pltpu.VMEM((8, LANES), F32),
+            pltpu.VMEM((parts, 5 * RANK, depth), BF16),
+            pltpu.VMEM(pairs.shape[1:], BF16),
+            pltpu.VMEM(flat[1:], BF16),
+            pltpu.SemaphoreType.DMA((remotes,)),
+            pltpu.SemaphoreType.DMA((remotes,)),
+            pltpu.SemaphoreType.DMA((4 + EXP_FF,)),
+            pltpu.SemaphoreType.DMA((4,)),
+        ],
+        compiler_params=pltpu.CompilerParams(
+            collective_id=1, has_side_effects=True, vmem_limit_bytes=56 * 2**20
+        ),
+    )(*smalls, *lefts, tokens, *blocks, pairs)
+
+
 def middle_back_kernel(cols, replicas, *refs):
     blocks, downs = refs[:EXP_FF], refs[EXP_FF : 2 * EXP_FF]
     adapter, norm, router, stat = refs[2 * EXP_FF : 2 * EXP_FF + 4]
-    sources = refs[2 * EXP_FF + 4 : 2 * EXP_FF + 10]
-    grad_middle, grad_whole, totals, branch, low_down = refs[2 * EXP_FF + 10 : 2 * EXP_FF + 15]
-    scratch = refs[2 * EXP_FF + 15 :]
-    pick_0, pick_1, lefts, hidden, middle, cot = scratch[:6]
+    sources = refs[2 * EXP_FF + 4 : 2 * EXP_FF + 9]
+    grad_middle, grad_whole, totals, branch, low_down = refs[2 * EXP_FF + 9 : 2 * EXP_FF + 14]
+    scratch = refs[2 * EXP_FF + 14 :]
+    picks_ffn, lefts, hidden, middle, cot = scratch[:5]
     rows, down_rows, exact_part, parts, extra, parts_in, extra_in, low, send, recv, local = (
-        scratch[6:]
+        scratch[5:]
     )
     col = lax.axis_index("col")
     count, wide = middle.shape
@@ -383,7 +591,7 @@
     ]
     near = fetch(
         [blocks[0], downs[0], *sources],
-        [rows.at[pl.ds(0, CAP_FF)], down_rows.at[pl.ds(0, CAP_FF)], *scratch[:6]],
+        [rows.at[pl.ds(0, CAP_FF)], down_rows.at[pl.ds(0, CAP_FF)], *scratch[:5]],
         local,
     )
     for copy in near:
@@ -402,16 +610,11 @@
         )
         for j in range(1, EXP_FF)
     ]
-    picks = [pick_0[...], pick_1[...]]
+    picks = [picks_ffn[0], picks_ffn[1]]
     any_pick = picks[0] + picks[1]
 
     def back(pick, source, start, size):
-        return lax.dot_general(
-            pick,
-            source[:, start : start + size],
-            (((0,), (0,)), ((), ())),
-            preferred_element_type=F32,
-        )
+        return jnp.dot(pick, source[:, start : start + size], preferred_element_type=F32)
 
     sub = lax.broadcasted_iota(jnp.int32, (LANES, LANES), 0)
     lane = lax.broadcasted_iota(jnp.int32, (LANES, LANES), 1)
@@ -513,7 +716,7 @@
             jax.ShapeDtypeStruct((count, wide * cols), BF16),
             jax.ShapeDtypeStruct((count, LANES), F32),
         ],
-        in_specs=[hbm] * (2 * EXP_FF) + [smem, vmem, vmem, vmem] + [hbm] * 6,
+        in_specs=[hbm] * (2 * EXP_FF) + [smem, vmem, vmem, vmem] + [hbm] * 5,
         out_specs=[vmem, hbm, vmem, vmem, vmem],
         scratch_shapes=[pltpu.VMEM(source.shape, source.dtype) for source in sources]
         + [
@@ -631,7 +834,7 @@
     )
     chosen_by = [
         [
-            jnp.where(adapters[jnp.bitwise_xor(row, m)] == a, 1.0, 0.0).astype(F32)
+            jnp.where(adapters[m] == a, 1.0, 0.0).astype(F32)
             for a in range(ADAPT)
         ]
         for m in range(parts_axis)
@@ -701,16 +904,16 @@
 
 def middle_kernel(parts_axis, cols, replicas, *refs):
     adapter, norm, router, route, low_rows, low_in = refs[:6]
-    sources = refs[6:12]
-    weights = refs[12:14]
-    outs = refs[14:]
+    sources = refs[6:11]
+    weights = refs[11:13]
+    outs = refs[13:]
     extra_chunks = parts_axis - 1
     chunks = [(None,) + tuple(outs[n * extra_chunks : (n + 1) * extra_chunks]) for n in (0, 1)]
     outs = outs[2 * extra_chunks :]
     hids = outs[:EXP_FF]
     hidden_out, middle, stat, totals = outs[EXP_FF : EXP_FF + 4]
     scratch = outs[EXP_FF + 4 :]
-    out_rows, pick_attn, pick_0, pick_1, lefts, tokens = scratch[:6]
+    out_rows, picks_attn, picks_ffn, lefts, tokens = scratch[:5]
     (
         exact_part,
         parts,
@@ -725,7 +928,7 @@
         send,
         recv,
         local,
-    ) = scratch[6:]
+    ) = scratch[5:]
     col = lax.axis_index("col")
     count, wide = tokens.shape
     width = hidden.shape[1]
@@ -733,7 +936,7 @@
     beside = [opposite("row", i) for i in range(1, replicas)]
     along = [opposite("col", i) for i in range(1, cols)]
     greet(across + beside + along)
-    near = fetch(sources, scratch[:6], local)
+    near = fetch(sources, scratch[:5], local)
     used = [0]
     started = []
 
@@ -760,8 +963,11 @@
         copy.wait()
 
     def back(source):
+        return jnp.dot(picks_attn[TOPK], source, preferred_element_type=F32)
+
+    def rows_of(matrix, value):
         return lax.dot_general(
-            pick_attn[...], source, (((0,), (0,)), ((), ())), preferred_element_type=F32
+            matrix, value, (((0,), (0,)), ((), ())), preferred_element_type=F32
         )
 
     sub = lax.broadcasted_iota(jnp.int32, (LANES, LANES), 0)
@@ -828,11 +1034,9 @@
         value = jnp.dot(value.astype(BF16), spread, preferred_element_type=F32)
         return jnp.where(mine, value, 0.0).astype(BF16)
 
-    picks = [pick_0[...], pick_1[...]]
+    picks = [picks_ffn[0], picks_ffn[1]]
     any_pick = picks[0] + picks[1]
-    message[:, width + 2 * LANES :] = jnp.dot(
-        any_pick, own_adapter(total, 2 * RANK), preferred_element_type=F32
-    ).astype(BF16)
+    message[:, width + 2 * LANES :] = rows_of(any_pick, own_adapter(total, 2 * RANK)).astype(BF16)
     for copy in hidden_copies:
         copy.wait_recv()
     kept = pltpu.make_async_copy(hidden, hidden_out, local.at[6])
@@ -844,37 +1048,26 @@
         )
 
     logits = times(router[...])
-    routes = [route[:, k : k + 1] for k in range(TOPK)]
-    chosen = []
-    for k in range(TOPK):
-        score = 0.0
-        for e in range(EXP_FF):
-            score += jnp.where(routes[k] == float(e), logits[:, e : e + 1], 0.0)
-        chosen.append(score)
-    top = jnp.maximum(chosen[0], chosen[1])
-    powers = [jnp.exp(score - top) for score in chosen]
-    gates = [power / (powers[0] + powers[1]) for power in powers]
+    routes = [route[:, 8 + k : 9 + k] for k in range(TOPK)]
+    chosen, gates = scores_of(routes, logits, EXP_FF)
     stat[...] = pack(
-        [*gates, *chosen, scale, *routes, route[:, 2:3]], range(8)
+        [*gates, *chosen, scale, *routes, route[:, 7:8]], range(8)
     )
     gate_rows = 0.0
     for k in range(TOPK):
         columns = pack([*split(gates[k])], range(2)).astype(BF16)
-        gate_rows += jnp.dot(picks[k], columns, preferred_element_type=F32)
+        gate_rows += rows_of(picks[k], columns)
     message[:, width + LANES : width + 2 * LANES] = gate_rows.astype(BF16)
     rank = times(lefts[3 * RANK : 4 * RANK])
     rank = jnp.concatenate([rank, jnp.zeros((count, LANES - RANK), F32)], axis=1)
-    message[:, width : width + LANES] = jnp.dot(
-        any_pick, own_adapter(rank, 0), preferred_element_type=F32
-    ).astype(BF16)
-    traded = []
-    for j in range(EXP_FF - 1, -1, -1):
-        rows = slice(j * CAP_FF, (j + 1) * CAP_FF)
-        message[rows, :width] = jnp.dot(
-            any_pick[rows], hidden[...], preferred_element_type=F32
-        ).astype(BF16)
-        if j:
-            traded.append(send_to(message.at[pl.ds(j * CAP_FF, CAP_FF)], hids[j], across[j - 1]))
+    message[:, width : width + LANES] = rows_of(any_pick, own_adapter(rank, 0)).astype(BF16)
+    for q in range(cols):
+        span = slice(q * wide, (q + 1) * wide)
+        message[:, span] = rows_of(any_pick, hidden[:, span]).astype(BF16)
+    traded = [
+        send_to(message.at[pl.ds(j * CAP_FF, CAP_FF)], hids[j], across[j - 1])
+        for j in range(EXP_FF - 1, 0, -1)
+    ]
     own = pltpu.make_async_copy(message.at[pl.ds(0, CAP_FF)], hids[0], local.at[7])
     own.start()
     for j in range(1, EXP_FF):
@@ -911,7 +1104,7 @@
             jax.ShapeDtypeStruct((count, LANES), F32),
             jax.ShapeDtypeStruct((count, LANES), F32),
         ],
-        in_specs=[smem] + [vmem] * 5 + [hbm] * 8,
+        in_specs=[smem] + [vmem] * 5 + [hbm] * 7,
         out_specs=[hbm] * (2 * parts_axis - 1 + EXP_FF) + [vmem] * 3,
         scratch_shapes=[pltpu.VMEM(source.shape, source.dtype) for source in sources]
         + [
@@ -1138,17 +1331,6 @@
         return result
 
     cols = lax.axis_size("col")
-    if rows_axis == 8:
-        kv_full, query_full, x_full, *cot_rows = gather_all(
-            lengths, ffn_route, inputs, cotangent, [kv_weight, query_weight], rows_axis, cols, replicas
-        )
-    else:
-        kv_full = lax.all_gather(kv_weight, "row", axis=1, tiled=True)
-        query_full = lax.all_gather(query_weight, "row", axis=1, tiled=True)
-        x_full = features(inputs)
-        cot_rows = None
-    out_full = lax.all_gather(later(out_weight, query_full), "row", axis=1, tiled=True)
-
     padding = -units % LANES
 
     def padded(value):
@@ -1156,25 +1338,79 @@
             return value
         return jnp.pad(value, [(0, 0)] * (value.ndim - 1) + [(0, padding)])
 
-    inner_flat = padded(inner_weight).reshape(EXP_FF, depth, 2 * (units + padding))
     down_flat = padded(down_weight)
 
-    picks = lax.all_gather(adapter_pick, "row", axis=0, tiled=True)
-    pick_onehot = (picks[:, None] == jnp.arange(ADAPT, dtype=jnp.int32)[None, :]).astype(BF16)
-    lefts_own = jnp.stack(
-        [query_left, kv_left, out_left, inner_left, down_left], axis=1
-    ).swapaxes(2, 3)
-    lefts_sent = mm(
-        "ga,ax->gx", pick_onehot, lefts_own.reshape(ADAPT, 5 * RANK * depth)
-    ).astype(BF16)
-    lefts = lax.all_to_all(
-        lefts_sent.reshape(rows_axis, 5 * RANK, depth), "row", 0, 0, tiled=False
-    )
-    lefts = lefts.swapaxes(0, 1).reshape(5, RANK, width)
-    left_query, left_kv, left_out, left_inner, left_down = (lefts[i] for i in range(5))
-    right_query = query_right[adapter].astype(F32)
-    right_kv = kv_right[adapter].astype(F32)
-    right_out = out_right[adapter].astype(F32)
+    rights = jnp.concatenate(
+        [
+            query_right[adapter],
+            kv_right[adapter][:, 0],
+            kv_right[adapter][:, 1],
+            out_right[adapter],
+        ]
+    )
+    lefts_own = [
+        value.swapaxes(1, 2)
+        for value in (query_left, kv_left, out_left, inner_left, down_left)
+    ]
+    (
+        inner_flat,
+        kv_full,
+        query_full,
+        out_full,
+        *cot_rows,
+        hidden_one,
+        lefts,
+        stat_attn,
+        low_in,
+        keys,
+        values,
+        queries,
+        attended,
+        probability,
+        attended_rows,
+        low_rows,
+        out_rows,
+        picks_attn,
+        picks_ffn,
+        ranks,
+        gate_rows,
+        picks,
+    ) = front(
+        [
+            lengths,
+            adapter_pick,
+            attn_route,
+            ffn_route,
+            cotangent,
+            norm_one[None, :],
+            router_attn.T,
+            jnp.concatenate([cosine, cosine], axis=1),
+            jnp.concatenate([-sine, sine], axis=1),
+            rights,
+        ],
+        lefts_own,
+        inputs,
+        [kv_weight, query_weight, out_weight],
+        padded(inner_weight),
+        rows_axis,
+        cols,
+        replicas,
+    )
+    picks = picks[:, 0, 0].astype(jnp.int32)
+    gates_attn = stat_attn[:, :TOPK]
+    query_width = keys.shape[1]
+    heads = query_width // HEAD_DIM
+    keys = keys.reshape(count, heads, HEAD_DIM)
+    values = values.reshape(count, heads, HEAD_DIM)
+    queries = queries.reshape(TOPK, count, heads, HEAD_DIM)
+    attended = attended.reshape(TOPK * count, query_width)
+    pick_attn_any = picks_attn[TOPK]
+    pick_attn_both = picks_attn[:TOPK]
+    rank_query = ranks[:, :RANK]
+    rank_kv = ranks[:, RANK:]
+    right_query = rights[:RANK]
+    right_kv = rights[RANK : 3 * RANK].reshape(2, RANK, query_width)
+    right_out = rights[3 * RANK :]
     right_inner_all = inner_right.reshape(ADAPT * RANK, 2, units)
     right_down_all = down_right.reshape(ADAPT * RANK, units)
     ffn_right = jnp.concatenate(
@@ -1182,101 +1418,14 @@
         axis=1,
     )
 
-    slots_attn = slot_rows(attn_route, EXP_ATT, CAP_ATT)
-    slots_ffn = slot_rows(ffn_route, EXP_FF, CAP_FF)
-    rows_attn = jnp.arange(EXP_ATT * CAP_ATT, dtype=jnp.int32)
-    pick_attn = [
-        (rows_attn[:, None] == slots_attn[None, :, k]).astype(BF16) for k in range(TOPK)
-    ]
-    pick_attn_any = pick_attn[0] + pick_attn[1]
-    pick_attn_both = jnp.concatenate(pick_attn, axis=1)
-    order = (expert ^ jnp.arange(EXP_FF, dtype=jnp.int32))[:, None] * CAP_FF
-    rows_ffn = (order + jnp.arange(CAP_FF, dtype=jnp.int32)[None, :]).reshape(EXP_FF * CAP_FF)
-    pick_ffn = [(rows_ffn[:, None] == slots_ffn[None, :, k]).astype(BF16) for k in range(TOPK)]
-    pick_ffn_any = pick_ffn[0] + pick_ffn[1]
-
-    def blocks_of(rows):
-        blocks = rows.reshape(EXP_FF, CAP_FF, rows.shape[1])
-        return [blocks[j] for j in range(EXP_FF)]
-
-    masked_cot = cotangent * valid.astype(BF16)[:, None]
-    left_down_own = lax.dynamic_slice_in_dim(left_down, col * slice_width, slice_width, 1)
-    grad_low_down_part = mm("td,rd->tr", masked_cot, left_down_own)
-    if cot_rows is None:
-        cot_rows = spread_cot(
-            blocks_of(mm("ct,td->cd", pick_ffn_any, masked_cot).astype(BF16)), cols, replicas
-        )
-
-    x_wide = x_full.astype(F32)
-    scale_one = lax.rsqrt(jnp.mean(x_wide * x_wide, axis=1, keepdims=True) + EPSILON)
-    hidden_one = (x_wide * scale_one * norm_one).astype(BF16)
-    chosen_attn = chosen_of(mm("td,de->te", hidden_one, router_attn), attn_route, EXP_ATT)
-    gates_attn = jax.nn.softmax(chosen_attn, axis=1)
-    rank_query = mm("td,rd->tr", hidden_one, left_query)
-    rank_kv = mm("td,rd->tr", hidden_one, left_kv)
-    kv_raw = mm("td,sdw->stw", hidden_one, kv_full) + mm(
-        "tr,rsw->stw", rank_kv.astype(BF16), right_kv.astype(BF16)
-    )
-    query_width = kv_raw.shape[2]
-    heads = query_width // HEAD_DIM
-    keys = rotate(
-        kv_raw[0].reshape(count, heads, HEAD_DIM), cosine[:, None], sine[:, None]
-    ).astype(BF16)
-    values = kv_raw[1].reshape(count, heads, HEAD_DIM).astype(BF16)
-    small = jnp.concatenate([rank_query, gates_attn, cosine, sine], axis=1)
-    small_rows = exact("ct,tx->cx", pick_attn_any.astype(F32), small)
-    rank_query_rows = small_rows[:, :RANK]
-    gate_rows = exact("ct,tx->cx", pick_attn[0].astype(F32), gates_attn[:, :1]) + exact(
-        "ct,tx->cx", pick_attn[1].astype(F32), gates_attn[:, 1:]
-    )
-    half = HEAD_DIM // 2
-    cosine_rows = small_rows[:, RANK + TOPK : RANK + TOPK + half]
-    sine_rows = small_rows[:, RANK + TOPK + half :]
-    hidden_rows = mm("ct,td->cd", pick_attn_any, hidden_one).astype(BF16)
-    query_rows = mm(
-        "ecd,edw->ecw", hidden_rows.reshape(EXP_ATT, CAP_ATT, width), query_full
-    ).reshape(EXP_ATT * CAP_ATT, query_width) + mm(
-        "cr,rw->cw", rank_query_rows.astype(BF16), right_query.astype(BF16)
-    )
-    query_rows = (
-        rotate(
-            query_rows.reshape(EXP_ATT * CAP_ATT, heads, HEAD_DIM),
-            cosine_rows[:, None],
-            sine_rows[:, None],
-        )
-        .astype(BF16)
-        .reshape(EXP_ATT * CAP_ATT, query_width)
-    )
-    queries = (
-        mm("cx,cw->xw", pick_attn_both, query_rows)
-        .astype(BF16)
-        .reshape(TOPK, count, heads, HEAD_DIM)
-    )
-    allowed = (position[None, :] <= position[:, None]) & (position[None, :] < length)
-    scores = mm("kbhd,jhd->hkbj", queries, keys) * scaling
-    scores = jnp.where(allowed[None, None], scores, -1e30)
-    exponent = jnp.exp(scores - jnp.max(scores, axis=-1, keepdims=True))
-    probability = exponent / jnp.sum(exponent, axis=-1, keepdims=True)
-    probs = probability.astype(BF16)
-    attended = mm("hkbj,jhd->kbhd", probs, values).astype(BF16).reshape(TOPK * count, query_width)
-    attended_rows = mm("cx,xw->cw", pick_attn_both, attended).astype(BF16)
-    attended_rows = later(attended_rows, inner_flat)
-    out_rows = mm(
-        "ecw,edw->ecd", attended_rows.reshape(EXP_ATT, CAP_ATT, query_width), out_full
-    ).reshape(EXP_ATT * CAP_ATT, width)
-    out_rows = (out_rows * gate_rows).astype(BF16)
-    low_rows = mm("cw,rw->cr", attended_rows, right_out.astype(BF16)) * gate_rows
-    low_rows = jnp.pad(low_rows.astype(BF16), ((0, 0), (RANK, LANES - 2 * RANK)))
-    lefts_flat = lefts.reshape(5 * RANK, width)
-
     *outs, hidden_two, middle, stat_ffn, totals_attn = middle_forward(
         adapter_pick,
         norm_two[None, :],
         router_ffn.T,
-        table_of(ffn_route[:, 0:1].astype(F32), ffn_route[:, 1:2].astype(F32), valid[:, None]),
+        stat_attn,
         low_rows,
-        jnp.pad(grad_low_down_part, ((0, 0), (2 * RANK, LANES - 3 * RANK))),
-        [out_rows, pick_attn_any, pick_ffn[0], pick_ffn[1], lefts_flat, inputs],
+        low_in,
+        [out_rows, picks_attn, picks_ffn, lefts, inputs],
         [inner_flat, down_flat],
         rows_axis,
         cols,
@@ -1293,7 +1442,7 @@
         norm_two[None, :],
         router_ffn.T,
         stat_ffn,
-        [pick_ffn[0], pick_ffn[1], lefts_flat, hidden_two, middle, cotangent],
+        [picks_ffn, lefts, hidden_two, middle, cotangent],
         cols,
         replicas,
     )
@@ -1305,21 +1454,17 @@
     branch_own = partials(branch_ffn)
     output = ((middle + branch_own) * valid[:, None]).astype(BF16)
 
-    grad_low_out = mm("td,rd->tr", grad_full, left_out)
-    grad_middle_rows = mm("ct,td->cd", pick_attn_any, grad_full).astype(BF16)
-    grad_low_rows = mm("ct,tr->cr", pick_attn_any, grad_low_out.astype(BF16)).astype(BF16)
+    grad_low_out = mm("td,rd->tr", grad_full, lefts[2 * RANK : 3 * RANK])
+    grad_middle_rows = mm("tc,td->cd", pick_attn_any, grad_full).astype(BF16)
+    grad_low_rows = mm("tc,tr->cr", pick_attn_any, grad_low_out.astype(BF16)).astype(BF16)
     grad_att_rows = mm(
         "ecd,edw->ecw", grad_middle_rows.reshape(EXP_ATT, CAP_ATT, width), out_full
-    ).reshape(EXP_ATT * CAP_ATT, query_width) + mm(
-        "cr,rw->cw", grad_low_rows, right_out.astype(BF16)
-    )
+    ).reshape(EXP_ATT * CAP_ATT, query_width) + mm("cr,rw->cw", grad_low_rows, right_out)
     gg_attn_rows = jnp.sum(attended_rows.astype(F32) * grad_att_rows, axis=1, keepdims=True)
-    grad_gates_attn_part = jnp.concatenate(
-        [exact("ct,cx->tx", pick_attn[k].astype(F32), gg_attn_rows) for k in range(TOPK)], axis=1
-    )
+    grad_gates_attn_part = exact("ktc,cx->ktx", pick_attn_both.astype(F32), gg_attn_rows)
     grad_att_rows = (grad_att_rows * gate_rows).astype(BF16)
     grad_attended = (
-        mm("cx,cw->xw", pick_attn_both, grad_att_rows)
+        mm("ktc,cw->ktw", pick_attn_both, grad_att_rows)
         .astype(BF16)
         .reshape(TOPK, count, heads, HEAD_DIM)
     )
@@ -1330,7 +1475,7 @@
     grad_scores = (probability * (grad_prob - centre)).astype(BF16)
     grad_queries = mm("hkbj,jhd->kbhd", grad_scores, keys) * scaling
     grad_keys = mm("hkbj,kbhd->jhd", grad_scores, queries) * scaling
-    grad_values = mm("hkbj,kbhd->jhd", probs, grad_attended)
+    grad_values = mm("hkbj,kbhd->jhd", probability.astype(BF16), grad_attended)
     grad_query_raw = (
         rotate(grad_queries, cosine[None, :, None], -sine[None, :, None])
         .astype(BF16)
@@ -1338,7 +1483,9 @@
     )
     grad_key_raw = rotate(grad_keys, cosine[:, None], -sine[:, None])
     grad_kv = jnp.stack([grad_key_raw, grad_values]).astype(BF16).reshape(2, count, query_width)
-    grad_query_rows = mm("cx,xw->cw", pick_attn_both, grad_query_raw).astype(BF16)
+    grad_query_rows = mm(
+        "ktc,ktw->cw", pick_attn_both, grad_query_raw.reshape(TOPK, count, query_width)
+    ).astype(BF16)
     grad_one_rows = (
         mm("ecw,edw->ecd", grad_query_rows.reshape(EXP_ATT, CAP_ATT, query_width), query_full)
         .astype(BF16)
@@ -1348,21 +1495,21 @@
         grad_query_raw.astype(F32).reshape(TOPK, count, query_width), axis=0
     )
     grad_query_sum_low = grad_query_sum.astype(BF16)
-    grad_rank_query = mm("tw,rw->tr", grad_query_sum_low, right_query.astype(BF16))
-    grad_rank_kv = mm("stw,rsw->tr", grad_kv, right_kv.astype(BF16))
+    grad_rank_query = mm("tw,rw->tr", grad_query_sum_low, right_query)
+    grad_rank_kv = mm("stw,srw->tr", grad_kv, right_kv)
     grad_one_part = (
-        mm("ct,cd->td", pick_attn_any, grad_one_rows)
+        mm("tc,cd->td", pick_attn_any, grad_one_rows)
         + mm("stw,sdw->td", grad_kv, kv_full)
         + mm(
             "tr,rd->td",
             jnp.concatenate([grad_rank_query, grad_rank_kv], axis=1).astype(BF16),
-            jnp.concatenate([left_query, left_kv], axis=0),
+            lefts[: 2 * RANK],
         )
     )
     grad_right_query = mm("tr,tw->rw", rank_query.astype(BF16), grad_query_sum_low)
     grad_right_kv = mm("tr,stw->rsw", rank_kv.astype(BF16), grad_kv)
-    cot_full = features(masked_cot)
-    small = table_of(grad_gates_attn_part[:, 0:1], None, grad_gates_attn_part[:, 1:2])
+    cot_full = features(cotangent * valid.astype(BF16)[:, None])
+    small = table_of(grad_gates_attn_part[0], None, grad_gates_attn_part[1])
     small += jnp.pad(
         jnp.concatenate([grad_rank_query, grad_rank_kv, low_down_part[:, RANK : 2 * RANK]], axis=1),
         ((0, 0), (RANK, LANES - 4 * RANK)),
@@ -1380,15 +1527,7 @@
         small,
         norm_one[None, :],
         router_attn.T,
-        table_of(
-            gates_attn[:, 0:1],
-            gates_attn[:, 1:2],
-            chosen_attn[:, 0:1],
-            chosen_attn[:, 1:2],
-            scale_one,
-            attn_route[:, 0:1].astype(F32),
-            attn_route[:, 1:2].astype(F32),
-        ),
+        stat_attn,
         lows,
         right_parts,
         [hidden_one, grad_full, hidden_two, cot_full, inputs, grad_middle],

time: 666 us -> 649 us (0.974)
  Pallas kernels: 418 us -> 502 us
  local copies, waits for them, and re-layouts: 81.7 us -> 44.1 us
  matrix products: 91.1 us -> 58.6 us
  blocking collectives: 8.37 us -> 0 us
  other arithmetic: 27.9 us -> 19.7 us
    pallas_call x1, Pallas kernels: 107 us -> 191 us  [front(): pl.pallas_call(functools.partial(front_kernel, parts, cols, replicas), ou...]
    dot_general x36 -> x19, matrix products: 84.3 us -> 56.9 us  [mm(): return jnp.einsum(spec, a, b, preferred_element_type=F32)]
    reshape x7 -> x4, local copies, waits for them, and re-layouts: 25.7 us -> 5.03 us  [the longest x2 2.23 us: on_device(): grad_attended = mm('ktc,cw->ktw', pick_attn_both, grad_att_rows).astype(B...]
    unnamed x1 -> x0, blocking collectives: 8.37 us -> none
    unnamed x248 -> x112, local copies, waits for them, and re-layouts: 31.8 us -> 28.2 us
  transfers between devices with their start and end apart: 5 -> 3, of which waited for: 1 -> 0; matrix products, arithmetic and copies ran while one was open for 24% -> 14% of each run, Pallas kernels for 15% -> 15%
where the time goes in v6:
time: 649 us; the launch traced here: 642 us
  Pallas kernels  502 us (77%)
  matrix products  58.6 us (9%)
  local copies, waits for them, and re-layouts  44.1 us (7%)
  other arithmetic  19.7 us (3%)
  between operations  17.7 us (3%)
    pallas_call x1, Pallas kernels, front(): pl.pallas_call(functools.partial(front_kernel, parts, cols, replicas), ou...  191 us
    pallas_call x1, Pallas kernels, middle_forward(): pl.pallas_call(functools.partial(middle_kernel, parts_axis, cols, replica...  132 us
    pallas_call x1, Pallas kernels, middle_back(): pl.pallas_call(functools.partial(middle_back_kernel, cols, replicas), out...  98.6 us
    dot_general x19, matrix products, mm(): return jnp.einsum(spec, a, b, preferred_element_type=F32)  56.9 us
    pallas_call x1, Pallas kernels, feed_forward(): pl.pallas_call(functools.partial(ffn_kernel, parts, depth, width, units),...  42.2 us
    pallas_call x1, Pallas kernels, input_back(): pl.pallas_call(functools.partial(input_back_kernel, parts_axis, cols), ou...  37.4 us
    unnamed x112, local copies, waits for them, and re-layouts  28.2 us
  transfers between devices with their start and end apart: 3, of which 0 were waited for; matrix products, arithmetic and copies ran while one was open for 14% of the time, Pallas kernels for 15%

profile of v6, /device:TPU:9, one launch (start us, length us, event | category | flops | bytes accessed | tf_op | source)
XLA Modules:
  0.0 642.4 jit_solution(6809481984247345339)
XLA Ops:
  9.7 1.5 copy.149.refs_2_
  11.2 1.5 copy.150.refs_3_
  12.7 1.2 copy.151
  15.2 0.8 pad_maximum_fusion.7
  16.1 1.1 pad_maximum_fusion.refs_24_
  17.8 191.5 %shard_map.328 = (bf16[4,256,2816]{2,1,0:T(8,128)(2,1)}, bf16[2,2048,512]{2,1,0:T(8,128)(2,1)}, bf16[8,2048,512]{2,1,0:T(8,128)(2,1)}, bf16[8,2048,512]{2,1,0:T(...) custom-call(s32[1]{0:T(128)} %copy.214.refs_0_, ...), custom_call_target="tpu_custom_call" | custom-call | tf_op jit(solution)/shard_map/pallas_call | solution.py:522
  209.3 1.1 copy-done.3
  210.4 1.0 copy-done.7
  211.3 0.9 copy-done.9
  212.2 0.9 copy-done.24
  213.2 0.9 copy-done.25
  214.1 132.2 %shard_map.329 = (bf16[256,2816]{1,0:T(8,128)(2,1)}, bf16[256,2816]{1,0:T(8,128)(2,1)}, bf16[256,2816]{1,0:T(8,128)(2,1)}, bf16[256,2816]{1,0:T(8,128)(2,1)}, bf...) custom-call(s32[1]{0:T(128)} %copy.215.refs_1_.refs_0_.refs_8_, ...), custom_call_target="tpu_custom_call" | custom-call | tf_op jit(solution)/shard_map/pallas_call | solution.py:1096
  346.3 0.8 copy-done.12
  347.2 0.9 copy-done.13
  348.0 0.9 copy-done.14
  348.9 0.9 copy-done.15
  349.8 0.9 copy-done.16
  350.8 42.2 %shard_map.330 = (bf16[160,2304]{1,0:T(8,128)(2,1)}, bf16[160,2304]{1,0:T(8,128)(2,1)}, bf16[160,2304]{1,0:T(8,128)(2,1)}, bf16[160,2304]{1,0:T(8,128)(2,1)}, bf...) custom-call(bf16[160,2432]{1,0:T(8,128)(2,1)} %get-tuple-element.98., ...), custom_call_target="tpu_custom_call" | custom-call | tf_op jit(solution)/shard_map/pallas_call | solution.py:1248
  393.1 1.1 copy-done.17
  394.1 1.1 copy-done.18
  395.2 1.1 copy-done.19
  396.3 1.1 copy-done.20
  397.4 98.6 %shard_map.331 = (f32[256,512]{1,0:T(8,128)S(1)}, bf16[256,2048]{1,0:T(8,128)(2,1)}, f32[256,128]{1,0:T(8,128)S(1)}, bf16[256,2048]{1,0:T(8,128)(2,1)}, f32[256,128]{1,0:T(8,128)S(1)}) custom-call(bf16[160,2304]{1,0:T(8,128)(2,1)} %get-tuple-element.120.refs_0_, bf16[160,2304]{1,0:T(8,128)(2,1)} %get-tuple-element.121.refs_1_, ...), custom_call_target="tpu_custom_call" | custom-call | tf_op jit(solution)/shard_map/pallas_call | solution.py:710
  496.1 0.8 copy-done.21
  497.2 0.8 broadcast_multiply_fusion
  498.0 1.6 fusion.28
  499.6 3.4 convolution_convert_fusion
  505.7 10.8 %fusion.51 = f32[8,80,512]{2,1,0:T(8,128)} fusion(bf16[8,80,2048]{2,1,0:T(8,128)(2,1)} %bitcast.164, bf16[8,2048,512]{2,1,0:T(8,128)(2,1)} %get-tuple-element.135), kind=kOutput, calls=%fused_computation.109 | convolution fusion | flops 1342177280 | bytes 20709376 | tf_op jit(solution)/shard_map/ecd,edw->ecw/dot_general | solution.py:27
  516.5 1.1 reduce.3
  517.7 3.6 multiply_reduce_fusion.1
  521.3 2.2 convolution_convert_fusion.2
  523.4 0.9 reshape.260
  524.4 1.3 copy.166
  525.7 1.7 reshape.261
  527.4 2.8 fusion.4
  530.2 2.5 multiply_reduce_fusion
  532.7 1.1 copy.186
  533.8 2.6 multiply_convert_fusion
  537.1 0.8 fusion.46
  537.9 0.8 convolution_convert_fusion.5
  539.9 1.8 copy.167
  541.7 1.8 copy.168
  543.5 1.3 convolution_convert_fusion.3
  545.0 1.7 fusion.52
  546.8 1.9 fusion.45
  550.2 0.8 slice.94
  551.0 1.6 fusion.1
  552.7 4.9 convolution_bitcast_fusion
  557.6 1.0 convert_reduce_fusion.refs_0_
  558.8 12.4 %convolution_convert_fusion.1 = bf16[8,80,2048]{2,1,0:T(8,128)(2,1)} fusion(bf16[8,80,512]{2,1,0:T(8,128)(2,1)S(1)} %bitcast.168, bf16[8,2048,512]{2,1,0:T(8,128)(2,1)} %get-tuple-element.138), kind=kOutput, calls=%fused_computation.1 | convolution fusion | flops 1343488000 | bytes 20054016 | tf_op jit(solution)/shard_map/ecw,edw->ecd/dot_general | solution.py:27
  571.8 1.5 fusion.22.refs_2_
  574.1 3.5 convolution_add_fusion
  577.6 1.8 convolution_add_fusion.1.refs_1_
  579.4 1.6 copy.173
  581.0 1.5 copy.174
  582.5 0.9 convert.51
  583.4 2.8 maximum_convert_fusion.1
  586.2 1.8 multiply_convert_fusion.2
  588.0 1.0 copy-done.22
  589.0 0.8 copy-done.23
  589.9 0.8 copy-done.26
  590.6 37.4 %shard_map.332 = (f32[256,512]{1,0:T(8,128)S(1)}, f32[8,16,256]{2,1,0:T(8,128)S(1)}, f32[8,16,256]{2,1,0:T(8,128)S(1)}, f32[8,16,256]{2,1,0:T(8,128)S(1)}, f32[8...) custom-call(s32[8]{0:T(128)S(1)} %convert_reduce_fusion.refs_0_, ...), custom_call_target="tpu_custom_call" | custom-call | tf_op jit(solution)/shard_map/pallas_call | solution.py:879
  628.1 1.2 copy.175
  629.3 0.8 copy.216
  (135 shorter events, 15.2 us)
Async XLA Ops:
  8.0 1.0 copy-start
  8.0 571.3 %all-reduce.4.cloned.1.call-start = ((), (), s32[]{:S(2)}) async-start(), calls=%async_computation.3 | async-start | bytes 2162688 | tf_op jit(solution)/shard_map/psum | solution.py:1449
  11.1 4.9 copy-start.37
  17.7 191.5 %copy-start.6 = (bf16[256,512]{1,0:T(8,128)(2,1)S(1)}, bf16[256,512]{1,0:T(8,128)(2,1)}, u32[]{:S(2)}) copy-start(bf16[256,512]{1,0:T(8,128)(2,1)} %refs_12_.3) | copy-start | bytes 786436
  17.7 191.5 %copy-start.27 = (bf16[2048,4]{0,1:T(4,128)(2,1)S(1)}, bf16[2048,4]{0,1:T(4,128)(2,1)}, u32[]{:S(2)}) copy-start(bf16[2048,4]{0,1:T(4,128)(2,1)} %param.34) | copy-start | bytes 49156
  17.8 191.5 %copy-start.28 = (f32[2048]{0:T(1024)S(1)}, f32[2048]{0:T(1024)}, u32[]{:S(2)}) copy-start(f32[2048]{0:T(1024)} %param.32) | copy-start | bytes 24580
  209.3 1.1 copy-start.3
  210.4 1.0 copy-start.7
  211.3 0.9 copy-start.9
  212.2 0.9 copy-start.24
  213.2 0.9 copy-start.25
  346.3 0.9 copy-start.12
  347.2 0.9 copy-start.13
  348.0 0.9 copy-start.14
  348.9 0.9 copy-start.15
  349.8 0.9 copy-start.16
  350.8 42.3 %copy-start.4 = (bf16[2,256,640]{2,1,0:T(8,128)(2,1)S(1)}, bf16[2,256,640]{2,1,0:T(8,128)(2,1)}, u32[]{:S(2)}) copy-start(bf16[2,256,640]{2,1,0:T(8,128)(2,1)} %get-tuple-element.94.refs_8_.refs_12_) | copy-start | bytes 1966084
  350.8 42.3 %copy-start.5 = (bf16[256,512]{1,0:T(8,128)(2,1)S(1)}, bf16[256,512]{1,0:T(8,128)(2,1)}, u32[]{:S(2)}) copy-start(bf16[256,512]{1,0:T(8,128)(2,1)} %refs_16_.5) | copy-start | bytes 786436
  350.8 42.3 %copy-start.8 = (bf16[80,2048]{1,0:T(8,128)(2,1)S(1)}, bf16[80,2048]{1,0:T(8,128)(2,1)}, u32[]{:S(2)}) copy-start(bf16[80,2048]{1,0:T(8,128)(2,1)} %get-tuple-element.95.refs_9_.refs_13_) | copy-start | bytes 983044
  393.0 193.2 %reduce-scatter.2.cloned.1.call-start = ((), (), s32[]{:S(2)}) async-start(), calls=%async_computation.1 | async-start | bytes 1310720 | tf_op jit(solution)/shard_map/reduce_scatter | solution.py:1314
  393.0 1.1 copy-start.17
  394.1 1.1 copy-start.18
  395.2 1.1 copy-start.19
  396.3 1.1 copy-start.20
  496.1 0.8 copy-start.21
  496.9 2.7 copy-start.2
  496.9 91.0 %all-gather.2.cloned.1.call-start = ((), (), s32[]{:S(2)}) async-start(), calls=%async_computation.2 | async-start | bytes 1310720 | tf_op jit(solution)/shard_map/all_gather | solution.py:1311
  499.6 18.1 %copy-start.40 = (f32[256,16]{0,1:T(8,128)}, f32[256,16]{0,1:T(8,128)S(1)}, u32[]{:S(2)}) copy-start(f32[256,16]{0,1:T(8,128)S(1)} %fusion.28) | copy-start | bytes 49156
  499.6 3.6 copy-start.10
  505.7 12.0 %copy-start.32 = (bf16[640,512]{1,0:T(8,128)(2,1)S(1)}, bf16[640,512]{1,0:T(8,128)(2,1)}, u32[]{:S(2)}) copy-start(bf16[640,512]{1,0:T(8,128)(2,1)} %get-tuple-element.146) | copy-start | bytes 1966084
  527.4 2.8 copy-start.30
  527.4 2.8 copy-start.31
  530.2 3.6 copy-start.42
  536.9 1.8 copy-start.35
  539.1 5.8 copy-start.34
  539.1 5.9 copy-start.47
  539.2 7.6 %copy-start.46 = (bf16[32,512]{1,0:T(8,128)(2,1)S(1)}, bf16[32,512]{1,0:T(8,128)(2,1)}, u32[]{:S(2)}) copy-start(bf16[32,512]{1,0:T(8,128)(2,1)} %pad_maximum_fusion.11) | copy-start | bytes 98308
  539.9 9.5 %copy-start.43 = (f32[256,16]{0,1:T(8,128)S(1)}, f32[256,16]{0,1:T(8,128)}, u32[]{:S(2)}) copy-start(f32[256,16]{0,1:T(8,128)} %get-tuple-element.251) | copy-start | bytes 49156
  550.2 2.5 copy-start.38
  550.2 2.5 copy-start.39
  552.6 5.9 copy-start.33
  552.6 5.9 copy-start.41
  558.8 12.5 %copy-start.44 = (bf16[16,512]{1,0:T(8,128)(2,1)S(1)}, bf16[16,512]{1,0:T(8,128)(2,1)}, u32[]{:S(2)}) copy-start(bf16[16,512]{1,0:T(8,128)(2,1)} %convolution_convert_fusion.5) | copy-start | bytes 49156
  558.8 14.6 %copy-start.49 = (pred[128]{0:T(512)(128)(4,1)S(1)}, pred[128]{0:T(512)(128)(4,1)}, u32[]{:S(2)}) copy-start(pred[128]{0:T(512)(128)(4,1)} %get-tuple-element.260) | copy-start | bytes 388
  574.0 3.5 copy-start.45
  574.1 3.5 copy-start.48
  579.4 3.1 copy-start.36
  583.4 4.5 copy-start.11
  583.4 4.5 copy-start.29
  588.0 1.0 copy-start.22
  589.0 0.8 copy-start.23
  589.9 0.8 copy-start.26
  628.0 6.7 %copy-start.1 = (bf16[8,16,2,512]{3,2,1,0:T(2,128)(2,1)S(1)}, bf16[8,16,2,512]{3,2,1,0:T(2,128)(2,1)}, u32[]{:S(2)}) copy-start(bf16[8,16,2,512]{3,2,1,0:T(2,128)(2,1)} %param.43) | copy-start | bytes 786436
Sparse Core Ops, SparseCore 0:
  393.1 65.6 all-reduce.3
Sparse Core Ops, SparseCore 1:
  497.0 24.2 reduce-scatter.1
  522.8 28.0 all-gather.1

commit v7 on v6

--- a/solution.py
+++ b/solution.py
@@ -23,28 +23,11 @@
 LANES = 128
 
 
-def mm(spec, a, b):
-    return jnp.einsum(spec, a, b, preferred_element_type=F32)
-
-
-def exact(spec, a, b):
-    return jnp.einsum(spec, a, b, precision=HIGHEST, preferred_element_type=F32)
-
-
 def tables(count, head_width):
     position = jnp.arange(count).astype(F32)
     frequency = ROPE_BASE ** (-jnp.arange(head_width // 2).astype(F32) * 2.0 / head_width)
     angle = position[:, None] * frequency[None, :]
     return (jnp.cos(angle), jnp.sin(angle))
-
-
-def rotate(values, cosine, sine):
-    half = values.shape[-1] // 2
-    first = values[..., :half]
-    second = values[..., half:]
-    return jnp.concatenate(
-        [first * cosine - second * sine, second * cosine + first * sine], axis=-1
-    )
 
 
 def opposite(axis, offset):
@@ -562,7 +545,7 @@
             pltpu.SemaphoreType.DMA((4,)),
         ],
         compiler_params=pltpu.CompilerParams(
-            collective_id=1, has_side_effects=True, vmem_limit_bytes=56 * 2**20
+            collective_id=1, has_side_effects=True, vmem_limit_bytes=62 * 2**20
         ),
     )(*smalls, *lefts, tokens, *blocks, pairs)
 
@@ -733,173 +716,374 @@
             pltpu.SemaphoreType.DMA((9,)),
         ],
         compiler_params=pltpu.CompilerParams(
-            collective_id=4, has_side_effects=True, vmem_limit_bytes=48 * 2**20
+            collective_id=4, has_side_effects=True, vmem_limit_bytes=62 * 2**20
         ),
     )(*blocks, *downs, adapter, norm, router, stat, *sources)
 
 
-def input_back_kernel(parts_axis, cols, *refs):
-    adapters, part, small_in, norm, router, stat, lows, rights = refs[:8]
-    sources = refs[8:14]
-    grad_inputs = refs[14]
-    left_outs = refs[15:20]
-    right_outs = refs[20:24]
-    hidden_one, grad_whole, hidden_two, cot_whole, tokens, grad_middle = refs[24:30]
-    parts, extra, parts_in, extra_in, lefts, lefts_in, rights_in, send, recv, local = refs[30:]
+def tail_kernel(parts_axis, cols, *refs):
+    (
+        adapters,
+        norm,
+        router,
+        stat,
+        cosine,
+        sine,
+        rights,
+        ranks,
+        gate_rows,
+        totals_attn,
+        totals_ffn,
+        low_down,
+    ) = refs[:12]
+    sources = refs[12:27]
+    branch, out_whole, query_whole, kv_whole = refs[27:31]
+    output, grad_inputs = refs[31:33]
+    left_outs = refs[33:38]
+    right_outs = refs[38:42]
+    (
+        grad_whole,
+        picks,
+        att_rows,
+        queries,
+        keys,
+        values,
+        probability,
+        attended,
+        lefts_whole,
+        hidden_one,
+        hidden_two,
+        grad_middle,
+        middle,
+        cot,
+        tokens,
+    ) = refs[42:57]
+    (
+        cot_own,
+        cot_whole,
+        branch_in,
+        rows,
+        grads,
+        buffer,
+        query_grads,
+        key_grad,
+        value_grad,
+        part,
+        parts,
+        extra,
+        parts_in,
+        extra_in,
+        right_parts,
+        rights_in,
+        lefts,
+        lefts_in,
+        send,
+        recv,
+        local,
+        load,
+    ) = refs[57:]
     row = lax.axis_index("row")
     col = lax.axis_index("col")
     count, wide = tokens.shape
     width = hidden_one.shape[1]
     depth = width // parts_axis
-    right_width = rights.shape[1] // 4
+    head_width = keys.shape[1]
+    heads = head_width // HEAD_DIM
     along = [opposite("col", i) for i in range(1, cols)]
     across = [opposite("row", m) for m in range(1, parts_axis)]
     greet(across + along)
-    near = fetch(sources, refs[24:30], local)
-    near[0].wait()
+    started = []
+
+    def send_to(source, target, device):
+        copy = remote(source, target, send, recv, len(started), device)
+        started.append(copy)
+        return copy
+
+    pair = 2
+    chunks = [
+        (whole, start)
+        for whole in (out_whole, query_whole, kv_whole)
+        for start in range(0, whole.shape[0], pair)
+    ]
+    loads = []
+    for n, (whole, start) in enumerate(chunks):
+        loads.append(
+            pltpu.make_async_copy(whole.at[pl.ds(start, pair)], buffer.at[n % 2], load.at[n % 2])
+        )
+    near = fetch(sources, refs[42:57], local)
+    loads[0].start()
+    loads[1].start()
+    first = pl.multiple_of(col * wide, wide)
+    here = pl.ds(first, wide)
+    valid = stat[:, 7:8]
+    branch_copies = []
+    for i in range(1, cols):
+        target = jnp.bitwise_xor(col, i)
+        theirs = pl.ds(pl.multiple_of(target * wide, wide), wide)
+        branch_copies.append(send_to(branch.at[:, theirs], branch_in.at[i - 1], along[i - 1]))
+    mine = pltpu.make_async_copy(branch.at[:, here], branch_in.at[cols - 1], local.at[15])
+    mine.start()
+    for copy in near:
+        copy.wait()
+    cot_own[...] = (cot[...].astype(F32) * valid).astype(BF16)
+    cot_whole[:, here] = cot_own[...]
+    cot_copies = [send_to(cot_own, cot_whole.at[:, here], device) for device in along]
+
+    def rows_of(matrix, value):
+        return lax.dot_general(
+            matrix, value, (((0,), (0,)), ((), ())), preferred_element_type=F32
+        )
+
+    def times(left, right):
+        return lax.dot_general(
+            left, right, (((1,), (1,)), ((), ())), preferred_element_type=F32
+        )
+
+    def dot(left, right):
+        return jnp.dot(left, right, preferred_element_type=F32)
+
+    any_pick = picks[TOPK]
+    low_grad = times(grad_whole[...], lefts_whole[2 * RANK : 3 * RANK])
+    low_rows = rows_of(any_pick, low_grad.astype(BF16)).astype(BF16)
+    for q in range(cols):
+        span = slice(q * wide, (q + 1) * wide)
+        rows[:, span] = rows_of(any_pick, grad_whole[:, span]).astype(BF16)
+    number = 0
+
+    def next_weights():
+        nonlocal number
+        loads[number].wait()
+        return buffer.at[number % 2]
+
+    def done_weights():
+        nonlocal number
+        if number + 2 < len(chunks):
+            loads[number + 2].start()
+        number += 1
+
+    for start in range(0, EXP_ATT, pair):
+        weight = next_weights()
+        for item in range(pair):
+            span = slice((start + item) * CAP_ATT, (start + item + 1) * CAP_ATT)
+            grads[span] = dot(rows[span], weight[item]) + dot(low_rows[span], rights[3 * RANK :])
+        done_weights()
+    value = grads[...]
+    gate_grad = jnp.sum(att_rows[...].astype(F32) * value, axis=1, keepdims=True)
+    gate_pack = pack([*split(gate_grad)], range(2)).astype(BF16)
+    gate_grads = []
+    gated = (value * gate_rows[...]).astype(BF16)
+    right_out = jnp.zeros((RANK, head_width), F32)
+    for k in range(TOPK):
+        both = dot(picks[k], gate_pack)
+        gate_grads.append(both[:, 0:1] + both[:, 1:2])
+        query_grads[k] = dot(picks[k], gated).astype(BF16)
+        right_out += rows_of((stat[:, k : k + 1] * low_grad).astype(BF16), attended[k])
+    scaling = HEAD_DIM ** (-0.5)
+    query_sum = []
+    for h in range(heads):
+        span = slice(h * HEAD_DIM, (h + 1) * HEAD_DIM)
+        key_total, value_total, sum_head = 0.0, 0.0, 0.0
+        for k in range(TOPK):
+            grad_att = query_grads[k, :, span]
+            probs = probability[h, k]
+            grad_prob = times(grad_att, values[:, span])
+            centre = jnp.sum(probs * grad_prob, axis=1, keepdims=True)
+            grad_score = (probs * (grad_prob - centre)).astype(BF16)
+            value_total += rows_of(probs.astype(BF16), grad_att)
+            key_total += rows_of(grad_score, queries[k, :, span])
+            grad_query = dot(grad_score, keys[:, span]) * scaling
+            turned = turn(grad_query, cosine[...], -sine[...]).astype(BF16)
+            query_grads[k, :, span] = turned
+            sum_head += turned.astype(F32)
+        key_grad[:, span] = turn(key_total * scaling, cosine[...], -sine[...]).astype(BF16)
+        value_grad[:, span] = value_total.astype(BF16)
+        query_sum.append(sum_head.astype(BF16))
+    query_sum = jnp.concatenate(query_sum, axis=1)
+    rank_query = ranks[:, :RANK].astype(BF16)
+    rank_kv = ranks[:, RANK:].astype(BF16)
+    right_values = [
+        rows_of(rank_query, query_sum),
+        rows_of(rank_kv, key_grad[...]),
+        rows_of(rank_kv, value_grad[...]),
+        right_out,
+    ]
+    for p in range(4):
+        right_parts[:, p * head_width : (p + 1) * head_width] = right_values[p].astype(BF16)
+    right_copies = [
+        send_to(right_parts, rights_in.at[m], across[m]) for m in range(parts_axis - 1)
+    ]
+    grad_rank_query = times(query_sum, rights[:RANK])
+    grad_rank_kv = times(key_grad[...], rights[RANK : 2 * RANK]) + times(
+        value_grad[...], rights[2 * RANK : 3 * RANK]
+    )
+    query_rows = (rows_of(picks[0], query_grads[0]) + rows_of(picks[1], query_grads[1])).astype(
+        BF16
+    )
+    for start in range(0, EXP_ATT, pair):
+        weight = next_weights()
+        for item in range(pair):
+            span = slice((start + item) * CAP_ATT, (start + item + 1) * CAP_ATT)
+            rows[span] = times(query_rows[span], weight[item]).astype(BF16)
+        done_weights()
+    weight = next_weights()
+    low = jnp.concatenate([grad_rank_query, grad_rank_kv], axis=1).astype(BF16)
     product = jnp.zeros((count, 1), F32)
     for q in range(cols):
-        value = part[:, q * wide : (q + 1) * wide]
-        product += jnp.sum(
-            value * hidden_one[:, q * wide : (q + 1) * wide].astype(F32), axis=1, keepdims=True
-        )
+        span = slice(q * wide, (q + 1) * wide)
+        value = (
+            dot(any_pick, rows[:, span])
+            + times(key_grad[...], weight[0, span])
+            + times(value_grad[...], weight[1, span])
+            + dot(low, lefts_whole[: 2 * RANK, span])
+        )
+        product += jnp.sum(value * hidden_one[:, span].astype(F32), axis=1, keepdims=True)
+        part[q] = value
         parts[q] = value.astype(BF16)
-    lane = lax.broadcasted_iota(jnp.int32, (count, LANES), 1)
-    columns = [*split(small_in[:, 0:1]), *split(small_in[:, 2:3]), *split(product)]
-    small = jnp.where(lane < RANK, 0.0, small_in[...]) + pack(columns, range(6))
+    columns = [*split(gate_grads[0]), *split(gate_grads[1]), *split(product)]
+    small = pack(columns, range(6)) + jnp.concatenate(
+        [
+            jnp.zeros((count, RANK), F32),
+            grad_rank_query,
+            grad_rank_kv,
+            low_down[:, RANK : 2 * RANK],
+            jnp.zeros((count, LANES - 4 * RANK), F32),
+        ],
+        axis=1,
+    )
     extra[...] = small.astype(BF16)
-    arrivals = []
+    extra_copies, part_copies = [], []
     for i in range(1, cols):
         target = jnp.bitwise_xor(col, i)
-        n = 2 * (i - 1)
-        arrivals.append(remote(extra, extra_in.at[i - 1], send, recv, n + 1, along[i - 1]))
-        arrivals.append(
-            remote(parts.at[target], parts_in.at[i - 1], send, recv, n, along[i - 1])
-        )
-    base = 2 * (cols - 1)
-    right_copies = [
-        remote(rights, rights_in.at[m], send, recv, base + m, across[m])
-        for m in range(parts_axis - 1)
-    ]
-    base += parts_axis - 1
-    total = small
-    for i in range(cols - 1):
-        arrivals[2 * i].wait_recv()
-        total += extra_in[i].astype(F32)
-    ranks = total.astype(BF16)
+        extra_copies.append(send_to(extra, extra_in.at[i - 1], along[i - 1]))
+        part_copies.append(send_to(parts.at[target], parts_in.at[i - 1], along[i - 1]))
+    mine.wait()
+    for copy in branch_copies:
+        copy.wait_recv()
+    result = middle[...]
+    for i in range(cols):
+        result += branch_in[i].astype(F32)
+    output[...] = (result * valid).astype(BF16)
+    for copy in cot_copies:
+        copy.wait_recv()
 
     def outer(left, right):
-        return lax.dot_general(
-            left, right, (((0,), (0,)), ((), ())), preferred_element_type=F32
-        ).astype(BF16)
-
-    for copy in near[1:]:
-        copy.wait()
-    whole = outer(ranks, hidden_one[...])
+        return rows_of(left, right).astype(BF16)
+
+    whole = outer(totals_attn[...].astype(BF16), grad_whole[...])
     for m in range(parts_axis):
-        lefts[m, : 2 * RANK] = whole[RANK : 3 * RANK, m * depth : (m + 1) * depth]
-    whole = outer(lows[...], grad_whole[...])
-    for m in range(parts_axis):
-        lefts[m, 2 * RANK : 3 * RANK] = whole[:RANK, m * depth : (m + 1) * depth]
-    whole = outer(lows[...], hidden_two[...])
+        lefts[m, 2 * RANK : 3 * RANK] = whole[RANK : 2 * RANK, m * depth : (m + 1) * depth]
+    whole = outer(totals_ffn[...].astype(BF16), hidden_two[...])
     for m in range(parts_axis):
         lefts[m, 3 * RANK : 4 * RANK] = whole[RANK : 2 * RANK, m * depth : (m + 1) * depth]
-    whole = outer(ranks, cot_whole[...])
-    for m in range(parts_axis):
-        lefts[m, 4 * RANK :] = whole[3 * RANK : 4 * RANK, m * depth : (m + 1) * depth]
-    left_copies = [
-        remote(
-            lefts.at[jnp.bitwise_xor(row, m)],
-            lefts_in.at[m - 1],
-            send,
-            recv,
-            base + m - 1,
-            across[m - 1],
-        )
-        for m in range(1, parts_axis)
-    ]
-    first = pl.multiple_of(col * wide, wide)
-    grad = part[:, pl.ds(first, wide)]
-    for i in range(cols - 1):
-        arrivals[2 * i + 1].wait_recv()
-        grad += parts_in[i].astype(F32)
-    gate_grads = [total[:, 0:1] + total[:, 1:2], total[:, 2:3] + total[:, 3:4]]
-    term, more = route_term(stat, gate_grads, router, first, wide)
-    inner = total[:, 4:5] + total[:, 5:6] + more
-    factor = stat[:, 4:5]
-    grad_inputs[...] = (
-        grad_middle[...]
-        + factor * ((grad + term) * norm[:, pl.ds(first, wide)])
-        - tokens[...].astype(F32) * (factor * factor * inner * (1.0 / width))
-    )
     chosen_by = [
-        [
-            jnp.where(adapters[m] == a, 1.0, 0.0).astype(F32)
-            for a in range(ADAPT)
-        ]
+        [jnp.where(adapters[m] == a, 1.0, 0.0).astype(F32) for a in range(ADAPT)]
         for m in range(parts_axis)
     ]
-    for copy in right_copies:
-        copy.wait_recv()
-    for p in range(4):
-        here = slice(p * right_width, (p + 1) * right_width)
-        values = [rights[:, here].astype(F32)] + [
-            rights_in[m, :, here].astype(F32) for m in range(parts_axis - 1)
-        ]
+
+    def share(values, target):
         for a in range(ADAPT):
             result = chosen_by[0][a] * values[0]
             for m in range(1, parts_axis):
                 result += chosen_by[m][a] * values[m]
-            right_outs[p][a] = result
+            target[a] = result
+
+    for copy in right_copies:
+        copy.wait_recv()
+    for p in range(4):
+        span = slice(p * head_width, (p + 1) * head_width)
+        share(
+            [right_parts[:, span].astype(F32)]
+            + [rights_in[m, :, span].astype(F32) for m in range(parts_axis - 1)],
+            right_outs[p],
+        )
+    total = small
+    for i in range(cols - 1):
+        extra_copies[i].wait_recv()
+        total += extra_in[i].astype(F32)
+    low_totals = total.astype(BF16)
+    whole = outer(low_totals, hidden_one[...])
+    for m in range(parts_axis):
+        lefts[m, : 2 * RANK] = whole[RANK : 3 * RANK, m * depth : (m + 1) * depth]
+    whole = outer(low_totals, cot_whole[...])
+    for m in range(parts_axis):
+        lefts[m, 4 * RANK :] = whole[3 * RANK : 4 * RANK, m * depth : (m + 1) * depth]
+    left_copies = [
+        send_to(lefts.at[jnp.bitwise_xor(row, m)], lefts_in.at[m - 1], across[m - 1])
+        for m in range(1, parts_axis)
+    ]
+    gate_totals = [total[:, 0:1] + total[:, 1:2], total[:, 2:3] + total[:, 3:4]]
+    term, more = route_term(stat, gate_totals, router, first, wide)
+    inner = total[:, 4:5] + total[:, 5:6] + more
+    grad = part[col] + term
+    for i in range(cols - 1):
+        part_copies[i].wait_recv()
+        grad += parts_in[i].astype(F32)
+    factor = stat[:, 4:5]
+    grad_inputs[...] = (
+        grad_middle[...]
+        + factor * (grad * norm[:, here])
+        - tokens[...].astype(F32) * (factor * factor * inner * (1.0 / width))
+    )
     for copy in left_copies:
         copy.wait_recv()
     for p in range(5):
-        here = slice(p * RANK, (p + 1) * RANK)
-        values = [lefts[row, here].astype(F32)] + [
-            lefts_in[m, here].astype(F32) for m in range(parts_axis - 1)
-        ]
-        for a in range(ADAPT):
-            result = chosen_by[0][a] * values[0]
-            for m in range(1, parts_axis):
-                result += chosen_by[m][a] * values[m]
-            left_outs[p][a] = result
-    for copy in arrivals + right_copies + left_copies:
+        span = slice(p * RANK, (p + 1) * RANK)
+        share(
+            [lefts[row, span].astype(F32)]
+            + [lefts_in[m, span].astype(F32) for m in range(parts_axis - 1)],
+            left_outs[p],
+        )
+    for copy in started:
         copy.wait_send()
 
 
-def input_back(adapters, part, small, norm, router, stat, lows, rights, sources, parts_axis, cols):
+def tail(smalls, sources, branch, wholes, parts_axis, cols):
     hbm = pl.BlockSpec(memory_space=pl.ANY)
     vmem = pl.BlockSpec(memory_space=pltpu.VMEM)
     smem = pl.BlockSpec(memory_space=pltpu.SMEM)
-    count, width = part.shape
-    wide = width // cols
+    count, wide = sources[-1].shape
+    width = wide * cols
     depth = width // parts_axis
-    right_width = rights.shape[1] // 4
-    total = 2 * (cols - 1) + 2 * (parts_axis - 1)
+    head_width = wholes[0].shape[2]
+    rows = EXP_ATT * CAP_ATT
+    shape = jax.ShapeDtypeStruct
+    total = 4 * (cols - 1) + 2 * (parts_axis - 1)
     return pl.pallas_call(
-        functools.partial(input_back_kernel, parts_axis, cols),
-        out_shape=[jax.ShapeDtypeStruct((count, wide), F32)]
-        + [jax.ShapeDtypeStruct((ADAPT, RANK, depth), F32)] * 5
-        + [jax.ShapeDtypeStruct((ADAPT, RANK, right_width), F32)] * 4,
-        in_specs=[smem] + [vmem] * 7 + [hbm] * 6,
-        out_specs=[vmem] * 10,
+        functools.partial(tail_kernel, parts_axis, cols),
+        out_shape=[shape((count, wide), BF16), shape((count, wide), F32)]
+        + [shape((ADAPT, RANK, depth), F32)] * 5
+        + [shape((ADAPT, RANK, head_width), F32)] * 4,
+        in_specs=[smem] + [vmem] * 11 + [hbm] * 19,
+        out_specs=[vmem] * 11,
         scratch_shapes=[pltpu.VMEM(source.shape, source.dtype) for source in sources]
         + [
+            pltpu.VMEM((count, wide), BF16),
+            pltpu.VMEM((count, width), BF16),
+            pltpu.VMEM((cols, count, wide), BF16),
+            pltpu.VMEM((rows, width), BF16),
+            pltpu.VMEM((rows, head_width), F32),
+            pltpu.VMEM((2, 2, width, head_width), BF16),
+            pltpu.VMEM((TOPK, count, head_width), BF16),
+            pltpu.VMEM((count, head_width), BF16),
+            pltpu.VMEM((count, head_width), BF16),
+            pltpu.VMEM((cols, count, wide), F32),
             pltpu.VMEM((cols, count, wide), BF16),
             pltpu.VMEM((count, LANES), BF16),
             pltpu.VMEM((cols - 1, count, wide), BF16),
             pltpu.VMEM((cols - 1, count, LANES), BF16),
+            pltpu.VMEM((RANK, 4 * head_width), BF16),
+            pltpu.VMEM((parts_axis - 1, RANK, 4 * head_width), BF16),
             pltpu.VMEM((parts_axis, 5 * RANK, depth), BF16),
             pltpu.VMEM((parts_axis - 1, 5 * RANK, depth), BF16),
-            pltpu.VMEM((parts_axis - 1, RANK, 4 * right_width), BF16),
             pltpu.SemaphoreType.DMA((total,)),
             pltpu.SemaphoreType.DMA((total,)),
-            pltpu.SemaphoreType.DMA((6,)),
+            pltpu.SemaphoreType.DMA((16,)),
+            pltpu.SemaphoreType.DMA((2,)),
         ],
         compiler_params=pltpu.CompilerParams(
-            collective_id=5, has_side_effects=True, vmem_limit_bytes=48 * 2**20
+            collective_id=5, has_side_effects=True, vmem_limit_bytes=62 * 2**20
         ),
-    )(adapters, part, small, norm, router, stat, lows, rights, *sources)
+    )(*smalls, *sources, branch, *wholes)
 
 
 def middle_kernel(parts_axis, cols, replicas, *refs):
@@ -1123,7 +1307,7 @@
             pltpu.SemaphoreType.DMA((8,)),
         ],
         compiler_params=pltpu.CompilerParams(
-            collective_id=3, has_side_effects=True, vmem_limit_bytes=48 * 2**20
+            collective_id=3, has_side_effects=True, vmem_limit_bytes=62 * 2**20
         ),
     )(adapter, norm, router, route, low_rows, low_in, *sources, *weights)
 
@@ -1260,7 +1444,7 @@
             pltpu.VMEM((rows, 1), F32),
             pltpu.SemaphoreType.DMA((3 * EXP_FF + 1 + 2 * parts,)),
         ],
-        compiler_params=pltpu.CompilerParams(vmem_limit_bytes=56 * 2**20),
+        compiler_params=pltpu.CompilerParams(vmem_limit_bytes=62 * 2**20),
     )(*hids, *cots, *inners, *lasts, rights)
 
 
@@ -1291,44 +1475,16 @@
     down_left,
     down_right,
 ):
-    count, slice_width = inputs.shape
-    width = router_attn.shape[0]
+    count = inputs.shape[0]
     rows_axis = lax.axis_size("row")
     replicas = rows_axis // EXP_FF
-    row = lax.axis_index("row")
-    col = lax.axis_index("col")
-    expert = row // replicas
-    depth = inner_weight.shape[1]
     units = inner_weight.shape[3]
-    length = lengths[0]
     adapter = adapter_pick[0]
-    position = jnp.arange(count)
-    valid = (position < length).astype(F32)
     cosine, sine = tables(count, HEAD_DIM)
-    scaling = HEAD_DIM ** (-0.5)
-
-    def features(part):
-        return lax.all_gather(part, "col", axis=1, tiled=True)
-
-    def partials(part):
-        return lax.psum_scatter(
-            part.astype(BF16), "col", scatter_dimension=1, tiled=True
-        ).astype(F32)
-
-    def own_columns(table):
-        return lax.dynamic_slice_in_dim(table, col * slice_width, slice_width, 0)
-
-    def later(value, *earlier):
-        return lax.optimization_barrier((value, *earlier))[0]
-
-    lanes = lax.broadcasted_iota(jnp.int32, (count, LANES), 1)
-
-    def table_of(*columns):
-        result = jnp.zeros((count, LANES), F32)
-        for n, column in enumerate(columns):
-            if column is not None:
-                result = jnp.where(lanes == n, column, result)
-        return result
+    turns = (
+        jnp.concatenate([cosine, cosine], axis=1),
+        jnp.concatenate([-sine, sine], axis=1),
+    )
 
     cols = lax.axis_size("col")
     padding = -units % LANES
@@ -1384,8 +1540,7 @@
             cotangent,
             norm_one[None, :],
             router_attn.T,
-            jnp.concatenate([cosine, cosine], axis=1),
-            jnp.concatenate([-sine, sine], axis=1),
+            *turns,
             rights,
         ],
         lefts_own,
@@ -1397,20 +1552,6 @@
         replicas,
     )
     picks = picks[:, 0, 0].astype(jnp.int32)
-    gates_attn = stat_attn[:, :TOPK]
-    query_width = keys.shape[1]
-    heads = query_width // HEAD_DIM
-    keys = keys.reshape(count, heads, HEAD_DIM)
-    values = values.reshape(count, heads, HEAD_DIM)
-    queries = queries.reshape(TOPK, count, heads, HEAD_DIM)
-    attended = attended.reshape(TOPK * count, query_width)
-    pick_attn_any = picks_attn[TOPK]
-    pick_attn_both = picks_attn[:TOPK]
-    rank_query = ranks[:, :RANK]
-    rank_kv = ranks[:, RANK:]
-    right_query = rights[:RANK]
-    right_kv = rights[RANK : 3 * RANK].reshape(2, RANK, query_width)
-    right_out = rights[3 * RANK :]
     right_inner_all = inner_right.reshape(ADAPT * RANK, 2, units)
     right_down_all = down_right.reshape(ADAPT * RANK, units)
     ffn_right = jnp.concatenate(
@@ -1446,91 +1587,44 @@
         cols,
         replicas,
     )
-    rights_ffn = lax.optimization_barrier(lax.psum(tuple(results[2 * EXP_FF :]), "row"))
+    rights_ffn = lax.optimization_barrier(lax.psum(lax.optimization_barrier((*results[2 * EXP_FF :], totals))[:3], "row"))
     rights_ffn = [
         value[:, :units].reshape(ADAPT, RANK, units).astype(F32) for value in rights_ffn
     ]
 
-    branch_own = partials(branch_ffn)
-    output = ((middle + branch_own) * valid[:, None]).astype(BF16)
-
-    grad_low_out = mm("td,rd->tr", grad_full, lefts[2 * RANK : 3 * RANK])
-    grad_middle_rows = mm("tc,td->cd", pick_attn_any, grad_full).astype(BF16)
-    grad_low_rows = mm("tc,tr->cr", pick_attn_any, grad_low_out.astype(BF16)).astype(BF16)
-    grad_att_rows = mm(
-        "ecd,edw->ecw", grad_middle_rows.reshape(EXP_ATT, CAP_ATT, width), out_full
-    ).reshape(EXP_ATT * CAP_ATT, query_width) + mm("cr,rw->cw", grad_low_rows, right_out)
-    gg_attn_rows = jnp.sum(attended_rows.astype(F32) * grad_att_rows, axis=1, keepdims=True)
-    grad_gates_attn_part = exact("ktc,cx->ktx", pick_attn_both.astype(F32), gg_attn_rows)
-    grad_att_rows = (grad_att_rows * gate_rows).astype(BF16)
-    grad_attended = (
-        mm("ktc,cw->ktw", pick_attn_both, grad_att_rows)
-        .astype(BF16)
-        .reshape(TOPK, count, heads, HEAD_DIM)
-    )
-    gated_low = (gates_attn.T[:, :, None] * grad_low_out[None]).reshape(TOPK * count, RANK)
-    grad_right_out = mm("xr,xw->rw", gated_low.astype(BF16), attended)
-    grad_prob = mm("kbhd,jhd->hkbj", grad_attended, values)
-    centre = jnp.sum(probability * grad_prob, axis=-1, keepdims=True)
-    grad_scores = (probability * (grad_prob - centre)).astype(BF16)
-    grad_queries = mm("hkbj,jhd->kbhd", grad_scores, keys) * scaling
-    grad_keys = mm("hkbj,kbhd->jhd", grad_scores, queries) * scaling
-    grad_values = mm("hkbj,kbhd->jhd", probability.astype(BF16), grad_attended)
-    grad_query_raw = (
-        rotate(grad_queries, cosine[None, :, None], -sine[None, :, None])
-        .astype(BF16)
-        .reshape(TOPK * count, query_width)
-    )
-    grad_key_raw = rotate(grad_keys, cosine[:, None], -sine[:, None])
-    grad_kv = jnp.stack([grad_key_raw, grad_values]).astype(BF16).reshape(2, count, query_width)
-    grad_query_rows = mm(
-        "ktc,ktw->cw", pick_attn_both, grad_query_raw.reshape(TOPK, count, query_width)
-    ).astype(BF16)
-    grad_one_rows = (
-        mm("ecw,edw->ecd", grad_query_rows.reshape(EXP_ATT, CAP_ATT, query_width), query_full)
-        .astype(BF16)
-        .reshape(EXP_ATT * CAP_ATT, width)
-    )
-    grad_query_sum = jnp.sum(
-        grad_query_raw.astype(F32).reshape(TOPK, count, query_width), axis=0
-    )
-    grad_query_sum_low = grad_query_sum.astype(BF16)
-    grad_rank_query = mm("tw,rw->tr", grad_query_sum_low, right_query)
-    grad_rank_kv = mm("stw,srw->tr", grad_kv, right_kv)
-    grad_one_part = (
-        mm("tc,cd->td", pick_attn_any, grad_one_rows)
-        + mm("stw,sdw->td", grad_kv, kv_full)
-        + mm(
-            "tr,rd->td",
-            jnp.concatenate([grad_rank_query, grad_rank_kv], axis=1).astype(BF16),
-            lefts[: 2 * RANK],
-        )
-    )
-    grad_right_query = mm("tr,tw->rw", rank_query.astype(BF16), grad_query_sum_low)
-    grad_right_kv = mm("tr,stw->rsw", rank_kv.astype(BF16), grad_kv)
-    cot_full = features(cotangent * valid.astype(BF16)[:, None])
-    small = table_of(grad_gates_attn_part[0], None, grad_gates_attn_part[1])
-    small += jnp.pad(
-        jnp.concatenate([grad_rank_query, grad_rank_kv, low_down_part[:, RANK : 2 * RANK]], axis=1),
-        ((0, 0), (RANK, LANES - 4 * RANK)),
-    )
-    lows = jnp.where(lanes < RANK, jnp.roll(totals_attn, -RANK, axis=1), 0.0) + jnp.where(
-        (lanes >= RANK) & (lanes < 2 * RANK), totals, 0.0
-    )
-    lows = lows.astype(BF16)
-    right_parts = jnp.concatenate(
-        [grad_right_query, grad_right_kv[:, 0], grad_right_kv[:, 1], grad_right_out], axis=1
-    ).astype(BF16)
-    grad_inputs, *grads = input_back(
-        picks,
-        later(grad_one_part, output, *rights_ffn),
-        small,
-        norm_one[None, :],
-        router_attn.T,
-        stat_attn,
-        lows,
-        right_parts,
-        [hidden_one, grad_full, hidden_two, cot_full, inputs, grad_middle],
+    output, grad_inputs, *grads = tail(
+        [
+            picks,
+            norm_one[None, :],
+            router_attn.T,
+            stat_attn,
+            *turns,
+            rights,
+            ranks,
+            gate_rows,
+            totals_attn,
+            totals,
+            low_down_part,
+        ],
+        [
+            grad_full,
+            picks_attn,
+            attended_rows,
+            queries,
+            keys,
+            values,
+            probability,
+            attended,
+            lefts,
+            hidden_one,
+            hidden_two,
+            grad_middle,
+            middle,
+            cotangent,
+            inputs,
+        ],
+        branch_ffn,
+        [out_full, query_full, kv_full],
         rows_axis,
         cols,
     )

time: 649 us -> 588 us (0.906)
  matrix products: 58.6 us -> 0 us
  Pallas kernels: 502 us -> 541 us
  local copies, waits for them, and re-layouts: 44.1 us -> 15.6 us
  other arithmetic: 19.7 us -> 9.33 us
    dot_general x20 -> x0, matrix products: 58.6 us -> none  [the longest x19 56.9 us: mm(): return jnp.einsum(spec, a, b, preferred_element_type=F32)]
    pallas_call x1, Pallas kernels: 37.4 us -> 82.7 us  [tail(): pl.pallas_call(functools.partial(tail_kernel, parts_axis, cols), out_shap...]
    unnamed x112 -> x39, local copies, waits for them, and re-layouts: 28.2 us -> 11.6 us
    pallas_call x1, Pallas kernels: 98.6 us -> 91 us  [middle_back(): pl.pallas_call(functools.partial(middle_back_kernel, cols, replicas), out...]
  transfers between devices with their start and end apart: 3 -> 1, of which waited for: 0 -> 0; matrix products, arithmetic and copies ran while one was open for 14% -> 1% of each run, Pallas kernels for 15% -> 14%
where the time goes in v7:
time: 588 us; the launch traced here: 582 us
  Pallas kernels  541 us (92%)
  between operations  16 us (3%)
  local copies, waits for them, and re-layouts  15.6 us (3%)
  other arithmetic  9.33 us (2%)
    pallas_call x1, Pallas kernels, front(): pl.pallas_call(functools.partial(front_kernel, parts, cols, replicas), ou...  192 us
    pallas_call x1, Pallas kernels, middle_forward(): pl.pallas_call(functools.partial(middle_kernel, parts_axis, cols, replica...  134 us
    pallas_call x1, Pallas kernels, middle_back(): pl.pallas_call(functools.partial(middle_back_kernel, cols, replicas), out...  91 us
    pallas_call x1, Pallas kernels, tail(): pl.pallas_call(functools.partial(tail_kernel, parts_axis, cols), out_shap...  82.7 us
    pallas_call x1, Pallas kernels, feed_forward(): pl.pallas_call(functools.partial(ffn_kernel, parts, depth, width, units),...  42.3 us
  transfers between devices with their start and end apart: 1, of which 0 were waited for; matrix products, arithmetic and copies ran while one was open for 1% of the time, Pallas kernels for 14%

profile of v7, /device:TPU:9, one launch (start us, length us, event | category | flops | bytes accessed | tf_op | source)
XLA Modules:
  0.0 582.0 jit_solution(13577562654376187641)
XLA Ops:
  7.2 0.0 copy-start
  7.2 0.0 all-reduce.3.cloned.1.call-start
  8.6 0.0 copy-done
  8.7 1.5 copy.45.refs_2_
  10.1 1.5 copy.46.refs_3_
  11.6 1.2 copy.47
  12.8 0.0 copy-start.4
  12.8 0.1 slice_bitcast_fusion.1
  12.9 0.8 dynamic-slice_bitcast_fusion
  13.7 0.5 fusion
  14.2 0.8 pad_maximum_fusion.2
  15.0 0.0 copy-done.4
  15.0 1.1 pad_maximum_fusion.refs_24_
  16.1 0.6 pad_maximum_fusion.4.refs_9_.refs_6_
  16.7 191.5 %shard_map.328 = (bf16[4,256,2816]{2,1,0:T(8,128)(2,1)}, bf16[2,2048,512]{2,1,0:T(8,128)(2,1)}, bf16[8,2048,512]{2,1,0:T(8,128)(2,1)}, bf16[8,2048,512]{2,1,0:T(...) custom-call(s32[1]{0:T(128)S(6)} %copy.65.refs_0_, ...), custom_call_target="tpu_custom_call" | custom-call | tf_op jit(solution)/shard_map/pallas_call | solution.py:505
  208.2 133.6 %shard_map.329 = (bf16[256,2816]{1,0:T(8,128)(2,1)}, bf16[256,2816]{1,0:T(8,128)(2,1)}, bf16[256,2816]{1,0:T(8,128)(2,1)}, bf16[256,2816]{1,0:T(8,128)(2,1)}, bf...) custom-call(s32[1]{0:T(128)} %copy.66.refs_1_.refs_0_.refs_8_, ...), custom_call_target="tpu_custom_call" | custom-call | tf_op jit(solution)/shard_map/pallas_call | solution.py:1280
  341.8 42.3 %shard_map.330 = (bf16[160,2304]{1,0:T(8,128)(2,1)}, bf16[160,2304]{1,0:T(8,128)(2,1)}, bf16[160,2304]{1,0:T(8,128)(2,1)}, bf16[160,2304]{1,0:T(8,128)(2,1)}, bf...) custom-call(bf16[160,2432]{1,0:T(8,128)(2,1)} %get-tuple-element.104, ...), custom_call_target="tpu_custom_call" | custom-call | tf_op jit(solution)/shard_map/pallas_call | solution.py:1432
  384.1 91.0 %shard_map.331 = (f32[256,512]{1,0:T(8,128)}, bf16[256,2048]{1,0:T(8,128)(2,1)}, f32[256,128]{1,0:T(8,128)}, bf16[256,2048]{1,0:T(8,128)(2,1)}, f32[256,128]{1,0:T(8,128)}) custom-call(bf16[160,2304]{1,0:T(8,128)(2,1)} %get-tuple-element.126.refs_0_, bf16[160,2304]{1,0:T(8,128)(2,1)} %get-tuple-element.127.refs_1_, ...), custom_call_target="tpu_custom_call" | custom-call | tf_op jit(solution)/shard_map/pallas_call | solution.py:693
  475.1 0.0 all-reduce.3.cloned.1.call-update
  475.1 1.5 convert_reduce_fusion.refs_0_
  476.6 82.7 %shard_map.332 = (bf16[256,512]{1,0:T(8,128)(2,1)}, f32[256,512]{1,0:T(8,128)}, f32[8,16,256]{2,1,0:T(8,128)}, f32[8,16,256]{2,1,0:T(8,128)}, f32[8,16,256]{2,1,...) custom-call(s32[8]{0:T(128)} %convert_reduce_fusion.refs_0_, ...), custom_call_target="tpu_custom_call" | custom-call | tf_op jit(solution)/shard_map/pallas_call | solution.py:1051
  559.3 1.1 pad_maximum_fusion.1
  560.4 1.2 copy.50
  561.6 0.0 all-reduce.3.cloned.1.call-done
  561.6 0.0 copy-start.3
  561.6 1.6 copy.49
  563.2 1.5 copy.48
  564.8 0.0 copy-done.3
  564.8 0.9 convert.4
  565.7 0.0 copy-start.7
  565.7 0.0 copy-start.2
  565.7 2.8 maximum_convert_fusion
  568.5 0.0 copy-done.7
  568.5 0.0 copy-start.12
  568.5 0.0 copy-start.6
  568.5 0.0 copy-start.11
  568.5 0.0 copy-start.10
  568.5 0.0 copy-start.5
  568.5 0.7 copy.67
  569.2 0.0 copy-done.2
  569.2 0.0 copy-start.9
  569.2 0.0 copy-start.8
  569.2 0.0 copy-start.1
  569.2 0.8 copy.68
  570.0 0.0 copy-done.12
  570.0 0.7 copy.69
  570.7 0.0 copy-done.6
  570.7 0.7 copy.70
  571.4 0.0 copy-done.11
  571.4 0.7 copy.71
  572.0 0.0 copy-done.10
  572.0 0.7 copy.72
  572.7 0.0 copy-done.5
  572.7 0.7 copy.73
  573.4 0.0 copy-done.9
  573.4 0.7 copy.74
  574.0 0.0 copy-done.8
  574.1 0.7 copy.75
  574.7 0.0 copy-done.1
  (5 shorter events, 0.1 us)
Async XLA Ops:
  7.2 1.4 copy-start
  7.2 554.4 %all-reduce.3.cloned.1.call-start = ((), (), s32[]{:S(2)}) async-start(), calls=%async_computation | async-start | bytes 2162688 | tf_op jit(solution)/shard_map/psum | solution.py:1590
  12.8 2.2 copy-start.4
  561.6 3.1 copy-start.3
  565.7 2.8 copy-start.7
  565.7 3.5 copy-start.2
  568.5 1.5 copy-start.12
  568.5 2.2 copy-start.6
  568.5 2.9 copy-start.11
  568.5 3.6 copy-start.10
  568.5 4.2 copy-start.5
  569.2 4.2 copy-start.9
  569.2 4.9 copy-start.8
  569.2 5.5 copy-start.1
Sparse Core Ops, SparseCore 0:
  475.2 59.9 all-reduce.2

commit v8 on v7

--- a/solution.py
+++ b/solution.py
@@ -97,9 +97,10 @@
 
 
 def dispatch_matrices(route, flip, experts, capacity):
-    count = route.shape[0]
+    route = [column.astype(jnp.int32) for column in route]
+    count = route[0].shape[0]
     lane = lax.broadcasted_iota(jnp.int32, (count, LANES), 1)
-    chosen = [(route[:, k : k + 1] == lane).astype(F32) for k in range(TOPK)]
+    chosen = [(route[k] == lane).astype(F32) for k in range(TOPK)]
     place = lax.broadcasted_iota(jnp.int32, (count, count), 0)
     other = lax.broadcasted_iota(jnp.int32, (count, count), 1)
     before = (other < place).astype(F32).astype(BF16)
@@ -110,7 +111,7 @@
     results = []
     for k in range(TOPK):
         position = jnp.sum(earlier * chosen[k], axis=1, keepdims=True).astype(jnp.int32)
-        mine = jnp.bitwise_xor(route[:, k : k + 1], flip) * capacity + position
+        mine = jnp.bitwise_xor(route[k], flip) * capacity + position
         results.append((rows == mine).astype(F32).astype(BF16))
     return results
 
@@ -137,14 +138,15 @@
 
 
 def front_kernel(parts, cols, replicas, *refs):
-    lengths, pick, route_attn, route_ffn, cot, norm, router, cosine, sine, rights = refs[:10]
-    left_refs = refs[10:15]
-    tokens = refs[15]
-    blocks = refs[16:19]
-    pairs = refs[19]
-    outs = refs[20:]
-    flat = outs[0]
-    outs = outs[1:]
+    lengths, pick, routes_attn, routes_ffn, cot, norm, router, cosine, sine = refs[:9]
+    query_right, kv_right, out_right = refs[9:12]
+    left_refs = refs[12:17]
+    tokens = refs[17]
+    blocks = refs[18:21]
+    pairs, pairs_right = refs[21:23]
+    outs = refs[23:]
+    flat, flat_right, rights = outs[:3]
+    outs = outs[3:]
     wholes = outs[:3]
     cot_wholes = outs[3 : 3 + EXP_FF]
     (
@@ -272,9 +274,34 @@
     for n in range(window):
         push_own(n)
 
+    table = jnp.concatenate(
+        [
+            routes_attn[...].astype(F32),
+            routes_ffn[...].astype(F32),
+            jnp.zeros((8 - 2 * TOPK, count), F32),
+        ]
+    )
+    same = lax.broadcasted_iota(jnp.int32, (8, LANES), 0) == lax.broadcasted_iota(
+        jnp.int32, (8, LANES), 1
+    )
+    table = lax.dot_general(
+        table.astype(BF16),
+        same.astype(F32).astype(BF16),
+        (((0,), (0,)), ((), ())),
+        preferred_element_type=F32,
+    )
+    route_attn = [table[:, k : k + 1] for k in range(TOPK)]
+    route_ffn = [table[:, TOPK + k : TOPK + k + 1] for k in range(TOPK)]
+    chosen_adapter = pick[0]
+    rights[:RANK] = query_right[chosen_adapter]
+    pair_right = kv_right[chosen_adapter].reshape(RANK, 2 * head_width)
+    rights[RANK : 2 * RANK] = pair_right[:, :head_width]
+    rights[2 * RANK : 3 * RANK] = pair_right[:, head_width:]
+    rights[3 * RANK :] = out_right[chosen_adapter]
+
     position = lax.broadcasted_iota(jnp.int32, (count, 1), 0)
     valid = position < lengths[0]
-    matrices = dispatch_matrices(route_ffn[...], row // replicas, EXP_FF, CAP_FF)
+    matrices = dispatch_matrices(route_ffn, row // replicas, EXP_FF, CAP_FF)
     for k in range(TOPK):
         picks_ffn[k] = matrices[k]
     masked = jnp.where(valid, cot[...].astype(F32), 0.0).astype(BF16)
@@ -296,7 +323,7 @@
         send_to(own_rows.at[j], landed.at[j - 1], across[j * replicas])
         for j in range(1, EXP_FF)
     ]
-    attn = dispatch_matrices(route_attn[...], 0, EXP_ATT, CAP_ATT)
+    attn = dispatch_matrices(route_attn, 0, EXP_ATT, CAP_ATT)
     for k in range(TOPK):
         picks_attn[k] = attn[k]
     attn_any = attn[0] + attn[1]
@@ -345,10 +372,9 @@
     relay(1)
     push_own(window + 1)
     logits = times(hidden[...], router[...])
-    routes = [route_attn[:, k : k + 1].astype(F32) for k in range(TOPK)]
-    chosen, gates = scores_of(routes, logits, EXP_ATT)
-    extras = [valid.astype(F32), *(route_ffn[:, k : k + 1].astype(F32) for k in range(TOPK))]
-    stat[...] = pack([*gates, *chosen, scale, *routes, *extras], range(10))
+    chosen, gates = scores_of(route_attn, logits, EXP_ATT)
+    columns = [*gates, *chosen, scale, *route_attn, valid.astype(F32), *route_ffn]
+    stat[...] = pack(columns, range(10))
     rank_both = times(hidden[...], lefts[: 2 * RANK])
     ranks[...] = rank_both
     rank_query = rank_both[:, :RANK].astype(BF16)
@@ -450,6 +476,21 @@
         copy.start()
         copy.wait()
 
+    near = pair_in.at[pl.ds(0, pairs_right.shape[0])]
+    copy = pltpu.make_async_copy(pairs_right, near, load.at[2])
+    copy.start()
+    copy.wait()
+    step = 64
+    pair_rows = pairs_right.shape[0]
+
+    @pl.loop(0, pair_rows // step)
+    def _(i):
+        span = pl.ds(pl.multiple_of(i * step, step), step)
+        pair_out[span] = pair_in[span].reshape(step, pair_out.shape[1])
+
+    copy = pltpu.make_async_copy(pair_out.at[pl.ds(0, pair_rows)], flat_right, load.at[3])
+    copy.start()
+    copy.wait()
     loads = {}
     total = len(chunks)
     for n in range(2, total + behind + 1):
@@ -485,7 +526,7 @@
     return wholes[array].at[pl.ds(start, pair)]
 
 
-def front(smalls, lefts, tokens, blocks, pairs, parts, cols, replicas):
+def front(smalls, lefts, tokens, blocks, pairs, pairs_right, parts, cols, replicas):
     hbm = pl.BlockSpec(memory_space=pl.ANY)
     vmem = pl.BlockSpec(memory_space=pltpu.VMEM)
     smem = pl.BlockSpec(memory_space=pltpu.SMEM)
@@ -504,7 +545,11 @@
     )
     return pl.pallas_call(
         functools.partial(front_kernel, parts, cols, replicas),
-        out_shape=[shape(flat, BF16)]
+        out_shape=[
+            shape(flat, BF16),
+            shape((pairs_right.shape[0], flat[2]), BF16),
+            shape((4 * RANK, head_width), BF16),
+        ]
         + [shape((b.shape[0], width, head_width), BF16) for b in blocks]
         + [shape((CAP_FF, width), BF16)] * EXP_FF
         + [
@@ -526,8 +571,8 @@
             shape((rows, 1), F32),
             shape((parts, 8, LANES), F32),
         ],
-        in_specs=[smem] * 2 + [vmem] * 13 + [hbm] * 5,
-        out_specs=[hbm] * (4 + EXP_FF) + [vmem] * 17,
+        in_specs=[smem] * 2 + [vmem] * 15 + [hbm] * 6,
+        out_specs=[hbm, hbm, vmem] + [hbm] * (3 + EXP_FF) + [vmem] * 17,
         scratch_shapes=[
             pltpu.VMEM((count, width), BF16),
             pltpu.VMEM((EXP_FF, CAP_FF, wide), BF16),
@@ -547,7 +592,7 @@
         compiler_params=pltpu.CompilerParams(
             collective_id=1, has_side_effects=True, vmem_limit_bytes=62 * 2**20
         ),
-    )(*smalls, *lefts, tokens, *blocks, pairs)
+    )(*smalls, *lefts, tokens, *blocks, pairs, pairs_right)
 
 
 def middle_back_kernel(cols, replicas, *refs):
@@ -566,22 +611,16 @@
     across = [opposite("row", j * replicas) for j in range(1, EXP_FF)]
     along = [opposite("col", i) for i in range(1, cols)]
     greet(across + along)
-    copies = [
-        remote(
-            blocks[j], rows.at[pl.ds(j * CAP_FF, CAP_FF)], send, recv, j - 1, across[j - 1]
-        )
-        for j in range(1, EXP_FF)
-    ]
     near = fetch(
-        [blocks[0], downs[0], *sources],
-        [rows.at[pl.ds(0, CAP_FF)], down_rows.at[pl.ds(0, CAP_FF)], *scratch[:5]],
+        [*blocks, downs[0], *sources],
+        [
+            *(rows.at[pl.ds(j * CAP_FF, CAP_FF)] for j in range(EXP_FF)),
+            down_rows.at[pl.ds(0, CAP_FF)],
+            *scratch[:5],
+        ],
         local,
     )
-    for copy in near:
-        copy.wait()
-    for copy in copies:
-        copy.wait_recv()
-    base = EXP_FF - 1
+    base = 0
     down_copies = [
         remote(
             downs[j],
@@ -593,6 +632,8 @@
         )
         for j in range(1, EXP_FF)
     ]
+    for copy in near:
+        copy.wait()
     picks = [picks_ffn[0], picks_ffn[1]]
     any_pick = picks[0] + picks[1]
 
@@ -658,7 +699,7 @@
     grad_middle[...] = result
     low[...] = result.astype(BF16)
     here = pl.ds(first, wide)
-    kept = pltpu.make_async_copy(low, grad_whole.at[:, here], local.at[8])
+    kept = pltpu.make_async_copy(low, grad_whole.at[:, here], local.at[10])
     kept.start()
     base += 2 * (cols - 1)
     last = [
@@ -678,7 +719,7 @@
         branch[:, here] = part.astype(BF16)
     for copy in last:
         copy.wait_recv()
-    for copy in copies + down_copies + arrivals + last:
+    for copy in down_copies + arrivals + last:
         copy.wait_send()
     kept.wait()
 
@@ -688,7 +729,7 @@
     vmem = pl.BlockSpec(memory_space=pltpu.VMEM)
     smem = pl.BlockSpec(memory_space=pltpu.SMEM)
     count, wide = sources[-1].shape
-    total = 2 * (EXP_FF - 1) + 3 * (cols - 1)
+    total = EXP_FF - 1 + 3 * (cols - 1)
     rows = EXP_FF * CAP_FF
     return pl.pallas_call(
         functools.partial(middle_back_kernel, cols, replicas),
@@ -713,7 +754,7 @@
             pltpu.VMEM((count, wide), BF16),
             pltpu.SemaphoreType.DMA((total,)),
             pltpu.SemaphoreType.DMA((total,)),
-            pltpu.SemaphoreType.DMA((9,)),
+            pltpu.SemaphoreType.DMA((11,)),
         ],
         compiler_params=pltpu.CompilerParams(
             collective_id=4, has_side_effects=True, vmem_limit_bytes=62 * 2**20
@@ -1317,12 +1358,15 @@
     cots = refs[EXP_FF : 2 * EXP_FF]
     inners = refs[2 * EXP_FF : 2 * EXP_FF + parts]
     lasts = refs[2 * EXP_FF + parts : 2 * EXP_FF + 2 * parts]
-    rights = refs[2 * EXP_FF + 2 * parts]
-    outs = refs[2 * EXP_FF + 2 * parts + 1 :]
+    rights = refs[2 * EXP_FF + 2 * parts : 2 * EXP_FF + 2 * parts + 2]
+    outs = refs[2 * EXP_FF + 2 * parts + 2 :]
     grads = outs[:EXP_FF]
     downs = outs[EXP_FF : 2 * EXP_FF]
     adapt = outs[2 * EXP_FF : 2 * EXP_FF + 3]
-    hid, cot, block, act, product, sems = outs[2 * EXP_FF + 3 :]
+    hid, cot, block, act, product, leaving, sems, send, recv = outs[2 * EXP_FF + 3 :]
+    replicas = parts // EXP_FF
+    across = [opposite("row", j * replicas) for j in range(1, EXP_FF)]
+    greet(across)
     row = lax.axis_index("row")
     wide = width + LANES
     copies = []
@@ -1335,17 +1379,19 @@
         near = cot.at[where, pl.ds(width, LANES)]
         low = hids[j].at[:, pl.ds(wide + LANES, LANES)]
         copies.append(pltpu.make_async_copy(low, near, sems.at[2 * EXP_FF + j]))
-    copies.append(pltpu.make_async_copy(rights, block.at[pl.ds(width, LANES)], sems.at[3 * EXP_FF]))
-    expert = row // (parts // EXP_FF)
+    for n, (start, size) in enumerate(((0, 2 * units), (2 * units, units))):
+        near = block.at[pl.ds(width, LANES), pl.ds(start, size)]
+        copies.append(pltpu.make_async_copy(rights[n], near, sems.at[3 * EXP_FF + n]))
+    expert = row // replicas
     for m in range(parts):
         owner = jnp.bitwise_xor(row, m)
         where = pl.ds(pl.multiple_of(owner * depth, depth), depth)
         inner = inners[m] if m else inners[0].at[expert]
         last = lasts[m] if m else lasts[0].at[expert]
         near = block.at[where, pl.ds(0, 2 * units)]
-        copies.append(pltpu.make_async_copy(inner, near, sems.at[3 * EXP_FF + 1 + m]))
+        copies.append(pltpu.make_async_copy(inner, near, sems.at[3 * EXP_FF + 2 + m]))
         near = block.at[where, pl.ds(2 * units, units)]
-        copies.append(pltpu.make_async_copy(last, near, sems.at[3 * EXP_FF + 1 + parts + m]))
+        copies.append(pltpu.make_async_copy(last, near, sems.at[3 * EXP_FF + 2 + parts + m]))
     for copy in copies:
         copy.start()
     for copy in copies:
@@ -1378,16 +1424,47 @@
     if units % step:
         forward(full * step, units % step)
 
+    total = product[...]
+    high = total.astype(BF16)
+    low = (total - high.astype(F32)).astype(BF16)
+    lane = lax.broadcasted_iota(jnp.int32, (EXP_FF * CAP_FF, LANES), 1)
+    packed = jnp.where(
+        lane == 0, high.astype(F32), jnp.where(lane == 1, low.astype(F32), 0.0)
+    ).astype(BF16)
+    traded = []
+    spans = [(start, 4 * LANES) for start in range(0, width, 4 * LANES)] + [(width, LANES)]
+    for start, size in spans:
+        here = pl.ds(start, size)
+        result = lax.dot_general(
+            act[:, : 2 * units],
+            block[here, : 2 * units],
+            (((1,), (1,)), ((), ())),
+            preferred_element_type=F32,
+        ).astype(BF16)
+        sent = here
+        if start == width:
+            result = jnp.concatenate([result, packed], axis=1)
+            sent = pl.ds(start, 2 * LANES)
+        grads[0][:, sent] = result[:CAP_FF]
+        for j in range(1, EXP_FF):
+            leaving[j - 1, :, sent] = result[j * CAP_FF : (j + 1) * CAP_FF]
+            traded.append(
+                remote(
+                    leaving.at[j - 1, :, sent],
+                    grads[j].at[:, sent],
+                    send,
+                    recv,
+                    len(traded),
+                    across[j - 1],
+                )
+            )
+
     def backward(start, size):
         here = pl.ds(start, size)
         result = lax.dot_general(
-            act[:, : 2 * units], block[here, : 2 * units], (((1,), (1,)), ((), ())),
-            preferred_element_type=F32,
-        ).astype(BF16)
-        for j in range(EXP_FF):
-            grads[j][:, here] = result[j * CAP_FF : (j + 1) * CAP_FF]
-        result = lax.dot_general(
-            act[:, 2 * units :], block[here, 2 * units :], (((1,), (1,)), ((), ())),
+            act[:, 2 * units :],
+            block[here, 2 * units :],
+            (((1,), (1,)), ((), ())),
             preferred_element_type=F32,
         )
         result = (result * gate_scale).astype(BF16)
@@ -1402,13 +1479,6 @@
 
     if wide % step:
         backward(full_rows * step, wide % step)
-    total = product[...]
-    high = total.astype(BF16)
-    low = (total - high.astype(F32)).astype(BF16)
-    lane = lax.broadcasted_iota(jnp.int32, (EXP_FF * CAP_FF, LANES), 1)
-    packed = jnp.where(lane == 0, high.astype(F32), jnp.where(lane == 1, low.astype(F32), 0.0)).astype(BF16)
-    for j in range(EXP_FF):
-        grads[j][:, wide:] = packed[j * CAP_FF : (j + 1) * CAP_FF]
     ext = hid[:, width:wide]
     low_ext = (cot[:, width:].astype(F32) * gate_scale).astype(BF16)
     for n, low_rows in enumerate((ext, ext, low_ext)):
@@ -1418,6 +1488,8 @@
             (((0,), (0,)), ((), ())),
             preferred_element_type=F32,
         ).astype(BF16)
+    for copy in traded:
+        copy.wait()
 
 
 def feed_forward(hids, cots, inners, lasts, rights):
@@ -1425,6 +1497,7 @@
     depth, units = lasts[1].shape
     triple = 3 * units
     width = depth * parts
+    remotes = (EXP_FF - 1) * (width // (4 * LANES) + 1)
     rows = EXP_FF * CAP_FF
     hbm = pl.BlockSpec(memory_space=pl.ANY)
     vmem = pl.BlockSpec(memory_space=pltpu.VMEM)
@@ -1434,18 +1507,23 @@
         out_shape=[jax.ShapeDtypeStruct((CAP_FF, wide + LANES), BF16)] * EXP_FF
         + [jax.ShapeDtypeStruct((CAP_FF, wide), BF16)] * EXP_FF
         + [jax.ShapeDtypeStruct((LANES, units), BF16)] * 3,
-        in_specs=[hbm] * (2 * EXP_FF + 2 * parts + 1),
-        out_specs=[vmem] * (2 * EXP_FF + 3),
+        in_specs=[hbm] * (2 * EXP_FF + 2 * parts + 2),
+        out_specs=[vmem] + [hbm] * (EXP_FF - 1) + [vmem] * (EXP_FF + 3),
         scratch_shapes=[
             pltpu.VMEM((rows, wide + LANES), BF16),
             pltpu.VMEM((rows, wide), BF16),
             pltpu.VMEM((wide, triple), BF16),
             pltpu.VMEM((rows, triple), BF16),
             pltpu.VMEM((rows, 1), F32),
-            pltpu.SemaphoreType.DMA((3 * EXP_FF + 1 + 2 * parts,)),
+            pltpu.VMEM((EXP_FF - 1, CAP_FF, wide + LANES), BF16),
+            pltpu.SemaphoreType.DMA((3 * EXP_FF + 2 + 2 * parts,)),
+            pltpu.SemaphoreType.DMA((remotes,)),
+            pltpu.SemaphoreType.DMA((remotes,)),
         ],
-        compiler_params=pltpu.CompilerParams(vmem_limit_bytes=62 * 2**20),
-    )(*hids, *cots, *inners, *lasts, rights)
+        compiler_params=pltpu.CompilerParams(
+            collective_id=2, has_side_effects=True, vmem_limit_bytes=62 * 2**20
+        ),
+    )(*hids, *cots, *inners, *lasts, *rights)
 
 
 def on_device(
@@ -1479,7 +1557,6 @@
     rows_axis = lax.axis_size("row")
     replicas = rows_axis // EXP_FF
     units = inner_weight.shape[3]
-    adapter = adapter_pick[0]
     cosine, sine = tables(count, HEAD_DIM)
     turns = (
         jnp.concatenate([cosine, cosine], axis=1),
@@ -1496,20 +1573,14 @@
 
     down_flat = padded(down_weight)
 
-    rights = jnp.concatenate(
-        [
-            query_right[adapter],
-            kv_right[adapter][:, 0],
-            kv_right[adapter][:, 1],
-            out_right[adapter],
-        ]
-    )
     lefts_own = [
         value.swapaxes(1, 2)
         for value in (query_left, kv_left, out_left, inner_left, down_left)
     ]
     (
         inner_flat,
+        inner_right_flat,
+        rights,
         kv_full,
         query_full,
         out_full,
@@ -1535,29 +1606,27 @@
         [
             lengths,
             adapter_pick,
-            attn_route,
-            ffn_route,
+            attn_route.T,
+            ffn_route.T,
             cotangent,
             norm_one[None, :],
             router_attn.T,
             *turns,
-            rights,
+            query_right,
+            kv_right,
+            out_right,
         ],
         lefts_own,
         inputs,
         [kv_weight, query_weight, out_weight],
         padded(inner_weight),
+        padded(inner_right).reshape(ADAPT * RANK, 2, units + padding),
         rows_axis,
         cols,
         replicas,
     )
     picks = picks[:, 0, 0].astype(jnp.int32)
-    right_inner_all = inner_right.reshape(ADAPT * RANK, 2, units)
-    right_down_all = down_right.reshape(ADAPT * RANK, units)
-    ffn_right = jnp.concatenate(
-        [padded(right_inner_all[:, 0]), padded(right_inner_all[:, 1]), padded(right_down_all)],
-        axis=1,
-    )
+    ffn_right = [inner_right_flat, padded(down_right).reshape(ADAPT * RANK, units + padding)]
 
     *outs, hidden_two, middle, stat_ffn, totals_attn = middle_forward(
         adapter_pick,
@@ -1587,7 +1656,8 @@
         cols,
         replicas,
     )
-    rights_ffn = lax.optimization_barrier(lax.psum(lax.optimization_barrier((*results[2 * EXP_FF :], totals))[:3], "row"))
+    rights_ffn = lax.optimization_barrier((*results[2 * EXP_FF :], totals))[:3]
+    rights_ffn = lax.optimization_barrier(lax.psum(rights_ffn, "row"))
     rights_ffn = [
         value[:, :units].reshape(ADAPT, RANK, units).astype(F32) for value in rights_ffn
     ]

time: 588 us -> 572 us (0.973)
  Pallas kernels: 541 us -> 532 us
    pallas_call x1, Pallas kernels: 91 us -> 59.2 us  [middle_back(): pl.pallas_call(functools.partial(middle_back_kernel, cols, replicas), out...]
    pallas_call x1, Pallas kernels: 42.3 us -> 63.8 us  [feed_forward(): pl.pallas_call(functools.partial(ffn_kernel, parts, depth, width, units),...]
  transfers between devices with their start and end apart: 1 -> 1, of which waited for: 0 -> 0; matrix products, arithmetic and copies ran while one was open for 1% -> 1% of each run, Pallas kernels for 14% -> 15%
where the time goes in v8:
time: 572 us; the launch traced here: 566 us
  Pallas kernels  532 us (93%)
  between operations  15.7 us (3%)
  local copies, waits for them, and re-layouts  10.5 us (2%)
  other arithmetic  7.64 us (1%)
    pallas_call x1, Pallas kernels, front(): pl.pallas_call(functools.partial(front_kernel, parts, cols, replicas), ou...  192 us
    pallas_call x1, Pallas kernels, middle_forward(): pl.pallas_call(functools.partial(middle_kernel, parts_axis, cols, replica...  134 us
    pallas_call x1, Pallas kernels, tail(): pl.pallas_call(functools.partial(tail_kernel, parts_axis, cols), out_shap...  83.7 us
    pallas_call x1, Pallas kernels, feed_forward(): pl.pallas_call(functools.partial(ffn_kernel, parts, depth, width, units),...  63.8 us
    pallas_call x1, Pallas kernels, middle_back(): pl.pallas_call(functools.partial(middle_back_kernel, cols, replicas), out...  59.2 us
  transfers between devices with their start and end apart: 1, of which 0 were waited for; matrix products, arithmetic and copies ran while one was open for 1% of the time, Pallas kernels for 15%

profile of v8, /device:TPU:9, one launch (start us, length us, event | category | flops | bytes accessed | tf_op | source)
XLA Modules:
  0.0 565.9 jit_solution(7132838075970738840)
XLA Ops:
  7.2 0.0 all-reduce.3.cloned.1.call-start
  8.5 0.5 fusion
  9.1 0.8 pad_maximum_fusion.1
  9.9 191.6 %shard_map.328 = (bf16[4,256,2816]{2,1,0:T(8,128)(2,1)}, bf16[128,2816]{1,0:T(8,128)(2,1)}, bf16[64,512]{1,0:T(8,128)(2,1)}, bf16[2,2048,512]{2,1,0:T(8,128)(2,1...) custom-call(s32[1]{0:T(128)S(6)} %copy.55.refs_0_, ...), custom_call_target="tpu_custom_call" | custom-call | tf_op jit(solution)/shard_map/pallas_call | solution.py:546
  201.6 133.6 %shard_map.329 = (bf16[256,2816]{1,0:T(8,128)(2,1)}, bf16[256,2816]{1,0:T(8,128)(2,1)}, bf16[256,2816]{1,0:T(8,128)(2,1)}, bf16[256,2816]{1,0:T(8,128)(2,1)}, bf...) custom-call(s32[1]{0:T(128)S(6)} %copy.56.refs_1_.refs_0_.refs_8_, ...), custom_call_target="tpu_custom_call" | custom-call | tf_op jit(solution)/shard_map/pallas_call | solution.py:1321
  335.1 63.8 %shard_map.330 = (bf16[160,2304]{1,0:T(8,128)(2,1)}, bf16[160,2304]{1,0:T(8,128)(2,1)}, bf16[160,2304]{1,0:T(8,128)(2,1)}, bf16[160,2304]{1,0:T(8,128)(2,1)}, bf...) custom-call(bf16[160,2432]{1,0:T(8,128)(2,1)} %get-tuple-element.107, ...), custom_call_target="tpu_custom_call" | custom-call | tf_op jit(solution)/shard_map/pallas_call | solution.py:1505
  399.0 59.2 %shard_map.331 = (f32[256,512]{1,0:T(8,128)}, bf16[256,2048]{1,0:T(8,128)(2,1)}, f32[256,128]{1,0:T(8,128)}, bf16[256,2048]{1,0:T(8,128)(2,1)}, f32[256,128]{1,0:T(8,128)}) custom-call(bf16[160,2304]{1,0:T(8,128)(2,1)} %get-tuple-element.130.refs_0_, bf16[160,2304]{1,0:T(8,128)(2,1)} %get-tuple-element.131.refs_1_, ...), custom_call_target="tpu_custom_call" | custom-call | tf_op jit(solution)/shard_map/pallas_call | solution.py:734
  458.2 0.0 all-reduce.3.cloned.1.call-update
  458.2 1.5 convert_reduce_fusion.refs_0_
  459.7 83.7 %shard_map.332 = (bf16[256,512]{1,0:T(8,128)(2,1)}, f32[256,512]{1,0:T(8,128)}, f32[8,16,256]{2,1,0:T(8,128)}, f32[8,16,256]{2,1,0:T(8,128)}, f32[8,16,256]{2,1,...) custom-call(s32[8]{0:T(128)} %convert_reduce_fusion.refs_0_, ...), custom_call_target="tpu_custom_call" | custom-call | tf_op jit(solution)/shard_map/pallas_call | solution.py:1092
  543.4 1.1 pad_maximum_fusion
  544.5 1.2 copy.42
  545.7 0.0 all-reduce.3.cloned.1.call-done
  545.7 0.0 copy-start.1
  545.7 1.6 copy.41
  547.3 1.5 copy.40
  548.9 0.0 copy-done.1
  548.9 0.9 convert.4
  549.8 0.0 copy-start.4
  549.8 0.0 copy-start
  549.8 2.8 maximum_convert_fusion
  552.6 0.0 copy-done.4
  552.6 0.0 copy-start.9
  552.6 0.0 copy-start.3
  552.6 0.0 copy-start.8
  552.6 0.0 copy-start.7
  552.6 0.0 copy-start.2
  552.6 0.7 copy.57
  553.3 0.0 copy-done
  553.3 0.0 copy-start.6
  553.3 0.0 copy-start.5
  553.3 0.8 copy.58
  554.1 0.0 copy-done.9
  554.1 0.7 copy.59
  554.8 0.0 copy-done.3
  554.8 0.7 copy.60
  555.5 0.0 copy-done.8
  555.5 0.7 copy.61
  556.1 0.0 copy-done.7
  556.1 0.7 copy.62
  556.8 0.0 copy-done.2
  556.8 0.7 copy.63
  557.5 0.0 copy-done.6
  557.5 0.7 copy.64
  558.1 0.0 copy-done.5
  558.1 0.7 copy.65
  (2 shorter events, 0.0 us)
Async XLA Ops:
  7.2 538.5 %all-reduce.3.cloned.1.call-start = ((), (), s32[]{:S(2)}) async-start(), calls=%async_computation | async-start | bytes 2162688 | tf_op jit(solution)/shard_map/psum | solution.py:1660
  545.7 3.1 copy-start.1
  549.8 2.8 copy-start.4
  549.8 3.5 copy-start
  552.6 1.5 copy-start.9
  552.6 2.2 copy-start.3
  552.6 2.9 copy-start.8
  552.6 3.6 copy-start.7
  552.6 4.2 copy-start.2
  553.3 4.2 copy-start.6
  553.3 4.8 copy-start.5
Sparse Core Ops, SparseCore 0:
  458.4 58.8 all-reduce.2

commit v9 on v8

--- a/solution.py
+++ b/solution.py
@@ -21,6 +21,7 @@
 F32 = jnp.float32
 BF16 = jnp.bfloat16
 LANES = 128
+EARLY = 2
 
 
 def tables(count, head_width):
@@ -143,10 +144,11 @@
     left_refs = refs[12:17]
     tokens = refs[17]
     blocks = refs[18:21]
-    pairs, pairs_right = refs[21:23]
-    outs = refs[23:]
+    pairs, pairs_right, downs = refs[21:24]
+    outs = refs[24:]
     flat, flat_right, rights = outs[:3]
-    outs = outs[3:]
+    early = outs[3 : 3 + EARLY]
+    outs = outs[3 + EARLY :]
     wholes = outs[:3]
     cot_wholes = outs[3 : 3 + EXP_FF]
     (
@@ -499,6 +501,10 @@
             push_own(n + window)
         if n - 2 < EXP_FF:
             flatten(n - 2)
+        if n == total - 1:
+            for j in range(1, EARLY + 1):
+                which = jnp.bitwise_xor(row // replicas, j)
+                send_to(downs.at[which], early[j - 1], across[j * replicas])
         for m in range(n - behind + 1) if n == 2 else [n - behind]:
             if 0 <= m < total:
                 if m == 0:
@@ -526,7 +532,7 @@
     return wholes[array].at[pl.ds(start, pair)]
 
 
-def front(smalls, lefts, tokens, blocks, pairs, pairs_right, parts, cols, replicas):
+def front(smalls, lefts, tokens, blocks, pairs, pairs_right, downs, parts, cols, replicas):
     hbm = pl.BlockSpec(memory_space=pl.ANY)
     vmem = pl.BlockSpec(memory_space=pltpu.VMEM)
     smem = pl.BlockSpec(memory_space=pltpu.SMEM)
@@ -541,7 +547,7 @@
     n_chunks = sum(block.shape[0] for block in blocks) // 2
     per_chunk = 8 if parts == 8 else parts - 1
     remotes = (
-        n_chunks * per_chunk + (cols - 1) * (1 + EXP_FF) + EXP_FF - 1 + 2 * (parts - 1)
+        n_chunks * per_chunk + (cols - 1) * (1 + EXP_FF) + EXP_FF - 1 + 2 * (parts - 1) + EARLY
     )
     return pl.pallas_call(
         functools.partial(front_kernel, parts, cols, replicas),
@@ -550,6 +556,7 @@
             shape((pairs_right.shape[0], flat[2]), BF16),
             shape((4 * RANK, head_width), BF16),
         ]
+        + [shape(downs.shape[1:], BF16)] * EARLY
         + [shape((b.shape[0], width, head_width), BF16) for b in blocks]
         + [shape((CAP_FF, width), BF16)] * EXP_FF
         + [
@@ -571,8 +578,8 @@
             shape((rows, 1), F32),
             shape((parts, 8, LANES), F32),
         ],
-        in_specs=[smem] * 2 + [vmem] * 15 + [hbm] * 6,
-        out_specs=[hbm, hbm, vmem] + [hbm] * (3 + EXP_FF) + [vmem] * 17,
+        in_specs=[smem] * 2 + [vmem] * 15 + [hbm] * 7,
+        out_specs=[hbm, hbm, vmem] + [hbm] * (EARLY + 3 + EXP_FF) + [vmem] * 17,
         scratch_shapes=[
             pltpu.VMEM((count, width), BF16),
             pltpu.VMEM((EXP_FF, CAP_FF, wide), BF16),
@@ -592,7 +599,7 @@
         compiler_params=pltpu.CompilerParams(
             collective_id=1, has_side_effects=True, vmem_limit_bytes=62 * 2**20
         ),
-    )(*smalls, *lefts, tokens, *blocks, pairs, pairs_right)
+    )(*smalls, *lefts, tokens, *blocks, pairs, pairs_right, downs)
 
 
 def middle_back_kernel(cols, replicas, *refs):
@@ -1131,10 +1138,16 @@
     adapter, norm, router, route, low_rows, low_in = refs[:6]
     sources = refs[6:11]
     weights = refs[11:13]
-    outs = refs[13:]
-    extra_chunks = parts_axis - 1
-    chunks = [(None,) + tuple(outs[n * extra_chunks : (n + 1) * extra_chunks]) for n in (0, 1)]
-    outs = outs[2 * extra_chunks :]
+    early = refs[13 : 13 + EARLY]
+    outs = refs[13 + EARLY :]
+    chunks = [[None, *outs[: parts_axis - 1]], [None]]
+    outs = outs[parts_axis - 1 :]
+    for m in range(1, parts_axis):
+        if m % replicas == 0 and m <= EARLY * replicas:
+            chunks[1].append(early[m // replicas - 1])
+        else:
+            chunks[1].append(outs[0])
+            outs = outs[1:]
     hids = outs[:EXP_FF]
     hidden_out, middle, stat, totals = outs[EXP_FF : EXP_FF + 4]
     scratch = outs[EXP_FF + 4 :]
@@ -1175,7 +1188,7 @@
     piece_copies = [
         [
             send_to(weights[n].at[jnp.bitwise_xor(expert, j)], chunks[n][j * replicas], across[j - 1])
-            for n in (0, 1)
+            for n in ((0,) if j <= EARLY else (0, 1))
         ]
         for j in range(1, EXP_FF)
     ]
@@ -1184,6 +1197,10 @@
         for i in range(1, replicas)
         for n in (0, 1)
     ]
+    for j in range(1, EARLY + 1):
+        for i in range(1, replicas):
+            m = j * replicas
+            sibling_copies.append(send_to(chunks[1][m], chunks[1][m + i], beside[i - 1]))
     for copy in near:
         copy.wait()
 
@@ -1296,7 +1313,7 @@
     own = pltpu.make_async_copy(message.at[pl.ds(0, CAP_FF)], hids[0], local.at[7])
     own.start()
     for j in range(1, EXP_FF):
-        for n in (0, 1):
+        for n in range(len(piece_copies[j - 1])):
             piece_copies[j - 1][n].wait_recv()
             for i in range(1, replicas):
                 m = j * replicas
@@ -1309,7 +1326,7 @@
     own.wait()
 
 
-def middle_forward(adapter, norm, router, route, low_rows, low_in, sources, weights, parts_axis, cols, replicas):
+def middle_forward(adapter, norm, router, route, low_rows, low_in, sources, weights, early, parts_axis, cols, replicas):
     hbm = pl.BlockSpec(memory_space=pl.ANY)
     vmem = pl.BlockSpec(memory_space=pltpu.VMEM)
     smem = pl.BlockSpec(memory_space=pltpu.SMEM)
@@ -1321,7 +1338,7 @@
     return pl.pallas_call(
         functools.partial(middle_kernel, parts_axis, cols, replicas),
         out_shape=[jax.ShapeDtypeStruct(weights[0].shape[1:], BF16)] * (parts_axis - 1)
-        + [jax.ShapeDtypeStruct(weights[1].shape[1:], BF16)] * (parts_axis - 1)
+        + [jax.ShapeDtypeStruct(weights[1].shape[1:], BF16)] * (parts_axis - 1 - EARLY)
         + [jax.ShapeDtypeStruct((CAP_FF, full), BF16)] * EXP_FF
         + [
             jax.ShapeDtypeStruct((count, width), BF16),
@@ -1329,8 +1346,8 @@
             jax.ShapeDtypeStruct((count, LANES), F32),
             jax.ShapeDtypeStruct((count, LANES), F32),
         ],
-        in_specs=[smem] + [vmem] * 5 + [hbm] * 7,
-        out_specs=[hbm] * (2 * parts_axis - 1 + EXP_FF) + [vmem] * 3,
+        in_specs=[smem] + [vmem] * 5 + [hbm] * (7 + EARLY),
+        out_specs=[hbm] * (2 * parts_axis - 1 - EARLY + EXP_FF) + [vmem] * 3,
         scratch_shapes=[pltpu.VMEM(source.shape, source.dtype) for source in sources]
         + [
             pltpu.VMEM((cols, count, wide), F32),
@@ -1350,7 +1367,7 @@
         compiler_params=pltpu.CompilerParams(
             collective_id=3, has_side_effects=True, vmem_limit_bytes=62 * 2**20
         ),
-    )(adapter, norm, router, route, low_rows, low_in, *sources, *weights)
+    )(adapter, norm, router, route, low_rows, low_in, *sources, *weights, *early)
 
 
 def ffn_kernel(parts, depth, width, units, *refs):
@@ -1581,6 +1598,33 @@
         inner_flat,
         inner_right_flat,
         rights,
+        *outs,
+    ) = front(
+        [
+            lengths,
+            adapter_pick,
+            attn_route.T,
+            ffn_route.T,
+            cotangent,
+            norm_one[None, :],
+            router_attn.T,
+            *turns,
+            query_right,
+            kv_right,
+            out_right,
+        ],
+        lefts_own,
+        inputs,
+        [kv_weight, query_weight, out_weight],
+        padded(inner_weight),
+        padded(inner_right).reshape(ADAPT * RANK, 2, units + padding),
+        down_flat,
+        rows_axis,
+        cols,
+        replicas,
+    )
+    early = outs[:EARLY]
+    (
         kv_full,
         query_full,
         out_full,
@@ -1602,29 +1646,7 @@
         ranks,
         gate_rows,
         picks,
-    ) = front(
-        [
-            lengths,
-            adapter_pick,
-            attn_route.T,
-            ffn_route.T,
-            cotangent,
-            norm_one[None, :],
-            router_attn.T,
-            *turns,
-            query_right,
-            kv_right,
-            out_right,
-        ],
-        lefts_own,
-        inputs,
-        [kv_weight, query_weight, out_weight],
-        padded(inner_weight),
-        padded(inner_right).reshape(ADAPT * RANK, 2, units + padding),
-        rows_axis,
-        cols,
-        replicas,
-    )
+    ) = outs[EARLY:]
     picks = picks[:, 0, 0].astype(jnp.int32)
     ffn_right = [inner_right_flat, padded(down_right).reshape(ADAPT * RANK, units + padding)]
 
@@ -1637,13 +1659,21 @@
         low_in,
         [out_rows, picks_attn, picks_ffn, lefts, inputs],
         [inner_flat, down_flat],
+        early,
         rows_axis,
         cols,
         replicas,
     )
     inners = [inner_flat, *outs[: rows_axis - 1]]
-    lasts = [down_flat, *outs[rows_axis - 1 : 2 * rows_axis - 2]]
-    hidden_in = outs[2 * rows_axis - 2 :]
+    outs = outs[rows_axis - 1 :]
+    lasts = [down_flat]
+    for m in range(1, rows_axis):
+        if m % replicas == 0 and m <= EARLY * replicas:
+            lasts.append(early[m // replicas - 1])
+        else:
+            lasts.append(outs[0])
+            outs = outs[1:]
+    hidden_in = outs
     results = feed_forward(hidden_in, cot_rows, inners, lasts, ffn_right)
     grad_middle, grad_full, totals, branch_ffn, low_down_part = middle_back(
         results[:EXP_FF],

time: 572 us -> 556 us (0.972)
  Pallas kernels: 532 us -> 516 us
    pallas_call x1, Pallas kernels: 134 us -> 118 us  [middle_forward(): pl.pallas_call(functools.partial(middle_kernel, parts_axis, cols, replica...]
where the time goes in v9:
time: 556 us; the launch traced here: 550 us
  Pallas kernels  516 us (93%)
  between operations  15.7 us (3%)
  local copies, waits for them, and re-layouts  10.5 us (2%)
  other arithmetic  7.64 us (1%)
    pallas_call x1, Pallas kernels, front(): pl.pallas_call(functools.partial(front_kernel, parts, cols, replicas), ou...  192 us
    pallas_call x1, Pallas kernels, middle_forward(): pl.pallas_call(functools.partial(middle_kernel, parts_axis, cols, replica...  118 us
    pallas_call x1, Pallas kernels, tail(): pl.pallas_call(functools.partial(tail_kernel, parts_axis, cols), out_shap...  83.6 us
    pallas_call x1, Pallas kernels, feed_forward(): pl.pallas_call(functools.partial(ffn_kernel, parts, depth, width, units),...  63.9 us
    pallas_call x1, Pallas kernels, middle_back(): pl.pallas_call(functools.partial(middle_back_kernel, cols, replicas), out...  59.3 us
  transfers between devices with their start and end apart: 1, of which 0 were waited for; matrix products, arithmetic and copies ran while one was open for 1% of the time, Pallas kernels for 15%

profile of v9, /device:TPU:9, one launch (start us, length us, event | category | flops | bytes accessed | tf_op | source)
XLA Modules:
  0.0 550.4 jit_solution(6278195257993370644)
XLA Ops:
  7.2 0.0 all-reduce.3.cloned.1.call-start
  8.5 0.5 fusion
  9.1 0.8 pad_maximum_fusion.1
  9.9 191.6 %shard_map.328 = (bf16[4,256,2816]{2,1,0:T(8,128)(2,1)}, bf16[128,2816]{1,0:T(8,128)(2,1)}, bf16[64,512]{1,0:T(8,128)(2,1)}, bf16[256,1408]{1,0:T(8,128)(2,1)}, ...) custom-call(s32[1]{0:T(128)S(6)} %copy.55.refs_0_, ...), custom_call_target="tpu_custom_call" | custom-call | tf_op jit(solution)/shard_map/pallas_call | solution.py:552
  201.5 118.1 %shard_map.329 = (bf16[256,2816]{1,0:T(8,128)(2,1)}, bf16[256,2816]{1,0:T(8,128)(2,1)}, bf16[256,2816]{1,0:T(8,128)(2,1)}, bf16[256,2816]{1,0:T(8,128)(2,1)}, bf...) custom-call(s32[1]{0:T(128)S(6)} %copy.56.refs_1_.refs_0_.refs_8_, ...), custom_call_target="tpu_custom_call" | custom-call | tf_op jit(solution)/shard_map/pallas_call | solution.py:1338
  319.7 63.9 %shard_map.330 = (bf16[160,2304]{1,0:T(8,128)(2,1)}, bf16[160,2304]{1,0:T(8,128)(2,1)}, bf16[160,2304]{1,0:T(8,128)(2,1)}, bf16[160,2304]{1,0:T(8,128)(2,1)}, bf...) custom-call(bf16[160,2432]{1,0:T(8,128)(2,1)} %get-tuple-element.109, ...), custom_call_target="tpu_custom_call" | custom-call | tf_op jit(solution)/shard_map/pallas_call | solution.py:1522
  383.5 59.3 %shard_map.331 = (f32[256,512]{1,0:T(8,128)}, bf16[256,2048]{1,0:T(8,128)(2,1)}, f32[256,128]{1,0:T(8,128)}, bf16[256,2048]{1,0:T(8,128)(2,1)}, f32[256,128]{1,0:T(8,128)}) custom-call(bf16[160,2304]{1,0:T(8,128)(2,1)} %get-tuple-element.130.refs_0_, bf16[160,2304]{1,0:T(8,128)(2,1)} %get-tuple-element.131.refs_1_, ...), custom_call_target="tpu_custom_call" | custom-call | tf_op jit(solution)/shard_map/pallas_call | solution.py:741
  442.8 0.0 all-reduce.3.cloned.1.call-update
  442.8 1.5 convert_reduce_fusion.refs_0_
  444.3 83.6 %shard_map.332 = (bf16[256,512]{1,0:T(8,128)(2,1)}, f32[256,512]{1,0:T(8,128)}, f32[8,16,256]{2,1,0:T(8,128)}, f32[8,16,256]{2,1,0:T(8,128)}, f32[8,16,256]{2,1,...) custom-call(s32[8]{0:T(128)} %convert_reduce_fusion.refs_0_, ...), custom_call_target="tpu_custom_call" | custom-call | tf_op jit(solution)/shard_map/pallas_call | solution.py:1099
  527.9 1.1 pad_maximum_fusion
  529.0 1.2 copy.42
  530.2 0.0 all-reduce.3.cloned.1.call-done
  530.2 0.0 copy-start.1
  530.2 1.6 copy.41
  531.8 1.5 copy.40
  533.4 0.0 copy-done.1
  533.4 0.9 convert.4
  534.3 0.0 copy-start.4
  534.3 0.0 copy-start
  534.3 2.8 maximum_convert_fusion
  537.1 0.0 copy-done.4
  537.1 0.0 copy-start.9
  537.1 0.0 copy-start.3
  537.1 0.0 copy-start.8
  537.1 0.0 copy-start.7
  537.1 0.0 copy-start.2
  537.1 0.7 copy.57
  537.8 0.0 copy-done
  537.8 0.0 copy-start.6
  537.8 0.0 copy-start.5
  537.8 0.8 copy.58
  538.6 0.0 copy-done.9
  538.6 0.7 copy.59
  539.3 0.0 copy-done.3
  539.3 0.7 copy.60
  540.0 0.0 copy-done.8
  540.0 0.7 copy.61
  540.6 0.0 copy-done.7
  540.6 0.7 copy.62
  541.3 0.0 copy-done.2
  541.3 0.7 copy.63
  542.0 0.0 copy-done.6
  542.0 0.7 copy.64
  542.6 0.0 copy-done.5
  542.6 0.7 copy.65
  (2 shorter events, 0.0 us)
Async XLA Ops:
  7.2 523.0 %all-reduce.3.cloned.1.call-start = ((), (), s32[]{:S(2)}) async-start(), calls=%async_computation | async-start | bytes 2162688 | tf_op jit(solution)/shard_map/psum | solution.py:1690
  530.2 3.1 copy-start.1
  534.3 2.8 copy-start.4
  534.3 3.5 copy-start
  537.1 1.5 copy-start.9
  537.1 2.2 copy-start.3
  537.1 2.9 copy-start.8
  537.1 3.6 copy-start.7
  537.1 4.2 copy-start.2
  537.8 4.2 copy-start.6
  537.8 4.8 copy-start.5
Sparse Core Ops, SparseCore 0:
  443.0 58.8 all-reduce.2

commit v10 on v9

--- a/solution.py
+++ b/solution.py
@@ -1400,16 +1400,25 @@
         near = block.at[pl.ds(width, LANES), pl.ds(start, size)]
         copies.append(pltpu.make_async_copy(rights[n], near, sems.at[3 * EXP_FF + n]))
     expert = row // replicas
+    step = 2 * LANES
+    full = units // step
+    early_tiles = full // 2 + 1
+    early = early_tiles * step
+    second = []
     for m in range(parts):
         owner = jnp.bitwise_xor(row, m)
         where = pl.ds(pl.multiple_of(owner * depth, depth), depth)
         inner = inners[m] if m else inners[0].at[expert]
         last = lasts[m] if m else lasts[0].at[expert]
-        near = block.at[where, pl.ds(0, 2 * units)]
-        copies.append(pltpu.make_async_copy(inner, near, sems.at[3 * EXP_FF + 2 + m]))
-        near = block.at[where, pl.ds(2 * units, units)]
-        copies.append(pltpu.make_async_copy(last, near, sems.at[3 * EXP_FF + 2 + parts + m]))
-    for copy in copies:
+        for n, (source, start) in enumerate(((inner, 0), (inner, units), (last, 0))):
+            for late, (begin, size) in enumerate(((0, early), (early, units - early))):
+                if size:
+                    near = block.at[where, pl.ds(n * units + begin, size)]
+                    near_sem = sems.at[3 * EXP_FF + 2 + 6 * m + 3 * late + n]
+                    far = source.at[:, pl.ds(start + begin, size)]
+                    copy = pltpu.make_async_copy(far, near, near_sem)
+                    (second if late else copies).append(copy)
+    for copy in copies + second:
         copy.start()
     for copy in copies:
         copy.wait()
@@ -1431,10 +1440,14 @@
         act[:, here] = (grad * up * sig * (1.0 + gate * (1.0 - sig))).astype(BF16)
         act[:, up_here] = (grad * gate * sig).astype(BF16)
 
-    step = 2 * LANES
-    full = units // step
-
-    @pl.loop(0, full)
+    @pl.loop(0, early_tiles)
+    def _(i):
+        forward(pl.multiple_of(i * step, step), step)
+
+    for copy in second:
+        copy.wait()
+
+    @pl.loop(early_tiles, full)
     def _(i):
         forward(pl.multiple_of(i * step, step), step)
 
@@ -1533,7 +1546,7 @@
             pltpu.VMEM((rows, triple), BF16),
             pltpu.VMEM((rows, 1), F32),
             pltpu.VMEM((EXP_FF - 1, CAP_FF, wide + LANES), BF16),
-            pltpu.SemaphoreType.DMA((3 * EXP_FF + 2 + 2 * parts,)),
+            pltpu.SemaphoreType.DMA((3 * EXP_FF + 2 + 6 * parts,)),
             pltpu.SemaphoreType.DMA((remotes,)),
             pltpu.SemaphoreType.DMA((remotes,)),
         ],

time: 556 us -> 554 us (level)
  no operation moved by 1% of the time
where the time goes in v10:
time: 554 us; the launch traced here: 548 us
  Pallas kernels  514 us (93%)
  between operations  15.7 us (3%)
  local copies, waits for them, and re-layouts  10.5 us (2%)
  other arithmetic  7.64 us (1%)
    pallas_call x1, Pallas kernels, front(): pl.pallas_call(functools.partial(front_kernel, parts, cols, replicas), ou...  192 us
    pallas_call x1, Pallas kernels, middle_forward(): pl.pallas_call(functools.partial(middle_kernel, parts_axis, cols, replica...  118 us
    pallas_call x1, Pallas kernels, tail(): pl.pallas_call(functools.partial(tail_kernel, parts_axis, cols), out_shap...  83.6 us
    pallas_call x1, Pallas kernels, feed_forward(): pl.pallas_call(functools.partial(ffn_kernel, parts, depth, width, units),...  61.9 us
    pallas_call x1, Pallas kernels, middle_back(): pl.pallas_call(functools.partial(middle_back_kernel, cols, replicas), out...  59.2 us
  transfers between devices with their start and end apart: 1, of which 0 were waited for; matrix products, arithmetic and copies ran while one was open for 1% of the time, Pallas kernels for 15%

profile of v10, /device:TPU:9, one launch (start us, length us, event | category | flops | bytes accessed | tf_op | source)
XLA Modules:
  0.0 548.4 jit_solution(8305962719100637622)
XLA Ops:
  7.2 0.0 all-reduce.3.cloned.1.call-start
  8.5 0.5 fusion
  9.1 0.8 pad_maximum_fusion.1
  9.9 191.6 %shard_map.328 = (bf16[4,256,2816]{2,1,0:T(8,128)(2,1)}, bf16[128,2816]{1,0:T(8,128)(2,1)}, bf16[64,512]{1,0:T(8,128)(2,1)}, bf16[256,1408]{1,0:T(8,128)(2,1)}, ...) custom-call(s32[1]{0:T(128)S(6)} %copy.55.refs_0_, ...), custom_call_target="tpu_custom_call" | custom-call | tf_op jit(solution)/shard_map/pallas_call | solution.py:552
  201.5 118.1 %shard_map.329 = (bf16[256,2816]{1,0:T(8,128)(2,1)}, bf16[256,2816]{1,0:T(8,128)(2,1)}, bf16[256,2816]{1,0:T(8,128)(2,1)}, bf16[256,2816]{1,0:T(8,128)(2,1)}, bf...) custom-call(s32[1]{0:T(128)S(6)} %copy.56.refs_1_.refs_0_.refs_8_, ...), custom_call_target="tpu_custom_call" | custom-call | tf_op jit(solution)/shard_map/pallas_call | solution.py:1338
  319.7 61.9 %shard_map.330 = (bf16[160,2304]{1,0:T(8,128)(2,1)}, bf16[160,2304]{1,0:T(8,128)(2,1)}, bf16[160,2304]{1,0:T(8,128)(2,1)}, bf16[160,2304]{1,0:T(8,128)(2,1)}, bf...) custom-call(bf16[160,2432]{1,0:T(8,128)(2,1)} %get-tuple-element.109, ...), custom_call_target="tpu_custom_call" | custom-call | tf_op jit(solution)/shard_map/pallas_call | solution.py:1535
  381.6 59.2 %shard_map.331 = (f32[256,512]{1,0:T(8,128)}, bf16[256,2048]{1,0:T(8,128)(2,1)}, f32[256,128]{1,0:T(8,128)}, bf16[256,2048]{1,0:T(8,128)(2,1)}, f32[256,128]{1,0:T(8,128)}) custom-call(bf16[160,2304]{1,0:T(8,128)(2,1)} %get-tuple-element.130.refs_0_, bf16[160,2304]{1,0:T(8,128)(2,1)} %get-tuple-element.131.refs_1_, ...), custom_call_target="tpu_custom_call" | custom-call | tf_op jit(solution)/shard_map/pallas_call | solution.py:741
  440.9 0.0 all-reduce.3.cloned.1.call-update
  440.9 1.5 convert_reduce_fusion.refs_0_
  442.4 83.6 %shard_map.332 = (bf16[256,512]{1,0:T(8,128)(2,1)}, f32[256,512]{1,0:T(8,128)}, f32[8,16,256]{2,1,0:T(8,128)}, f32[8,16,256]{2,1,0:T(8,128)}, f32[8,16,256]{2,1,...) custom-call(s32[8]{0:T(128)} %convert_reduce_fusion.refs_0_, ...), custom_call_target="tpu_custom_call" | custom-call | tf_op jit(solution)/shard_map/pallas_call | solution.py:1099
  526.0 1.1 pad_maximum_fusion
  527.1 1.2 copy.42
  528.3 0.0 all-reduce.3.cloned.1.call-done
  528.3 0.0 copy-start.1
  528.3 1.6 copy.41
  529.9 1.5 copy.40
  531.4 0.0 copy-done.1
  531.4 0.9 convert.4
  532.3 0.0 copy-start.4
  532.3 0.0 copy-start
  532.3 2.8 maximum_convert_fusion
  535.1 0.0 copy-done.4
  535.1 0.0 copy-start.9
  535.1 0.0 copy-start.3
  535.1 0.0 copy-start.8
  535.1 0.0 copy-start.7
  535.1 0.0 copy-start.2
  535.1 0.7 copy.57
  535.8 0.0 copy-done
  535.8 0.0 copy-start.6
  535.8 0.0 copy-start.5
  535.8 0.8 copy.58
  536.6 0.0 copy-done.9
  536.6 0.7 copy.59
  537.3 0.0 copy-done.3
  537.3 0.7 copy.60
  538.0 0.0 copy-done.8
  538.0 0.7 copy.61
  538.7 0.0 copy-done.7
  538.7 0.7 copy.62
  539.3 0.0 copy-done.2
  539.3 0.7 copy.63
  540.0 0.0 copy-done.6
  540.0 0.7 copy.64
  540.7 0.0 copy-done.5
  540.7 0.7 copy.65
  (2 shorter events, 0.0 us)
Async XLA Ops:
  7.2 521.1 %all-reduce.3.cloned.1.call-start = ((), (), s32[]{:S(2)}) async-start(), calls=%async_computation | async-start | bytes 2162688 | tf_op jit(solution)/shard_map/psum | solution.py:1703
  528.3 3.1 copy-start.1
  532.3 2.8 copy-start.4
  532.3 3.5 copy-start
  535.1 1.5 copy-start.9
  535.1 2.2 copy-start.3
  535.1 2.9 copy-start.8
  535.1 3.6 copy-start.7
  535.1 4.2 copy-start.2
  535.8 4.2 copy-start.6
  535.8 4.8 copy-start.5
Sparse Core Ops, SparseCore 0:
  441.0 58.8 all-reduce.2
